TPU v7x, 32 devices: a whole 2x2x4 slice. The times are simulated.
32 devices in a mesh: groups: 2 (over y), patch: 16 (over z, x, core).
Axes of the slice: x: 2, y: 2, z: 4, core: 2. Of those that a mesh axis runs over, the one named last changes fastest.
Arguments:
- nodes: bfloat16 [8192, 512], P(('groups', 'patch')), parts along dimension 0, may hold values from -6 to 6
- fine_edges: bfloat16 [16384, 512], P(('groups', 'patch')), parts along dimension 0, may hold values from -6 to 6
- coarse_edges: bfloat16 [4096, 512], P(('groups', 'patch')), parts along dimension 0, may hold values from -6 to 6
- fine_send: int32 [16384], P(('groups', 'patch')), parts along dimension 0, may hold values from 0 to 767
- fine_recv: int32 [16384], P(('groups', 'patch')), parts along dimension 0, may hold values from 0 to 255
- coarse_send: int32 [4096], P(('groups', 'patch')), parts along dimension 0, may hold values from 0 to 127
- coarse_recv: int32 [4096], P(('groups', 'patch')), parts along dimension 0, may hold values from 0 to 127
- halo_rows: int32 [32, 4, 128], P(('groups', 'patch')), parts along dimension 0, may hold values from 0 to 255
- edge_count: int32 [32], P(('groups', 'patch')), parts along dimension 0, may hold values from 1 to 512, 4915 in all
- edge_w1: bfloat16 [1536, 512], replicated, may hold values from -0.15625 to 0.15625
- edge_w2: bfloat16 [512, 512], replicated, may hold values from -0.25 to 0.25
- edge_gain: float32 [512], replicated, may hold values from 0.1 to 1.9
- node_w1: bfloat16 [1024, 512], replicated, may hold values from -0.1875 to 0.1875
- node_w2: bfloat16 [512, 512], replicated, may hold values from -0.25 to 0.25
- node_gain: float32 [512], replicated, may hold values from 0.1 to 1.9
- d_nodes: bfloat16 [8192, 512], P(('groups', 'patch')), parts along dimension 0, may hold values from -6 to 6
- d_fine: bfloat16 [16384, 512], P(('groups', 'patch')), parts along dimension 0, may hold values from -6 to 6
- d_coarse: bfloat16 [4096, 512], P(('groups', 'patch')), parts along dimension 0, may hold values from -6 to 6
Outputs:
- new_nodes: bfloat16 [8192, 512], P(('groups', 'patch')), parts along dimension 0
- new_fine: bfloat16 [16384, 512], P(('groups', 'patch')), parts along dimension 0
- new_coarse: bfloat16 [4096, 512], P(('groups', 'patch')), parts along dimension 0
- g_nodes: bfloat16 [8192, 512], P(('groups', 'patch')), parts along dimension 0
- g_fine: bfloat16 [16384, 512], P(('groups', 'patch')), parts along dimension 0
- g_coarse: bfloat16 [4096, 512], P(('groups', 'patch')), parts along dimension 0
- g_edge_w1: float32 [3072, 512], P(('groups', 'patch')), parts along dimension 0
- g_edge_w2: float32 [1024, 512], P(('groups', 'patch')), parts along dimension 0
- g_node_w1: float32 [2048, 512], P(('groups', 'patch')), parts along dimension 0
- g_node_w2: float32 [1024, 512], P(('groups', 'patch')), parts along dimension 0
There are 2 independent parts, one for each index of `groups`. A program takes and returns all parts, laid end to end along the dimension named above; an argument that names none is the same for every part. Nothing has to cross between parts.
Inputs may be any that keep to these rules, and one draw needn't show every extreme that they name: `halo_rows`: local node rows of the sending patch, for the slot order of the steps. `fine_send`: rows below 256 are the patch's own nodes; the others index the received tiles in slot order. `coarse_send`: coarse node c is row c mod 8 of patch c // 8. The live fine edges of a patch are its first edge_count slots; in every draw some patch has all 512 slots live.
All inputs are finite; a program needn't handle non-finite values. No bound on the sum of `edge_count` on one device may be relied on, other than what follows from the above.
Results may differ from a plain program's by a relative error of at most 0.007.
Values may be sent and summed in bfloat16 or wider, within the bound.
No kernel may reach another device: no remote copies, remote signals or barrier semaphores. Data moves between devices by JAX's collectives and lax.ppermute only.
A program may use at most 128 MiB of HBM per device.

v0:
```python
import jax
import jax.numpy as jnp
from jax import lax
from jax.sharding import PartitionSpec as P

COARSE_DEV = 8


EPSILON = 1e-05


def passed_along(block, axis, distance):
    devices = range(lax.axis_size(axis))
    route = [((i - distance) % len(devices), i) for i in devices]
    return lax.ppermute(block, axis, route)


def swish_and_slope(pre_act):
    sigmoid = jax.nn.sigmoid(pre_act)
    return (pre_act * sigmoid, sigmoid * (1.0 + pre_act * (1.0 - sigmoid)))


def mlp_forward(inputs, first_w, second_w, gain):
    pre_act = jnp.dot(inputs, first_w, preferred_element_type=jnp.float32)
    activ, slope = swish_and_slope(pre_act)
    hidden = activ.astype(jnp.bfloat16)
    output = jnp.dot(hidden, second_w, preferred_element_type=jnp.float32)
    centred = output - jnp.mean(output, axis=-1, keepdims=True)
    inv_std = lax.rsqrt(jnp.mean(centred * centred, axis=-1, keepdims=True) + EPSILON)
    normed = centred * inv_std
    return (normed * gain, (hidden, slope, normed, inv_std))


def mlp_backward(inputs, first_w, second_w, gain, saved, cotan):
    hidden, slope, normed, inv_std = saved
    scaled = cotan * gain
    back_out = inv_std * (
        scaled
        - jnp.mean(scaled, axis=-1, keepdims=True)
        - normed * jnp.mean(scaled * normed, axis=-1, keepdims=True)
    )
    back_out = back_out.astype(jnp.bfloat16)
    grad_second = lax.dot_general(
        hidden, back_out, (((0,), (0,)), ((), ())), preferred_element_type=jnp.float32
    )
    back_hidden = lax.dot_general(
        back_out, second_w, (((1,), (1,)), ((), ())), preferred_element_type=jnp.float32
    )
    back_pre = (back_hidden * slope).astype(jnp.bfloat16)
    grad_first = lax.dot_general(
        inputs, back_pre, (((0,), (0,)), ((), ())), preferred_element_type=jnp.float32
    )
    back_in = lax.dot_general(
        back_pre, first_w, (((1,), (1,)), ((), ())), preferred_element_type=jnp.float32
    )
    return (grad_first, grad_second, back_in)


def peer_offsets(hops):
    return list(range(1, hops + 1)) + [-step_k for step_k in range(1, hops + 1)]


def local(
    nodes,
    fine_edges,
    coarse_edges,
    fine_send,
    fine_recv,
    coarse_send,
    coarse_recv,
    halo_rows,
    edge_count,
    edge_w1,
    edge_w2,
    edge_gain,
    node_w1,
    node_w2,
    node_gain,
    d_nodes,
    d_fine,
    d_coarse,
):
    count_nodes = nodes.shape[0]
    width = nodes.shape[1]
    count_edges = fine_edges.shape[0]
    tile_rows = halo_rows[0]
    hops = tile_rows.shape[0] // 2
    tile_size = tile_rows.shape[1]
    offsets = peer_offsets(hops)
    tiles = nodes[tile_rows.reshape(-1)].reshape(2 * hops, tile_size, width)
    received = []
    for slot, offset in enumerate(offsets):
        received.append(passed_along(tiles[slot], "patch", offset))
    space = jnp.concatenate([nodes] + received, 0)
    coarse_all = lax.all_gather(nodes[:COARSE_DEV], "patch", axis=0, tiled=True)
    total_coarse = coarse_all.shape[0]
    fine_in = jnp.concatenate([fine_edges, space[fine_send], nodes[fine_recv]], 1)
    coarse_in = jnp.concatenate([coarse_edges, coarse_all[coarse_send], coarse_all[coarse_recv]], 1)
    inputs = jnp.concatenate([fine_in, coarse_in], 0)
    alive = (jnp.arange(count_edges) < edge_count[0]).astype(jnp.float32)[:, None]
    message, saved = mlp_forward(inputs, edge_w1, edge_w2, edge_gain)
    fine_msg = message[:count_edges] * alive
    coarse_msg = message[count_edges:]
    new_fine = (fine_edges.astype(jnp.float32) + fine_msg).astype(jnp.bfloat16)
    new_coarse = (coarse_edges.astype(jnp.float32) + coarse_msg).astype(jnp.bfloat16)
    fine_agg = jax.ops.segment_sum(fine_msg, fine_recv, num_segments=count_nodes)
    partial_agg = jax.ops.segment_sum(coarse_msg, coarse_recv, num_segments=total_coarse)
    whole_agg = lax.psum(partial_agg, "patch")
    share = lax.dynamic_slice_in_dim(whole_agg, lax.axis_index("patch") * COARSE_DEV, COARSE_DEV, 0)
    aggregate = fine_agg.at[:COARSE_DEV].add(share)
    node_inputs = jnp.concatenate([nodes, aggregate.astype(jnp.bfloat16)], 1)
    update, node_saved = mlp_forward(node_inputs, node_w1, node_w2, node_gain)
    new_nodes = (nodes.astype(jnp.float32) + update).astype(jnp.bfloat16)
    node_cot = d_nodes.astype(jnp.float32)
    grad_nw1, grad_nw2, node_dz = mlp_backward(
        node_inputs, node_w1, node_w2, node_gain, node_saved, node_cot
    )
    d_aggregate = node_dz[:, width:]
    dagg_coarse = lax.all_gather(d_aggregate[:COARSE_DEV], "patch", axis=0, tiled=True)
    cot_fine = alive * (d_fine.astype(jnp.float32) + d_aggregate[fine_recv])
    cot_coarse = d_coarse.astype(jnp.float32) + dagg_coarse[coarse_recv]
    grad_ew1, grad_ew2, back_in = mlp_backward(
        inputs, edge_w1, edge_w2, edge_gain, saved, jnp.concatenate([cot_fine, cot_coarse], 0)
    )
    fine_dz = back_in[:count_edges]
    coarse_dz = back_in[count_edges:]
    g_fine = (d_fine.astype(jnp.float32) + fine_dz[:, :width]).astype(jnp.bfloat16)
    g_coarse = (d_coarse.astype(jnp.float32) + coarse_dz[:, :width]).astype(jnp.bfloat16)
    space_grad = jax.ops.segment_sum(
        fine_dz[:, width : 2 * width], fine_send, num_segments=count_nodes + 2 * hops * tile_size
    )
    grad_nodes = node_cot + node_dz[:, :width] + space_grad[:count_nodes]
    grad_nodes = grad_nodes + jax.ops.segment_sum(
        fine_dz[:, 2 * width :], fine_recv, num_segments=count_nodes
    )
    for slot, offset in enumerate(offsets):
        piece = space_grad[count_nodes + slot * tile_size : count_nodes + (slot + 1) * tile_size]
        returned = passed_along(piece.astype(jnp.bfloat16), "patch", -offset).astype(piece.dtype)
        grad_nodes = grad_nodes.at[tile_rows[slot]].add(returned)
    coarse_part = jax.ops.segment_sum(
        coarse_dz[:, width : 2 * width], coarse_send, num_segments=total_coarse
    )
    coarse_part = coarse_part + jax.ops.segment_sum(
        coarse_dz[:, 2 * width :], coarse_recv, num_segments=total_coarse
    )
    grad_nodes = grad_nodes.at[:COARSE_DEV].add(
        lax.psum_scatter(coarse_part, "patch", scatter_dimension=0, tiled=True)
    )
    g_nodes = grad_nodes.astype(jnp.bfloat16)
    weight_parts = (
        lax.psum_scatter(grad_ew1, "patch", scatter_dimension=0, tiled=True),
        lax.psum_scatter(grad_ew2, "patch", scatter_dimension=0, tiled=True),
        lax.psum_scatter(grad_nw1, "patch", scatter_dimension=0, tiled=True),
        lax.psum_scatter(grad_nw2, "patch", scatter_dimension=0, tiled=True),
    )
    return (
        new_nodes,
        new_fine,
        new_coarse,
        g_nodes,
        g_fine,
        g_coarse,
        weight_parts[0],
        weight_parts[1],
        weight_parts[2],
        weight_parts[3],
    )


def solution(mesh):
    placed = (
        P(("groups", "patch"), None),
        P(("groups", "patch"), None),
        P(("groups", "patch"), None),
        P(("groups", "patch")),
        P(("groups", "patch")),
        P(("groups", "patch")),
        P(("groups", "patch")),
        P(("groups", "patch"), None, None),
        P(("groups", "patch")),
        P(),
        P(),
        P(),
        P(),
        P(),
        P(),
        P(("groups", "patch"), None),
        P(("groups", "patch"), None),
        P(("groups", "patch"), None),
    )
    return jax.shard_map(
        local,
        mesh=mesh,
        in_specs=placed,
        out_specs=(
            P(("groups", "patch"), None),
            P(("groups", "patch"), None),
            P(("groups", "patch"), None),
            P(("groups", "patch"), None),
            P(("groups", "patch"), None),
            P(("groups", "patch"), None),
            P(("groups", "patch"), None),
            P(("groups", "patch"), None),
            P(("groups", "patch"), None),
            P(("groups", "patch"), None),
        ),
        check_vma=False,
    )
```

profile of v0, /device:TPU:0, one launch (start us, length us, event | category | flops | bytes accessed | tf_op | source)
XLA Modules:
  0.0 516.6 jit_solution(16336203616627796600)
XLA Ops:
  7.2 0.8 compare_select_fusion
  8.1 3.0 gather_fusion
  11.2 0.8 fusion.56
  12.0 6.0 %collective-permute-start.3 = (bf16[128,512]{1,0:T(8,128)(2,1)}, bf16[128,512]{1,0:T(8,128)(2,1)}, u32[]{:S(2)}, u32[]{:S(2)}) collective-permute-start(bf16[128,512]{1,0:T(8,128)(2,1)} %get-tuple-element.67), channel_id=1, source_target_pairs={{2,0},{3,1},{4,2},{5,3},{6,4},{7,5},{8,6},{9,7},{10,8},{11,9},{12,... | collective-permute-start | bytes 393224 | tf_op jit(solution)/shard_map/ppermute | solution.py:15
  17.9 1.2 collective-permute-start.1
  20.0 21.2 %all_gather.6 = bf16[128,512]{1,0:T(8,128)(2,1)S(1)} all-gather(bf16[8,512]{1,0:T(8,128)(2,1)S(1)} %slice-done), channel_id=1, replica_groups=mesh['groups'=2,'patch'=16] {'patch'}, dimensions={0}, use_global_device_ids=true | all-gather | bytes 139264 | tf_op jit(solution)/shard_map/all_gather | solution.py:95
  41.2 1.5 gather_fusion.3
  42.7 1.5 gather_fusion.4
  45.1 2.0 gather_fusion.2
  47.1 2.3 copy.44
  49.3 2.0 copy.42
  51.4 0.9 constant_dynamic-update-slice_fusion.3
  52.3 0.9 constant_dynamic-update-slice_fusion.2
  53.2 0.9 constant_dynamic-update-slice_fusion.1
  54.2 0.9 constant_dynamic-update-slice_fusion
  55.1 2.6 gather_fusion.1
  57.7 3.8 multiply_convert_fusion.1
  64.1 0.8 copy.41
  65.0 2.4 scatter_custom_fusion.1
  67.5 2.4 add_convert_fusion
  69.8 2.6 copy.40
  72.5 4.6 scatter_custom_fusion
  77.0 76.7 %all-reduce.2.cloned.1.call-done = f32[128,512]{1,0:T(8,128)} async-done(((f32[128,512]{1,0:T(8,128)}), f32[128,512]{1,0:T(8,128)}) %all-reduce.2.cloned.1.call-update) | async-done | bytes 262160 | tf_op jit(solution)/shard_map/psum | solution.py:108
  153.7 0.8 fusion.41
  156.1 0.9 fusion.13
  159.4 1.0 copy-done.6
  160.4 21.6 %all_gather.7 = f32[128,512]{1,0:T(8,128)S(1)} all-gather(f32[8,512]{1,0:T(8,128)S(1)} %slice.184), channel_id=1, replica_groups=mesh['groups'=2,'patch'=16] {'patch'}, dimensions={0}, use_global_device_ids=true | all-gather | bytes 278528 | tf_op jit(solution)/shard_map/all_gather | solution.py:119
  182.0 0.9 gather_fusion.6
  182.9 0.8 copy.47
  183.7 1.8 gather_fusion.5
  185.5 1.3 copy.45
  186.8 1.1 convert_add_fusion.4
  187.9 1.4 fusion.2
  191.1 0.8 fusion
  191.9 0.9 copy-done.48
  192.8 3.1 fusion.60
  195.9 1.9 scatter_custom_fusion.9
  197.8 1.8 scatter_custom_fusion.8
  200.5 2.8 fusion.49
  203.4 1.6 fusion.61
  205.1 2.9 fusion.19
  209.3 4.4 fusion.51
  214.8 1.0 copy.50
  216.6 1.7 slice.196
  218.2 2.3 slice.195
  220.5 4.7 scatter_custom_fusion.2
  225.2 1.8 copy.55
  227.0 2.6 copy.54
  229.7 0.8 fusion.55
  230.9 4.4 collective-permute-start.5
  235.3 1.4 collective-permute-start.4
  236.7 0.9 fusion.18
  237.8 0.8 copy.53
  238.6 1.0 copy.52
  239.6 4.5 scatter_custom_fusion.3
  244.2 2.0 scatter_custom_fusion.4
  246.2 2.0 scatter_custom_fusion.5
  248.1 2.0 scatter_custom_fusion.6
  250.1 2.0 scatter_custom_fusion.7
  252.1 1.3 reduce-scatter.6.cloned.1.call-done
  254.8 59.2 %reduce-scatter.14.cloned.1.call-done = f32[32,512]{1,0:T(8,128)} async-done(((f32[512,512]{1,0:T(8,128)}), f32[32,512]{1,0:T(8,128)}) %reduce-scatter.14.cloned.1.call-update) | async-done | bytes 65552 | tf_op jit(solution)/shard_map/reduce_scatter | solution.py:154
  314.0 61.0 %reduce-scatter.10.cloned.1.call-done = f32[32,512]{1,0:T(8,128)} async-done(((f32[512,512]{1,0:T(8,128)}), f32[32,512]{1,0:T(8,128)}) %reduce-scatter.10.cloned.1.call-update) | async-done | bytes 65552 | tf_op jit(solution)/shard_map/reduce_scatter | solution.py:152
  375.0 64.8 %reduce-scatter.12.cloned.1.call-done = f32[64,512]{1,0:T(8,128)} async-done(((f32[1024,512]{1,0:T(8,128)}), f32[64,512]{1,0:T(8,128)}) %reduce-scatter.12.cloned.1.call-update) | async-done | bytes 131088 | tf_op jit(solution)/shard_map/reduce_scatter | solution.py:153
  439.7 70.0 %reduce-scatter.8.cloned.1.call-done = f32[96,512]{1,0:T(8,128)} async-done(((f32[1536,512]{1,0:T(8,128)}), f32[96,512]{1,0:T(8,128)}) %reduce-scatter.8.cloned.1.call-update) | async-done | bytes 196624 | tf_op jit(solution)/shard_map/reduce_scatter | solution.py:151
  (167 shorter events, 15.5 us)
Async XLA Ops:
  7.2 50.5 %copy-start = (bf16[1536,512]{1,0:T(8,128)(2,1)S(1)}, bf16[1536,512]{1,0:T(8,128)(2,1)}, u32[]{:S(2)}) copy-start(bf16[1536,512]{1,0:T(8,128)(2,1)} %param.31) | copy-start | bytes 4718596
  7.2 146.5 %all-reduce.2.cloned.1.call-start = ((), (), s32[]{:S(2)}) async-start(), calls=%async_computation.5 | async-start | bytes 524288 | tf_op jit(solution)/shard_map/psum | solution.py:108
  8.0 11.1 %copy-start.1 = (bf16[256,512]{1,0:T(8,128)(2,1)S(1)}, bf16[256,512]{1,0:T(8,128)(2,1)}, u32[]{:S(2)}) copy-start(bf16[256,512]{1,0:T(8,128)(2,1)} %param.22) | copy-start | bytes 786436
  11.1 8.7 %copy-start.40 = (s32[512]{0:T(512)S(1)}, s32[512]{0:T(512)}, u32[]{:S(2)}) copy-start(s32[512]{0:T(512)} %param.25) | copy-start | bytes 6148
  11.1 8.7 %copy-start.41 = (s32[512]{0:T(512)S(1)}, s32[512]{0:T(512)}, u32[]{:S(2)}) copy-start(s32[512]{0:T(512)} %param.26) | copy-start | bytes 6148
  11.1 8.8 %copy-start.45 = (s32[128]{0:T(128)S(1)}, s32[128]{0:T(128)}, u32[]{:S(2)}) copy-start(s32[128]{0:T(128)} %param.28) | copy-start | bytes 1540
  11.1 8.8 %copy-start.46 = (s32[128]{0:T(128)S(1)}, s32[128]{0:T(128)}, u32[]{:S(2)}) copy-start(s32[128]{0:T(128)} %param.27) | copy-start | bytes 1540
  11.1 8.8 %slice-start = ((bf16[256,512]{1,0:T(8,128)(2,1)}), bf16[8,512]{1,0:T(8,128)(2,1)S(1)}, s32[]{:S(2)}) async-start(bf16[256,512]{1,0:T(8,128)(2,1)} %param.22), calls=%async_computation.11 | async-start | bytes 16384 | tf_op jit(solution)/shard_map/slice | solution.py:95
  12.0 32.3 %copy-start.28 = (bf16[128,512]{1,0:T(8,128)(2,1)S(1)}, bf16[128,512]{1,0:T(8,128)(2,1)}, u32[]{:S(2)}) copy-start(bf16[128,512]{1,0:T(8,128)(2,1)} %param.39) | copy-start | bytes 393220
  12.0 42.2 %collective-permute-start.3 = (bf16[128,512]{1,0:T(8,128)(2,1)}, bf16[128,512]{1,0:T(8,128)(2,1)}, u32[]{:S(2)}, u32[]{:S(2)}) collective-permute-start(bf16[128,512]{1,0:T(8,128)(2,1)} %get-tuple-element.67), channel_id=1, source_target_pairs={{2,0},{3,1},{4,2},{5,3},{6,4},{7,5},{8,6},{9,7},{10,8},{11,9},{12,... | collective-permute-start | bytes 393224 | tf_op jit(solution)/shard_map/ppermute | solution.py:15
  17.9 35.3 %collective-permute-start.2 = (bf16[128,512]{1,0:T(8,128)(2,1)}, bf16[128,512]{1,0:T(8,128)(2,1)}, u32[]{:S(2)}, u32[]{:S(2)}) collective-permute-start(bf16[128,512]{1,0:T(8,128)(2,1)} %get-tuple-element.68), channel_id=1, source_target_pairs={{1,0},{2,1},{3,2},{4,3},{5,4},{6,5},{7,6},{8,7},{9,8},{10,9},{11,1... | collective-permute-start | bytes 393224 | tf_op jit(solution)/shard_map/ppermute | solution.py:15
  17.9 34.4 %collective-permute-start.1 = (bf16[128,512]{1,0:T(8,128)(2,1)}, bf16[128,512]{1,0:T(8,128)(2,1)}, u32[]{:S(2)}, u32[]{:S(2)}) collective-permute-start(bf16[128,512]{1,0:T(8,128)(2,1)} %get-tuple-element.69), channel_id=1, source_target_pairs={{14,0},{15,1},{0,2},{1,3},{2,4},{3,5},{4,6},{5,7},{6,8},{7,9},{8,1... | collective-permute-start | bytes 393224 | tf_op jit(solution)/shard_map/ppermute | solution.py:15
  19.1 32.3 %collective-permute-start = (bf16[128,512]{1,0:T(8,128)(2,1)}, bf16[128,512]{1,0:T(8,128)(2,1)}, u32[]{:S(2)}, u32[]{:S(2)}) collective-permute-start(bf16[128,512]{1,0:T(8,128)(2,1)} %get-tuple-element.70), channel_id=1, source_target_pairs={{15,0},{0,1},{1,2},{2,3},{3,4},{4,5},{5,6},{6,7},{7,8},{8,9},{9,10... | collective-permute-start | bytes 393224 | tf_op jit(solution)/shard_map/ppermute | solution.py:15
  19.1 25.2 %copy-start.29 = (bf16[128,512]{1,0:T(8,128)(2,1)S(1)}, bf16[128,512]{1,0:T(8,128)(2,1)}, u32[]{:S(2)}) copy-start(bf16[128,512]{1,0:T(8,128)(2,1)} %param.24) | copy-start | bytes 393220
  19.9 25.2 %copy-start.35 = (s32[1024]{0:T(1024)}, s32[1024]{0:T(1024)S(1)}, u32[]{:S(2)}) copy-start(s32[1024]{0:T(1024)S(1)} %pad_clamp_fusion) | copy-start | bytes 12292
  20.0 27.1 %copy-start.31 = (s32[1024]{0:T(1024)}, s32[1024]{0:T(1024)S(1)}, u32[]{:S(2)}) copy-start(s32[1024]{0:T(1024)S(1)} %get-tuple-element.83) | copy-start | bytes 12292
  47.1 10.6 %copy-start.22 = (bf16[512,512]{1,0:T(8,128)(2,1)}, bf16[512,512]{1,0:T(8,128)(2,1)S(1)}, u32[]{:S(2)}) copy-start(bf16[512,512]{1,0:T(8,128)(2,1)S(1)} %gather_fusion.2) | copy-start | bytes 1572868
  57.7 3.8 copy-start.20
  61.5 0.8 copy-start.9
  61.5 0.9 copy-start.30
  62.2 1.1 copy-start.2
  62.4 1.1 copy-start.27
  67.4 186.0 %reduce-scatter.6.cloned.1.call-start = ((), (), s32[]{:S(2)}) async-start(), calls=%async_computation.6 | async-start | bytes 278528 | tf_op jit(solution)/shard_map/reduce_scatter | solution.py:147
  69.8 84.7 %copy-start.16 = (bf16[1024,512]{1,0:T(8,128)(2,1)S(1)}, bf16[1024,512]{1,0:T(8,128)(2,1)}, u32[]{:S(2)}) copy-start(bf16[1024,512]{1,0:T(8,128)(2,1)} %param.34) | copy-start | bytes 3145732
  153.7 1.3 copy-start.47
  154.5 0.9 copy-start.18
  155.0 2.1 copy-start.49
  155.0 1.1 copy-start.14
  155.0 1.1 copy-start.38
  155.4 1.7 copy-start.12
  155.4 1.6 copy-start.32
  156.1 1.0 copy-start.36
  158.7 0.7 copy-start.19
  159.4 1.0 copy-start.6
  185.5 2.4 copy-start.4
  186.8 2.5 copy-start.3
  189.6 1.0 copy-start.21
  189.6 1.5 copy-start.50
  191.9 0.9 copy-start.48
  195.9 4.6 copy-start.15
  195.9 4.6 copy-start.33
  195.9 4.6 copy-start.37
  195.9 4.6 copy-start.39
  195.9 4.6 copy-start.43
  200.4 3.0 copy-start.10
  200.4 113.6 %reduce-scatter.14.cloned.1.call-start = ((), (), s32[]{:S(2)}) async-start(), calls=%async_computation.10 | async-start | bytes 1114112 | tf_op jit(solution)/shard_map/reduce_scatter | solution.py:154
  203.3 171.7 %reduce-scatter.10.cloned.1.call-start = ((), (), s32[]{:S(2)}) async-start(), calls=%async_computation.8 | async-start | bytes 1114112 | tf_op jit(solution)/shard_map/reduce_scatter | solution.py:152
  205.0 234.7 %reduce-scatter.12.cloned.1.call-start = ((), (), s32[]{:S(2)}) async-start(), calls=%async_computation.9 | async-start | bytes 2228224 | tf_op jit(solution)/shard_map/reduce_scatter | solution.py:153
  207.9 1.0 copy-start.23
  207.9 1.2 copy-start.24
  207.9 1.4 copy-start.25
  208.0 301.8 %reduce-scatter.8.cloned.1.call-start = ((), (), s32[]{:S(2)}) async-start(), calls=%async_computation.7 | async-start | bytes 3342336 | tf_op jit(solution)/shard_map/reduce_scatter | solution.py:151
  213.7 0.7 copy-start.34
  213.7 1.1 copy-start.13
  213.7 2.1 copy-start.26
  229.6 7.1 %copy-start.7 = (f32[256,1024]{1,0:T(8,128)S(1)}, f32[256,1024]{1,0:T(8,128)}, u32[]{:S(2)}) copy-start(f32[256,1024]{1,0:T(8,128)} %copy-done.6) | copy-start | bytes 3145732
  229.7 7.9 %copy-start.5 = (bf16[512,512]{0,1:T(8,128)(2,1)S(1)}, bf16[512,512]{0,1:T(8,128)(2,1)}, u32[]{:S(2)}) copy-start(bf16[512,512]{0,1:T(8,128)(2,1)} %copy.44) | copy-start | bytes 1572868
  229.7 7.9 %copy-start.8 = (f32[512,512]{0,1:T(8,128)S(1)}, f32[512,512]{0,1:T(8,128)}, u32[]{:S(2)}) copy-start(f32[512,512]{0,1:T(8,128)} %copy.54) | copy-start | bytes 3145732
  230.5 19.6 %collective-permute-start.7 = (bf16[128,512]{1,0:T(8,128)(2,1)}, bf16[128,512]{1,0:T(8,128)(2,1)}, u32[]{:S(2)}, u32[]{:S(2)}) collective-permute-start(bf16[128,512]{1,0:T(8,128)(2,1)} %get-tuple-element.62), channel_id=1, source_target_pairs={{14,0},{15,1},{0,2},{1,3},{2,4},{3,5},{4,6},{5,7},{6,8},{7,9},{8,1... | collective-permute-start | bytes 393224 | tf_op jit(solution)/shard_map/ppermute | solution.py:15
  230.5 17.6 %collective-permute-start.6 = (bf16[128,512]{1,0:T(8,128)(2,1)}, bf16[128,512]{1,0:T(8,128)(2,1)}, u32[]{:S(2)}, u32[]{:S(2)}) collective-permute-start(bf16[128,512]{1,0:T(8,128)(2,1)} %get-tuple-element.63), channel_id=1, source_target_pairs={{15,0},{0,1},{1,2},{2,3},{3,4},{4,5},{5,6},{6,7},{7,8},{8,9},{9,10... | collective-permute-start | bytes 393224 | tf_op jit(solution)/shard_map/ppermute | solution.py:15
  230.9 15.3 %collective-permute-start.5 = (bf16[128,512]{1,0:T(8,128)(2,1)}, bf16[128,512]{1,0:T(8,128)(2,1)}, u32[]{:S(2)}, u32[]{:S(2)}) collective-permute-start(bf16[128,512]{1,0:T(8,128)(2,1)} %get-tuple-element.64), channel_id=1, source_target_pairs={{2,0},{3,1},{4,2},{5,3},{6,4},{7,5},{8,6},{9,7},{10,8},{11,9},{12,... | collective-permute-start | bytes 393224 | tf_op jit(solution)/shard_map/ppermute | solution.py:15
  235.3 2.5 copy-start.17
  235.3 8.9 %collective-permute-start.4 = (bf16[128,512]{1,0:T(8,128)(2,1)}, bf16[128,512]{1,0:T(8,128)(2,1)}, u32[]{:S(2)}, u32[]{:S(2)}) collective-permute-start(bf16[128,512]{1,0:T(8,128)(2,1)} %get-tuple-element.65), channel_id=1, source_target_pairs={{1,0},{2,1},{3,2},{4,3},{5,4},{6,5},{7,6},{8,7},{9,8},{10,9},{11,1... | collective-permute-start | bytes 393224 | tf_op jit(solution)/shard_map/ppermute | solution.py:15
  237.6 2.0 copy-start.11
  (2 other events, 1.1 us)
Sparse Core Ops, SparseCore 0:
  67.5 86.1 all-reduce.1
  200.5 52.7 reduce-scatter.5
  257.6 56.3 reduce-scatter.13
  318.5 56.4 reduce-scatter.9
  379.1 60.5 reduce-scatter.11
  444.5 65.2 reduce-scatter.7
where the time goes:
time: 518 us; the launch traced here: 517 us
  waiting for transfers between devices  333 us (64%)
  local copies, waits for them, and re-layouts  49 us (9%)
  blocking collectives  42.8 us (8%)
  other arithmetic  40.5 us (8%)
  matrix products  21.8 us (4%)
  between operations  15.6 us (3%)
  starting transfers between devices  13.8 us (3%)
    psum x1, waiting for transfers between devices, local(): whole_agg = lax.psum(partial_agg, 'patch')  76.7 us
    reduce_scatter x1, waiting for transfers between devices, local(): lax.psum_scatter(grad_ew1, 'patch', scatter_dimension=0, tiled=True)  70 us
    reduce_scatter x1, waiting for transfers between devices, local(): lax.psum_scatter(grad_nw1, 'patch', scatter_dimension=0, tiled=True)  64.8 us
    reduce_scatter x1, waiting for transfers between devices, local(): lax.psum_scatter(grad_ew2, 'patch', scatter_dimension=0, tiled=True)  61 us
    reduce_scatter x1, waiting for transfers between devices, local(): lax.psum_scatter(grad_nw2, 'patch', scatter_dimension=0, tiled=True)  59.2 us
    unnamed x116, local copies, waits for them, and re-layouts  23.7 us
    all_gather x1, blocking collectives, local(): lax.all_gather(d_aggregate[:COARSE_DEV], 'patch', axis=0, tiled=True)  21.6 us
    all_gather x1, blocking collectives, local(): coarse_all = lax.all_gather(nodes[:COARSE_DEV], 'patch', axis=0, tiled=True)  21.2 us
  transfers between devices with their start and end apart: 14, of which 6 were waited for; matrix products, arithmetic and copies ran while one was open for 13% of the time, Pallas kernels for 0%

commit v1 on v0

v1 whole, which is shorter than its diff:
```python
import functools

import jax
import jax.numpy as jnp
from jax import lax
from jax.experimental import pallas as pl
from jax.experimental.pallas import tpu as pltpu
from jax.sharding import PartitionSpec as P

COARSE_DEV = 8
EPSILON = 1e-05
F32 = jnp.float32
BF16 = jnp.bfloat16
VMEM_LIMIT = 44 * 1024 * 1024


def mm(a, b):
    return lax.dot_general(a, b, (((1,), (0,)), ((), ())), preferred_element_type=F32)


def mm_nt(a, b):
    return lax.dot_general(a, b, (((1,), (1,)), ((), ())), preferred_element_type=F32)


def mm_tn(a, b):
    return lax.dot_general(a, b, (((0,), (0,)), ((), ())), preferred_element_type=F32)


def halves(value):
    high = value.astype(BF16)
    low = (value - high.astype(F32)).astype(BF16)
    return high, low


def one_hot(index, rows):
    row = lax.broadcasted_iota(jnp.int32, (rows, index.shape[1]), 0)
    return jnp.where(row == index, 1.0, 0.0).astype(BF16)


def pick(hot, table):
    return mm_tn(hot, table)


def pick_wide(hot, table):
    high, low = halves(table)
    return mm_tn(hot, high) + mm_tn(hot, low)


def put_wide(hot, rows):
    high, low = halves(rows)
    return mm(hot, high) + mm(hot, low)


def row_mean(value):
    return jnp.mean(value, axis=-1, keepdims=True)


def tail_of_forward(pre, second_w, gain):
    sigmoid = jax.nn.sigmoid(pre)
    hidden = (pre * sigmoid).astype(BF16)
    slope = sigmoid * (1.0 + pre * (1.0 - sigmoid))
    output = mm(hidden, second_w)
    centred = output - row_mean(output)
    inv_std = lax.rsqrt(row_mean(centred * centred) + EPSILON)
    normed = centred * inv_std
    return normed * gain, hidden, slope, normed, inv_std


def head_of_backward(cotan, second_w, gain, slope, normed, inv_std):
    scaled = cotan * gain
    back_out = inv_std * (scaled - row_mean(scaled) - normed * row_mean(scaled * normed))
    back_out = back_out.astype(BF16)
    back_pre = (mm_nt(back_out, second_w) * slope).astype(BF16)
    return back_out, back_pre


def tiles_kernel(nodes_ref, halo_ref, *outs):
    spread_ref = outs[-1]
    nodes = nodes_ref[...]
    for slot, out in enumerate(outs[:-1]):
        hot = one_hot(halo_ref[slot : slot + 1, :], nodes.shape[0])
        out[...] = pick(hot, nodes).astype(BF16)
    rows = nodes_ref[0:16, :].astype(F32)[:COARSE_DEV].astype(BF16)
    for peer in range(spread_ref.shape[0]):
        spread_ref[peer] = rows


def gathered(ref):
    value = ref[...].astype(F32)
    return value.reshape(value.shape[0] * value.shape[1], value.shape[2])


def coarse_forward_kernel(
    all_ref, edges_ref, send_ref, recv_ref, w1_ref, w2_ref, gain_ref,
    new_ref, part_ref, zs_ref, zr_ref, hidden_ref, slope_ref, normed_ref, std_ref,
):
    width = edges_ref.shape[1]
    table = gathered(all_ref).astype(BF16)
    hot_s = one_hot(send_ref[...], table.shape[0])
    hot_r = one_hot(recv_ref[...], table.shape[0])
    edges = edges_ref[...]
    zs = pick(hot_s, table).astype(BF16)
    zr = pick(hot_r, table).astype(BF16)
    pre = (
        mm(edges, w1_ref[0:width, :])
        + mm(zs, w1_ref[width : 2 * width, :])
        + mm(zr, w1_ref[2 * width : 3 * width, :])
    )
    message, hidden, slope, normed, inv_std = tail_of_forward(pre, w2_ref[...], gain_ref[...])
    total = put_wide(hot_r, message)
    part_ref[...] = total.reshape(part_ref.shape).astype(BF16)
    new_ref[...] = (edges.astype(F32) + message).astype(BF16)
    zs_ref[...] = zs
    zr_ref[...] = zr
    hidden_ref[...] = hidden
    slope_ref[...] = slope
    normed_ref[...] = normed
    std_ref[...] = jnp.broadcast_to(inv_std, std_ref.shape)


def fine_forward_kernel(
    count_ref, nodes_ref, *refs, slots,
):
    tile_refs = refs[:slots]
    (
        edges_ref, send_ref, recv_ref, w1_ref, w2_ref, gain_ref,
        new_ref, agg_ref, zs_ref, zr_ref, hidden_ref, slope_ref, normed_ref, std_ref, space_ref,
    ) = refs[slots:]
    step = pl.program_id(0)
    rows, width = edges_ref.shape
    own = nodes_ref.shape[0]
    tile = tile_refs[0].shape[0]

    @pl.when(step == 0)
    def _():
        space_ref[0:own, :] = nodes_ref[...]
        for slot in range(slots):
            space_ref[own + slot * tile : own + (slot + 1) * tile, :] = tile_refs[slot][...]
        agg_ref[...] = jnp.zeros_like(agg_ref)

    edges = edges_ref[...]
    hot_s = one_hot(send_ref[...], space_ref.shape[0])
    hot_r = one_hot(recv_ref[...], own)
    zs = pick(hot_s, space_ref[...]).astype(BF16)
    zr = pick(hot_r, nodes_ref[...]).astype(BF16)
    pre = (
        mm(edges, w1_ref[0:width, :])
        + mm(zs, w1_ref[width : 2 * width, :])
        + mm(zr, w1_ref[2 * width : 3 * width, :])
    )
    message, hidden, slope, normed, inv_std = tail_of_forward(pre, w2_ref[...], gain_ref[...])
    place = step * rows + lax.broadcasted_iota(jnp.int32, (rows, 1), 0)
    message = jnp.where(place < count_ref[0], message, 0.0)
    agg_ref[...] += put_wide(hot_r, message)
    new_ref[...] = (edges.astype(F32) + message).astype(BF16)
    zs_ref[...] = zs
    zr_ref[...] = zr
    hidden_ref[...] = hidden
    slope_ref[...] = slope
    normed_ref[...] = normed
    std_ref[...] = jnp.broadcast_to(inv_std, std_ref.shape)


def by_distance(me, peers, firsts, seconds, kept_ref, given_ref):
    rows1 = firsts.shape[0] // peers
    rows2 = seconds.shape[0] // peers
    for r in range(peers):
        to = jnp.bitwise_xor(me, r)
        first = firsts[pl.ds(pl.multiple_of(to * rows1, 16), rows1), :]
        second = seconds[pl.ds(pl.multiple_of(to * rows2, 16), rows2), :]
        out = given_ref if r % 2 else kept_ref
        out[r // 2, 0:rows1, :] = first.astype(out.dtype)
        out[r // 2, rows1 : rows1 + rows2, :] = second.astype(out.dtype)


def node_kernel(
    me_ref, nodes_ref, agg_ref, share_ref, d_ref, w1_ref, w2_ref, gain_ref,
    new_ref, base_ref, dagg_ref, spread_ref, *rest, ordered,
):
    if ordered:
        kept_ref, given_ref, total_ref, g1_ref, g2_ref = rest
    else:
        g1_ref, g2_ref, total_ref = rest
    width = nodes_ref.shape[1]
    total_ref[...] = agg_ref[...]
    total_ref[0:COARSE_DEV, :] += jnp.sum(share_ref[...].astype(F32), 0)
    nodes = nodes_ref[...]
    agg = total_ref[...].astype(BF16)
    pre = mm(nodes, w1_ref[0:width, :]) + mm(agg, w1_ref[width : 2 * width, :])
    update, hidden, slope, normed, inv_std = tail_of_forward(pre, w2_ref[...], gain_ref[...])
    new_ref[...] = (nodes.astype(F32) + update).astype(BF16)
    cotan = d_ref[...].astype(F32)
    back_out, back_pre = head_of_backward(cotan, w2_ref[...], gain_ref[...], slope, normed, inv_std)
    dagg = mm_nt(back_pre, w1_ref[width : 2 * width, :])
    dagg_ref[...] = dagg
    rows = dagg[:COARSE_DEV].astype(BF16)
    for peer in range(spread_ref.shape[0]):
        spread_ref[peer] = rows
    base_ref[...] = cotan + mm_nt(back_pre, w1_ref[0:width, :])
    g1_ref[0:width, :] = mm_tn(nodes, back_pre)
    g1_ref[width : 2 * width, :] = mm_tn(agg, back_pre)
    g2_ref[...] = mm_tn(hidden, back_out)
    if ordered:
        by_distance(me_ref[0], spread_ref.shape[0], g1_ref, g2_ref, kept_ref, given_ref)


def fine_backward_kernel(
    count_ref, edges_ref, d_ref, send_ref, recv_ref, w1_ref, w2_ref, gain_ref, dagg_ref, base_ref,
    zs_ref, zr_ref, hidden_ref, slope_ref, normed_ref, std_ref,
    g_ref, g1_ref, g2_ref, own_ref, *rest,
):
    piece_refs, space_ref, received_ref = rest[:-2], rest[-2], rest[-1]
    step = pl.program_id(0)
    rows, width = edges_ref.shape
    own = base_ref.shape[0]

    @pl.when(step == 0)
    def _():
        g1_ref[...] = jnp.zeros_like(g1_ref)
        g2_ref[...] = jnp.zeros_like(g2_ref)
        space_ref[...] = jnp.zeros_like(space_ref)
        received_ref[...] = jnp.zeros_like(received_ref)

    hot_r = one_hot(recv_ref[...], own)
    d_edges = d_ref[...].astype(F32)
    place = step * rows + lax.broadcasted_iota(jnp.int32, (rows, 1), 0)
    cotan = jnp.where(place < count_ref[0], d_edges + pick_wide(hot_r, dagg_ref[...]), 0.0)
    back_out, back_pre = head_of_backward(
        cotan, w2_ref[...], gain_ref[...], slope_ref[...], normed_ref[...], std_ref[:, 0:1]
    )
    g2_ref[...] += mm_tn(hidden_ref[...], back_out)
    g1_ref[0:width, :] += mm_tn(edges_ref[...], back_pre)
    g1_ref[width : 2 * width, :] += mm_tn(zs_ref[...], back_pre)
    g1_ref[2 * width : 3 * width, :] += mm_tn(zr_ref[...], back_pre)
    g_ref[...] = (d_edges + mm_nt(back_pre, w1_ref[0:width, :])).astype(BF16)
    hot_s = one_hot(send_ref[...], space_ref.shape[0])
    space_ref[...] += put_wide(hot_s, mm_nt(back_pre, w1_ref[width : 2 * width, :]))
    received_ref[...] += put_wide(hot_r, mm_nt(back_pre, w1_ref[2 * width : 3 * width, :]))

    @pl.when(step == pl.num_programs(0) - 1)
    def _():
        own_ref[...] = base_ref[...] + received_ref[...] + space_ref[0:own, :]
        tile = piece_refs[0].shape[0]
        for slot, piece in enumerate(piece_refs):
            piece[...] = space_ref[own + slot * tile : own + (slot + 1) * tile, :].astype(BF16)


def coarse_backward_kernel(
    me_ref, all_ref, edges_ref, d_ref, send_ref, recv_ref, w1_ref, w2_ref, gain_ref,
    zs_ref, zr_ref, hidden_ref, slope_ref, normed_ref, std_ref, f1_ref, f2_ref,
    g_ref, part_ref, *rest, ordered,
):
    if ordered:
        kept_ref, given_ref, g1_ref, g2_ref = rest
    else:
        g1_ref, g2_ref = rest
    width = edges_ref.shape[1]
    table = gathered(all_ref).astype(BF16)
    hot_r = one_hot(recv_ref[...], table.shape[0])
    d_edges = d_ref[...].astype(F32)
    cotan = d_edges + pick(hot_r, table)
    back_out, back_pre = head_of_backward(
        cotan, w2_ref[...], gain_ref[...], slope_ref[...], normed_ref[...], std_ref[:, 0:1]
    )
    g2_ref[...] = f2_ref[...] + mm_tn(hidden_ref[...], back_out)
    g1_ref[0:width, :] = f1_ref[0:width, :] + mm_tn(edges_ref[...], back_pre)
    g1_ref[width : 2 * width, :] = f1_ref[width : 2 * width, :] + mm_tn(zs_ref[...], back_pre)
    g1_ref[2 * width : 3 * width, :] = f1_ref[2 * width : 3 * width, :] + mm_tn(zr_ref[...], back_pre)
    if ordered:
        by_distance(me_ref[0], part_ref.shape[0], g1_ref, g2_ref, kept_ref, given_ref)
    g_ref[...] = (d_edges + mm_nt(back_pre, w1_ref[0:width, :])).astype(BF16)
    hot_s = one_hot(send_ref[...], table.shape[0])
    total = put_wide(hot_s, mm_nt(back_pre, w1_ref[width : 2 * width, :]))
    total = total + put_wide(hot_r, mm_nt(back_pre, w1_ref[2 * width : 3 * width, :]))
    part_ref[...] = total.reshape(part_ref.shape).astype(BF16)


def node_gradient_kernel(own_ref, halo_ref, share_ref, *refs):
    piece_refs, g_ref, total_ref = refs[:-2], refs[-2], refs[-1]
    arrived = None
    for slot, piece in enumerate(piece_refs):
        hot = one_hot(halo_ref[slot : slot + 1, :], own_ref.shape[0])
        part = mm(hot, piece[...])
        arrived = part if arrived is None else arrived + part
    total_ref[...] = own_ref[...] + arrived
    total_ref[0:COARSE_DEV, :] += jnp.sum(share_ref[...].astype(F32), 0)
    g_ref[...] = total_ref[...].astype(BF16)


VM = pl.BlockSpec(memory_space=pltpu.VMEM)
SM = pl.BlockSpec(memory_space=pltpu.SMEM)


def shape(dims, dtype):
    return jax.ShapeDtypeStruct(tuple(dims), dtype)


def call(kernel, name, ins, in_specs, outs, out_specs=None, scratch=(), grid=(), flops=0):
    moved = sum(a.size * a.dtype.itemsize for a in list(ins) + list(outs))
    return pl.pallas_call(
        kernel,
        out_shape=tuple(outs),
        grid=grid,
        in_specs=in_specs,
        out_specs=tuple([VM] * len(outs) if out_specs is None else out_specs),
        scratch_shapes=list(scratch),
        name=name,
        cost_estimate=pl.CostEstimate(flops=flops, bytes_accessed=moved, transcendentals=0),
        compiler_params=pltpu.CompilerParams(vmem_limit_bytes=VMEM_LIMIT),
    )(*ins)


def passed_along(block, axis, distance):
    count = lax.axis_size(axis)
    route = [((i - distance) % count, i) for i in range(count)]
    return lax.ppermute(block, axis, route)


def exchanged(block, axis, distance):
    return lax.ppermute(block, axis, [(i, i ^ distance) for i in range(lax.axis_size(axis))])


def exchanged_with_all(blocks, axis):
    return lax.all_to_all(blocks, axis, 0, 0)


def owners_sum(kept, given, axis):
    total = kept + exchanged(given, axis, 1).astype(F32)
    pairs = total.reshape((total.shape[0] // 2, 2) + total.shape[1:])
    total = pairs[:, 0] + exchanged(pairs[:, 1].astype(BF16), axis, 2).astype(F32)
    result = total[0]
    taken = [exchanged(total[k].astype(BF16), axis, 4 * k) for k in range(1, total.shape[0])]
    for block in taken:
        result = result + block.astype(F32)
    return result


def local(
    nodes,
    fine_edges,
    coarse_edges,
    fine_send,
    fine_recv,
    coarse_send,
    coarse_recv,
    halo_rows,
    edge_count,
    edge_w1,
    edge_w2,
    edge_gain,
    node_w1,
    node_w2,
    node_gain,
    d_nodes,
    d_fine,
    d_coarse,
):
    axis = "patch"
    peers = lax.axis_size(axis)
    own, width = nodes.shape
    fine = fine_edges.shape[0]
    coarse = coarse_edges.shape[0]
    halo = halo_rows[0]
    slots, tile = halo.shape
    hops = slots // 2
    offsets = list(range(1, hops + 1)) + [-k for k in range(1, hops + 1)]
    ordered = peers == 16 and all(
        w.shape[0] % (16 * peers) == 0 for w in (edge_w1, edge_w2, node_w1, node_w2)
    )
    me = lax.axis_index(axis).astype(jnp.int32).reshape(1)
    fs, fr = fine_send.reshape(1, fine), fine_recv.reshape(1, fine)
    cs, cr = coarse_send.reshape(1, coarse), coarse_recv.reshape(1, coarse)
    eg, ng = edge_gain.reshape(1, width), node_gain.reshape(1, width)
    every = shape((peers, COARSE_DEV, width), BF16)

    made = call(
        tiles_kernel, "tiles", (nodes, halo), [VM, VM],
        [shape((tile, width), BF16)] * slots + [every],
    )
    received = [passed_along(made[slot], axis, offset) for slot, offset in enumerate(offsets)]
    coarse_all = exchanged_with_all(made[-1], axis)

    def saved_shapes(rows):
        return [
            shape((rows, width), BF16), shape((rows, width), BF16), shape((rows, width), BF16),
            shape((rows, width), F32), shape((rows, width), F32), shape((rows, 128), F32),
        ]

    new_coarse, coarse_part, *coarse_saved = call(
        coarse_forward_kernel, "coarse_forward",
        (coarse_all, coarse_edges, cs, cr, edge_w1, edge_w2, eg), [VM] * 7,
        [shape((coarse, width), BF16), every] + saved_shapes(coarse),
        flops=2 * coarse * width * width * 4,
    )
    share = exchanged_with_all(coarse_part, axis)

    rows = 256 if fine % 256 == 0 else fine
    grid = (fine // rows,)

    def whole(dims):
        return pl.BlockSpec(dims, lambda i: (0,) * len(dims))

    by_rows = pl.BlockSpec((rows, width), lambda i: (i, 0))
    by_lanes = pl.BlockSpec((1, rows), lambda i: (0, i))
    std_rows = pl.BlockSpec((rows, 128), lambda i: (i, 0))
    saved_specs = [by_rows] * 5 + [std_rows]
    weight_specs = [whole(edge_w1.shape), whole(edge_w2.shape), whole(eg.shape)]
    space_rows = own + slots * tile
    new_fine, fine_agg, *fine_saved = call(
        functools.partial(fine_forward_kernel, slots=slots), "fine_forward",
        (edge_count, nodes, *received, fine_edges, fs, fr, edge_w1, edge_w2, eg),
        [SM, whole(nodes.shape)] + [whole((tile, width))] * slots + [by_rows, by_lanes, by_lanes] + weight_specs,
        [shape((fine, width), BF16), shape((own, width), F32)] + saved_shapes(fine),
        [by_rows, whole((own, width))] + saved_specs,
        scratch=[pltpu.VMEM((space_rows, width), BF16)],
        grid=grid,
        flops=2 * fine * width * (4 * width + space_rows + 3 * own),
    )

    def weight_shapes(w1, w2):
        if not ordered:
            return [shape(w1.shape, F32), shape(w2.shape, F32)], []
        block = (w1.shape[0] + w2.shape[0]) // peers
        outs = [shape((peers // 2, block, width), F32), shape((peers // 2, block, width), BF16)]
        return outs, [pltpu.VMEM(w1.shape, F32), pltpu.VMEM(w2.shape, F32)]

    def weight_sums(parts, w1, w2):
        if not ordered:
            return [lax.psum_scatter(g, axis, scatter_dimension=0, tiled=True) for g in parts]
        block = owners_sum(parts[0], parts[1], axis)
        cut = w1.shape[0] // peers
        return [block[:cut], block[cut:]]

    sum_shapes, sum_scratch = weight_shapes(node_w1, node_w2)
    new_nodes, base, dagg, dagg_spread, *node_parts = call(
        functools.partial(node_kernel, ordered=ordered), "node_both",
        (me, nodes, fine_agg, share, d_nodes, node_w1, node_w2, ng), [SM] + [VM] * 7,
        [shape((own, width), BF16), shape((own, width), F32), shape((own, width), F32), every] + sum_shapes,
        scratch=[pltpu.VMEM((own, width), F32)] + sum_scratch,
        flops=2 * own * width * width * 9,
    )
    dagg_all = exchanged_with_all(dagg_spread, axis)

    g_fine, fine_g1, fine_g2, own_grad, *pieces = call(
        fine_backward_kernel, "fine_backward",
        (edge_count, fine_edges, d_fine, fs, fr, edge_w1, edge_w2, eg, dagg, base, *fine_saved),
        [SM, by_rows, by_rows, by_lanes, by_lanes] + weight_specs
        + [whole((own, width))] * 2 + saved_specs,
        [shape((fine, width), BF16), shape(edge_w1.shape, F32), shape(edge_w2.shape, F32), shape((own, width), F32)]
        + [shape((tile, width), BF16)] * slots,
        [by_rows, whole(edge_w1.shape), whole(edge_w2.shape), whole((own, width))] + [whole((tile, width))] * slots,
        scratch=[pltpu.VMEM((space_rows, width), F32), pltpu.VMEM((own, width), F32)],
        grid=grid,
        flops=2 * fine * width * (8 * width + 2 * space_rows + 4 * own),
    )
    returned = [passed_along(pieces[slot], axis, -offset) for slot, offset in enumerate(offsets)]

    sum_shapes, sum_scratch = weight_shapes(edge_w1, edge_w2)
    g_coarse, coarse_part, *edge_parts = call(
        functools.partial(coarse_backward_kernel, ordered=ordered), "coarse_backward",
        (me, dagg_all, coarse_edges, d_coarse, cs, cr, edge_w1, edge_w2, eg, *coarse_saved, fine_g1, fine_g2),
        [SM] + [VM] * 16,
        [shape((coarse, width), BF16), every] + sum_shapes,
        scratch=sum_scratch,
        flops=2 * coarse * width * width * 8,
    )
    g_ew1, g_ew2 = weight_sums(edge_parts, edge_w1, edge_w2)
    g_nw1, g_nw2 = weight_sums(node_parts, node_w1, node_w2)
    coarse_share = exchanged_with_all(coarse_part, axis)
    (g_nodes,) = call(
        node_gradient_kernel, "node_gradient",
        (own_grad, halo, coarse_share, *returned), [VM] * (3 + slots),
        [shape((own, width), BF16)],
        scratch=[pltpu.VMEM((own, width), F32)],
        flops=2 * own * width * slots * tile,
    )
    return (new_nodes, new_fine, new_coarse, g_nodes, g_fine, g_coarse, g_ew1, g_ew2, g_nw1, g_nw2)


def solution(mesh):
    split = P(("groups", "patch"))
    rows = P(("groups", "patch"), None)
    return jax.shard_map(
        local,
        mesh=mesh,
        in_specs=(
            rows, rows, rows, split, split, split, split, P(("groups", "patch"), None, None), split,
            P(), P(), P(), P(), P(), P(), rows, rows, rows,
        ),
        out_specs=(rows,) * 10,
        check_vma=False,
    )
```

time: 518 us -> 161 us (0.31)
  waiting for transfers between devices: 333 us -> 24.1 us
  blocking collectives: 42.8 us -> 0 us
  other arithmetic: 40.5 us -> 7.57 us
  starting transfers between devices: 13.8 us -> 46.3 us
  Pallas kernels: 0 us -> 22.7 us
  matrix products: 21.8 us -> 0 us
  between operations: 15.6 us -> 1.61 us
  local copies, waits for them, and re-layouts: 49 us -> 56.6 us
    reduce_scatter x5 -> x0, waiting for transfers between devices: 256 us -> none  [the longest x1 70 us: local(): lax.psum_scatter(grad_ew1, 'patch', scatter_dimension=0, tiled=True)]
    psum x1 -> x0, waiting for transfers between devices: 76.7 us -> none  [local(): whole_agg = lax.psum(partial_agg, 'patch')]
    all_gather x2 -> x0, blocking collectives: 42.8 us -> none  [the longest x1 21.6 us: local(): lax.all_gather(d_aggregate[:COARSE_DEV], 'patch', axis=0, tiled=True)]
    scatter-add x12 -> x0, other arithmetic: 29.2 us -> none  [the longest x4 7.81 us: local(): grad_nodes = grad_nodes.at[tile_rows[slot]].add(returned)]
    unnamed x116 -> x148, local copies, waits for them, and re-layouts: 23.7 us -> 51.1 us
    pallas_call x0 -> x7, Pallas kernels: none -> 22.7 us  [call(): pl.pallas_call(kernel, out_shape=tuple(outs), grid=grid, in_specs=in_spec...]
    all_to_all x0 -> x4, starting transfers between devices: none -> 22.6 us  [exchanged_with_all(): return lax.all_to_all(blocks, axis, 0, 0)]
    ppermute x0 -> x10, waiting for transfers between devices: none -> 22 us  [exchanged(): lax.ppermute(block, axis, [(i, i ^ distance) for i in range(lax.axis_size...]
  transfers between devices with their start and end apart: 14 -> 22, of which waited for: 6 -> 6; matrix products, arithmetic and copies ran while one was open for 13% -> 7% of each run, Pallas kernels for 0% -> 12%
where the time goes in v1:
time: 161 us; the launch traced here: 159 us
  local copies, waits for them, and re-layouts  56.6 us (35%)
  starting transfers between devices  46.3 us (29%)
  waiting for transfers between devices  24.1 us (15%)
  Pallas kernels  22.7 us (14%)
  other arithmetic  7.57 us (5%)
  between operations  1.61 us (1%)
    unnamed x148, local copies, waits for them, and re-layouts  51.1 us
    pallas_call x7, Pallas kernels, call(): pl.pallas_call(kernel, out_shape=tuple(outs), grid=grid, in_specs=in_spec...  22.7 us
    all_to_all x4, starting transfers between devices, exchanged_with_all(): return lax.all_to_all(blocks, axis, 0, 0)  22.6 us
    ppermute x10, waiting for transfers between devices, exchanged(): lax.ppermute(block, axis, [(i, i ^ distance) for i in range(lax.axis_size...  22 us
    ppermute x8, starting transfers between devices, passed_along(): return lax.ppermute(block, axis, route)  13.2 us
    ppermute x10, starting transfers between devices, exchanged(): lax.ppermute(block, axis, [(i, i ^ distance) for i in range(lax.axis_size...  10.5 us
    add x2, other arithmetic, owners_sum(): total = kept + exchanged(given, axis, 1).astype(F32)  4.82 us
  transfers between devices with their start and end apart: 22, of which 6 were waited for; matrix products, arithmetic and copies ran while one was open for 7% of the time, Pallas kernels for 12%

profile of v1, /device:TPU:0, one launch (start us, length us, event | category | flops | bytes accessed | tf_op | source)
XLA Modules:
  0.0 159.0 jit_solution(932857407880729528)
XLA Ops:
  0.7 1.0 copy-done.15
  2.4 0.9 tiles.1
  3.3 7.4 %all-to-all-start = ((bf16[16,8,512]{2,1,0:T(8,128)(2,1)}), bf16[16,8,512]{2,1,0:T(8,128)(2,1)S(1)}, u32[]{:S(2)}, u32[]{:S(2)}) async-start(bf16[16,8,512]{2,1,0:T(8,128)(2,1)} %get-tuple-element.54), calls=%async_computation | async-start | bytes 262144 | tf_op jit(solution)/shard_map/all_to_all | solution.py:324
  11.0 1.7 %collective-permute-start.1 = (bf16[128,512]{1,0:T(8,128)(2,1)S(1)}, bf16[128,512]{1,0:T(8,128)(2,1)S(1)}, u32[]{:S(2)}, u32[]{:S(2)}) collective-permute-start(bf16[128,512]{1,0:T(8,128)(2,1)S(1)} %get-tuple-element.50), channel_id=1, source_target_pairs={{14,0},{15,1},{0,2},{1,3},{2,4},{3,5},{4,6},{5,7},{6,8},{7,9},{8,1... | collective-permute-start | bytes 393224 | tf_op jit(solution)/shard_map/ppermute | solution.py:316
  12.7 4.0 %collective-permute-start.2 = (bf16[128,512]{1,0:T(8,128)(2,1)S(1)}, bf16[128,512]{1,0:T(8,128)(2,1)S(1)}, u32[]{:S(2)}, u32[]{:S(2)}) collective-permute-start(bf16[128,512]{1,0:T(8,128)(2,1)S(1)} %get-tuple-element.51), channel_id=1, source_target_pairs={{1,0},{2,1},{3,2},{4,3},{5,4},{6,5},{7,6},{8,7},{9,8},{10,9},{11,1... | collective-permute-start | bytes 393224 | tf_op jit(solution)/shard_map/ppermute | solution.py:316
  17.0 2.0 %all-to-all-done.all_ref = bf16[16,8,512]{2,1,0:T(8,128)(2,1)S(1)} async-done(((bf16[16,8,512]{2,1,0:T(8,128)(2,1)}), bf16[16,8,512]{2,1,0:T(8,128)(2,1)S(1)}, u32[]{:S(2)}, u32[]{:S(2)}) %all-to-all-start) | async-done | bytes 131104 | tf_op jit(solution)/shard_map/all_to_all | solution.py:324
  19.1 1.4 copy-done
  20.5 1.0 copy-done.2
  21.5 0.9 copy-done.7
  24.4 1.8 %coarse_forward.1 = (bf16[128,512]{1,0:T(8,128)(2,1)}, bf16[16,8,512]{2,1,0:T(8,128)(2,1)}, bf16[128,512]{1,0:T(8,128)(2,1)S(1)}, bf16[128,512]{1,0:T(8,128)(2,1...) custom-call(bf16[16,8,512]{2,1,0:T(8,128)(2,1)S(1)} %all-to-all-done, ...), custom_call_target="tpu_custom_call" | custom-call | flops 268435456 | bytes 3607552 | tf_op jit(solution)/shard_map/coarse_forward/pallas_call | solution.py:300
  30.2 3.5 %all-to-all-start.1 = ((bf16[16,8,512]{2,1,0:T(8,128)(2,1)}), bf16[16,8,512]{2,1,0:T(8,128)(2,1)S(1)}, u32[]{:S(2)}, u32[]{:S(2)}) async-start(bf16[16,8,512]{2,1,0:T(8,128)(2,1)} %get-tuple-element.55), calls=%async_computation.1 | async-start | bytes 262144 | tf_op jit(solution)/shard_map/all_to_all | solution.py:324
  37.1 1.0 copy-done.38
  38.1 0.9 copy-done.44
  39.0 0.9 copy-done.46
  39.9 0.9 copy-done.48
  40.8 0.9 copy-done.50
  41.7 4.0 %fine_forward.1 = (bf16[512,512]{1,0:T(8,128)(2,1)}, f32[256,512]{1,0:T(8,128)S(1)}, bf16[512,512]{1,0:T(8,128)(2,1)S(1)}, bf16[512,512]{1,0:T(8,128)(2,1)S(1)},...) custom-call(s32[1]{0:T(128)S(6)} %copy.50.count_ref, ...), custom_call_target="tpu_custom_call" | custom-call | flops 1879048192 | bytes 8394756 | tf_op jit(solution)/shard_map/fine_forward/pallas_call | solution.py:300
  46.5 1.0 copy-done.61
  47.5 1.0 copy-done.63
  51.6 1.0 copy-done.37
  52.6 0.9 copy-done.41
  53.6 1.0 copy-done.60
  54.6 2.9 %node_both.1 = (bf16[256,512]{1,0:T(8,128)(2,1)}, f32[256,512]{1,0:T(8,128)S(1)}, f32[256,512]{1,0:T(8,128)S(1)}, bf16[16,8,512]{2,1,0:T(8,128)(2,1)}, f32[8,96,...) custom-call(s32[1]{0:T(128)} %bitcast.me_ref, bf16[256,512]{1,0:T(8,128)(2,1)S(1)} %copy-done.16, ...), custom_call_target="tpu_custom_call" | custom-call | flops 1207959552 | bytes 6555652 | tf_op jit(solution)/shard_map/node_both/pallas_call | solution.py:300
  57.5 1.2 copy-done.6
  58.7 0.9 copy-done.36
  61.2 6.0 %all-to-all-start.2 = ((bf16[16,8,512]{2,1,0:T(8,128)(2,1)}), bf16[16,8,512]{2,1,0:T(8,128)(2,1)S(1)}, u32[]{:S(2)}, u32[]{:S(2)}) async-start(bf16[16,8,512]{2,1,0:T(8,128)(2,1)} %get-tuple-element.68), calls=%async_computation.2 | async-start | bytes 262144 | tf_op jit(solution)/shard_map/all_to_all | solution.py:324
  67.5 1.0 copy-done.39
  68.6 1.0 copy-done.40
  70.3 1.0 copy-done.56
  71.3 1.0 copy-done.58
  72.4 1.2 copy-done.62
  73.6 1.2 copy-done.64
  74.8 1.0 copy-done.66
  75.9 1.0 copy-done.68
  76.9 1.0 copy-done.70
  78.0 0.9 copy-done.72
  78.9 7.7 %fine_backward.1 = (bf16[512,512]{1,0:T(8,128)(2,1)}, f32[1536,512]{1,0:T(8,128)}, f32[512,512]{1,0:T(8,128)S(1)}, f32[256,512]{1,0:T(8,128)S(1)}, bf16[128,512]...) custom-call(s32[1]{0:T(128)S(6)} %copy.50.count_ref, ...), custom_call_target="tpu_custom_call" | custom-call | flops 3489660928 | bytes 13899780 | tf_op jit(solution)/shard_map/fine_backward/pallas_call | solution.py:300
  88.1 0.9 copy-done.12
  89.1 0.9 copy-done.14
  90.0 0.9 copy-done.19
  90.9 0.9 copy-done.21
  91.8 0.9 copy-done.23
  93.6 4.3 %coarse_backward.1 = (bf16[128,512]{1,0:T(8,128)(2,1)}, bf16[16,8,512]{2,1,0:T(8,128)(2,1)S(1)}, f32[8,128,512]{2,1,0:T(8,128)S(1)}, bf16[8,128,512]{2,1,0:T(8,128)(2,1)}) custom-call(s32[1]{0:T(128)} %bitcast.me_ref, bf16[16,8,512]{2,1,0:T(8,128)(2,1)S(1)} %all-to-all-done.2.all_ref, bf16[128,512]{1,0:T(8,128)(2,1)S(1)} %copy-done.8, ...), custom_call_target="tpu_custom_call" | custom-call | flops 536870912 | bytes 11078660 | tf_op jit(solution)/shard_map/coarse_backward/pallas_call | solution.py:300
  97.9 1.3 copy-done.4
  100.0 4.3 %collective-permute-start.4 = (bf16[128,512]{1,0:T(8,128)(2,1)}, bf16[128,512]{1,0:T(8,128)(2,1)S(1)}, u32[]{:S(2)}, u32[]{:S(2)}) collective-permute-start(bf16[128,512]{1,0:T(8,128)(2,1)} %get-tuple-element.78), channel_id=1, source_target_pairs={{1,0},{2,1},{3,2},{4,3},{5,4},{6,5},{7,6},{8,7},{9,8},{10,9},{11,1... | collective-permute-start | bytes 393224 | tf_op jit(solution)/shard_map/ppermute | solution.py:316
  104.9 5.8 %all-to-all-start.3 = ((bf16[16,8,512]{2,1,0:T(8,128)(2,1)}), bf16[16,8,512]{2,1,0:T(8,128)(2,1)S(1)}, u32[]{:S(2)}, u32[]{:S(2)}) async-start(bf16[16,8,512]{2,1,0:T(8,128)(2,1)} %copy-done.24), calls=%async_computation.3 | async-start | bytes 262144 | tf_op jit(solution)/shard_map/all_to_all | solution.py:324
  110.8 2.0 %collective-permute-start.7 = (bf16[128,512]{1,0:T(8,128)(2,1)}, bf16[128,512]{1,0:T(8,128)(2,1)S(1)}, u32[]{:S(2)}, u32[]{:S(2)}) collective-permute-start(bf16[128,512]{1,0:T(8,128)(2,1)} %copy-done.42), channel_id=1, source_target_pairs={{14,0},{15,1},{0,2},{1,3},{2,4},{3,5},{4,6},{5,7},{6,8},{7,9},{8,1... | collective-permute-start | bytes 393224 | tf_op jit(solution)/shard_map/ppermute | solution.py:316
  112.7 3.2 %convert_add_fusion.1 = f32[8,96,512]{2,1,0:T(8,128)} fusion(f32[8,96,512]{2,1,0:T(8,128)} %copy-done.6, bf16[8,96,512]{2,1,0:T(8,128)(2,1)} %collective-permute-done.13), kind=kLoop, calls=%fused_computation.1 | loop fusion | flops 786432 | bytes 3932160 | tf_op jit(solution)/shard_map/add | solution.py:328
  115.9 2.0 %fusion.3 = bf16[4,96,512]{2,1,0:T(8,128)(2,1)} fusion(f32[4,2,96,512]{3,2,1,0:T(8,128)} %bitcast.15), kind=kLoop, calls=%fused_computation.9 | loop fusion | bytes 786432 | tf_op jit(solution)/shard_map/convert_element_type | solution.py:330
  117.9 1.5 collective-permute-start.14
  119.4 1.6 %convert_add_fusion = f32[8,128,512]{2,1,0:T(8,128)S(1)} fusion(f32[8,128,512]{2,1,0:T(8,128)S(1)} %copy-done.5, bf16[8,128,512]{2,1,0:T(8,128)(2,1)} %copy-done.73), kind=kLoop, calls=%fused_computation | loop fusion | flops 1048576 | bytes 5242880 | tf_op jit(solution)/shard_map/add | solution.py:328
  121.0 0.9 fusion.2
  121.9 1.0 collective-permute-start.9
  122.9 1.1 node_gradient.1
  124.0 6.2 %collective-permute-done.14 = bf16[4,96,512]{2,1,0:T(8,128)(2,1)} collective-permute-done((bf16[4,96,512]{2,1,0:T(8,128)(2,1)}, bf16[4,96,512]{2,1,0:T(8,128)(2,1)}, u32[]{:S(2)}, u32[]{:S(2)}) %collective-permute-start.14) | collective-permute-done | bytes 393248 | tf_op jit(solution)/shard_map/ppermute | solution.py:320
  130.2 1.4 fusion.10
  131.6 1.5 collective-permute-start.15
  133.2 2.4 %collective-permute-start.17 = (bf16[96,512]{1,0:T(8,128)(2,1)S(1)}, bf16[96,512]{1,0:T(8,128)(2,1)S(1)}, u32[]{:S(2)}, u32[]{:S(2)}) collective-permute-start(bf16[96,512]{1,0:T(8,128)(2,1)S(1)} %get-tuple-element.96), channel_id=1, source_target_pairs={{0,12},{1,13},{2,14},{3,15},{4,8},{5,9},{6,10},{7,11},{8,4},{9,5},... | collective-permute-start | bytes 294920 | tf_op jit(solution)/shard_map/ppermute | solution.py:320
  135.5 5.7 %collective-permute-done.9 = bf16[4,128,512]{2,1,0:T(8,128)(2,1)} collective-permute-done((bf16[4,128,512]{2,1,0:T(8,128)(2,1)}, bf16[4,128,512]{2,1,0:T(8,128)(2,1)}, u32[]{:S(2)}, u32[]{:S(2)}) %collective-permute-start.9) | collective-permute-done | bytes 524320 | tf_op jit(solution)/shard_map/ppermute | solution.py:320
  141.3 1.2 fusion.12
  143.2 2.4 %collective-permute-start.12 = (bf16[128,512]{1,0:T(8,128)(2,1)S(1)}, bf16[128,512]{1,0:T(8,128)(2,1)S(1)}, u32[]{:S(2)}, u32[]{:S(2)}) collective-permute-start(bf16[128,512]{1,0:T(8,128)(2,1)S(1)} %get-tuple-element.93), channel_id=1, source_target_pairs={{0,12},{1,13},{2,14},{3,15},{4,8},{5,9},{6,10},{7,11},{8,4},{9,5},... | collective-permute-start | bytes 393224 | tf_op jit(solution)/shard_map/ppermute | solution.py:320
  147.5 1.4 collective-permute-done.10
  148.9 3.9 %collective-permute-done.12 = bf16[128,512]{1,0:T(8,128)(2,1)S(1)} collective-permute-done((bf16[128,512]{1,0:T(8,128)(2,1)S(1)}, bf16[128,512]{1,0:T(8,128)(2,1)S(1)}, u32[]{:S(2)}, u32[]{:S(2)}) %collective-permute-start.12) | collective-permute-done | bytes 131104 | tf_op jit(solution)/shard_map/ppermute | solution.py:320
  152.8 4.8 %collective-permute-done.11 = bf16[128,512]{1,0:T(8,128)(2,1)S(1)} collective-permute-done((bf16[128,512]{1,0:T(8,128)(2,1)S(1)}, bf16[128,512]{1,0:T(8,128)(2,1)S(1)}, u32[]{:S(2)}, u32[]{:S(2)}) %collective-permute-start.11) | collective-permute-done | bytes 131104 | tf_op jit(solution)/shard_map/ppermute | solution.py:320
  (149 shorter events, 24.3 us)
Async XLA Ops:
  0.6 36.4 %copy-start.3 = (bf16[512,512]{1,0:T(8,128)(2,1)S(1)}, bf16[512,512]{1,0:T(8,128)(2,1)}, u32[]{:S(2)}) copy-start(bf16[512,512]{1,0:T(8,128)(2,1)} %w2_ref.7) | copy-start | bytes 1572868
  0.7 1.0 copy-start.15
  2.3 34.7 %copy-start.28 = (f32[512]{0:T(512)S(1)}, f32[512]{0:T(512)}, u32[]{:S(2)}) copy-start(f32[512]{0:T(512)} %param.29) | copy-start | bytes 6148
  2.3 34.7 %copy-start.52 = (s32[512]{0:T(512)S(1)}, s32[512]{0:T(512)}, u32[]{:S(2)}) copy-start(s32[512]{0:T(512)} %param.21) | copy-start | bytes 6148
  2.4 34.7 %copy-start.53 = (s32[512]{0:T(512)S(1)}, s32[512]{0:T(512)}, u32[]{:S(2)}) copy-start(s32[512]{0:T(512)} %param.22) | copy-start | bytes 6148
  3.3 15.8 %all-to-all-start = ((bf16[16,8,512]{2,1,0:T(8,128)(2,1)}), bf16[16,8,512]{2,1,0:T(8,128)(2,1)S(1)}, u32[]{:S(2)}, u32[]{:S(2)}) async-start(bf16[16,8,512]{2,1,0:T(8,128)(2,1)} %get-tuple-element.54), calls=%async_computation | async-start | bytes 262144 | tf_op jit(solution)/shard_map/all_to_all | solution.py:324
  10.6 23.8 %collective-permute-start = (bf16[128,512]{1,0:T(8,128)(2,1)S(1)}, bf16[128,512]{1,0:T(8,128)(2,1)S(1)}, u32[]{:S(2)}, u32[]{:S(2)}) collective-permute-start(bf16[128,512]{1,0:T(8,128)(2,1)S(1)} %get-tuple-element.49), channel_id=1, source_target_pairs={{15,0},{0,1},{1,2},{2,3},{3,4},{4,5},{5,6},{6,7},{7,8},{8,9},{9,10... | collective-permute-start | bytes 393224 | tf_op jit(solution)/shard_map/ppermute | solution.py:316
  11.0 24.0 %collective-permute-start.1 = (bf16[128,512]{1,0:T(8,128)(2,1)S(1)}, bf16[128,512]{1,0:T(8,128)(2,1)S(1)}, u32[]{:S(2)}, u32[]{:S(2)}) collective-permute-start(bf16[128,512]{1,0:T(8,128)(2,1)S(1)} %get-tuple-element.50), channel_id=1, source_target_pairs={{14,0},{15,1},{0,2},{1,3},{2,4},{3,5},{4,6},{5,7},{6,8},{7,9},{8,1... | collective-permute-start | bytes 393224 | tf_op jit(solution)/shard_map/ppermute | solution.py:316
  12.7 23.0 %collective-permute-start.2 = (bf16[128,512]{1,0:T(8,128)(2,1)S(1)}, bf16[128,512]{1,0:T(8,128)(2,1)S(1)}, u32[]{:S(2)}, u32[]{:S(2)}) collective-permute-start(bf16[128,512]{1,0:T(8,128)(2,1)S(1)} %get-tuple-element.51), channel_id=1, source_target_pairs={{1,0},{2,1},{3,2},{4,3},{5,4},{6,5},{7,6},{8,7},{9,8},{10,9},{11,1... | collective-permute-start | bytes 393224 | tf_op jit(solution)/shard_map/ppermute | solution.py:316
  16.7 19.7 %collective-permute-start.3 = (bf16[128,512]{1,0:T(8,128)(2,1)S(1)}, bf16[128,512]{1,0:T(8,128)(2,1)S(1)}, u32[]{:S(2)}, u32[]{:S(2)}) collective-permute-start(bf16[128,512]{1,0:T(8,128)(2,1)S(1)} %get-tuple-element.52), channel_id=1, source_target_pairs={{2,0},{3,1},{4,2},{5,3},{6,4},{7,5},{8,6},{9,7},{10,8},{11,9},{12,... | collective-permute-start | bytes 393224 | tf_op jit(solution)/shard_map/ppermute | solution.py:316
  19.1 1.4 copy-start
  20.5 1.0 copy-start.2
  21.5 0.9 copy-start.7
  24.4 12.7 %copy-start.1 = (bf16[1536,512]{1,0:T(8,128)(2,1)S(1)}, bf16[1536,512]{1,0:T(8,128)(2,1)}, u32[]{:S(2)}) copy-start(bf16[1536,512]{1,0:T(8,128)(2,1)} %w1_ref.7) | copy-start | bytes 4718596
  24.4 12.7 %copy-start.16 = (bf16[256,512]{1,0:T(8,128)(2,1)S(1)}, bf16[256,512]{1,0:T(8,128)(2,1)}, u32[]{:S(2)}) copy-start(bf16[256,512]{1,0:T(8,128)(2,1)} %nodes_ref.5) | copy-start | bytes 786436
  30.2 21.3 %all-to-all-start.1 = ((bf16[16,8,512]{2,1,0:T(8,128)(2,1)}), bf16[16,8,512]{2,1,0:T(8,128)(2,1)S(1)}, u32[]{:S(2)}, u32[]{:S(2)}) async-start(bf16[16,8,512]{2,1,0:T(8,128)(2,1)} %get-tuple-element.55), calls=%async_computation.1 | async-start | bytes 262144 | tf_op jit(solution)/shard_map/all_to_all | solution.py:324
  37.1 1.0 copy-start.38
  40.8 0.9 copy-start.50
  41.7 9.8 %copy-start.35 = (bf16[1024,512]{1,0:T(8,128)(2,1)S(1)}, bf16[1024,512]{1,0:T(8,128)(2,1)}, u32[]{:S(2)}) copy-start(bf16[1024,512]{1,0:T(8,128)(2,1)} %w1_ref.5) | copy-start | bytes 3145732
  41.7 9.8 %copy-start.51 = (f32[512]{0:T(512)S(1)}, f32[512]{0:T(512)}, u32[]{:S(2)}) copy-start(f32[512]{0:T(512)} %param.32) | copy-start | bytes 6148
  46.5 1.0 copy-start.61
  47.5 1.0 copy-start.63
  51.6 1.0 copy-start.37
  52.6 0.9 copy-start.41
  53.6 1.0 copy-start.60
  57.5 1.2 copy-start.6
  61.2 26.9 %all-to-all-start.2 = ((bf16[16,8,512]{2,1,0:T(8,128)(2,1)}), bf16[16,8,512]{2,1,0:T(8,128)(2,1)S(1)}, u32[]{:S(2)}, u32[]{:S(2)}) async-start(bf16[16,8,512]{2,1,0:T(8,128)(2,1)} %get-tuple-element.68), calls=%async_computation.2 | async-start | bytes 262144 | tf_op jit(solution)/shard_map/all_to_all | solution.py:324
  67.1 43.6 %collective-permute-start.13 = (bf16[8,96,512]{2,1,0:T(8,128)(2,1)}, bf16[8,96,512]{2,1,0:T(8,128)(2,1)}, u32[]{:S(2)}, u32[]{:S(2)}) collective-permute-start(bf16[8,96,512]{2,1,0:T(8,128)(2,1)} %copy-done.36), channel_id=1, source_target_pairs={{0,1},{1,0},{2,3},{3,2},{4,5},{5,4},{6,7},{7,6},{8,9},{9,8},{10,11... | collective-permute-start | bytes 2359304 | tf_op jit(solution)/shard_map/ppermute | solution.py:320
  67.5 1.0 copy-start.39
  68.6 1.0 copy-start.40
  70.3 1.0 copy-start.56
  71.3 1.0 copy-start.58
  72.4 1.2 copy-start.62
  73.6 1.2 copy-start.64
  74.8 1.0 copy-start.66
  75.9 1.0 copy-start.68
  76.9 1.0 copy-start.70
  78.0 0.9 copy-start.72
  78.9 9.2 %copy-start.8 = (bf16[128,512]{1,0:T(8,128)(2,1)S(1)}, bf16[128,512]{1,0:T(8,128)(2,1)}, u32[]{:S(2)}) copy-start(bf16[128,512]{1,0:T(8,128)(2,1)} %edges_ref.5) | copy-start | bytes 393220
  78.9 9.2 %copy-start.17 = (bf16[128,512]{1,0:T(8,128)(2,1)S(1)}, bf16[128,512]{1,0:T(8,128)(2,1)}, u32[]{:S(2)}) copy-start(bf16[128,512]{1,0:T(8,128)(2,1)} %d_ref.5) | copy-start | bytes 393220
  78.9 9.2 %copy-start.32 = (s32[128]{0:T(128)S(1)}, s32[128]{0:T(128)}, u32[]{:S(2)}) copy-start(s32[128]{0:T(128)} %param.23) | copy-start | bytes 1540
  78.9 9.2 %copy-start.34 = (s32[128]{0:T(128)S(1)}, s32[128]{0:T(128)}, u32[]{:S(2)}) copy-start(s32[128]{0:T(128)} %param.24) | copy-start | bytes 1540
  88.1 1.0 copy-start.12
  89.1 0.9 copy-start.14
  90.0 0.9 copy-start.19
  97.9 1.3 copy-start.4
  99.9 18.0 %collective-permute-start.8 = (bf16[8,128,512]{2,1,0:T(8,128)(2,1)}, bf16[8,128,512]{2,1,0:T(8,128)(2,1)S(1)}, u32[]{:S(2)}, u32[]{:S(2)}) collective-permute-start(bf16[8,128,512]{2,1,0:T(8,128)(2,1)} %get-tuple-element.85), channel_id=1, source_target_pairs={{0,1},{1,0},{2,3},{3,2},{4,5},{5,4},{6,7},{7,6},{8,9},{9,8},{10,11... | collective-permute-start | bytes 3145736 | tf_op jit(solution)/shard_map/ppermute | solution.py:320
  100.0 21.9 %collective-permute-start.4 = (bf16[128,512]{1,0:T(8,128)(2,1)}, bf16[128,512]{1,0:T(8,128)(2,1)S(1)}, u32[]{:S(2)}, u32[]{:S(2)}) collective-permute-start(bf16[128,512]{1,0:T(8,128)(2,1)} %get-tuple-element.78), channel_id=1, source_target_pairs={{1,0},{2,1},{3,2},{4,3},{5,4},{6,5},{7,6},{8,7},{9,8},{10,9},{11,1... | collective-permute-start | bytes 393224 | tf_op jit(solution)/shard_map/ppermute | solution.py:316
  104.4 18.5 %collective-permute-start.5 = (bf16[128,512]{1,0:T(8,128)(2,1)}, bf16[128,512]{1,0:T(8,128)(2,1)S(1)}, u32[]{:S(2)}, u32[]{:S(2)}) collective-permute-start(bf16[128,512]{1,0:T(8,128)(2,1)} %get-tuple-element.79), channel_id=1, source_target_pairs={{2,0},{3,1},{4,2},{5,3},{6,4},{7,5},{8,6},{9,7},{10,8},{11,9},{12,... | collective-permute-start | bytes 393224 | tf_op jit(solution)/shard_map/ppermute | solution.py:316
  104.9 18.0 %collective-permute-start.6 = (bf16[128,512]{1,0:T(8,128)(2,1)}, bf16[128,512]{1,0:T(8,128)(2,1)S(1)}, u32[]{:S(2)}, u32[]{:S(2)}) collective-permute-start(bf16[128,512]{1,0:T(8,128)(2,1)} %get-tuple-element.80), channel_id=1, source_target_pairs={{15,0},{0,1},{1,2},{2,3},{3,4},{4,5},{5,6},{6,7},{7,8},{8,9},{9,10... | collective-permute-start | bytes 393224 | tf_op jit(solution)/shard_map/ppermute | solution.py:316
  104.9 18.0 %all-to-all-start.3 = ((bf16[16,8,512]{2,1,0:T(8,128)(2,1)}), bf16[16,8,512]{2,1,0:T(8,128)(2,1)S(1)}, u32[]{:S(2)}, u32[]{:S(2)}) async-start(bf16[16,8,512]{2,1,0:T(8,128)(2,1)} %copy-done.24), calls=%async_computation.3 | async-start | bytes 262144 | tf_op jit(solution)/shard_map/all_to_all | solution.py:324
  110.8 12.1 %collective-permute-start.7 = (bf16[128,512]{1,0:T(8,128)(2,1)}, bf16[128,512]{1,0:T(8,128)(2,1)S(1)}, u32[]{:S(2)}, u32[]{:S(2)}) collective-permute-start(bf16[128,512]{1,0:T(8,128)(2,1)} %copy-done.42), channel_id=1, source_target_pairs={{14,0},{15,1},{0,2},{1,3},{2,4},{3,5},{4,6},{5,7},{6,8},{7,9},{8,1... | collective-permute-start | bytes 393224 | tf_op jit(solution)/shard_map/ppermute | solution.py:316
  112.7 6.6 %copy-start.5 = (f32[8,128,512]{2,1,0:T(8,128)S(1)}, f32[8,128,512]{2,1,0:T(8,128)}, u32[]{:S(2)}) copy-start(f32[8,128,512]{2,1,0:T(8,128)} %copy-done.4) | copy-start | bytes 6291460
  117.9 1.5 copy-start.73
  117.9 12.3 %collective-permute-start.14 = (bf16[4,96,512]{2,1,0:T(8,128)(2,1)}, bf16[4,96,512]{2,1,0:T(8,128)(2,1)}, u32[]{:S(2)}, u32[]{:S(2)}) collective-permute-start(bf16[4,96,512]{2,1,0:T(8,128)(2,1)} %fusion.3), channel_id=1, source_target_pairs={{0,2},{1,3},{2,0},{3,1},{4,6},{5,7},{6,4},{7,5},{8,10},{9,11},{10,... | collective-permute-start | bytes 1179656 | tf_op jit(solution)/shard_map/ppermute | solution.py:320
  119.4 3.5 %copy-start.10 = (f32[256,512]{1,0:T(8,128)S(1)}, f32[256,512]{1,0:T(8,128)}, u32[]{:S(2)}) copy-start(f32[256,512]{1,0:T(8,128)} %copy-done.9) | copy-start | bytes 1572868
  119.4 3.5 %copy-start.30 = (s32[1,4,128]{2,1,0:T(4,128)S(1)}, s32[1,4,128]{2,1,0:T(4,128)}, u32[]{:S(2)}) copy-start(s32[1,4,128]{2,1,0:T(4,128)} %param.25) | copy-start | bytes 6148
  121.9 19.4 %collective-permute-start.9 = (bf16[4,128,512]{2,1,0:T(8,128)(2,1)}, bf16[4,128,512]{2,1,0:T(8,128)(2,1)}, u32[]{:S(2)}, u32[]{:S(2)}) collective-permute-start(bf16[4,128,512]{2,1,0:T(8,128)(2,1)} %fusion.2), channel_id=1, source_target_pairs={{0,2},{1,3},{2,0},{3,1},{4,6},{5,7},{6,4},{7,5},{8,10},{9,11},{10,... | collective-permute-start | bytes 1572872 | tf_op jit(solution)/shard_map/ppermute | solution.py:320
  131.6 13.9 %collective-permute-start.15 = (bf16[96,512]{1,0:T(8,128)(2,1)S(1)}, bf16[96,512]{1,0:T(8,128)(2,1)S(1)}, u32[]{:S(2)}, u32[]{:S(2)}) collective-permute-start(bf16[96,512]{1,0:T(8,128)(2,1)S(1)} %get-tuple-element.95), channel_id=1, source_target_pairs={{0,4},{1,5},{2,6},{3,7},{4,0},{5,1},{6,2},{7,3},{8,12},{9,13},{10,... | collective-permute-start | bytes 294920 | tf_op jit(solution)/shard_map/ppermute | solution.py:320
  133.2 12.9 %collective-permute-start.17 = (bf16[96,512]{1,0:T(8,128)(2,1)S(1)}, bf16[96,512]{1,0:T(8,128)(2,1)S(1)}, u32[]{:S(2)}, u32[]{:S(2)}) collective-permute-start(bf16[96,512]{1,0:T(8,128)(2,1)S(1)} %get-tuple-element.96), channel_id=1, source_target_pairs={{0,12},{1,13},{2,14},{3,15},{4,8},{5,9},{6,10},{7,11},{8,4},{9,5},... | collective-permute-start | bytes 294920 | tf_op jit(solution)/shard_map/ppermute | solution.py:320
  135.5 10.6 %collective-permute-start.16 = (bf16[96,512]{1,0:T(8,128)(2,1)S(1)}, bf16[96,512]{1,0:T(8,128)(2,1)S(1)}, u32[]{:S(2)}, u32[]{:S(2)}) collective-permute-start(bf16[96,512]{1,0:T(8,128)(2,1)S(1)} %get-tuple-element.97), channel_id=1, source_target_pairs={{0,8},{1,9},{2,10},{3,11},{4,12},{5,13},{6,14},{7,15},{8,0},{9,1},... | collective-permute-start | bytes 294920 | tf_op jit(solution)/shard_map/ppermute | solution.py:320
  142.6 6.3 %collective-permute-start.10 = (bf16[128,512]{1,0:T(8,128)(2,1)S(1)}, bf16[128,512]{1,0:T(8,128)(2,1)S(1)}, u32[]{:S(2)}, u32[]{:S(2)}) collective-permute-start(bf16[128,512]{1,0:T(8,128)(2,1)S(1)} %get-tuple-element.92), channel_id=1, source_target_pairs={{0,4},{1,5},{2,6},{3,7},{4,0},{5,1},{6,2},{7,3},{8,12},{9,13},{10,... | collective-permute-start | bytes 393224 | tf_op jit(solution)/shard_map/ppermute | solution.py:320
  143.2 9.6 %collective-permute-start.12 = (bf16[128,512]{1,0:T(8,128)(2,1)S(1)}, bf16[128,512]{1,0:T(8,128)(2,1)S(1)}, u32[]{:S(2)}, u32[]{:S(2)}) collective-permute-start(bf16[128,512]{1,0:T(8,128)(2,1)S(1)} %get-tuple-element.93), channel_id=1, source_target_pairs={{0,12},{1,13},{2,14},{3,15},{4,8},{5,9},{6,10},{7,11},{8,4},{9,5},... | collective-permute-start | bytes 393224 | tf_op jit(solution)/shard_map/ppermute | solution.py:320
  145.5 12.1 %collective-permute-start.11 = (bf16[128,512]{1,0:T(8,128)(2,1)S(1)}, bf16[128,512]{1,0:T(8,128)(2,1)S(1)}, u32[]{:S(2)}, u32[]{:S(2)}) collective-permute-start(bf16[128,512]{1,0:T(8,128)(2,1)S(1)} %get-tuple-element.94), channel_id=1, source_target_pairs={{0,8},{1,9},{2,10},{3,11},{4,12},{5,13},{6,14},{7,15},{8,0},{9,1},... | collective-permute-start | bytes 393224 | tf_op jit(solution)/shard_map/ppermute | solution.py:320
  (32 other events, 23.8 us)

commit v2 on v1

--- a/solution.py
+++ b/solution.py
@@ -11,7 +11,7 @@
 EPSILON = 1e-05
 F32 = jnp.float32
 BF16 = jnp.bfloat16
-VMEM_LIMIT = 44 * 1024 * 1024
+VMEM_LIMIT = 16 * 1024 * 1024
 
 
 def mm(a, b):
@@ -118,47 +118,42 @@
     std_ref[...] = jnp.broadcast_to(inv_std, std_ref.shape)
 
 
-def fine_forward_kernel(
-    count_ref, nodes_ref, *refs, slots,
-):
+def fine_forward_kernel(count_ref, nodes_ref, *refs, slots, block):
     tile_refs = refs[:slots]
     (
         edges_ref, send_ref, recv_ref, w1_ref, w2_ref, gain_ref,
         new_ref, agg_ref, zs_ref, zr_ref, hidden_ref, slope_ref, normed_ref, std_ref, space_ref,
     ) = refs[slots:]
-    step = pl.program_id(0)
-    rows, width = edges_ref.shape
+    count, width = edges_ref.shape
     own = nodes_ref.shape[0]
     tile = tile_refs[0].shape[0]
-
-    @pl.when(step == 0)
-    def _():
-        space_ref[0:own, :] = nodes_ref[...]
-        for slot in range(slots):
-            space_ref[own + slot * tile : own + (slot + 1) * tile, :] = tile_refs[slot][...]
-        agg_ref[...] = jnp.zeros_like(agg_ref)
-
-    edges = edges_ref[...]
-    hot_s = one_hot(send_ref[...], space_ref.shape[0])
-    hot_r = one_hot(recv_ref[...], own)
-    zs = pick(hot_s, space_ref[...]).astype(BF16)
-    zr = pick(hot_r, nodes_ref[...]).astype(BF16)
-    pre = (
-        mm(edges, w1_ref[0:width, :])
-        + mm(zs, w1_ref[width : 2 * width, :])
-        + mm(zr, w1_ref[2 * width : 3 * width, :])
-    )
-    message, hidden, slope, normed, inv_std = tail_of_forward(pre, w2_ref[...], gain_ref[...])
-    place = step * rows + lax.broadcasted_iota(jnp.int32, (rows, 1), 0)
-    message = jnp.where(place < count_ref[0], message, 0.0)
-    agg_ref[...] += put_wide(hot_r, message)
-    new_ref[...] = (edges.astype(F32) + message).astype(BF16)
-    zs_ref[...] = zs
-    zr_ref[...] = zr
-    hidden_ref[...] = hidden
-    slope_ref[...] = slope
-    normed_ref[...] = normed
-    std_ref[...] = jnp.broadcast_to(inv_std, std_ref.shape)
+    space_ref[0:own, :] = nodes_ref[...]
+    for slot in range(slots):
+        space_ref[own + slot * tile : own + (slot + 1) * tile, :] = tile_refs[slot][...]
+    for start in range(0, count, block):
+        rows = slice(start, start + block)
+        edges = edges_ref[rows, :]
+        hot_s = one_hot(send_ref[:, rows], space_ref.shape[0])
+        hot_r = one_hot(recv_ref[:, rows], own)
+        zs = pick(hot_s, space_ref[...]).astype(BF16)
+        zr = pick(hot_r, nodes_ref[...]).astype(BF16)
+        pre = (
+            mm(edges, w1_ref[0:width, :])
+            + mm(zs, w1_ref[width : 2 * width, :])
+            + mm(zr, w1_ref[2 * width : 3 * width, :])
+        )
+        message, hidden, slope, normed, inv_std = tail_of_forward(pre, w2_ref[...], gain_ref[...])
+        place = start + lax.broadcasted_iota(jnp.int32, (block, 1), 0)
+        message = jnp.where(place < count_ref[0], message, 0.0)
+        arrived = put_wide(hot_r, message)
+        agg_ref[...] = arrived if start == 0 else agg_ref[...] + arrived
+        new_ref[rows, :] = (edges.astype(F32) + message).astype(BF16)
+        zs_ref[rows, :] = zs
+        zr_ref[rows, :] = zr
+        hidden_ref[rows, :] = hidden
+        slope_ref[rows, :] = slope
+        normed_ref[rows, :] = normed
+        std_ref[rows, :] = jnp.broadcast_to(inv_std, (block, std_ref.shape[1]))
 
 
 def by_distance(me, peers, firsts, seconds, kept_ref, given_ref):
@@ -207,42 +202,38 @@
 def fine_backward_kernel(
     count_ref, edges_ref, d_ref, send_ref, recv_ref, w1_ref, w2_ref, gain_ref, dagg_ref, base_ref,
     zs_ref, zr_ref, hidden_ref, slope_ref, normed_ref, std_ref,
-    g_ref, g1_ref, g2_ref, own_ref, *rest,
+    g_ref, g1_ref, g2_ref, own_ref, *rest, block,
 ):
-    piece_refs, space_ref, received_ref = rest[:-2], rest[-2], rest[-1]
-    step = pl.program_id(0)
-    rows, width = edges_ref.shape
+    piece_refs = rest[:-4]
+    space_ref, received_ref, out_ref, pre_ref = rest[-4:]
+    count, width = edges_ref.shape
     own = base_ref.shape[0]
-
-    @pl.when(step == 0)
-    def _():
-        g1_ref[...] = jnp.zeros_like(g1_ref)
-        g2_ref[...] = jnp.zeros_like(g2_ref)
-        space_ref[...] = jnp.zeros_like(space_ref)
-        received_ref[...] = jnp.zeros_like(received_ref)
-
-    hot_r = one_hot(recv_ref[...], own)
-    d_edges = d_ref[...].astype(F32)
-    place = step * rows + lax.broadcasted_iota(jnp.int32, (rows, 1), 0)
-    cotan = jnp.where(place < count_ref[0], d_edges + pick_wide(hot_r, dagg_ref[...]), 0.0)
-    back_out, back_pre = head_of_backward(
-        cotan, w2_ref[...], gain_ref[...], slope_ref[...], normed_ref[...], std_ref[:, 0:1]
-    )
-    g2_ref[...] += mm_tn(hidden_ref[...], back_out)
-    g1_ref[0:width, :] += mm_tn(edges_ref[...], back_pre)
-    g1_ref[width : 2 * width, :] += mm_tn(zs_ref[...], back_pre)
-    g1_ref[2 * width : 3 * width, :] += mm_tn(zr_ref[...], back_pre)
-    g_ref[...] = (d_edges + mm_nt(back_pre, w1_ref[0:width, :])).astype(BF16)
-    hot_s = one_hot(send_ref[...], space_ref.shape[0])
-    space_ref[...] += put_wide(hot_s, mm_nt(back_pre, w1_ref[width : 2 * width, :]))
-    received_ref[...] += put_wide(hot_r, mm_nt(back_pre, w1_ref[2 * width : 3 * width, :]))
-
-    @pl.when(step == pl.num_programs(0) - 1)
-    def _():
-        own_ref[...] = base_ref[...] + received_ref[...] + space_ref[0:own, :]
-        tile = piece_refs[0].shape[0]
-        for slot, piece in enumerate(piece_refs):
-            piece[...] = space_ref[own + slot * tile : own + (slot + 1) * tile, :].astype(BF16)
+    for start in range(0, count, block):
+        rows = slice(start, start + block)
+        hot_r = one_hot(recv_ref[:, rows], own)
+        hot_s = one_hot(send_ref[:, rows], space_ref.shape[0])
+        d_edges = d_ref[rows, :].astype(F32)
+        place = start + lax.broadcasted_iota(jnp.int32, (block, 1), 0)
+        cotan = jnp.where(place < count_ref[0], d_edges + pick_wide(hot_r, dagg_ref[...]), 0.0)
+        back_out, back_pre = head_of_backward(
+            cotan, w2_ref[...], gain_ref[...],
+            slope_ref[rows, :], normed_ref[rows, :], std_ref[rows, 0:1],
+        )
+        out_ref[rows, :] = back_out
+        pre_ref[rows, :] = back_pre
+        g_ref[rows, :] = (d_edges + mm_nt(back_pre, w1_ref[0:width, :])).astype(BF16)
+        sent = mm(hot_s, mm_nt(back_pre, w1_ref[width : 2 * width, :]).astype(BF16))
+        received = mm(hot_r, mm_nt(back_pre, w1_ref[2 * width : 3 * width, :]).astype(BF16))
+        space_ref[...] = sent if start == 0 else space_ref[...] + sent
+        received_ref[...] = received if start == 0 else received_ref[...] + received
+    own_ref[...] = base_ref[...] + received_ref[...] + space_ref[0:own, :]
+    for slot, piece in enumerate(piece_refs):
+        tile = piece.shape[0]
+        piece[...] = space_ref[own + slot * tile : own + (slot + 1) * tile, :].astype(BF16)
+    g2_ref[...] = mm_tn(hidden_ref[...], out_ref[...])
+    g1_ref[0:width, :] = mm_tn(edges_ref[...], pre_ref[...])
+    g1_ref[width : 2 * width, :] = mm_tn(zs_ref[...], pre_ref[...])
+    g1_ref[2 * width : 3 * width, :] = mm_tn(zr_ref[...], pre_ref[...])
 
 
 def coarse_backward_kernel(
@@ -287,20 +278,50 @@
     g_ref[...] = total_ref[...].astype(BF16)
 
 
+def first_halving_kernel(kept_ref, taken_ref, *refs):
+    keep_ref, give_ref = refs if len(refs) == 2 else refs[1:3]
+    for j in range(kept_ref.shape[0]):
+        total = kept_ref[j] + taken_ref[j].astype(F32)
+        if j % 2:
+            give_ref[j // 2] = total.astype(BF16)
+        else:
+            keep_ref[j // 2] = total
+
+
+def second_halving_kernel(kept_ref, taken_ref, keep_ref, *give_refs):
+    for j in range(kept_ref.shape[0]):
+        total = kept_ref[j] + taken_ref[j].astype(F32)
+        if j:
+            give_refs[j - 1][...] = total.astype(BF16)
+        else:
+            keep_ref[...] = total
+
+
+def last_sum_kernel(kept_ref, *refs):
+    taken, (first_ref, second_ref) = refs[:-2], refs[-2:]
+    cut = first_ref.shape[0]
+    total = kept_ref[...]
+    for ref in taken:
+        total = total + ref[...].astype(F32)
+    first_ref[...] = total[:cut]
+    second_ref[...] = total[cut:]
+
+
 VM = pl.BlockSpec(memory_space=pltpu.VMEM)
 SM = pl.BlockSpec(memory_space=pltpu.SMEM)
+ANY = pl.BlockSpec(memory_space=pl.ANY)
 
 
 def shape(dims, dtype):
     return jax.ShapeDtypeStruct(tuple(dims), dtype)
 
 
-def call(kernel, name, ins, in_specs, outs, out_specs=None, scratch=(), grid=(), flops=0):
+def call(kernel, name, ins, in_specs, outs, out_specs=None, scratch=(), aliases=None, flops=0):
     moved = sum(a.size * a.dtype.itemsize for a in list(ins) + list(outs))
     return pl.pallas_call(
         kernel,
         out_shape=tuple(outs),
-        grid=grid,
+        input_output_aliases=aliases or {},
         in_specs=in_specs,
         out_specs=tuple([VM] * len(outs) if out_specs is None else out_specs),
         scratch_shapes=list(scratch),
@@ -324,15 +345,28 @@
     return lax.all_to_all(blocks, axis, 0, 0)
 
 
-def owners_sum(kept, given, axis):
-    total = kept + exchanged(given, axis, 1).astype(F32)
-    pairs = total.reshape((total.shape[0] // 2, 2) + total.shape[1:])
-    total = pairs[:, 0] + exchanged(pairs[:, 1].astype(BF16), axis, 2).astype(F32)
-    result = total[0]
-    taken = [exchanged(total[k].astype(BF16), axis, 4 * k) for k in range(1, total.shape[0])]
-    for block in taken:
-        result = result + block.astype(F32)
-    return result
+def first_halving(kept, taken, passing=None):
+    half = (kept.shape[0] // 2,) + kept.shape[1:]
+    outs = [shape(half, F32), shape(half, BF16)]
+    if passing is None:
+        return call(first_halving_kernel, "first_halving", (kept, taken), [VM, VM], outs)
+    outs.append(shape(passing.shape, passing.dtype))
+    return call(
+        first_halving_kernel, "first_halving", (kept, taken, passing), [VM, VM, ANY],
+        outs, [VM, VM, ANY], aliases={2: 2},
+    )
+
+
+def second_halving(kept, taken):
+    block = kept.shape[1:]
+    outs = [shape(block, F32)] + [shape(block, BF16)] * (kept.shape[0] - 1)
+    return call(second_halving_kernel, "second_halving", (kept, taken), [VM, VM], outs)
+
+
+def last_sum(kept, taken, first_rows):
+    rows, width = kept.shape
+    outs = [shape((first_rows, width), F32), shape((rows - first_rows, width), F32)]
+    return call(last_sum_kernel, "last_sum", (kept, *taken), [VM] * (1 + len(taken)), outs)
 
 
 def local(
@@ -394,42 +428,23 @@
     )
     share = exchanged_with_all(coarse_part, axis)
 
-    rows = 256 if fine % 256 == 0 else fine
-    grid = (fine // rows,)
-
-    def whole(dims):
-        return pl.BlockSpec(dims, lambda i: (0,) * len(dims))
-
-    by_rows = pl.BlockSpec((rows, width), lambda i: (i, 0))
-    by_lanes = pl.BlockSpec((1, rows), lambda i: (0, i))
-    std_rows = pl.BlockSpec((rows, 128), lambda i: (i, 0))
-    saved_specs = [by_rows] * 5 + [std_rows]
-    weight_specs = [whole(edge_w1.shape), whole(edge_w2.shape), whole(eg.shape)]
+    block = 256 if fine % 256 == 0 else fine
     space_rows = own + slots * tile
     new_fine, fine_agg, *fine_saved = call(
-        functools.partial(fine_forward_kernel, slots=slots), "fine_forward",
+        functools.partial(fine_forward_kernel, slots=slots, block=block), "fine_forward",
         (edge_count, nodes, *received, fine_edges, fs, fr, edge_w1, edge_w2, eg),
-        [SM, whole(nodes.shape)] + [whole((tile, width))] * slots + [by_rows, by_lanes, by_lanes] + weight_specs,
+        [SM] + [VM] * (slots + 7),
         [shape((fine, width), BF16), shape((own, width), F32)] + saved_shapes(fine),
-        [by_rows, whole((own, width))] + saved_specs,
         scratch=[pltpu.VMEM((space_rows, width), BF16)],
-        grid=grid,
         flops=2 * fine * width * (4 * width + space_rows + 3 * own),
     )
 
     def weight_shapes(w1, w2):
         if not ordered:
             return [shape(w1.shape, F32), shape(w2.shape, F32)], []
-        block = (w1.shape[0] + w2.shape[0]) // peers
-        outs = [shape((peers // 2, block, width), F32), shape((peers // 2, block, width), BF16)]
+        rows = (w1.shape[0] + w2.shape[0]) // peers
+        outs = [shape((peers // 2, rows, width), F32), shape((peers // 2, rows, width), BF16)]
         return outs, [pltpu.VMEM(w1.shape, F32), pltpu.VMEM(w2.shape, F32)]
-
-    def weight_sums(parts, w1, w2):
-        if not ordered:
-            return [lax.psum_scatter(g, axis, scatter_dimension=0, tiled=True) for g in parts]
-        block = owners_sum(parts[0], parts[1], axis)
-        cut = w1.shape[0] // peers
-        return [block[:cut], block[cut:]]
 
     sum_shapes, sum_scratch = weight_shapes(node_w1, node_w2)
     new_nodes, base, dagg, dagg_spread, *node_parts = call(
@@ -440,19 +455,24 @@
         flops=2 * own * width * width * 9,
     )
     dagg_all = exchanged_with_all(dagg_spread, axis)
+    if ordered:
+        node_taken = exchanged(node_parts[1], axis, 1)
 
     g_fine, fine_g1, fine_g2, own_grad, *pieces = call(
-        fine_backward_kernel, "fine_backward",
+        functools.partial(fine_backward_kernel, block=block), "fine_backward",
         (edge_count, fine_edges, d_fine, fs, fr, edge_w1, edge_w2, eg, dagg, base, *fine_saved),
-        [SM, by_rows, by_rows, by_lanes, by_lanes] + weight_specs
-        + [whole((own, width))] * 2 + saved_specs,
+        [SM] + [VM] * 15,
         [shape((fine, width), BF16), shape(edge_w1.shape, F32), shape(edge_w2.shape, F32), shape((own, width), F32)]
         + [shape((tile, width), BF16)] * slots,
-        [by_rows, whole(edge_w1.shape), whole(edge_w2.shape), whole((own, width))] + [whole((tile, width))] * slots,
-        scratch=[pltpu.VMEM((space_rows, width), F32), pltpu.VMEM((own, width), F32)],
-        grid=grid,
+        scratch=[
+            pltpu.VMEM((space_rows, width), F32), pltpu.VMEM((own, width), F32),
+            pltpu.VMEM((fine, width), BF16), pltpu.VMEM((fine, width), BF16),
+        ],
         flops=2 * fine * width * (8 * width + 2 * space_rows + 4 * own),
     )
+    if ordered:
+        node_kept, node_given, fine_g2 = first_halving(node_parts[0], node_taken, fine_g2)
+        node_taken = exchanged(node_given, axis, 2)
     returned = [passed_along(pieces[slot], axis, -offset) for slot, offset in enumerate(offsets)]
 
     sum_shapes, sum_scratch = weight_shapes(edge_w1, edge_w2)
@@ -464,8 +484,20 @@
         scratch=sum_scratch,
         flops=2 * coarse * width * width * 8,
     )
-    g_ew1, g_ew2 = weight_sums(edge_parts, edge_w1, edge_w2)
-    g_nw1, g_nw2 = weight_sums(node_parts, node_w1, node_w2)
+    if ordered:
+        edge_taken = exchanged(edge_parts[1], axis, 1)
+        edge_kept, edge_given, coarse_part = first_halving(edge_parts[0], edge_taken, coarse_part)
+        edge_taken = exchanged(edge_given, axis, 2)
+        node_kept, *given = second_halving(node_kept, node_taken)
+        node_taken = [exchanged(part, axis, 4 * (k + 1)) for k, part in enumerate(given)]
+        g_nw1, g_nw2 = last_sum(node_kept, node_taken, node_w1.shape[0] // peers)
+        edge_kept, *given = second_halving(edge_kept, edge_taken)
+        edge_taken = [exchanged(part, axis, 4 * (k + 1)) for k, part in enumerate(given)]
+        g_ew1, g_ew2 = last_sum(edge_kept, edge_taken, edge_w1.shape[0] // peers)
+    else:
+        g_nw1, g_nw2, g_ew1, g_ew2 = [
+            lax.psum_scatter(g, axis, scatter_dimension=0, tiled=True) for g in node_parts + edge_parts
+        ]
     coarse_share = exchanged_with_all(coarse_part, axis)
     (g_nodes,) = call(
         node_gradient_kernel, "node_gradient",

time: 161 us -> 154 us (0.957)
  the two profiles are of different devices: /device:TPU:0 before, /device:TPU:10 now
where the time goes in v2:
time: 154 us; the launch traced here: 153 us
  local copies, waits for them, and re-layouts  47.9 us (31%)
  starting transfers between devices  42.4 us (28%)
  waiting for transfers between devices  37.2 us (24%)
  Pallas kernels  23.8 us (15%)
  between operations  1.56 us (1%)
    unnamed x140, local copies, waits for them, and re-layouts  47.9 us
    ppermute x10, waiting for transfers between devices, exchanged(): lax.ppermute(block, axis, [(i, i ^ distance) for i in range(lax.axis_size...  36.6 us
    all_to_all x4, starting transfers between devices, exchanged_with_all(): return lax.all_to_all(blocks, axis, 0, 0)  26.1 us
    pallas_call x13, Pallas kernels, call(): pl.pallas_call(kernel, out_shape=tuple(outs), input_output_aliases=aliase...  23.8 us
    ppermute x10, starting transfers between devices, exchanged(): lax.ppermute(block, axis, [(i, i ^ distance) for i in range(lax.axis_size...  10.1 us
    ppermute x8, starting transfers between devices, passed_along(): return lax.ppermute(block, axis, route)  6.22 us
  transfers between devices with their start and end apart: 22, of which 7 were waited for; matrix products, arithmetic and copies ran while one was open for 0% of the time, Pallas kernels for 10%

profile of v2, /device:TPU:10, one launch (start us, length us, event | category | flops | bytes accessed | tf_op | source)
XLA Modules:
  0.0 152.8 jit_solution(13532303194545924008)
XLA Ops:
  0.7 1.0 copy-done.18
  2.4 0.9 tiles.1
  3.3 6.2 %all-to-all-start = ((bf16[16,8,512]{2,1,0:T(8,128)(2,1)}), bf16[16,8,512]{2,1,0:T(8,128)(2,1)S(1)}, u32[]{:S(2)}, u32[]{:S(2)}) async-start(bf16[16,8,512]{2,1,0:T(8,128)(2,1)} %get-tuple-element.72), calls=%async_computation | async-start | bytes 262144 | tf_op jit(solution)/shard_map/all_to_all | solution.py:345
  9.7 1.5 collective-permute-start.1
  11.1 1.3 collective-permute-start.2
  12.4 1.5 collective-permute-start.3
  14.4 1.4 copy-done
  15.8 1.0 copy-done.4
  16.9 0.9 copy-done.10
  19.8 1.8 %coarse_forward.1 = (bf16[128,512]{1,0:T(8,128)(2,1)}, bf16[16,8,512]{2,1,0:T(8,128)(2,1)}, bf16[128,512]{1,0:T(8,128)(2,1)S(1)}, bf16[128,512]{1,0:T(8,128)(2,1...) custom-call(bf16[16,8,512]{2,1,0:T(8,128)(2,1)S(1)} %all-to-all-done, ...), custom_call_target="tpu_custom_call" | custom-call | flops 268435456 | bytes 3607552 | tf_op jit(solution)/shard_map/coarse_forward/pallas_call | solution.py:321
  25.6 7.0 %all-to-all-start.1 = ((bf16[16,8,512]{2,1,0:T(8,128)(2,1)}), bf16[16,8,512]{2,1,0:T(8,128)(2,1)S(1)}, u32[]{:S(2)}, u32[]{:S(2)}) async-start(bf16[16,8,512]{2,1,0:T(8,128)(2,1)} %get-tuple-element.73), calls=%async_computation.1 | async-start | bytes 262144 | tf_op jit(solution)/shard_map/all_to_all | solution.py:345
  34.6 1.0 copy-done.39
  35.6 0.9 copy-done.46
  36.5 0.9 copy-done.48
  37.4 3.9 %fine_forward.1 = (bf16[512,512]{1,0:T(8,128)(2,1)}, f32[256,512]{1,0:T(8,128)S(1)}, bf16[512,512]{1,0:T(8,128)(2,1)S(1)}, bf16[512,512]{1,0:T(8,128)(2,1)S(1)},...) custom-call(s32[1]{0:T(128)S(6)} %copy.32.count_ref, ...), custom_call_target="tpu_custom_call" | custom-call | flops 1879048192 | bytes 8394756 | tf_op jit(solution)/shard_map/fine_forward/pallas_call | solution.py:321
  41.3 0.8 copy-done.56
  42.1 1.0 copy-done.58
  43.0 1.0 copy-done.60
  44.0 0.8 copy-done.62
  44.8 0.8 copy-done.64
  45.6 0.8 copy-done.66
  47.2 1.2 copy-done.37
  48.4 1.0 copy-done.57
  49.5 3.1 %node_both.1 = (bf16[256,512]{1,0:T(8,128)(2,1)}, f32[256,512]{1,0:T(8,128)S(1)}, f32[256,512]{1,0:T(8,128)S(1)}, bf16[16,8,512]{2,1,0:T(8,128)(2,1)}, f32[8,96,...) custom-call(s32[1]{0:T(128)} %bitcast.me_ref, bf16[256,512]{1,0:T(8,128)(2,1)S(1)} %copy-done.19, ...), custom_call_target="tpu_custom_call" | custom-call | flops 1207959552 | bytes 6555652 | tf_op jit(solution)/shard_map/node_both/pallas_call | solution.py:321
  52.6 1.2 copy-done.6
  53.8 0.8 copy-done.52
  54.6 0.8 copy-done.54
  55.5 6.1 %all-to-all-start.2 = ((bf16[16,8,512]{2,1,0:T(8,128)(2,1)}), bf16[16,8,512]{2,1,0:T(8,128)(2,1)S(1)}, u32[]{:S(2)}, u32[]{:S(2)}) async-start(bf16[16,8,512]{2,1,0:T(8,128)(2,1)} %get-tuple-element.86), calls=%async_computation.2 | async-start | bytes 262144 | tf_op jit(solution)/shard_map/all_to_all | solution.py:345
  61.6 1.0 copy-done.40
  62.7 1.0 copy-done.41
  63.7 1.0 copy-done.53
  64.7 1.0 copy-done.55
  65.8 1.2 copy-done.59
  67.0 1.2 copy-done.61
  68.2 1.0 copy-done.63
  69.3 1.0 copy-done.65
  70.3 1.0 copy-done.67
  71.4 4.7 %fine_backward.1 = (bf16[512,512]{1,0:T(8,128)(2,1)}, f32[1536,512]{1,0:T(8,128)S(1)}, f32[512,512]{1,0:T(8,128)S(1)}, f32[256,512]{1,0:T(8,128)S(1)}, bf16[128,...) custom-call(s32[1]{0:T(128)S(6)} %copy.32.count_ref, ...), custom_call_target="tpu_custom_call" | custom-call | flops 3489660928 | bytes 13899780 | tf_op jit(solution)/shard_map/fine_backward/pallas_call | solution.py:321
  76.0 1.6 %copy-done.2 = f32[1536,512]{1,0:T(8,128)} copy-done((f32[1536,512]{1,0:T(8,128)}, f32[1536,512]{1,0:T(8,128)S(1)}, u32[]{:S(2)}) %copy-start.2) | copy-done | bytes 3145752
  77.7 0.8 copy-done.12
  79.8 2.1 %first_halving.2 = (f32[4,96,512]{2,1,0:T(8,128)S(1)}, bf16[4,96,512]{2,1,0:T(8,128)(2,1)}, f32[512,512]{1,0:T(8,128)S(1)}) custom-call(f32[8,96,512]{2,1,0:T(8,128)S(1)} %copy-done.7, bf16[8,96,512]{2,1,0:T(8,128)(2,1)} %collective-permute-done.4.taken_ref, f32[512,512]{1,0:T(8,128)S(1)} %get-tuple-element.96.refs_0_), custom_call_target="tpu_custom_call", output_to_operand_aliasing={{2}: (2, {})} | custom-call | bytes 5636096 | tf_op jit(solution)/shard_map/first_halving/pallas_call | solution.py:321
  81.9 0.9 copy-done.8
  82.8 1.9 %copy-done.3 = f32[1536,512]{1,0:T(8,128)S(1)} copy-done((f32[1536,512]{1,0:T(8,128)S(1)}, f32[1536,512]{1,0:T(8,128)}, u32[]{:S(2)}) %copy-start.3) | copy-done | bytes 3145752
  84.7 0.9 copy-done.15
  85.7 0.9 copy-done.17
  86.6 0.9 copy-done.22
  87.5 0.9 copy-done.24
  88.4 0.9 copy-done.26
  89.3 0.8 copy-done.28
  90.2 2.8 %coarse_backward.1 = (bf16[128,512]{1,0:T(8,128)(2,1)}, bf16[16,8,512]{2,1,0:T(8,128)(2,1)}, f32[8,128,512]{2,1,0:T(8,128)S(1)}, bf16[8,128,512]{2,1,0:T(8,128)(2,1)S(1)}) custom-call(s32[1]{0:T(128)} %bitcast.me_ref, bf16[16,8,512]{2,1,0:T(8,128)(2,1)S(1)} %all-to-all-done.2.all_ref, bf16[128,512]{1,0:T(8,128)(2,1)S(1)} %copy-done.11, ...), custom_call_target="tpu_custom_call" | custom-call | flops 536870912 | bytes 11078660 | tf_op jit(solution)/shard_map/coarse_backward/pallas_call | solution.py:321
  93.1 2.5 %collective-permute-done.5.taken_ref = bf16[8,128,512]{2,1,0:T(8,128)(2,1)S(1)} collective-permute-done((bf16[8,128,512]{2,1,0:T(8,128)(2,1)S(1)}, bf16[8,128,512]{2,1,0:T(8,128)(2,1)S(1)}, u32[]{:S(2)}, u32[]{:S(2)}) %collective-permute-start.5) | collective-permute-done | bytes 1048608 | tf_op jit(solution)/shard_map/ppermute | solution.py:341
  95.6 0.9 first_halving.3
  97.2 1.5 collective-permute-start.14
  98.6 1.2 collective-permute-start.7
  99.8 6.8 %all-to-all-start.3 = ((bf16[16,8,512]{2,1,0:T(8,128)(2,1)}), bf16[16,8,512]{2,1,0:T(8,128)(2,1)S(1)}, u32[]{:S(2)}, u32[]{:S(2)}) async-start(bf16[16,8,512]{2,1,0:T(8,128)(2,1)} %get-tuple-element.101), calls=%async_computation.3 | async-start | bytes 262144 | tf_op jit(solution)/shard_map/all_to_all | solution.py:345
  106.7 18.0 %collective-permute-done.14.taken_ref = bf16[4,96,512]{2,1,0:T(8,128)(2,1)S(1)} collective-permute-done((bf16[4,96,512]{2,1,0:T(8,128)(2,1)}, bf16[4,96,512]{2,1,0:T(8,128)(2,1)S(1)}, u32[]{:S(2)}, u32[]{:S(2)}) %collective-permute-start.14) | collective-permute-done | bytes 393248 | tf_op jit(solution)/shard_map/ppermute | solution.py:341
  125.4 2.4 %collective-permute-start.16 = (bf16[96,512]{1,0:T(8,128)(2,1)S(1)}, bf16[96,512]{1,0:T(8,128)(2,1)S(1)}, u32[]{:S(2)}, u32[]{:S(2)}) collective-permute-start(bf16[96,512]{1,0:T(8,128)(2,1)S(1)} %get-tuple-element.120), channel_id=1, source_target_pairs={{0,8},{1,9},{2,10},{3,11},{4,12},{5,13},{6,14},{7,15},{8,0},{9,1},... | collective-permute-start | bytes 294920 | tf_op jit(solution)/shard_map/ppermute | solution.py:341
  129.0 1.2 collective-permute-done.15.refs_0_
  130.9 3.6 %collective-permute-done.16.refs_1_ = bf16[96,512]{1,0:T(8,128)(2,1)S(1)} collective-permute-done((bf16[96,512]{1,0:T(8,128)(2,1)S(1)}, bf16[96,512]{1,0:T(8,128)(2,1)S(1)}, u32[]{:S(2)}, u32[]{:S(2)}) %collective-permute-start.16) | collective-permute-done | bytes 98336 | tf_op jit(solution)/shard_map/ppermute | solution.py:341
  134.4 3.5 %collective-permute-start.12 = (bf16[128,512]{1,0:T(8,128)(2,1)S(1)}, bf16[128,512]{1,0:T(8,128)(2,1)S(1)}, u32[]{:S(2)}, u32[]{:S(2)}) collective-permute-start(bf16[128,512]{1,0:T(8,128)(2,1)S(1)} %get-tuple-element.112), channel_id=1, source_target_pairs={{0,8},{1,9},{2,10},{3,11},{4,12},{5,13},{6,14},{7,15},{8,0},{9,1},... | collective-permute-start | bytes 393224 | tf_op jit(solution)/shard_map/ppermute | solution.py:341
  138.0 9.2 %collective-permute-done.17.refs_2_ = bf16[96,512]{1,0:T(8,128)(2,1)S(1)} collective-permute-done((bf16[96,512]{1,0:T(8,128)(2,1)S(1)}, bf16[96,512]{1,0:T(8,128)(2,1)S(1)}, u32[]{:S(2)}, u32[]{:S(2)}) %collective-permute-start.17) | collective-permute-done | bytes 98336 | tf_op jit(solution)/shard_map/ppermute | solution.py:341
  147.9 2.0 %node_gradient.1 = bf16[256,512]{1,0:T(8,128)(2,1)} custom-call(f32[256,512]{1,0:T(8,128)S(1)} %copy-done.13, s32[4,128]{1,0:T(4,128)S(1)} %bitcast.13, bf16[16,8,512]{2,1,0:T(8,128)(2,1)S(1)} %all-to-all-done.3.share_ref, bf16[128,512]{1,0:T(8,128)(2,1)S(1)} %collective-permute-done.6.refs_0_, bf16[128,512]{1,0:T(8,128)(2,1)} %collective-permute-done.7.refs_1_, ...), custom_call_target="tpu_custom_call" | custom-call | flops 134217728 | bytes 1443840 | tf_op jit(solution)/shard_map/node_gradient/pallas_call | solution.py:321
  149.9 2.2 %collective-permute-done.13.refs_2_ = bf16[128,512]{1,0:T(8,128)(2,1)S(1)} collective-permute-done((bf16[128,512]{1,0:T(8,128)(2,1)S(1)}, bf16[128,512]{1,0:T(8,128)(2,1)S(1)}, u32[]{:S(2)}, u32[]{:S(2)}) %collective-permute-start.13) | collective-permute-done | bytes 131104 | tf_op jit(solution)/shard_map/ppermute | solution.py:341
  152.1 0.7 last_sum.2
  (133 shorter events, 15.0 us)
Async XLA Ops:
  0.6 33.9 %copy-start.5 = (bf16[512,512]{1,0:T(8,128)(2,1)S(1)}, bf16[512,512]{1,0:T(8,128)(2,1)}, u32[]{:S(2)}) copy-start(bf16[512,512]{1,0:T(8,128)(2,1)} %w2_ref.7) | copy-start | bytes 1572868
  0.7 1.0 copy-start.18
  2.3 32.2 %copy-start.30 = (f32[512]{0:T(512)S(1)}, f32[512]{0:T(512)}, u32[]{:S(2)}) copy-start(f32[512]{0:T(512)} %param.29) | copy-start | bytes 6148
  2.3 32.2 %copy-start.50 = (s32[512]{0:T(512)S(1)}, s32[512]{0:T(512)}, u32[]{:S(2)}) copy-start(s32[512]{0:T(512)} %param.21) | copy-start | bytes 6148
  2.4 32.2 %copy-start.51 = (s32[512]{0:T(512)S(1)}, s32[512]{0:T(512)}, u32[]{:S(2)}) copy-start(s32[512]{0:T(512)} %param.22) | copy-start | bytes 6148
  3.3 11.1 %all-to-all-start = ((bf16[16,8,512]{2,1,0:T(8,128)(2,1)}), bf16[16,8,512]{2,1,0:T(8,128)(2,1)S(1)}, u32[]{:S(2)}, u32[]{:S(2)}) async-start(bf16[16,8,512]{2,1,0:T(8,128)(2,1)} %get-tuple-element.72), calls=%async_computation | async-start | bytes 262144 | tf_op jit(solution)/shard_map/all_to_all | solution.py:345
  9.5 23.7 %collective-permute-start = (bf16[128,512]{1,0:T(8,128)(2,1)S(1)}, bf16[128,512]{1,0:T(8,128)(2,1)S(1)}, u32[]{:S(2)}, u32[]{:S(2)}) collective-permute-start(bf16[128,512]{1,0:T(8,128)(2,1)S(1)} %get-tuple-element.67), channel_id=1, source_target_pairs={{15,0},{0,1},{1,2},{2,3},{3,4},{4,5},{5,6},{6,7},{7,8},{8,9},{9,10... | collective-permute-start | bytes 393224 | tf_op jit(solution)/shard_map/ppermute | solution.py:337
  9.7 23.5 %collective-permute-start.1 = (bf16[128,512]{1,0:T(8,128)(2,1)S(1)}, bf16[128,512]{1,0:T(8,128)(2,1)S(1)}, u32[]{:S(2)}, u32[]{:S(2)}) collective-permute-start(bf16[128,512]{1,0:T(8,128)(2,1)S(1)} %get-tuple-element.68), channel_id=1, source_target_pairs={{14,0},{15,1},{0,2},{1,3},{2,4},{3,5},{4,6},{5,7},{6,8},{7,9},{8,1... | collective-permute-start | bytes 393224 | tf_op jit(solution)/shard_map/ppermute | solution.py:337
  11.1 22.1 %collective-permute-start.2 = (bf16[128,512]{1,0:T(8,128)(2,1)S(1)}, bf16[128,512]{1,0:T(8,128)(2,1)S(1)}, u32[]{:S(2)}, u32[]{:S(2)}) collective-permute-start(bf16[128,512]{1,0:T(8,128)(2,1)S(1)} %get-tuple-element.69), channel_id=1, source_target_pairs={{1,0},{2,1},{3,2},{4,3},{5,4},{6,5},{7,6},{8,7},{9,8},{10,9},{11,1... | collective-permute-start | bytes 393224 | tf_op jit(solution)/shard_map/ppermute | solution.py:337
  12.4 21.4 %collective-permute-start.3 = (bf16[128,512]{1,0:T(8,128)(2,1)S(1)}, bf16[128,512]{1,0:T(8,128)(2,1)S(1)}, u32[]{:S(2)}, u32[]{:S(2)}) collective-permute-start(bf16[128,512]{1,0:T(8,128)(2,1)S(1)} %get-tuple-element.70), channel_id=1, source_target_pairs={{2,0},{3,1},{4,2},{5,3},{6,4},{7,5},{8,6},{9,7},{10,8},{11,9},{12,... | collective-permute-start | bytes 393224 | tf_op jit(solution)/shard_map/ppermute | solution.py:337
  14.4 1.4 copy-start
  15.8 1.0 copy-start.4
  19.8 14.8 %copy-start.1 = (bf16[1536,512]{1,0:T(8,128)(2,1)S(1)}, bf16[1536,512]{1,0:T(8,128)(2,1)}, u32[]{:S(2)}) copy-start(bf16[1536,512]{1,0:T(8,128)(2,1)} %w1_ref.7) | copy-start | bytes 4718596
  19.8 14.8 %copy-start.19 = (bf16[256,512]{1,0:T(8,128)(2,1)S(1)}, bf16[256,512]{1,0:T(8,128)(2,1)}, u32[]{:S(2)}) copy-start(bf16[256,512]{1,0:T(8,128)(2,1)} %nodes_ref.5) | copy-start | bytes 786436
  25.6 21.6 %all-to-all-start.1 = ((bf16[16,8,512]{2,1,0:T(8,128)(2,1)}), bf16[16,8,512]{2,1,0:T(8,128)(2,1)S(1)}, u32[]{:S(2)}, u32[]{:S(2)}) async-start(bf16[16,8,512]{2,1,0:T(8,128)(2,1)} %get-tuple-element.73), calls=%async_computation.1 | async-start | bytes 262144 | tf_op jit(solution)/shard_map/all_to_all | solution.py:345
  34.6 1.0 copy-start.39
  35.6 0.9 copy-start.46
  37.4 9.8 %copy-start.38 = (bf16[512,512]{1,0:T(8,128)(2,1)S(1)}, bf16[512,512]{1,0:T(8,128)(2,1)}, u32[]{:S(2)}) copy-start(bf16[512,512]{1,0:T(8,128)(2,1)} %w2_ref.5) | copy-start | bytes 1572868
  37.4 9.8 %copy-start.42 = (bf16[256,512]{1,0:T(8,128)(2,1)S(1)}, bf16[256,512]{1,0:T(8,128)(2,1)}, u32[]{:S(2)}) copy-start(bf16[256,512]{1,0:T(8,128)(2,1)} %d_ref.3) | copy-start | bytes 786436
  37.4 9.8 %copy-start.49 = (f32[512]{0:T(512)S(1)}, f32[512]{0:T(512)}, u32[]{:S(2)}) copy-start(f32[512]{0:T(512)} %param.32) | copy-start | bytes 6148
  42.1 1.0 copy-start.58
  43.0 1.0 copy-start.60
  47.2 1.2 copy-start.37
  48.4 1.0 copy-start.57
  49.5 12.1 %copy-start.69 = (f32[512,128]{1,0:T(8,128)S(1)}, f32[512,128]{1,0:T(8,128)}, u32[]{:S(2)}) copy-start(f32[512,128]{1,0:T(8,128)} %copy-done.68) | copy-start | bytes 786436
  52.6 1.2 copy-start.6
  55.4 24.5 %collective-permute-start.4 = (bf16[8,96,512]{2,1,0:T(8,128)(2,1)}, bf16[8,96,512]{2,1,0:T(8,128)(2,1)}, u32[]{:S(2)}, u32[]{:S(2)}) collective-permute-start(bf16[8,96,512]{2,1,0:T(8,128)(2,1)} %get-tuple-element.95), channel_id=1, source_target_pairs={{0,1},{1,0},{2,3},{3,2},{4,5},{5,4},{6,7},{7,6},{8,9},{9,8},{10,11... | collective-permute-start | bytes 2359304 | tf_op jit(solution)/shard_map/ppermute | solution.py:341
  55.5 27.3 %all-to-all-start.2 = ((bf16[16,8,512]{2,1,0:T(8,128)(2,1)}), bf16[16,8,512]{2,1,0:T(8,128)(2,1)S(1)}, u32[]{:S(2)}, u32[]{:S(2)}) async-start(bf16[16,8,512]{2,1,0:T(8,128)(2,1)} %get-tuple-element.86), calls=%async_computation.2 | async-start | bytes 262144 | tf_op jit(solution)/shard_map/all_to_all | solution.py:345
  61.6 1.0 copy-start.40
  62.7 1.0 copy-start.41
  63.7 1.0 copy-start.53
  64.7 1.0 copy-start.55
  65.8 1.2 copy-start.59
  67.0 1.2 copy-start.61
  68.2 1.0 copy-start.63
  69.3 1.0 copy-start.65
  70.3 1.0 copy-start.67
  71.4 8.5 %copy-start.7 = (f32[8,96,512]{2,1,0:T(8,128)S(1)}, f32[8,96,512]{2,1,0:T(8,128)}, u32[]{:S(2)}) copy-start(f32[8,96,512]{2,1,0:T(8,128)} %copy-done.6) | copy-start | bytes 4718596
  76.0 1.6 %copy-start.2 = (f32[1536,512]{1,0:T(8,128)}, f32[1536,512]{1,0:T(8,128)S(1)}, u32[]{:S(2)}) copy-start(f32[1536,512]{1,0:T(8,128)S(1)} %get-tuple-element.93.f1_ref) | copy-start | bytes 9437188
  79.8 3.0 %copy-start.11 = (bf16[128,512]{1,0:T(8,128)(2,1)S(1)}, bf16[128,512]{1,0:T(8,128)(2,1)}, u32[]{:S(2)}) copy-start(bf16[128,512]{1,0:T(8,128)(2,1)} %edges_ref.5) | copy-start | bytes 393220
  79.8 3.0 %copy-start.20 = (bf16[128,512]{1,0:T(8,128)(2,1)S(1)}, bf16[128,512]{1,0:T(8,128)(2,1)}, u32[]{:S(2)}) copy-start(bf16[128,512]{1,0:T(8,128)(2,1)} %d_ref.5) | copy-start | bytes 393220
  79.8 3.0 %copy-start.34 = (s32[128]{0:T(128)S(1)}, s32[128]{0:T(128)}, u32[]{:S(2)}) copy-start(s32[128]{0:T(128)} %param.23) | copy-start | bytes 1540
  79.8 3.0 %copy-start.36 = (s32[128]{0:T(128)S(1)}, s32[128]{0:T(128)}, u32[]{:S(2)}) copy-start(s32[128]{0:T(128)} %param.24) | copy-start | bytes 1540
  81.9 0.9 copy-start.8
  82.8 1.9 %copy-start.3 = (f32[1536,512]{1,0:T(8,128)S(1)}, f32[1536,512]{1,0:T(8,128)}, u32[]{:S(2)}) copy-start(f32[1536,512]{1,0:T(8,128)} %copy-done.2) | copy-start | bytes 9437188
  84.7 0.9 copy-start.15
  85.7 0.9 copy-start.17
  93.0 31.7 %copy-start.9 = (f32[4,96,512]{2,1,0:T(8,128)S(1)}, f32[4,96,512]{2,1,0:T(8,128)}, u32[]{:S(2)}) copy-start(f32[4,96,512]{2,1,0:T(8,128)} %copy-done.8) | copy-start | bytes 2359300
  93.0 2.7 %collective-permute-start.5 = (bf16[8,128,512]{2,1,0:T(8,128)(2,1)S(1)}, bf16[8,128,512]{2,1,0:T(8,128)(2,1)S(1)}, u32[]{:S(2)}, u32[]{:S(2)}) collective-permute-start(bf16[8,128,512]{2,1,0:T(8,128)(2,1)S(1)} %get-tuple-element.99), channel_id=1, source_target_pairs={{0,1},{1,0},{2,3},{3,2},{4,5},{5,4},{6,7},{7,6},{8,9},{9,8},{10,11... | collective-permute-start | bytes 3145736 | tf_op jit(solution)/shard_map/ppermute | solution.py:341
  96.6 51.3 %copy-start.13 = (f32[256,512]{1,0:T(8,128)S(1)}, f32[256,512]{1,0:T(8,128)}, u32[]{:S(2)}) copy-start(f32[256,512]{1,0:T(8,128)} %copy-done.12) | copy-start | bytes 1572868
  96.6 51.3 %copy-start.32 = (s32[1,4,128]{2,1,0:T(4,128)S(1)}, s32[1,4,128]{2,1,0:T(4,128)}, u32[]{:S(2)}) copy-start(s32[1,4,128]{2,1,0:T(4,128)} %param.25) | copy-start | bytes 6148
  96.6 31.7 %collective-permute-start.10 = (bf16[4,128,512]{2,1,0:T(8,128)(2,1)}, bf16[4,128,512]{2,1,0:T(8,128)(2,1)S(1)}, u32[]{:S(2)}, u32[]{:S(2)}) collective-permute-start(bf16[4,128,512]{2,1,0:T(8,128)(2,1)} %get-tuple-element.109), channel_id=1, source_target_pairs={{0,2},{1,3},{2,0},{3,1},{4,6},{5,7},{6,4},{7,5},{8,10},{9,11},{10,... | collective-permute-start | bytes 1572872 | tf_op jit(solution)/shard_map/ppermute | solution.py:341
  97.2 27.5 %collective-permute-start.14 = (bf16[4,96,512]{2,1,0:T(8,128)(2,1)}, bf16[4,96,512]{2,1,0:T(8,128)(2,1)S(1)}, u32[]{:S(2)}, u32[]{:S(2)}) collective-permute-start(bf16[4,96,512]{2,1,0:T(8,128)(2,1)} %get-tuple-element.117), channel_id=1, source_target_pairs={{0,2},{1,3},{2,0},{3,1},{4,6},{5,7},{6,4},{7,5},{8,10},{9,11},{10,... | collective-permute-start | bytes 1179656 | tf_op jit(solution)/shard_map/ppermute | solution.py:341
  98.6 29.1 %collective-permute-start.6 = (bf16[128,512]{1,0:T(8,128)(2,1)}, bf16[128,512]{1,0:T(8,128)(2,1)S(1)}, u32[]{:S(2)}, u32[]{:S(2)}) collective-permute-start(bf16[128,512]{1,0:T(8,128)(2,1)} %get-tuple-element.102), channel_id=1, source_target_pairs={{1,0},{2,1},{3,2},{4,3},{5,4},{6,5},{7,6},{8,7},{9,8},{10,9},{11,1... | collective-permute-start | bytes 393224 | tf_op jit(solution)/shard_map/ppermute | solution.py:337
  98.6 29.7 %collective-permute-start.7 = (bf16[128,512]{1,0:T(8,128)(2,1)}, bf16[128,512]{1,0:T(8,128)(2,1)}, u32[]{:S(2)}, u32[]{:S(2)}) collective-permute-start(bf16[128,512]{1,0:T(8,128)(2,1)} %get-tuple-element.103), channel_id=1, source_target_pairs={{2,0},{3,1},{4,2},{5,3},{6,4},{7,5},{8,6},{9,7},{10,8},{11,9},{12,... | collective-permute-start | bytes 393224 | tf_op jit(solution)/shard_map/ppermute | solution.py:337
  99.8 48.0 %all-to-all-start.3 = ((bf16[16,8,512]{2,1,0:T(8,128)(2,1)}), bf16[16,8,512]{2,1,0:T(8,128)(2,1)S(1)}, u32[]{:S(2)}, u32[]{:S(2)}) async-start(bf16[16,8,512]{2,1,0:T(8,128)(2,1)} %get-tuple-element.101), calls=%async_computation.3 | async-start | bytes 262144 | tf_op jit(solution)/shard_map/all_to_all | solution.py:345
  124.7 5.5 %collective-permute-start.15 = (bf16[96,512]{1,0:T(8,128)(2,1)S(1)}, bf16[96,512]{1,0:T(8,128)(2,1)S(1)}, u32[]{:S(2)}, u32[]{:S(2)}) collective-permute-start(bf16[96,512]{1,0:T(8,128)(2,1)S(1)} %get-tuple-element.119), channel_id=1, source_target_pairs={{0,4},{1,5},{2,6},{3,7},{4,0},{5,1},{6,2},{7,3},{8,12},{9,13},{10,... | collective-permute-start | bytes 294920 | tf_op jit(solution)/shard_map/ppermute | solution.py:341
  125.4 9.1 %collective-permute-start.16 = (bf16[96,512]{1,0:T(8,128)(2,1)S(1)}, bf16[96,512]{1,0:T(8,128)(2,1)S(1)}, u32[]{:S(2)}, u32[]{:S(2)}) collective-permute-start(bf16[96,512]{1,0:T(8,128)(2,1)S(1)} %get-tuple-element.120), channel_id=1, source_target_pairs={{0,8},{1,9},{2,10},{3,11},{4,12},{5,13},{6,14},{7,15},{8,0},{9,1},... | collective-permute-start | bytes 294920 | tf_op jit(solution)/shard_map/ppermute | solution.py:341
  127.7 19.4 %collective-permute-start.17 = (bf16[96,512]{1,0:T(8,128)(2,1)S(1)}, bf16[96,512]{1,0:T(8,128)(2,1)S(1)}, u32[]{:S(2)}, u32[]{:S(2)}) collective-permute-start(bf16[96,512]{1,0:T(8,128)(2,1)S(1)} %get-tuple-element.121), channel_id=1, source_target_pairs={{0,12},{1,13},{2,14},{3,15},{4,8},{5,9},{6,10},{7,11},{8,4},{9,5},... | collective-permute-start | bytes 294920 | tf_op jit(solution)/shard_map/ppermute | solution.py:341
  128.3 19.5 %collective-permute-start.8 = (bf16[128,512]{1,0:T(8,128)(2,1)}, bf16[128,512]{1,0:T(8,128)(2,1)S(1)}, u32[]{:S(2)}, u32[]{:S(2)}) collective-permute-start(bf16[128,512]{1,0:T(8,128)(2,1)} %copy-done.44), channel_id=1, source_target_pairs={{15,0},{0,1},{1,2},{2,3},{3,4},{4,5},{5,6},{6,7},{7,8},{8,9},{9,10... | collective-permute-start | bytes 393224 | tf_op jit(solution)/shard_map/ppermute | solution.py:337
  128.3 19.5 %collective-permute-start.9 = (bf16[128,512]{1,0:T(8,128)(2,1)}, bf16[128,512]{1,0:T(8,128)(2,1)S(1)}, u32[]{:S(2)}, u32[]{:S(2)}) collective-permute-start(bf16[128,512]{1,0:T(8,128)(2,1)} %copy-done.43), channel_id=1, source_target_pairs={{14,0},{15,1},{0,2},{1,3},{2,4},{3,5},{4,6},{5,7},{6,8},{7,9},{8,1... | collective-permute-start | bytes 393224 | tf_op jit(solution)/shard_map/ppermute | solution.py:337
  130.2 19.7 %collective-permute-start.11 = (bf16[128,512]{1,0:T(8,128)(2,1)S(1)}, bf16[128,512]{1,0:T(8,128)(2,1)S(1)}, u32[]{:S(2)}, u32[]{:S(2)}) collective-permute-start(bf16[128,512]{1,0:T(8,128)(2,1)S(1)} %get-tuple-element.111), channel_id=1, source_target_pairs={{0,4},{1,5},{2,6},{3,7},{4,0},{5,1},{6,2},{7,3},{8,12},{9,13},{10,... | collective-permute-start | bytes 393224 | tf_op jit(solution)/shard_map/ppermute | solution.py:341
  134.4 15.5 %collective-permute-start.12 = (bf16[128,512]{1,0:T(8,128)(2,1)S(1)}, bf16[128,512]{1,0:T(8,128)(2,1)S(1)}, u32[]{:S(2)}, u32[]{:S(2)}) collective-permute-start(bf16[128,512]{1,0:T(8,128)(2,1)S(1)} %get-tuple-element.112), channel_id=1, source_target_pairs={{0,8},{1,9},{2,10},{3,11},{4,12},{5,13},{6,14},{7,15},{8,0},{9,1},... | collective-permute-start | bytes 393224 | tf_op jit(solution)/shard_map/ppermute | solution.py:341
  147.1 5.0 %collective-permute-start.13 = (bf16[128,512]{1,0:T(8,128)(2,1)S(1)}, bf16[128,512]{1,0:T(8,128)(2,1)S(1)}, u32[]{:S(2)}, u32[]{:S(2)}) collective-permute-start(bf16[128,512]{1,0:T(8,128)(2,1)S(1)} %get-tuple-element.113), channel_id=1, source_target_pairs={{0,12},{1,13},{2,14},{3,15},{4,8},{5,9},{6,10},{7,11},{8,4},{9,5},... | collective-permute-start | bytes 393224 | tf_op jit(solution)/shard_map/ppermute | solution.py:341
  (28 other events, 21.0 us)

commit v3 on v2

--- a/solution.py
+++ b/solution.py
@@ -11,7 +11,7 @@
 EPSILON = 1e-05
 F32 = jnp.float32
 BF16 = jnp.bfloat16
-VMEM_LIMIT = 16 * 1024 * 1024
+VMEM_LIMIT = 60 * 1024 * 1024
 
 
 def mm(a, b):
@@ -80,6 +80,7 @@
     for slot, out in enumerate(outs[:-1]):
         hot = one_hot(halo_ref[slot : slot + 1, :], nodes.shape[0])
         out[...] = pick(hot, nodes).astype(BF16)
+        out.done()
     rows = nodes_ref[0:16, :].astype(F32)[:COARSE_DEV].astype(BF16)
     for peer in range(spread_ref.shape[0]):
         spread_ref[peer] = rows
@@ -109,6 +110,7 @@
     message, hidden, slope, normed, inv_std = tail_of_forward(pre, w2_ref[...], gain_ref[...])
     total = put_wide(hot_r, message)
     part_ref[...] = total.reshape(part_ref.shape).astype(BF16)
+    part_ref.done()
     new_ref[...] = (edges.astype(F32) + message).astype(BF16)
     zs_ref[...] = zs
     zr_ref[...] = zr
@@ -159,7 +161,9 @@
 def by_distance(me, peers, firsts, seconds, kept_ref, given_ref):
     rows1 = firsts.shape[0] // peers
     rows2 = seconds.shape[0] // peers
-    for r in range(peers):
+    for r in list(range(1, peers, 2)) + list(range(0, peers, 2)):
+        if r == 0:
+            given_ref.done()
         to = jnp.bitwise_xor(me, r)
         first = firsts[pl.ds(pl.multiple_of(to * rows1, 16), rows1), :]
         second = seconds[pl.ds(pl.multiple_of(to * rows2, 16), rows2), :]
@@ -226,11 +230,15 @@
         received = mm(hot_r, mm_nt(back_pre, w1_ref[2 * width : 3 * width, :]).astype(BF16))
         space_ref[...] = sent if start == 0 else space_ref[...] + sent
         received_ref[...] = received if start == 0 else received_ref[...] + received
+    g_ref.done()
     own_ref[...] = base_ref[...] + received_ref[...] + space_ref[0:own, :]
+    own_ref.done()
     for slot, piece in enumerate(piece_refs):
         tile = piece.shape[0]
         piece[...] = space_ref[own + slot * tile : own + (slot + 1) * tile, :].astype(BF16)
+        piece.done()
     g2_ref[...] = mm_tn(hidden_ref[...], out_ref[...])
+    g2_ref.done()
     g1_ref[0:width, :] = mm_tn(edges_ref[...], pre_ref[...])
     g1_ref[width : 2 * width, :] = mm_tn(zs_ref[...], pre_ref[...])
     g1_ref[2 * width : 3 * width, :] = mm_tn(zr_ref[...], pre_ref[...])
@@ -279,7 +287,7 @@
 
 
 def first_halving_kernel(kept_ref, taken_ref, *refs):
-    keep_ref, give_ref = refs if len(refs) == 2 else refs[1:3]
+    keep_ref, give_ref = refs
     for j in range(kept_ref.shape[0]):
         total = kept_ref[j] + taken_ref[j].astype(F32)
         if j % 2:
@@ -316,15 +324,81 @@
     return jax.ShapeDtypeStruct(tuple(dims), dtype)
 
 
+class Fetched:
+    def __init__(self, source, buffer, semaphore):
+        self.buffer = buffer
+        self.shape = buffer.shape
+        self.copy = pltpu.make_async_copy(source, buffer, semaphore)
+        self.copy.start()
+        self.waiting = True
+
+    def ready(self):
+        if self.waiting:
+            self.copy.wait()
+            self.waiting = False
+
+    def __getitem__(self, index):
+        self.ready()
+        return self.buffer[index]
+
+
+class Stored:
+    def __init__(self, target, buffer, semaphore):
+        self.buffer = buffer
+        self.shape = buffer.shape
+        self.dtype = buffer.dtype
+        self.copy = pltpu.make_async_copy(buffer, target, semaphore)
+        self.started = False
+
+    def __getitem__(self, index):
+        return self.buffer[index]
+
+    def __setitem__(self, index, value):
+        self.buffer[index] = value
+
+    def done(self):
+        if not self.started:
+            self.copy.start()
+            self.started = True
+
+
+def staged_kernel(body, in_specs, out_specs, *refs):
+    ins, outs = refs[: len(in_specs)], refs[len(in_specs) : len(in_specs) + len(out_specs)]
+    rest = refs[len(in_specs) + len(out_specs) :]
+    fetched, stored, taken = [], [], 0
+    semaphores, buffers = rest[0], rest[1:]
+    for ref, spec in zip(ins, in_specs):
+        if spec is VM:
+            fetched.append(Fetched(ref, buffers[taken], semaphores.at[taken]))
+            taken += 1
+        elif spec is SM:
+            fetched.append(ref)
+    for ref, spec in zip(outs, out_specs):
+        if spec is VM:
+            stored.append(Stored(ref, buffers[taken], semaphores.at[taken]))
+            taken += 1
+    body(*fetched, *stored, *buffers[taken:])
+    for ref in fetched:
+        if isinstance(ref, Fetched):
+            ref.ready()
+    for ref in stored:
+        ref.done()
+    for ref in stored:
+        ref.copy.wait()
+
+
 def call(kernel, name, ins, in_specs, outs, out_specs=None, scratch=(), aliases=None, flops=0):
+    out_specs = [VM] * len(outs) if out_specs is None else out_specs
     moved = sum(a.size * a.dtype.itemsize for a in list(ins) + list(outs))
+    staged = [a for a, spec in zip(list(ins) + list(outs), list(in_specs) + list(out_specs)) if spec is VM]
+    buffers = [pltpu.VMEM(a.shape, a.dtype) for a in staged]
     return pl.pallas_call(
-        kernel,
+        functools.partial(staged_kernel, kernel, in_specs, out_specs),
         out_shape=tuple(outs),
         input_output_aliases=aliases or {},
-        in_specs=in_specs,
-        out_specs=tuple([VM] * len(outs) if out_specs is None else out_specs),
-        scratch_shapes=list(scratch),
+        in_specs=[SM if spec is SM else ANY for spec in in_specs],
+        out_specs=tuple([ANY] * len(outs)),
+        scratch_shapes=[pltpu.SemaphoreType.DMA((len(buffers),))] + buffers + list(scratch),
         name=name,
         cost_estimate=pl.CostEstimate(flops=flops, bytes_accessed=moved, transcendentals=0),
         compiler_params=pltpu.CompilerParams(vmem_limit_bytes=VMEM_LIMIT),
@@ -457,6 +531,8 @@
     dagg_all = exchanged_with_all(dagg_spread, axis)
     if ordered:
         node_taken = exchanged(node_parts[1], axis, 1)
+        node_kept, node_given, base = first_halving(node_parts[0], node_taken, base)
+        node_taken = exchanged(node_given, axis, 2)
 
     g_fine, fine_g1, fine_g2, own_grad, *pieces = call(
         functools.partial(fine_backward_kernel, block=block), "fine_backward",
@@ -470,9 +546,6 @@
         ],
         flops=2 * fine * width * (8 * width + 2 * space_rows + 4 * own),
     )
-    if ordered:
-        node_kept, node_given, fine_g2 = first_halving(node_parts[0], node_taken, fine_g2)
-        node_taken = exchanged(node_given, axis, 2)
     returned = [passed_along(pieces[slot], axis, -offset) for slot, offset in enumerate(offsets)]
 
     sum_shapes, sum_scratch = weight_shapes(edge_w1, edge_w2)

time: 154 us -> 139 us (0.903)
  the two profiles are of different devices: /device:TPU:10 before, /device:TPU:14 now
where the time goes in v3:
time: 139 us
  Pallas kernels  53.6 us (39%)
  starting transfers between devices  43.4 us (31%)
  waiting for transfers between devices  32.1 us (23%)
  local copies, waits for them, and re-layouts  7.66 us (6%)
  between operations  1.88 us (1%)
    pallas_call x13, Pallas kernels, call(): pl.pallas_call(functools.partial(staged_kernel, kernel, in_specs, out_spe...  53.6 us
    ppermute x10, waiting for transfers between devices, exchanged(): lax.ppermute(block, axis, [(i, i ^ distance) for i in range(lax.axis_size...  31.5 us
    all_to_all x4, starting transfers between devices, exchanged_with_all(): return lax.all_to_all(blocks, axis, 0, 0)  26.2 us
    ppermute x10, starting transfers between devices, exchanged(): lax.ppermute(block, axis, [(i, i ^ distance) for i in range(lax.axis_size...  11 us
    unnamed x54, local copies, waits for them, and re-layouts  7.66 us
    ppermute x8, starting transfers between devices, passed_along(): return lax.ppermute(block, axis, route)  6.16 us
  transfers between devices with their start and end apart: 22, of which 5 were waited for; matrix products, arithmetic and copies ran while one was open for 0% of the time, Pallas kernels for 24%

profile of v3, /device:TPU:14, one launch (start us, length us, event | category | flops | bytes accessed | tf_op | source)
XLA Modules:
  0.0 138.6 jit_solution(6932680856182072165)
XLA Ops:
  0.6 2.1 %tiles.1 = (bf16[128,512]{1,0:T(8,128)(2,1)}, bf16[128,512]{1,0:T(8,128)(2,1)}, bf16[128,512]{1,0:T(8,128)(2,1)}, bf16[128,512]{1,0:T(8,128)(2,1)}, bf16[16,8,512]{2,1,0:T(8,128)(2,1)}) custom-call(bf16[256,512]{1,0:T(8,128)(2,1)} %refs_1_.6, s32[4,128]{1,0:T(4,128)} %bitcast.12), custom_call_target="tpu_custom_call" | custom-call | bytes 919552 | tf_op jit(solution)/shard_map/tiles/pallas_call | solution.py:395
  2.7 6.3 %all-to-all-start = ((bf16[16,8,512]{2,1,0:T(8,128)(2,1)}), bf16[16,8,512]{2,1,0:T(8,128)(2,1)S(1)}, u32[]{:S(2)}, u32[]{:S(2)}) async-start(bf16[16,8,512]{2,1,0:T(8,128)(2,1)} %get-tuple-element.72), calls=%async_computation | async-start | bytes 262144 | tf_op jit(solution)/shard_map/all_to_all | solution.py:419
  9.0 0.1 collective-permute-start
  9.1 1.5 %collective-permute-start.1 = (bf16[128,512]{1,0:T(8,128)(2,1)}, bf16[128,512]{1,0:T(8,128)(2,1)S(1)}, u32[]{:S(2)}, u32[]{:S(2)}) collective-permute-start(bf16[128,512]{1,0:T(8,128)(2,1)} %get-tuple-element.68), channel_id=1, source_target_pairs={{14,0},{15,1},{0,2},{1,3},{2,4},{3,5},{4,6},{5,7},{6,8},{7,9},{8,1... | collective-permute-start | bytes 393224 | tf_op jit(solution)/shard_map/ppermute | solution.py:411
  10.6 1.3 collective-permute-start.2
  11.9 1.5 %collective-permute-start.3 = (bf16[128,512]{1,0:T(8,128)(2,1)}, bf16[128,512]{1,0:T(8,128)(2,1)S(1)}, u32[]{:S(2)}, u32[]{:S(2)}) collective-permute-start(bf16[128,512]{1,0:T(8,128)(2,1)} %get-tuple-element.70), channel_id=1, source_target_pairs={{2,0},{3,1},{4,2},{5,3},{6,4},{7,5},{8,6},{9,7},{10,8},{11,9},{12,... | collective-permute-start | bytes 393224 | tf_op jit(solution)/shard_map/ppermute | solution.py:411
  13.4 0.5 all-to-all-done.refs_0_
  13.9 0.7 copy-done.4
  14.6 3.8 %coarse_forward.1 = (bf16[128,512]{1,0:T(8,128)(2,1)}, bf16[16,8,512]{2,1,0:T(8,128)(2,1)}, bf16[128,512]{1,0:T(8,128)(2,1)}, bf16[128,512]{1,0:T(8,128)(2,1)}, ...) custom-call(bf16[16,8,512]{2,1,0:T(8,128)(2,1)} %copy-done.4, ...), custom_call_target="tpu_custom_call" | custom-call | flops 268435456 | bytes 3607552 | tf_op jit(solution)/shard_map/coarse_forward/pallas_call | solution.py:395
  18.4 7.0 %all-to-all-start.1 = ((bf16[16,8,512]{2,1,0:T(8,128)(2,1)}), bf16[16,8,512]{2,1,0:T(8,128)(2,1)S(1)}, u32[]{:S(2)}, u32[]{:S(2)}) async-start(bf16[16,8,512]{2,1,0:T(8,128)(2,1)} %get-tuple-element.73), calls=%async_computation.1 | async-start | bytes 262144 | tf_op jit(solution)/shard_map/all_to_all | solution.py:419
  26.0 0.0 copy-start.23
  26.0 0.0 copy-start.24
  26.0 0.0 copy-start.25
  26.1 0.0 copy-start.26
  26.1 0.6 copy-done.23
  26.6 0.0 copy-done.24
  26.7 0.0 copy-done.25
  26.7 0.0 copy-done.26
  26.8 7.2 %fine_forward.1 = (bf16[512,512]{1,0:T(8,128)(2,1)}, f32[256,512]{1,0:T(8,128)}, bf16[512,512]{1,0:T(8,128)(2,1)}, bf16[512,512]{1,0:T(8,128)(2,1)}, bf16[512,51...) custom-call(s32[1]{0:T(128)S(6)} %copy.32.refs_0_, bf16[256,512]{1,0:T(8,128)(2,1)} %refs_1_.6, ...), custom_call_target="tpu_custom_call" | custom-call | flops 1879048192 | bytes 8394756 | tf_op jit(solution)/shard_map/fine_forward/pallas_call | solution.py:395
  34.0 0.0 copy-start.10
  34.0 0.6 copy-done.10
  34.7 5.9 %node_both.1 = (bf16[256,512]{1,0:T(8,128)(2,1)}, f32[256,512]{1,0:T(8,128)}, f32[256,512]{1,0:T(8,128)}, bf16[16,8,512]{2,1,0:T(8,128)(2,1)}, f32[8,96,512]{2,1,0:T(8,128)}, /*index=5*/bf16[8,96,512]{2,1,0:T(8,128)(2,1)}) custom-call(s32[1]{0:T(128)} %bitcast.refs_0_, bf16[256,512]{1,0:T(8,128)(2,1)} %refs_1_.6, f32[256,512]{1,0:T(8,128)} %get-tuple-element.71.refs_2_, ...), custom_call_target="tpu_custom_call" | custom-call | flops 1207959552 | bytes 6555652 | tf_op jit(solution)/shard_map/node_both/pallas_call | solution.py:395
  40.5 0.2 collective-permute-start.4
  40.7 6.1 %all-to-all-start.2 = ((bf16[16,8,512]{2,1,0:T(8,128)(2,1)}), bf16[16,8,512]{2,1,0:T(8,128)(2,1)S(1)}, u32[]{:S(2)}, u32[]{:S(2)}) async-start(bf16[16,8,512]{2,1,0:T(8,128)(2,1)} %get-tuple-element.89), calls=%async_computation.2 | async-start | bytes 262144 | tf_op jit(solution)/shard_map/all_to_all | solution.py:419
  46.8 0.9 copy-done.1
  47.7 2.7 %first_halving.2 = (f32[4,96,512]{2,1,0:T(8,128)}, bf16[4,96,512]{2,1,0:T(8,128)(2,1)}, f32[256,512]{1,0:T(8,128)}) custom-call(f32[8,96,512]{2,1,0:T(8,128)} %get-tuple-element.78.refs_0_, bf16[8,96,512]{2,1,0:T(8,128)(2,1)} %copy-done.1, f32[256,512]{1,0:T(8,128)} %get-tuple-element.80.refs_2_), custom_call_target="tpu_custom_call", output_to_operand_aliasing={{2}: (2, {})} | custom-call | bytes 4587520 | tf_op jit(solution)/shard_map/first_halving/pallas_call | solution.py:395
  50.5 10.3 %fine_backward.1 = (bf16[512,512]{1,0:T(8,128)(2,1)}, f32[1536,512]{1,0:T(8,128)}, f32[512,512]{1,0:T(8,128)}, f32[256,512]{1,0:T(8,128)}, bf16[128,512]{1,0:T(8...) custom-call(s32[1]{0:T(128)S(6)} %copy.32.refs_0_, ...), custom_call_target="tpu_custom_call" | custom-call | flops 3489660928 | bytes 13899780 | tf_op jit(solution)/shard_map/fine_backward/pallas_call | solution.py:395
  60.8 0.0 copy-start.2
  60.8 0.6 copy-done.2
  61.5 7.8 %coarse_backward.1 = (bf16[128,512]{1,0:T(8,128)(2,1)}, bf16[16,8,512]{2,1,0:T(8,128)(2,1)}, f32[8,128,512]{2,1,0:T(8,128)}, bf16[8,128,512]{2,1,0:T(8,128)(2,1)}) custom-call(s32[1]{0:T(128)} %bitcast.refs_0_, bf16[16,8,512]{2,1,0:T(8,128)(2,1)} %copy-done.2, bf16[128,512]{1,0:T(8,128)(2,1)} %refs_2_.3, bf16[128,512]{1,0:T(8,128)(2,1)} %refs_3_.1, ...), custom_call_target="tpu_custom_call" | custom-call | flops 536870912 | bytes 11078660 | tf_op jit(solution)/shard_map/coarse_backward/pallas_call | solution.py:395
  69.4 0.0 copy-start.22
  69.4 0.2 collective-permute-start.5
  69.6 2.7 %collective-permute-done.5.refs_1_ = bf16[8,128,512]{2,1,0:T(8,128)(2,1)S(1)} collective-permute-done((bf16[8,128,512]{2,1,0:T(8,128)(2,1)}, bf16[8,128,512]{2,1,0:T(8,128)(2,1)S(1)}, u32[]{:S(2)}, u32[]{:S(2)}) %collective-permute-start.5) | collective-permute-done | bytes 1048608 | tf_op jit(solution)/shard_map/ppermute | solution.py:415
  72.3 1.0 copy-done
  73.3 3.2 %first_halving.3 = (f32[4,128,512]{2,1,0:T(8,128)}, bf16[4,128,512]{2,1,0:T(8,128)(2,1)}, bf16[16,8,512]{2,1,0:T(8,128)(2,1)}) custom-call(f32[8,128,512]{2,1,0:T(8,128)} %get-tuple-element.98.refs_0_, bf16[8,128,512]{2,1,0:T(8,128)(2,1)} %copy-done, bf16[16,8,512]{2,1,0:T(8,128)(2,1)} %get-tuple-element.100.refs_2_), custom_call_target="tpu_custom_call", output_to_operand_aliasing={{2}: (2, {})} | custom-call | bytes 4980736 | tf_op jit(solution)/shard_map/first_halving/pallas_call | solution.py:395
  76.5 0.6 collective-permute-start.10
  77.1 1.5 %collective-permute-start.14 = (bf16[4,96,512]{2,1,0:T(8,128)(2,1)S(1)}, bf16[4,96,512]{2,1,0:T(8,128)(2,1)S(1)}, u32[]{:S(2)}, u32[]{:S(2)}) collective-permute-start(bf16[4,96,512]{2,1,0:T(8,128)(2,1)S(1)} %copy-done.18), channel_id=1, source_target_pairs={{0,2},{1,3},{2,0},{3,1},{4,6},{5,7},{6,4},{7,5},{8,10},{9,11},{10,... | collective-permute-start | bytes 1179656 | tf_op jit(solution)/shard_map/ppermute | solution.py:415
  78.6 1.2 collective-permute-start.7
  79.8 6.9 %all-to-all-start.3 = ((bf16[16,8,512]{2,1,0:T(8,128)(2,1)}), bf16[16,8,512]{2,1,0:T(8,128)(2,1)S(1)}, u32[]{:S(2)}, u32[]{:S(2)}) async-start(bf16[16,8,512]{2,1,0:T(8,128)(2,1)} %get-tuple-element.101), calls=%async_computation.3 | async-start | bytes 262144 | tf_op jit(solution)/shard_map/all_to_all | solution.py:419
  86.7 17.9 %collective-permute-done.14.refs_1_ = bf16[4,96,512]{2,1,0:T(8,128)(2,1)S(1)} collective-permute-done((bf16[4,96,512]{2,1,0:T(8,128)(2,1)S(1)}, bf16[4,96,512]{2,1,0:T(8,128)(2,1)S(1)}, u32[]{:S(2)}, u32[]{:S(2)}) %collective-permute-start.14) | collective-permute-done | bytes 393248 | tf_op jit(solution)/shard_map/ppermute | solution.py:415
  104.6 0.8 copy-done.6
  105.4 2.1 %second_halving.3 = (f32[96,512]{1,0:T(8,128)}, bf16[96,512]{1,0:T(8,128)(2,1)}, bf16[96,512]{1,0:T(8,128)(2,1)}, bf16[96,512]{1,0:T(8,128)(2,1)}) custom-call(f32[4,96,512]{2,1,0:T(8,128)} %get-tuple-element.116.refs_0_, bf16[4,96,512]{2,1,0:T(8,128)(2,1)} %copy-done.6), custom_call_target="tpu_custom_call" | custom-call | bytes 1671168 | tf_op jit(solution)/shard_map/second_halving/pallas_call | solution.py:395
  107.5 0.6 collective-permute-start.15
  108.1 2.3 %collective-permute-start.16 = (bf16[96,512]{1,0:T(8,128)(2,1)}, bf16[96,512]{1,0:T(8,128)(2,1)S(1)}, u32[]{:S(2)}, u32[]{:S(2)}) collective-permute-start(bf16[96,512]{1,0:T(8,128)(2,1)} %get-tuple-element.120), channel_id=1, source_target_pairs={{0,8},{1,9},{2,10},{3,11},{4,12},{5,13},{6,14},{7,15},{8,0},{9,1},... | collective-permute-start | bytes 294920 | tf_op jit(solution)/shard_map/ppermute | solution.py:415
  110.5 0.6 collective-permute-start.17
  111.0 0.1 collective-permute-start.8
  111.1 0.5 collective-permute-start.9
  111.6 0.3 copy-done.3
  111.9 2.3 %second_halving.2 = (f32[128,512]{1,0:T(8,128)}, bf16[128,512]{1,0:T(8,128)(2,1)}, bf16[128,512]{1,0:T(8,128)(2,1)}, bf16[128,512]{1,0:T(8,128)(2,1)}) custom-call(f32[4,128,512]{2,1,0:T(8,128)} %get-tuple-element.108.refs_0_, bf16[4,128,512]{2,1,0:T(8,128)(2,1)} %copy-done.3), custom_call_target="tpu_custom_call" | custom-call | bytes 2228224 | tf_op jit(solution)/shard_map/second_halving/pallas_call | solution.py:395
  114.2 1.5 %collective-permute-start.11 = (bf16[128,512]{1,0:T(8,128)(2,1)}, bf16[128,512]{1,0:T(8,128)(2,1)S(1)}, u32[]{:S(2)}, u32[]{:S(2)}) collective-permute-start(bf16[128,512]{1,0:T(8,128)(2,1)} %get-tuple-element.111), channel_id=1, source_target_pairs={{0,4},{1,5},{2,6},{3,7},{4,0},{5,1},{6,2},{7,3},{8,12},{9,13},{10,... | collective-permute-start | bytes 393224 | tf_op jit(solution)/shard_map/ppermute | solution.py:415
  115.8 1.7 %collective-permute-done.16.refs_2_ = bf16[96,512]{1,0:T(8,128)(2,1)S(1)} collective-permute-done((bf16[96,512]{1,0:T(8,128)(2,1)}, bf16[96,512]{1,0:T(8,128)(2,1)S(1)}, u32[]{:S(2)}, u32[]{:S(2)}) %collective-permute-start.16) | collective-permute-done | bytes 98336 | tf_op jit(solution)/shard_map/ppermute | solution.py:415
  117.5 3.4 %collective-permute-start.12 = (bf16[128,512]{1,0:T(8,128)(2,1)}, bf16[128,512]{1,0:T(8,128)(2,1)S(1)}, u32[]{:S(2)}, u32[]{:S(2)}) collective-permute-start(bf16[128,512]{1,0:T(8,128)(2,1)} %get-tuple-element.112), channel_id=1, source_target_pairs={{0,8},{1,9},{2,10},{3,11},{4,12},{5,13},{6,14},{7,15},{8,0},{9,1},... | collective-permute-start | bytes 393224 | tf_op jit(solution)/shard_map/ppermute | solution.py:415
  120.9 9.2 %collective-permute-done.17.refs_3_ = bf16[96,512]{1,0:T(8,128)(2,1)S(1)} collective-permute-done((bf16[96,512]{1,0:T(8,128)(2,1)}, bf16[96,512]{1,0:T(8,128)(2,1)S(1)}, u32[]{:S(2)}, u32[]{:S(2)}) %collective-permute-start.17) | collective-permute-done | bytes 98336 | tf_op jit(solution)/shard_map/ppermute | solution.py:415
  130.1 0.6 copy-done.17
  130.7 1.8 %last_sum.3 = (f32[64,512]{1,0:T(8,128)}, f32[32,512]{1,0:T(8,128)}) custom-call(f32[96,512]{1,0:T(8,128)} %get-tuple-element.118.refs_0_, bf16[96,512]{1,0:T(8,128)(2,1)} %copy-done.15, bf16[96,512]{1,0:T(8,128)(2,1)} %copy-done.16, bf16[96,512]{1,0:T(8,128)(2,1)} %copy-done.17), custom_call_target="tpu_custom_call" | custom-call | bytes 688128 | tf_op jit(solution)/shard_map/last_sum/pallas_call | solution.py:395
  132.6 0.0 copy-start.5
  132.6 0.6 copy-done.13
  133.2 0.1 copy-done.14
  133.3 0.0 copy-done.5
  133.3 2.5 %node_gradient.1 = bf16[256,512]{1,0:T(8,128)(2,1)} custom-call(f32[256,512]{1,0:T(8,128)} %get-tuple-element.88.refs_0_, s32[4,128]{1,0:T(4,128)} %bitcast.13, bf16[16,8,512]{2,1,0:T(8,128)(2,1)} %copy-done.5, bf16[128,512]{1,0:T(8,128)(2,1)} %copy-done.11, bf16[128,512]{1,0:T(8,128)(2,1)} %copy-done.12, bf16[128,512]{1,0:T(8,128)(2,1)} %copy-done.13, ...), custom_call_target="tpu_custom_call" | custom-call | flops 134217728 | bytes 1443840 | tf_op jit(solution)/shard_map/node_gradient/pallas_call | solution.py:395
  135.8 0.6 copy-done.7
  136.4 0.1 copy-done.8
  136.5 0.0 copy-done.9
  136.6 1.9 %last_sum.2 = (f32[96,512]{1,0:T(8,128)}, f32[32,512]{1,0:T(8,128)}) custom-call(f32[128,512]{1,0:T(8,128)} %get-tuple-element.110.refs_0_, bf16[128,512]{1,0:T(8,128)(2,1)} %copy-done.7, bf16[128,512]{1,0:T(8,128)(2,1)} %copy-done.8, bf16[128,512]{1,0:T(8,128)(2,1)} %copy-done.9), custom_call_target="tpu_custom_call" | custom-call | bytes 917504 | tf_op jit(solution)/shard_map/last_sum/pallas_call | solution.py:395
  (47 shorter events, 0.1 us)
Async XLA Ops:
  2.7 11.2 %all-to-all-start = ((bf16[16,8,512]{2,1,0:T(8,128)(2,1)}), bf16[16,8,512]{2,1,0:T(8,128)(2,1)S(1)}, u32[]{:S(2)}, u32[]{:S(2)}) async-start(bf16[16,8,512]{2,1,0:T(8,128)(2,1)} %get-tuple-element.72), calls=%async_computation | async-start | bytes 262144 | tf_op jit(solution)/shard_map/all_to_all | solution.py:419
  9.0 17.0 %collective-permute-start = (bf16[128,512]{1,0:T(8,128)(2,1)}, bf16[128,512]{1,0:T(8,128)(2,1)S(1)}, u32[]{:S(2)}, u32[]{:S(2)}) collective-permute-start(bf16[128,512]{1,0:T(8,128)(2,1)} %get-tuple-element.67), channel_id=1, source_target_pairs={{15,0},{0,1},{1,2},{2,3},{3,4},{4,5},{5,6},{6,7},{7,8},{8,9},{9,10... | collective-permute-start | bytes 393224 | tf_op jit(solution)/shard_map/ppermute | solution.py:411
  9.1 16.9 %collective-permute-start.1 = (bf16[128,512]{1,0:T(8,128)(2,1)}, bf16[128,512]{1,0:T(8,128)(2,1)S(1)}, u32[]{:S(2)}, u32[]{:S(2)}) collective-permute-start(bf16[128,512]{1,0:T(8,128)(2,1)} %get-tuple-element.68), channel_id=1, source_target_pairs={{14,0},{15,1},{0,2},{1,3},{2,4},{3,5},{4,6},{5,7},{6,8},{7,9},{8,1... | collective-permute-start | bytes 393224 | tf_op jit(solution)/shard_map/ppermute | solution.py:411
  10.6 15.4 %collective-permute-start.2 = (bf16[128,512]{1,0:T(8,128)(2,1)}, bf16[128,512]{1,0:T(8,128)(2,1)S(1)}, u32[]{:S(2)}, u32[]{:S(2)}) collective-permute-start(bf16[128,512]{1,0:T(8,128)(2,1)} %get-tuple-element.69), channel_id=1, source_target_pairs={{1,0},{2,1},{3,2},{4,3},{5,4},{6,5},{7,6},{8,7},{9,8},{10,9},{11,1... | collective-permute-start | bytes 393224 | tf_op jit(solution)/shard_map/ppermute | solution.py:411
  11.9 14.1 %collective-permute-start.3 = (bf16[128,512]{1,0:T(8,128)(2,1)}, bf16[128,512]{1,0:T(8,128)(2,1)S(1)}, u32[]{:S(2)}, u32[]{:S(2)}) collective-permute-start(bf16[128,512]{1,0:T(8,128)(2,1)} %get-tuple-element.70), channel_id=1, source_target_pairs={{2,0},{3,1},{4,2},{5,3},{6,4},{7,5},{8,6},{9,7},{10,8},{11,9},{12,... | collective-permute-start | bytes 393224 | tf_op jit(solution)/shard_map/ppermute | solution.py:411
  13.9 0.7 copy-start.4
  18.4 15.6 %all-to-all-start.1 = ((bf16[16,8,512]{2,1,0:T(8,128)(2,1)}), bf16[16,8,512]{2,1,0:T(8,128)(2,1)S(1)}, u32[]{:S(2)}, u32[]{:S(2)}) async-start(bf16[16,8,512]{2,1,0:T(8,128)(2,1)} %get-tuple-element.73), calls=%async_computation.1 | async-start | bytes 262144 | tf_op jit(solution)/shard_map/all_to_all | solution.py:419
  26.0 0.7 copy-start.23
  26.0 0.7 copy-start.24
  26.0 0.7 copy-start.25
  26.1 0.7 copy-start.26
  34.0 0.7 copy-start.10
  40.5 6.3 %collective-permute-start.4 = (bf16[8,96,512]{2,1,0:T(8,128)(2,1)}, bf16[8,96,512]{2,1,0:T(8,128)(2,1)S(1)}, u32[]{:S(2)}, u32[]{:S(2)}) collective-permute-start(bf16[8,96,512]{2,1,0:T(8,128)(2,1)} %get-tuple-element.79), channel_id=1, source_target_pairs={{0,1},{1,0},{2,3},{3,2},{4,5},{5,4},{6,7},{7,6},{8,9},{9,8},{10,11... | collective-permute-start | bytes 2359304 | tf_op jit(solution)/shard_map/ppermute | solution.py:415
  40.7 20.1 %all-to-all-start.2 = ((bf16[16,8,512]{2,1,0:T(8,128)(2,1)}), bf16[16,8,512]{2,1,0:T(8,128)(2,1)S(1)}, u32[]{:S(2)}, u32[]{:S(2)}) async-start(bf16[16,8,512]{2,1,0:T(8,128)(2,1)} %get-tuple-element.89), calls=%async_computation.2 | async-start | bytes 262144 | tf_op jit(solution)/shard_map/all_to_all | solution.py:419
  46.8 0.9 copy-start.1
  60.8 0.7 copy-start.2
  69.3 7.8 %copy-start.18 = (bf16[4,96,512]{2,1,0:T(8,128)(2,1)S(1)}, bf16[4,96,512]{2,1,0:T(8,128)(2,1)}, u32[]{:S(2)}) copy-start(bf16[4,96,512]{2,1,0:T(8,128)(2,1)} %get-tuple-element.117) | copy-start | bytes 1179652
  69.4 9.2 %copy-start.22 = (bf16[128,512]{1,0:T(8,128)(2,1)S(1)}, bf16[128,512]{1,0:T(8,128)(2,1)}, u32[]{:S(2)}) copy-start(bf16[128,512]{1,0:T(8,128)(2,1)} %get-tuple-element.102) | copy-start | bytes 393220
  69.4 9.2 %copy-start.21 = (bf16[128,512]{1,0:T(8,128)(2,1)S(1)}, bf16[128,512]{1,0:T(8,128)(2,1)}, u32[]{:S(2)}) copy-start(bf16[128,512]{1,0:T(8,128)(2,1)} %get-tuple-element.103) | copy-start | bytes 393220
  69.4 2.9 %collective-permute-start.5 = (bf16[8,128,512]{2,1,0:T(8,128)(2,1)}, bf16[8,128,512]{2,1,0:T(8,128)(2,1)S(1)}, u32[]{:S(2)}, u32[]{:S(2)}) collective-permute-start(bf16[8,128,512]{2,1,0:T(8,128)(2,1)} %get-tuple-element.99), channel_id=1, source_target_pairs={{0,1},{1,0},{2,3},{3,2},{4,5},{5,4},{6,7},{7,6},{8,9},{9,8},{10,11... | collective-permute-start | bytes 3145736 | tf_op jit(solution)/shard_map/ppermute | solution.py:415
  72.3 1.0 copy-start
  73.3 37.7 %copy-start.20 = (bf16[128,512]{1,0:T(8,128)(2,1)S(1)}, bf16[128,512]{1,0:T(8,128)(2,1)}, u32[]{:S(2)}) copy-start(bf16[128,512]{1,0:T(8,128)(2,1)} %get-tuple-element.104) | copy-start | bytes 393220
  73.3 37.8 %copy-start.19 = (bf16[128,512]{1,0:T(8,128)(2,1)S(1)}, bf16[128,512]{1,0:T(8,128)(2,1)}, u32[]{:S(2)}) copy-start(bf16[128,512]{1,0:T(8,128)(2,1)} %get-tuple-element.105) | copy-start | bytes 393220
  76.5 34.6 %collective-permute-start.10 = (bf16[4,128,512]{2,1,0:T(8,128)(2,1)}, bf16[4,128,512]{2,1,0:T(8,128)(2,1)S(1)}, u32[]{:S(2)}, u32[]{:S(2)}) collective-permute-start(bf16[4,128,512]{2,1,0:T(8,128)(2,1)} %get-tuple-element.109), channel_id=1, source_target_pairs={{0,2},{1,3},{2,0},{3,1},{4,6},{5,7},{6,4},{7,5},{8,10},{9,11},{10,... | collective-permute-start | bytes 1572872 | tf_op jit(solution)/shard_map/ppermute | solution.py:415
  77.1 27.5 %collective-permute-start.14 = (bf16[4,96,512]{2,1,0:T(8,128)(2,1)S(1)}, bf16[4,96,512]{2,1,0:T(8,128)(2,1)S(1)}, u32[]{:S(2)}, u32[]{:S(2)}) collective-permute-start(bf16[4,96,512]{2,1,0:T(8,128)(2,1)S(1)} %copy-done.18), channel_id=1, source_target_pairs={{0,2},{1,3},{2,0},{3,1},{4,6},{5,7},{6,4},{7,5},{8,10},{9,11},{10,... | collective-permute-start | bytes 1179656 | tf_op jit(solution)/shard_map/ppermute | solution.py:415
  78.6 31.9 %collective-permute-start.6 = (bf16[128,512]{1,0:T(8,128)(2,1)S(1)}, bf16[128,512]{1,0:T(8,128)(2,1)S(1)}, u32[]{:S(2)}, u32[]{:S(2)}) collective-permute-start(bf16[128,512]{1,0:T(8,128)(2,1)S(1)} %copy-done.22), channel_id=1, source_target_pairs={{1,0},{2,1},{3,2},{4,3},{5,4},{6,5},{7,6},{8,7},{9,8},{10,9},{11,1... | collective-permute-start | bytes 393224 | tf_op jit(solution)/shard_map/ppermute | solution.py:411
  78.6 32.4 %collective-permute-start.7 = (bf16[128,512]{1,0:T(8,128)(2,1)S(1)}, bf16[128,512]{1,0:T(8,128)(2,1)S(1)}, u32[]{:S(2)}, u32[]{:S(2)}) collective-permute-start(bf16[128,512]{1,0:T(8,128)(2,1)S(1)} %copy-done.21), channel_id=1, source_target_pairs={{2,0},{3,1},{4,2},{5,3},{6,4},{7,5},{8,6},{9,7},{10,8},{11,9},{12,... | collective-permute-start | bytes 393224 | tf_op jit(solution)/shard_map/ppermute | solution.py:411
  79.8 52.7 %all-to-all-start.3 = ((bf16[16,8,512]{2,1,0:T(8,128)(2,1)}), bf16[16,8,512]{2,1,0:T(8,128)(2,1)S(1)}, u32[]{:S(2)}, u32[]{:S(2)}) async-start(bf16[16,8,512]{2,1,0:T(8,128)(2,1)} %get-tuple-element.101), calls=%async_computation.3 | async-start | bytes 262144 | tf_op jit(solution)/shard_map/all_to_all | solution.py:419
  104.6 0.8 copy-start.6
  107.5 6.7 %collective-permute-start.15 = (bf16[96,512]{1,0:T(8,128)(2,1)}, bf16[96,512]{1,0:T(8,128)(2,1)S(1)}, u32[]{:S(2)}, u32[]{:S(2)}) collective-permute-start(bf16[96,512]{1,0:T(8,128)(2,1)} %get-tuple-element.119), channel_id=1, source_target_pairs={{0,4},{1,5},{2,6},{3,7},{4,0},{5,1},{6,2},{7,3},{8,12},{9,13},{10,... | collective-permute-start | bytes 294920 | tf_op jit(solution)/shard_map/ppermute | solution.py:415
  108.1 9.4 %collective-permute-start.16 = (bf16[96,512]{1,0:T(8,128)(2,1)}, bf16[96,512]{1,0:T(8,128)(2,1)S(1)}, u32[]{:S(2)}, u32[]{:S(2)}) collective-permute-start(bf16[96,512]{1,0:T(8,128)(2,1)} %get-tuple-element.120), channel_id=1, source_target_pairs={{0,8},{1,9},{2,10},{3,11},{4,12},{5,13},{6,14},{7,15},{8,0},{9,1},... | collective-permute-start | bytes 294920 | tf_op jit(solution)/shard_map/ppermute | solution.py:415
  110.5 22.1 %copy-start.11 = (bf16[128,512]{1,0:T(8,128)(2,1)}, bf16[128,512]{1,0:T(8,128)(2,1)S(1)}, u32[]{:S(2)}) copy-start(bf16[128,512]{1,0:T(8,128)(2,1)S(1)} %collective-permute-done.6.refs_3_) | copy-start | bytes 393220
  110.5 19.6 %collective-permute-start.17 = (bf16[96,512]{1,0:T(8,128)(2,1)}, bf16[96,512]{1,0:T(8,128)(2,1)S(1)}, u32[]{:S(2)}, u32[]{:S(2)}) collective-permute-start(bf16[96,512]{1,0:T(8,128)(2,1)} %get-tuple-element.121), channel_id=1, source_target_pairs={{0,12},{1,13},{2,14},{3,15},{4,8},{5,9},{6,10},{7,11},{8,4},{9,5},... | collective-permute-start | bytes 294920 | tf_op jit(solution)/shard_map/ppermute | solution.py:415
  111.0 21.6 %copy-start.12 = (bf16[128,512]{1,0:T(8,128)(2,1)}, bf16[128,512]{1,0:T(8,128)(2,1)S(1)}, u32[]{:S(2)}) copy-start(bf16[128,512]{1,0:T(8,128)(2,1)S(1)} %collective-permute-done.7.refs_4_) | copy-start | bytes 393220
  111.0 21.5 %collective-permute-start.8 = (bf16[128,512]{1,0:T(8,128)(2,1)S(1)}, bf16[128,512]{1,0:T(8,128)(2,1)S(1)}, u32[]{:S(2)}, u32[]{:S(2)}) collective-permute-start(bf16[128,512]{1,0:T(8,128)(2,1)S(1)} %copy-done.20), channel_id=1, source_target_pairs={{15,0},{0,1},{1,2},{2,3},{3,4},{4,5},{5,6},{6,7},{7,8},{8,9},{9,10... | collective-permute-start | bytes 393224 | tf_op jit(solution)/shard_map/ppermute | solution.py:411
  111.1 0.8 copy-start.3
  111.1 21.4 %collective-permute-start.9 = (bf16[128,512]{1,0:T(8,128)(2,1)S(1)}, bf16[128,512]{1,0:T(8,128)(2,1)S(1)}, u32[]{:S(2)}, u32[]{:S(2)}) collective-permute-start(bf16[128,512]{1,0:T(8,128)(2,1)S(1)} %copy-done.19), channel_id=1, source_target_pairs={{14,0},{15,1},{0,2},{1,3},{2,4},{3,5},{4,6},{5,7},{6,8},{7,9},{8,1... | collective-permute-start | bytes 393224 | tf_op jit(solution)/shard_map/ppermute | solution.py:411
  114.2 15.9 %copy-start.15 = (bf16[96,512]{1,0:T(8,128)(2,1)}, bf16[96,512]{1,0:T(8,128)(2,1)S(1)}, u32[]{:S(2)}) copy-start(bf16[96,512]{1,0:T(8,128)(2,1)S(1)} %collective-permute-done.15.refs_1_) | copy-start | bytes 294916
  114.2 21.6 %collective-permute-start.11 = (bf16[128,512]{1,0:T(8,128)(2,1)}, bf16[128,512]{1,0:T(8,128)(2,1)S(1)}, u32[]{:S(2)}, u32[]{:S(2)}) collective-permute-start(bf16[128,512]{1,0:T(8,128)(2,1)} %get-tuple-element.111), channel_id=1, source_target_pairs={{0,4},{1,5},{2,6},{3,7},{4,0},{5,1},{6,2},{7,3},{8,12},{9,13},{10,... | collective-permute-start | bytes 393224 | tf_op jit(solution)/shard_map/ppermute | solution.py:415
  117.5 12.6 %copy-start.16 = (bf16[96,512]{1,0:T(8,128)(2,1)}, bf16[96,512]{1,0:T(8,128)(2,1)S(1)}, u32[]{:S(2)}) copy-start(bf16[96,512]{1,0:T(8,128)(2,1)S(1)} %collective-permute-done.16.refs_2_) | copy-start | bytes 294916
  117.5 18.3 %collective-permute-start.12 = (bf16[128,512]{1,0:T(8,128)(2,1)}, bf16[128,512]{1,0:T(8,128)(2,1)S(1)}, u32[]{:S(2)}, u32[]{:S(2)}) collective-permute-start(bf16[128,512]{1,0:T(8,128)(2,1)} %get-tuple-element.112), channel_id=1, source_target_pairs={{0,8},{1,9},{2,10},{3,11},{4,12},{5,13},{6,14},{7,15},{8,0},{9,1},... | collective-permute-start | bytes 393224 | tf_op jit(solution)/shard_map/ppermute | solution.py:415
  130.1 0.6 copy-start.17
  130.1 5.7 %collective-permute-start.13 = (bf16[128,512]{1,0:T(8,128)(2,1)}, bf16[128,512]{1,0:T(8,128)(2,1)S(1)}, u32[]{:S(2)}, u32[]{:S(2)}) collective-permute-start(bf16[128,512]{1,0:T(8,128)(2,1)} %get-tuple-element.113), channel_id=1, source_target_pairs={{0,12},{1,13},{2,14},{3,15},{4,8},{5,9},{6,10},{7,11},{8,4},{9,5},... | collective-permute-start | bytes 393224 | tf_op jit(solution)/shard_map/ppermute | solution.py:415
  132.5 0.7 copy-start.13
  132.6 0.7 copy-start.14
  132.6 0.7 copy-start.5
  135.8 0.6 copy-start.7
  135.8 0.7 copy-start.8
  135.8 0.7 copy-start.9

commit v4 on v3

v4 whole, which is shorter than its diff:
```python
import functools

import jax
import jax.numpy as jnp
from jax import lax
from jax.experimental import pallas as pl
from jax.experimental.pallas import tpu as pltpu
from jax.sharding import PartitionSpec as P

COARSE_DEV = 8
EPSILON = 1e-05
F32 = jnp.float32
BF16 = jnp.bfloat16
VMEM_LIMIT = 60 * 1024 * 1024
SMALL_LIMIT = 16 * 1024 * 1024


def mm(a, b):
    return lax.dot_general(a, b, (((1,), (0,)), ((), ())), preferred_element_type=F32)


def mm_nt(a, b):
    return lax.dot_general(a, b, (((1,), (1,)), ((), ())), preferred_element_type=F32)


def mm_tn(a, b):
    return lax.dot_general(a, b, (((0,), (0,)), ((), ())), preferred_element_type=F32)


def halves(value):
    high = value.astype(BF16)
    low = (value - high.astype(F32)).astype(BF16)
    return high, low


def one_hot(index, rows):
    row = lax.broadcasted_iota(jnp.int32, (rows, index.shape[1]), 0)
    return jnp.where(row == index, 1.0, 0.0).astype(BF16)


def pick(hot, table):
    return mm_tn(hot, table)


def pick_wide(hot, table):
    high, low = halves(table)
    return mm_tn(hot, high) + mm_tn(hot, low)


def put_wide(hot, rows):
    high, low = halves(rows)
    return mm(hot, high) + mm(hot, low)


def row_mean(value):
    return jnp.mean(value, axis=-1, keepdims=True)


def tail_of_forward(pre, second_w, gain):
    sigmoid = jax.nn.sigmoid(pre)
    hidden = (pre * sigmoid).astype(BF16)
    slope = sigmoid * (1.0 + pre * (1.0 - sigmoid))
    output = mm(hidden, second_w)
    centred = output - row_mean(output)
    inv_std = lax.rsqrt(row_mean(centred * centred) + EPSILON)
    normed = centred * inv_std
    return normed * gain, hidden, slope, normed, inv_std


def head_of_backward(cotan, second_w, gain, slope, normed, inv_std):
    scaled = cotan * gain
    back_out = inv_std * (scaled - row_mean(scaled) - normed * row_mean(scaled * normed))
    back_out = back_out.astype(BF16)
    back_pre = (mm_nt(back_out, second_w) * slope).astype(BF16)
    return back_out, back_pre


def tiles_kernel(nodes_ref, halo_ref, *outs):
    spread_ref = outs[-1]
    nodes = nodes_ref[...]
    for slot, out in enumerate(outs[:-1]):
        hot = one_hot(halo_ref[slot : slot + 1, :], nodes.shape[0])
        out[...] = pick(hot, nodes).astype(BF16)
        out.done()
    rows = nodes_ref[0:16, :].astype(F32)[:COARSE_DEV].astype(BF16)
    for peer in range(spread_ref.shape[0]):
        spread_ref[peer] = rows


def gathered(ref):
    value = ref[...].astype(F32)
    return value.reshape(value.shape[0] * value.shape[1], value.shape[2])


def coarse_forward_kernel(
    all_ref, edges_ref, send_ref, recv_ref, w1_ref, w2_ref, gain_ref,
    new_ref, part_ref, zs_ref, zr_ref, hidden_ref, slope_ref, normed_ref, std_ref,
):
    width = edges_ref.shape[1]
    table = gathered(all_ref).astype(BF16)
    hot_s = one_hot(send_ref[...], table.shape[0])
    hot_r = one_hot(recv_ref[...], table.shape[0])
    edges = edges_ref[...]
    zs = pick(hot_s, table).astype(BF16)
    zr = pick(hot_r, table).astype(BF16)
    pre = (
        mm(edges, w1_ref[0:width, :])
        + mm(zs, w1_ref[width : 2 * width, :])
        + mm(zr, w1_ref[2 * width : 3 * width, :])
    )
    message, hidden, slope, normed, inv_std = tail_of_forward(pre, w2_ref[...], gain_ref[...])
    total = put_wide(hot_r, message)
    part_ref[...] = total.reshape(part_ref.shape).astype(BF16)
    part_ref.done()
    new_ref[...] = (edges.astype(F32) + message).astype(BF16)
    zs_ref[...] = zs
    zr_ref[...] = zr
    hidden_ref[...] = hidden
    slope_ref[...] = slope.astype(BF16)
    normed_ref[...] = normed.astype(BF16)
    std_ref[...] = jnp.broadcast_to(inv_std, std_ref.shape)


def fine_forward_kernel(count_ref, nodes_ref, *refs, slots, block):
    tile_refs = refs[:slots]
    (
        edges_ref, send_ref, recv_ref, w1_ref, w2_ref, gain_ref,
        new_ref, agg_ref, zs_ref, zr_ref, hidden_ref, slope_ref, normed_ref, std_ref, space_ref,
    ) = refs[slots:]
    count, width = edges_ref.shape
    own = nodes_ref.shape[0]
    tile = tile_refs[0].shape[0]
    space_ref[0:own, :] = nodes_ref[...]
    for slot in range(slots):
        space_ref[own + slot * tile : own + (slot + 1) * tile, :] = tile_refs[slot][...]
    for start in range(0, count, block):
        rows = slice(start, start + block)
        edges = edges_ref[rows, :]
        hot_s = one_hot(send_ref[:, rows], space_ref.shape[0])
        hot_r = one_hot(recv_ref[:, rows], own)
        zs = pick(hot_s, space_ref[...]).astype(BF16)
        zr = pick(hot_r, nodes_ref[...]).astype(BF16)
        pre = (
            mm(edges, w1_ref[0:width, :])
            + mm(zs, w1_ref[width : 2 * width, :])
            + mm(zr, w1_ref[2 * width : 3 * width, :])
        )
        message, hidden, slope, normed, inv_std = tail_of_forward(pre, w2_ref[...], gain_ref[...])
        place = start + lax.broadcasted_iota(jnp.int32, (block, 1), 0)
        message = jnp.where(place < count_ref[0], message, 0.0)
        arrived = put_wide(hot_r, message)
        agg_ref[...] = arrived if start == 0 else agg_ref[...] + arrived
        new_ref[rows, :] = (edges.astype(F32) + message).astype(BF16)
        zs_ref[rows, :] = zs
        zr_ref[rows, :] = zr
        hidden_ref[rows, :] = hidden
        slope_ref[rows, :] = slope.astype(BF16)
        normed_ref[rows, :] = normed.astype(BF16)
        std_ref[rows, :] = jnp.broadcast_to(inv_std, (block, std_ref.shape[1]))
        for ref in (new_ref, zs_ref, zr_ref, hidden_ref, slope_ref, normed_ref, std_ref):
            ref.done(rows)


def by_distance(me, peers, sums, kept_ref, given_ref):
    for r in list(range(1, peers, 2)) + list(range(0, peers, 2)):
        if r == 0:
            given_ref.done()
        to = jnp.bitwise_xor(me, r)
        out = given_ref if r % 2 else kept_ref
        place = 0
        for total in sums:
            rows = total.shape[0] // peers
            part = total[pl.ds(pl.multiple_of(to * rows, 8), rows), :]
            if rows % 16:
                part = jnp.concatenate([part, jnp.zeros((-rows % 16, part.shape[1]), F32)], 0)
            out[r // 2, place : place + part.shape[0], :] = part.astype(BF16)
            place += part.shape[0]


def node_kernel(
    me_ref, nodes_ref, agg_ref, share_ref, d_ref, w1_ref, w2_ref, gain_ref,
    new_ref, base_ref, dagg_ref, spread_ref, *rest, ordered,
):
    if ordered:
        kept_ref, given_ref, total_ref, g1_ref, g2_ref = rest
    else:
        g1_ref, g2_ref, total_ref = rest
    width = nodes_ref.shape[1]
    total_ref[...] = agg_ref[...]
    total_ref[0:COARSE_DEV, :] += jnp.sum(share_ref[...].astype(F32), 0)
    nodes = nodes_ref[...]
    agg = total_ref[...].astype(BF16)
    pre = mm(nodes, w1_ref[0:width, :]) + mm(agg, w1_ref[width : 2 * width, :])
    update, hidden, slope, normed, inv_std = tail_of_forward(pre, w2_ref[...], gain_ref[...])
    new_ref[...] = (nodes.astype(F32) + update).astype(BF16)
    cotan = d_ref[...].astype(F32)
    back_out, back_pre = head_of_backward(cotan, w2_ref[...], gain_ref[...], slope, normed, inv_std)
    dagg = mm_nt(back_pre, w1_ref[width : 2 * width, :])
    dagg_ref[...] = dagg.astype(BF16)
    rows = dagg[:COARSE_DEV].astype(BF16)
    for peer in range(spread_ref.shape[0]):
        spread_ref[peer] = rows
    base_ref[...] = cotan + mm_nt(back_pre, w1_ref[0:width, :])
    g1_ref[0:width, :] = mm_tn(nodes, back_pre)
    g1_ref[width : 2 * width, :] = mm_tn(agg, back_pre)
    g2_ref[...] = mm_tn(hidden, back_out)
    if ordered:
        by_distance(me_ref[0], spread_ref.shape[0], (g1_ref, g2_ref), kept_ref, given_ref)


def fine_backward_kernel(
    count_ref, recv_ref, dagg_ref, d_ref, gain_ref, std_ref, normed_ref, w2_ref, slope_ref,
    w1_ref, send_ref, base_ref,
    out_ref, pre_ref, g_ref, own_ref, *rest, block,
):
    piece_refs, space_ref = rest[:-1], rest[-1]
    count, width = d_ref.shape
    own = base_ref.shape[0]
    received = None
    for start in range(0, count, block):
        rows = slice(start, start + block)
        hot_r = one_hot(recv_ref[:, rows], own)
        d_edges = d_ref[rows, :].astype(F32)
        place = start + lax.broadcasted_iota(jnp.int32, (block, 1), 0)
        cotan = jnp.where(place < count_ref[0], d_edges + pick(hot_r, dagg_ref[...]), 0.0)
        back_out, back_pre = head_of_backward(
            cotan, w2_ref[...], gain_ref[...], slope_ref[rows, :].astype(F32),
            normed_ref[rows, :].astype(F32), std_ref[rows, 0:1],
        )
        out_ref[rows, :] = back_out
        pre_ref[rows, :] = back_pre
        out_ref.done(rows)
        pre_ref.done(rows)
        g_ref[rows, :] = (d_edges + mm_nt(back_pre, w1_ref[0:width, :])).astype(BF16)
        g_ref.done(rows)
        dz_send = mm_nt(back_pre, w1_ref[width : 2 * width, :]).astype(BF16)
        dz_recv = mm_nt(back_pre, w1_ref[2 * width : 3 * width, :]).astype(BF16)
        sent = mm(one_hot(send_ref[:, rows], space_ref.shape[0]), dz_send)
        space_ref[...] = sent if start == 0 else space_ref[...] + sent
        arrived = mm(hot_r, dz_recv)
        received = arrived if received is None else received + arrived
    for slot, piece in enumerate(piece_refs):
        tile = piece.shape[0]
        piece[...] = space_ref[own + slot * tile : own + (slot + 1) * tile, :].astype(BF16)
        piece.done()
    own_ref[...] = base_ref[...] + received + space_ref[0:own, :]


def coarse_backward_kernel(
    me_ref, recv_ref, all_ref, d_ref, gain_ref, std_ref, normed_ref, w2_ref, slope_ref,
    hidden_ref, out_ref, pre_ref, edges_ref, zs_ref, zr_ref, w1_ref, send_ref,
    g_ref, *rest, ordered,
):
    if ordered:
        kept_ref, given_ref, part_ref, g1_ref, g2_ref = rest
    else:
        part_ref, g1_ref, g2_ref = rest
    width = d_ref.shape[1]
    count = hidden_ref.shape[0]
    rows = slice(count - d_ref.shape[0], count)
    table = gathered(all_ref).astype(BF16)
    hot_r = one_hot(recv_ref[...], table.shape[0])
    d_edges = d_ref[...].astype(F32)
    cotan = d_edges + pick(hot_r, table)
    back_out, back_pre = head_of_backward(
        cotan, w2_ref[...], gain_ref[...], slope_ref[...].astype(F32), normed_ref[...].astype(F32), std_ref[:, 0:1]
    )
    out_ref[rows, :] = back_out
    pre_ref[rows, :] = back_pre
    g2_ref[...] = mm_tn(hidden_ref[...], out_ref[...])
    g1_ref[0:width, :] = mm_tn(edges_ref[...], pre_ref[...])
    g1_ref[width : 2 * width, :] = mm_tn(zs_ref[...], pre_ref[...])
    g1_ref[2 * width : 3 * width, :] = mm_tn(zr_ref[...], pre_ref[...])
    dz_send = mm_nt(back_pre, w1_ref[width : 2 * width, :]).astype(BF16)
    dz_recv = mm_nt(back_pre, w1_ref[2 * width : 3 * width, :]).astype(BF16)
    total = mm(one_hot(send_ref[...], table.shape[0]), dz_send) + mm(hot_r, dz_recv)
    if ordered:
        part_ref[...] = total
        by_distance(me_ref[0], 2 * kept_ref.shape[0], (g1_ref, g2_ref, part_ref), kept_ref, given_ref)
        kept_ref.done()
    else:
        part_ref[...] = total.reshape(part_ref.shape).astype(BF16)
    g_ref[...] = (d_edges + mm_nt(back_pre, w1_ref[0:width, :])).astype(BF16)


def node_gradient_kernel(own_ref, halo_ref, *refs, slots):
    piece_refs, out_ref = refs[:slots], refs[len(refs) - 1 - (len(refs) - 1 - slots) // 2]
    arrived = None
    for slot, piece in enumerate(piece_refs):
        part = mm(one_hot(halo_ref[slot : slot + 1, :], own_ref.shape[0]), piece[...])
        arrived = part if arrived is None else arrived + part
    out_ref[...] = own_ref[...] + arrived


def coarse_gradient_kernel(total_ref, share_ref, g_ref):
    share = jnp.sum(share_ref[...].astype(F32), 0)
    first = total_ref[0:16, :] + jnp.concatenate([share, jnp.zeros_like(share)], 0)
    g_ref[...] = total_ref[...].astype(BF16)
    g_ref[0:16, :] = first.astype(BF16)


def first_halving_kernel(kept_ref, taken_ref, *refs):
    passing = (len(refs) - 2) // 2
    keep_ref, give_ref = refs[passing : passing + 2]
    for j in range(kept_ref.shape[0]):
        total = (kept_ref[j].astype(F32) + taken_ref[j].astype(F32)).astype(BF16)
        out = give_ref if j % 2 else keep_ref
        out[j // 2] = total


def second_halving_kernel(kept_ref, taken_ref, *refs, passing):
    keep_ref, give_refs = refs[passing], refs[passing + 1 : len(refs) - passing]
    for j in range(kept_ref.shape[0]):
        total = kept_ref[j].astype(F32) + taken_ref[j].astype(F32)
        if j:
            give_refs[j - 1][...] = total.astype(BF16)
        else:
            keep_ref[...] = total


def last_sum_kernel(kept_ref, *refs, taken, with_nodes, passing):
    total = kept_ref[...]
    for ref in refs[:taken]:
        total = total + ref[...].astype(F32)
    if with_nodes:
        nodes_ref, first_ref, second_ref, g_ref = refs[taken:]
    else:
        first_ref, second_ref = refs[taken + passing : len(refs) - passing]
    cut = first_ref.shape[0]
    end = cut + second_ref.shape[0]
    first_ref[...] = total[:cut]
    second_ref[...] = total[cut:end]
    if with_nodes:
        g_ref[...] = nodes_ref[...].astype(BF16)
        g_ref[0:16, :] = (nodes_ref[0:16, :] + total[end : end + 16]).astype(BF16)


VM = pl.BlockSpec(memory_space=pltpu.VMEM)
SM = pl.BlockSpec(memory_space=pltpu.SMEM)
ANY = pl.BlockSpec(memory_space=pl.ANY)


def shape(dims, dtype):
    return jax.ShapeDtypeStruct(tuple(dims), dtype)


class Rows:
    def __init__(self, parts=1, joined=1, extra=0):
        self.parts = parts
        self.joined = joined
        self.extra = extra


class Fetched:
    def __init__(self, sources, buffer, semaphores, parts):
        self.buffer = buffer
        self.shape = buffer.shape
        self.waiting = []
        place = 0
        for source in sources:
            rows = source.shape[0] // parts
            for part in range(parts):
                if source.shape == buffer.shape and parts == 1:
                    copy = pltpu.make_async_copy(source, buffer, next(semaphores))
                else:
                    copy = pltpu.make_async_copy(
                        source.at[pl.ds(part * rows, rows)], buffer.at[pl.ds(place, rows)], next(semaphores)
                    )
                copy.start()
                self.waiting.append((place, place + rows, copy))
                place += rows

    def ready(self, low=0, high=None):
        left = []
        for first, last, copy in self.waiting:
            if high is None or (first < high and low < last):
                copy.wait()
            else:
                left.append((first, last, copy))
        self.waiting = left

    def __getitem__(self, index):
        rows = index[0] if isinstance(index, tuple) else None
        if isinstance(rows, slice) and rows.start is not None:
            self.ready(rows.start, rows.stop)
        else:
            self.ready()
        return self.buffer[index]

    def __setitem__(self, index, value):
        self.buffer[index] = value


class Stored:
    def __init__(self, target, buffer, semaphores):
        self.target = target
        self.buffer = buffer
        self.shape = buffer.shape
        self.dtype = buffer.dtype
        self.semaphores = semaphores
        self.copies = []

    def __getitem__(self, index):
        return self.buffer[index]

    def __setitem__(self, index, value):
        self.buffer[index] = value

    def done(self, rows=None):
        if rows is None:
            copy = pltpu.make_async_copy(self.buffer, self.target, next(self.semaphores))
        else:
            part = pl.ds(rows.start, rows.stop - rows.start)
            copy = pltpu.make_async_copy(self.buffer.at[part], self.target.at[part], next(self.semaphores))
        copy.start()
        self.copies.append(copy)


SEMAPHORES = 64


def staged_kernel(body, in_specs, out_specs, *refs):
    ins, outs = refs[: len(in_specs)], refs[len(in_specs) : len(in_specs) + len(out_specs)]
    rest = refs[len(in_specs) + len(out_specs) :]
    semaphores = iter([rest[0].at[i] for i in range(SEMAPHORES)])
    buffers = iter(rest[1:])
    fetched, stored = [], []
    for place, (ref, spec) in enumerate(zip(ins, in_specs)):
        if spec is VM:
            fetched.append(Fetched([ref], next(buffers), semaphores, 1))
        elif spec is SM:
            fetched.append(ref)
        elif isinstance(spec, Rows):
            fetched.append(Fetched(ins[place : place + spec.joined], next(buffers), semaphores, spec.parts))
    for ref, spec in zip(outs, out_specs):
        stored.append(Stored(ref, next(buffers), semaphores))
    body(*fetched, *stored, *buffers)
    for ref in fetched:
        if isinstance(ref, Fetched):
            ref.ready()
    for ref in stored:
        if not ref.copies:
            ref.done()
    for ref in stored:
        for copy in ref.copies:
            copy.wait()


def cost(ins, outs, flops):
    moved = sum(a.size * a.dtype.itemsize for a in list(ins) + list(outs))
    return pl.CostEstimate(flops=flops, bytes_accessed=moved, transcendentals=0)


def call(kernel, name, ins, in_specs, outs, scratch=(), flops=0):
    out_specs = [VM] * len(outs)
    buffers = []
    for place, spec in enumerate(in_specs):
        if spec is VM:
            buffers.append(pltpu.VMEM(ins[place].shape, ins[place].dtype))
        elif isinstance(spec, Rows):
            joined = ins[place : place + spec.joined]
            rows = sum(a.shape[0] for a in joined) + spec.extra
            buffers.append(pltpu.VMEM((rows,) + joined[0].shape[1:], joined[0].dtype))
    buffers += [pltpu.VMEM(a.shape, a.dtype) for a in outs]
    return pl.pallas_call(
        functools.partial(staged_kernel, kernel, in_specs, out_specs),
        out_shape=tuple(outs),
        in_specs=[SM if spec is SM else ANY for spec in in_specs],
        out_specs=tuple([ANY] * len(outs)),
        scratch_shapes=[pltpu.SemaphoreType.DMA((SEMAPHORES,))] + buffers + list(scratch),
        name=name,
        cost_estimate=cost(ins, outs, flops),
        compiler_params=pltpu.CompilerParams(vmem_limit_bytes=VMEM_LIMIT),
    )(*ins)


def small_call(kernel, name, ins, outs, passing=()):
    first = len(ins)
    last = len(outs)
    outs = list(outs) + [shape(a.shape, a.dtype) for a in passing]
    return pl.pallas_call(
        kernel,
        out_shape=tuple(outs),
        input_output_aliases={first + i: last + i for i in range(len(passing))},
        in_specs=[VM] * first + [ANY] * len(passing),
        out_specs=tuple([VM] * last + [ANY] * len(passing)),
        name=name,
        cost_estimate=cost(ins, outs, 0),
        compiler_params=pltpu.CompilerParams(vmem_limit_bytes=SMALL_LIMIT),
    )(*ins, *passing)


def passed_along(block, axis, distance):
    count = lax.axis_size(axis)
    route = [((i - distance) % count, i) for i in range(count)]
    return lax.ppermute(block, axis, route)


def exchanged(block, axis, distance):
    return lax.ppermute(block, axis, [(i, i ^ distance) for i in range(lax.axis_size(axis))])


def exchanged_with_all(blocks, axis):
    return lax.all_to_all(blocks, axis, 0, 0)


def first_halving(kept, taken, passing=()):
    half = shape((kept.shape[0] // 2,) + kept.shape[1:], BF16)
    return small_call(first_halving_kernel, "first_halving", (kept, taken), [half, half], passing)


def second_halving(kept, taken, passing=()):
    block = kept.shape[1:]
    outs = [shape(block, F32)] + [shape(block, BF16)] * (kept.shape[0] - 1)
    kernel = functools.partial(second_halving_kernel, passing=len(passing))
    return small_call(kernel, "second_halving", (kept, taken), outs, passing)


def last_sum(kept, taken, first_rows, second_rows, nodes=None, passing=()):
    width = kept.shape[1]
    outs = [shape((first_rows, width), F32), shape((second_rows, width), F32)]
    ins = (kept, *taken)
    if nodes is not None:
        outs.append(shape(nodes.shape, BF16))
        ins += (nodes,)
    kernel = functools.partial(
        last_sum_kernel, taken=len(taken), with_nodes=nodes is not None, passing=len(passing)
    )
    return small_call(kernel, "last_sum", ins, outs, passing)


def local(
    nodes,
    fine_edges,
    coarse_edges,
    fine_send,
    fine_recv,
    coarse_send,
    coarse_recv,
    halo_rows,
    edge_count,
    edge_w1,
    edge_w2,
    edge_gain,
    node_w1,
    node_w2,
    node_gain,
    d_nodes,
    d_fine,
    d_coarse,
):
    axis = "patch"
    peers = lax.axis_size(axis)
    own, width = nodes.shape
    fine = fine_edges.shape[0]
    coarse = coarse_edges.shape[0]
    halo = halo_rows[0]
    slots, tile = halo.shape
    hops = slots // 2
    offsets = list(range(1, hops + 1)) + [-k for k in range(1, hops + 1)]
    ordered = peers == 16 and all(
        w.shape[0] % (16 * peers) == 0 for w in (edge_w1, edge_w2, node_w1, node_w2)
    )
    me = lax.axis_index(axis).astype(jnp.int32).reshape(1)
    fs, fr = fine_send.reshape(1, fine), fine_recv.reshape(1, fine)
    cs, cr = coarse_send.reshape(1, coarse), coarse_recv.reshape(1, coarse)
    eg, ng = edge_gain.reshape(1, width), node_gain.reshape(1, width)
    every = shape((peers, COARSE_DEV, width), BF16)

    made = call(
        tiles_kernel, "tiles", (nodes, halo), [VM, VM],
        [shape((tile, width), BF16)] * slots + [every],
    )
    received = [passed_along(made[slot], axis, offset) for slot, offset in enumerate(offsets)]
    coarse_all = exchanged_with_all(made[-1], axis)

    def saved_shapes(rows):
        return [
            shape((rows, width), BF16), shape((rows, width), BF16), shape((rows, width), BF16),
            shape((rows, width), BF16), shape((rows, width), BF16), shape((rows, 128), F32),
        ]

    new_coarse, coarse_part, *coarse_saved = call(
        coarse_forward_kernel, "coarse_forward",
        (coarse_all, coarse_edges, cs, cr, edge_w1, edge_w2, eg), [VM] * 4 + [Rows(3), VM, VM],
        [shape((coarse, width), BF16), every] + saved_shapes(coarse),
        flops=2 * coarse * width * width * 4,
    )
    share = exchanged_with_all(coarse_part, axis)

    block = 256 if fine % 256 == 0 else fine
    space_rows = own + slots * tile
    new_fine, fine_agg, *fine_saved = call(
        functools.partial(fine_forward_kernel, slots=slots, block=block), "fine_forward",
        (edge_count, nodes, *received, fine_edges, fs, fr, edge_w1, edge_w2, eg),
        [SM] + [VM] * (slots + 4) + [Rows(3), VM, VM],
        [shape((fine, width), BF16), shape((own, width), F32)] + saved_shapes(fine),
        scratch=[pltpu.VMEM((space_rows, width), BF16)],
        flops=2 * fine * width * (4 * width + space_rows + 3 * own),
    )

    def weight_shapes(w1, w2, more):
        if not ordered:
            return [shape(w1.shape, F32), shape(w2.shape, F32)], []
        rows = (w1.shape[0] + w2.shape[0]) // peers + more
        outs = [shape((peers // 2, rows, width), BF16)] * 2
        return outs, [pltpu.VMEM(w1.shape, F32), pltpu.VMEM(w2.shape, F32)]

    sum_shapes, sum_scratch = weight_shapes(node_w1, node_w2, 0)
    new_nodes, base, dagg, dagg_spread, *node_parts = call(
        functools.partial(node_kernel, ordered=ordered), "node_both",
        (me, nodes, fine_agg, share, d_nodes, node_w1, node_w2, ng), [SM] + [VM] * 4 + [Rows(2), VM, VM],
        [shape((own, width), BF16), shape((own, width), F32), shape((own, width), BF16), every] + sum_shapes,
        scratch=[pltpu.VMEM((own, width), F32)] + sum_scratch,
        flops=2 * own * width * width * 9,
    )
    dagg_all = exchanged_with_all(dagg_spread, axis)
    if ordered:
        node_taken = exchanged(node_parts[1], axis, 1)
        node_kept, node_given, base = first_halving(node_parts[0], node_taken, (base,))
        node_taken = exchanged(node_given, axis, 2)

    sum_shapes, sum_scratch = weight_shapes(edge_w1, edge_w2, 16)
    f_zs, f_zr, f_hidden, f_slope, f_normed, f_std = fine_saved
    c_zs, c_zr, c_hidden, c_slope, c_normed, c_std = coarse_saved
    fine_out, fine_pre, g_fine, own_grad, *pieces = call(
        functools.partial(fine_backward_kernel, block=block), "fine_backward",
        (edge_count, fr, dagg, d_fine, eg, f_std, f_normed, edge_w2, f_slope, edge_w1, fs, base),
        [SM] + [VM] * 8 + [Rows(3), VM, VM],
        [shape((fine, width), BF16)] * 3 + [shape((own, width), F32)] + [shape((tile, width), BF16)] * slots,
        scratch=[pltpu.VMEM((space_rows, width), F32)],
        flops=2 * fine * width * (4 * width + space_rows + 2 * own),
    )
    returned = [passed_along(pieces[slot], axis, -offset) for slot, offset in enumerate(offsets)]

    pair = [Rows(joined=2), None]
    more = [Rows(extra=coarse)]
    order = (node_taken,) if ordered else ()
    g_coarse, *edge_parts = call(
        functools.partial(coarse_backward_kernel, ordered=ordered), "coarse_backward",
        (
            me, cr, dagg_all, d_coarse, eg, c_std, c_normed, edge_w2, c_slope, f_hidden, c_hidden,
            fine_out, fine_pre, fine_edges, coarse_edges, f_zs, c_zs, f_zr, c_zr, edge_w1, cs, *order,
        ),
        [SM] + [VM] * 8 + pair + more * 2 + pair * 3 + [Rows(3), VM] + [None] * len(order),
        [shape((coarse, width), BF16)] + ([] if ordered else [every]) + sum_shapes,
        scratch=([pltpu.VMEM((peers * COARSE_DEV, width), F32)] if ordered else []) + sum_scratch,
        flops=2 * width * width * (4 * fine + 12 * coarse),
    )

    def rows_of(w):
        return w.shape[0] // peers

    def returned_tiles(passing=()):
        return small_call(
            functools.partial(node_gradient_kernel, slots=slots), "node_gradient",
            (own_grad, halo, *returned), [shape((own, width), F32)], passing,
        )

    if ordered:
        edge_kept, edge_given = edge_parts
        edge_taken = exchanged(edge_given, axis, 1)
        total, edge_kept = returned_tiles((edge_kept,))
        node_kept, *given, edge_kept = second_halving(node_kept, node_taken, (edge_kept,))
        node_taken = [exchanged(part, axis, 4 * (k + 1)) for k, part in enumerate(given)]
        edge_kept, edge_given = first_halving(edge_kept, edge_taken)
        edge_taken = exchanged(edge_given, axis, 2)
        g_nw1, g_nw2, edge_kept = last_sum(
            node_kept, node_taken, rows_of(node_w1), rows_of(node_w2), passing=(edge_kept,)
        )
        edge_kept, *given = second_halving(edge_kept, edge_taken)
        edge_taken = [exchanged(part, axis, 4 * (k + 1)) for k, part in enumerate(given)]
        g_ew1, g_ew2, g_nodes = last_sum(edge_kept, edge_taken, rows_of(edge_w1), rows_of(edge_w2), total)
    else:
        coarse_share = exchanged_with_all(edge_parts[0], axis)
        (g_nodes,) = small_call(
            coarse_gradient_kernel, "coarse_gradient", (*returned_tiles(), coarse_share),
            [shape((own, width), BF16)],
        )
        g_nw1, g_nw2, g_ew1, g_ew2 = [
            lax.psum_scatter(g, axis, scatter_dimension=0, tiled=True) for g in node_parts + edge_parts[1:]
        ]
    return (new_nodes, new_fine, new_coarse, g_nodes, g_fine, g_coarse, g_ew1, g_ew2, g_nw1, g_nw2)


def solution(mesh):
    split = P(("groups", "patch"))
    rows = P(("groups", "patch"), None)
    return jax.shard_map(
        local,
        mesh=mesh,
        in_specs=(
            rows, rows, rows, split, split, split, split, P(("groups", "patch"), None, None), split,
            P(), P(), P(), P(), P(), P(), rows, rows, rows,
        ),
        out_specs=(rows,) * 10,
        check_vma=False,
    )
```

time: 139 us -> 122 us (0.88)
  the two profiles are of different devices: /device:TPU:14 before, /device:TPU:0 now
where the time goes in v4:
time: 122 us; the launch traced here: 121 us
  starting transfers between devices  38.5 us (32%)
  Pallas kernels  35.4 us (29%)
  waiting for transfers between devices  33.7 us (28%)
  local copies, waits for them, and re-layouts  11.7 us (10%)
  between operations  1.57 us (1%)
    pallas_call x6, Pallas kernels, call(): pl.pallas_call(functools.partial(staged_kernel, kernel, in_specs, out_spe...  32.8 us
    ppermute x10, waiting for transfers between devices, exchanged(): lax.ppermute(block, axis, [(i, i ^ distance) for i in range(lax.axis_size...  22.6 us
    all_to_all x3, starting transfers between devices, exchanged_with_all(): return lax.all_to_all(blocks, axis, 0, 0)  15.6 us
    unnamed x46, local copies, waits for them, and re-layouts  11.7 us
    ppermute x8, starting transfers between devices, passed_along(): return lax.ppermute(block, axis, route)  11.7 us
    ppermute x10, starting transfers between devices, exchanged(): lax.ppermute(block, axis, [(i, i ^ distance) for i in range(lax.axis_size...  11.2 us
    ppermute x8, waiting for transfers between devices, passed_along(): return lax.ppermute(block, axis, route)  7.55 us
    all_to_all x3, waiting for transfers between devices, exchanged_with_all(): return lax.all_to_all(blocks, axis, 0, 0)  3.58 us
  transfers between devices with their start and end apart: 21, of which 12 were waited for; matrix products, arithmetic and copies ran while one was open for 0% of the time, Pallas kernels for 15%

profile of v4, /device:TPU:0, one launch (start us, length us, event | category | flops | bytes accessed | tf_op | source)
XLA Modules:
  0.0 120.9 jit_solution(2562101530901268665)
XLA Ops:
  0.6 2.6 %tiles.1 = (bf16[128,512]{1,0:T(8,128)(2,1)}, bf16[128,512]{1,0:T(8,128)(2,1)}, bf16[128,512]{1,0:T(8,128)(2,1)}, bf16[128,512]{1,0:T(8,128)(2,1)}, bf16[16,8,512]{2,1,0:T(8,128)(2,1)}) custom-call(bf16[256,512]{1,0:T(8,128)(2,1)} %refs_1_.5, s32[4,128]{1,0:T(4,128)} %bitcast.8), custom_call_target="tpu_custom_call" | custom-call | bytes 919552 | tf_op jit(solution)/shard_map/tiles/pallas_call | solution.py:465
  3.2 7.4 %all-to-all-start = ((bf16[16,8,512]{2,1,0:T(8,128)(2,1)}), bf16[16,8,512]{2,1,0:T(8,128)(2,1)S(1)}, u32[]{:S(2)}, u32[]{:S(2)}) async-start(bf16[16,8,512]{2,1,0:T(8,128)(2,1)} %get-tuple-element.75), calls=%async_computation | async-start | bytes 262144 | tf_op jit(solution)/shard_map/all_to_all | solution.py:504
  10.6 0.4 collective-permute-start
  11.0 1.7 %collective-permute-start.1 = (bf16[128,512]{1,0:T(8,128)(2,1)}, bf16[128,512]{1,0:T(8,128)(2,1)S(1)}, u32[]{:S(2)}, u32[]{:S(2)}) collective-permute-start(bf16[128,512]{1,0:T(8,128)(2,1)} %get-tuple-element.71), channel_id=1, source_target_pairs={{14,0},{15,1},{0,2},{1,3},{2,4},{3,5},{4,6},{5,7},{6,8},{7,9},{8,1... | collective-permute-start | bytes 393224 | tf_op jit(solution)/shard_map/ppermute | solution.py:496
  12.7 4.0 %collective-permute-start.2 = (bf16[128,512]{1,0:T(8,128)(2,1)}, bf16[128,512]{1,0:T(8,128)(2,1)S(1)}, u32[]{:S(2)}, u32[]{:S(2)}) collective-permute-start(bf16[128,512]{1,0:T(8,128)(2,1)} %get-tuple-element.72), channel_id=1, source_target_pairs={{1,0},{2,1},{3,2},{4,3},{5,4},{6,5},{7,6},{8,7},{9,8},{10,9},{11,1... | collective-permute-start | bytes 393224 | tf_op jit(solution)/shard_map/ppermute | solution.py:496
  16.7 0.3 collective-permute-start.3
  17.0 2.0 %all-to-all-done.refs_0_ = bf16[16,8,512]{2,1,0:T(8,128)(2,1)S(1)} async-done(((bf16[16,8,512]{2,1,0:T(8,128)(2,1)}), bf16[16,8,512]{2,1,0:T(8,128)(2,1)S(1)}, u32[]{:S(2)}, u32[]{:S(2)}) %all-to-all-start) | async-done | bytes 131104 | tf_op jit(solution)/shard_map/all_to_all | solution.py:504
  19.1 0.7 copy-done.12
  19.7 4.0 %coarse_forward.1 = (bf16[128,512]{1,0:T(8,128)(2,1)}, bf16[16,8,512]{2,1,0:T(8,128)(2,1)}, bf16[128,512]{1,0:T(8,128)(2,1)}, bf16[128,512]{1,0:T(8,128)(2,1)}, ...) custom-call(bf16[16,8,512]{2,1,0:T(8,128)(2,1)} %copy-done.12, ...), custom_call_target="tpu_custom_call" | custom-call | flops 268435456 | bytes 3345408 | tf_op jit(solution)/shard_map/coarse_forward/pallas_call | solution.py:465
  23.7 3.5 %all-to-all-start.1 = ((bf16[16,8,512]{2,1,0:T(8,128)(2,1)}), bf16[16,8,512]{2,1,0:T(8,128)(2,1)S(1)}, u32[]{:S(2)}, u32[]{:S(2)}) async-start(bf16[16,8,512]{2,1,0:T(8,128)(2,1)} %get-tuple-element.76), calls=%async_computation.1 | async-start | bytes 262144 | tf_op jit(solution)/shard_map/all_to_all | solution.py:504
  27.9 0.0 copy-start.16
  27.9 0.0 copy-start.20
  28.0 0.6 copy-done.16
  28.6 0.0 copy-done.18
  28.6 0.0 copy-done.20
  28.6 0.0 copy-done.22
  28.7 6.8 %fine_forward.1 = (bf16[512,512]{1,0:T(8,128)(2,1)}, f32[256,512]{1,0:T(8,128)}, bf16[512,512]{1,0:T(8,128)(2,1)}, bf16[512,512]{1,0:T(8,128)(2,1)}, bf16[512,51...) custom-call(s32[1]{0:T(128)S(6)} %copy.36.refs_0_, ...), custom_call_target="tpu_custom_call" | custom-call | flops 1879048192 | bytes 7346180 | tf_op jit(solution)/shard_map/fine_forward/pallas_call | solution.py:465
  35.5 0.0 copy-start.13
  35.5 0.6 copy-done.13
  36.1 5.8 %node_both.1 = (bf16[256,512]{1,0:T(8,128)(2,1)}, f32[256,512]{1,0:T(8,128)}, bf16[256,512]{1,0:T(8,128)(2,1)}, bf16[16,8,512]{2,1,0:T(8,128)(2,1)}, bf16[8,96,5...) custom-call(s32[1]{0:T(128)} %bitcast.refs_0_, bf16[256,512]{1,0:T(8,128)(2,1)} %refs_1_.5, ...), custom_call_target="tpu_custom_call" | custom-call | flops 1207959552 | bytes 5507076 | tf_op jit(solution)/shard_map/node_both/pallas_call | solution.py:465
  42.0 0.4 collective-permute-start.4
  42.3 2.2 %collective-permute-done.4.taken_ref = bf16[8,96,512]{2,1,0:T(8,128)(2,1)S(1)} collective-permute-done((bf16[8,96,512]{2,1,0:T(8,128)(2,1)}, bf16[8,96,512]{2,1,0:T(8,128)(2,1)S(1)}, u32[]{:S(2)}, u32[]{:S(2)}) %collective-permute-start.4) | collective-permute-done | bytes 786464 | tf_op jit(solution)/shard_map/ppermute | solution.py:500
  44.5 1.1 copy-done.5
  45.7 1.0 copy-done.7
  46.7 0.2 first_halving.2
  46.9 0.8 copy-done.8
  47.7 1.8 %collective-permute-start.5 = (bf16[4,96,512]{2,1,0:T(8,128)(2,1)S(1)}, bf16[4,96,512]{2,1,0:T(8,128)(2,1)S(1)}, u32[]{:S(2)}, u32[]{:S(2)}) collective-permute-start(bf16[4,96,512]{2,1,0:T(8,128)(2,1)S(1)} %get-tuple-element.84), channel_id=1, source_target_pairs={{0,2},{1,3},{2,0},{3,1},{4,6},{5,7},{6,4},{7,5},{8,10},{9,11},{10,... | collective-permute-start | bytes 1179656 | tf_op jit(solution)/shard_map/ppermute | solution.py:500
  49.5 4.7 %all-to-all-start.2 = ((bf16[16,8,512]{2,1,0:T(8,128)(2,1)}), bf16[16,8,512]{2,1,0:T(8,128)(2,1)S(1)}, u32[]{:S(2)}, u32[]{:S(2)}) async-start(bf16[16,8,512]{2,1,0:T(8,128)(2,1)} %get-tuple-element.95), calls=%async_computation.2 | async-start | bytes 262144 | tf_op jit(solution)/shard_map/all_to_all | solution.py:504
  54.3 6.4 %fine_backward.1 = (bf16[512,512]{1,0:T(8,128)(2,1)}, bf16[512,512]{1,0:T(8,128)(2,1)}, bf16[512,512]{1,0:T(8,128)(2,1)}, f32[256,512]{1,0:T(8,128)}, bf16[128,5...) custom-call(s32[1]{0:T(128)S(6)} %copy.36.refs_0_, ...), custom_call_target="tpu_custom_call" | custom-call | flops 1744830464 | bytes 7346180 | tf_op jit(solution)/shard_map/fine_backward/pallas_call | solution.py:465
  60.7 1.5 %all-to-all-done.2.refs_2_ = bf16[16,8,512]{2,1,0:T(8,128)(2,1)S(1)} async-done(((bf16[16,8,512]{2,1,0:T(8,128)(2,1)}), bf16[16,8,512]{2,1,0:T(8,128)(2,1)S(1)}, u32[]{:S(2)}, u32[]{:S(2)}) %all-to-all-start.2) | async-done | bytes 131104 | tf_op jit(solution)/shard_map/all_to_all | solution.py:504
  62.2 0.6 copy-done.14
  62.8 0.1 copy-done.9
  63.0 7.2 %coarse_backward.1 = (bf16[128,512]{1,0:T(8,128)(2,1)}, bf16[8,144,512]{2,1,0:T(8,128)(2,1)}, bf16[8,144,512]{2,1,0:T(8,128)(2,1)}) custom-call(s32[1]{0:T(128)} %bitcast.refs_0_, s32[1,128]{1,0:T(1,128)} %bitcast.17, bf16[16,8,512]{2,1,0:T(8,128)(2,1)} %copy-done.14, bf16[128,512]{1,0:T(8,128)(2,1)} %refs_3_.3, f32[1,512]{1,0:T(1,128)} %bitcast.13, ...), custom_call_target="tpu_custom_call" | custom-call | flops 1879048192 | bytes 9243652 | tf_op jit(solution)/shard_map/coarse_backward/pallas_call | solution.py:465
  70.2 0.1 collective-permute-start.13
  70.3 3.2 %collective-permute-start.6 = (bf16[128,512]{1,0:T(8,128)(2,1)S(1)}, bf16[128,512]{1,0:T(8,128)(2,1)S(1)}, u32[]{:S(2)}, u32[]{:S(2)}) collective-permute-start(bf16[128,512]{1,0:T(8,128)(2,1)S(1)} %copy-done.21), channel_id=1, source_target_pairs={{1,0},{2,1},{3,2},{4,3},{5,4},{6,5},{7,6},{8,7},{9,8},{10,9},{11,1... | collective-permute-start | bytes 393224 | tf_op jit(solution)/shard_map/ppermute | solution.py:496
  73.5 0.6 collective-permute-start.7
  74.1 1.5 %collective-permute-start.9 = (bf16[128,512]{1,0:T(8,128)(2,1)S(1)}, bf16[128,512]{1,0:T(8,128)(2,1)S(1)}, u32[]{:S(2)}, u32[]{:S(2)}) collective-permute-start(bf16[128,512]{1,0:T(8,128)(2,1)S(1)} %copy-done.15), channel_id=1, source_target_pairs={{14,0},{15,1},{0,2},{1,3},{2,4},{3,5},{4,6},{5,7},{6,8},{7,9},{8,1... | collective-permute-start | bytes 393224 | tf_op jit(solution)/shard_map/ppermute | solution.py:496
  75.6 1.4 %collective-permute-done.6.refs_0_ = bf16[128,512]{1,0:T(8,128)(2,1)S(1)} collective-permute-done((bf16[128,512]{1,0:T(8,128)(2,1)S(1)}, bf16[128,512]{1,0:T(8,128)(2,1)S(1)}, u32[]{:S(2)}, u32[]{:S(2)}) %collective-permute-start.6) | collective-permute-done | bytes 131104 | tf_op jit(solution)/shard_map/ppermute | solution.py:496
  77.0 1.5 %collective-permute-done.7.refs_1_ = bf16[128,512]{1,0:T(8,128)(2,1)S(1)} collective-permute-done((bf16[128,512]{1,0:T(8,128)(2,1)S(1)}, bf16[128,512]{1,0:T(8,128)(2,1)S(1)}, u32[]{:S(2)}, u32[]{:S(2)}) %collective-permute-start.7) | collective-permute-done | bytes 131104 | tf_op jit(solution)/shard_map/ppermute | solution.py:496
  78.5 3.5 %collective-permute-done.8.refs_2_ = bf16[128,512]{1,0:T(8,128)(2,1)S(1)} collective-permute-done((bf16[128,512]{1,0:T(8,128)(2,1)S(1)}, bf16[128,512]{1,0:T(8,128)(2,1)S(1)}, u32[]{:S(2)}, u32[]{:S(2)}) %collective-permute-start.8) | collective-permute-done | bytes 131104 | tf_op jit(solution)/shard_map/ppermute | solution.py:496
  82.0 1.2 collective-permute-done.9.refs_3_
  83.2 1.3 %copy-done = bf16[8,144,512]{2,1,0:T(8,128)(2,1)S(1)} copy-done((bf16[8,144,512]{2,1,0:T(8,128)(2,1)S(1)}, bf16[8,144,512]{2,1,0:T(8,128)(2,1)}, u32[]{:S(2)}) %copy-start) | copy-done | bytes 1179672
  84.4 0.4 node_gradient.1
  84.9 1.0 copy-done.1
  85.9 1.3 %copy-done.2 = bf16[8,144,512]{2,1,0:T(8,128)(2,1)S(1)} copy-done((bf16[8,144,512]{2,1,0:T(8,128)(2,1)S(1)}, bf16[8,144,512]{2,1,0:T(8,128)(2,1)}, u32[]{:S(2)}) %copy-start.2) | copy-done | bytes 1179672
  87.2 0.1 second_halving.2
  87.3 1.0 copy-done.3
  88.3 1.3 %copy-done.4 = bf16[8,144,512]{2,1,0:T(8,128)(2,1)S(1)} copy-done((bf16[8,144,512]{2,1,0:T(8,128)(2,1)S(1)}, bf16[8,144,512]{2,1,0:T(8,128)(2,1)}, u32[]{:S(2)}) %copy-start.4) | copy-done | bytes 1179672
  89.6 0.3 first_halving.3
  89.9 0.1 collective-permute-start.14
  90.0 0.2 collective-permute-start.10
  90.2 3.9 %collective-permute-start.11 = (bf16[96,512]{1,0:T(8,128)(2,1)S(1)}, bf16[96,512]{1,0:T(8,128)(2,1)S(1)}, u32[]{:S(2)}, u32[]{:S(2)}) collective-permute-start(bf16[96,512]{1,0:T(8,128)(2,1)S(1)} %get-tuple-element.111), channel_id=1, source_target_pairs={{0,8},{1,9},{2,10},{3,11},{4,12},{5,13},{6,14},{7,15},{8,0},{9,1},... | collective-permute-start | bytes 294920 | tf_op jit(solution)/shard_map/ppermute | solution.py:500
  94.0 0.4 collective-permute-start.12
  94.4 2.6 %collective-permute-done.10.refs_0_ = bf16[96,512]{1,0:T(8,128)(2,1)S(1)} collective-permute-done((bf16[96,512]{1,0:T(8,128)(2,1)S(1)}, bf16[96,512]{1,0:T(8,128)(2,1)S(1)}, u32[]{:S(2)}, u32[]{:S(2)}) %collective-permute-start.10) | collective-permute-done | bytes 98336 | tf_op jit(solution)/shard_map/ppermute | solution.py:500
  97.0 4.9 %collective-permute-done.11.refs_1_ = bf16[96,512]{1,0:T(8,128)(2,1)S(1)} collective-permute-done((bf16[96,512]{1,0:T(8,128)(2,1)S(1)}, bf16[96,512]{1,0:T(8,128)(2,1)S(1)}, u32[]{:S(2)}, u32[]{:S(2)}) %collective-permute-start.11) | collective-permute-done | bytes 98336 | tf_op jit(solution)/shard_map/ppermute | solution.py:500
  101.9 0.7 last_sum.2
  102.6 3.2 %collective-permute-done.14.taken_ref = bf16[4,144,512]{2,1,0:T(8,128)(2,1)S(1)} collective-permute-done((bf16[4,144,512]{2,1,0:T(8,128)(2,1)S(1)}, bf16[4,144,512]{2,1,0:T(8,128)(2,1)S(1)}, u32[]{:S(2)}, u32[]{:S(2)}) %collective-permute-start.14) | collective-permute-done | bytes 589856 | tf_op jit(solution)/shard_map/ppermute | solution.py:500
  105.8 0.1 second_halving.3
  106.0 0.1 collective-permute-start.15
  106.0 2.3 %collective-permute-start.16 = (bf16[144,512]{1,0:T(8,128)(2,1)S(1)}, bf16[144,512]{1,0:T(8,128)(2,1)S(1)}, u32[]{:S(2)}, u32[]{:S(2)}) collective-permute-start(bf16[144,512]{1,0:T(8,128)(2,1)S(1)} %get-tuple-element.120), channel_id=1, source_target_pairs={{0,8},{1,9},{2,10},{3,11},{4,12},{5,13},{6,14},{7,15},{8,0},{9,1},... | collective-permute-start | bytes 442376 | tf_op jit(solution)/shard_map/ppermute | solution.py:500
  108.4 2.0 %collective-permute-start.17 = (bf16[144,512]{1,0:T(8,128)(2,1)S(1)}, bf16[144,512]{1,0:T(8,128)(2,1)S(1)}, u32[]{:S(2)}, u32[]{:S(2)}) collective-permute-start(bf16[144,512]{1,0:T(8,128)(2,1)S(1)} %get-tuple-element.121), channel_id=1, source_target_pairs={{0,12},{1,13},{2,14},{3,15},{4,8},{5,9},{6,10},{7,11},{8,4},{9,5},... | collective-permute-start | bytes 442376 | tf_op jit(solution)/shard_map/ppermute | solution.py:500
  110.4 3.4 %collective-permute-done.15.refs_0_ = bf16[144,512]{1,0:T(8,128)(2,1)S(1)} collective-permute-done((bf16[144,512]{1,0:T(8,128)(2,1)S(1)}, bf16[144,512]{1,0:T(8,128)(2,1)S(1)}, u32[]{:S(2)}, u32[]{:S(2)}) %collective-permute-start.15) | collective-permute-done | bytes 147488 | tf_op jit(solution)/shard_map/ppermute | solution.py:500
  113.9 6.2 %collective-permute-done.16.refs_1_ = bf16[144,512]{1,0:T(8,128)(2,1)S(1)} collective-permute-done((bf16[144,512]{1,0:T(8,128)(2,1)S(1)}, bf16[144,512]{1,0:T(8,128)(2,1)S(1)}, u32[]{:S(2)}, u32[]{:S(2)}) %collective-permute-start.16) | collective-permute-done | bytes 147488 | tf_op jit(solution)/shard_map/ppermute | solution.py:500
  120.1 0.9 last_sum.3
  (37 shorter events, 0.1 us)
Async XLA Ops:
  3.2 15.8 %all-to-all-start = ((bf16[16,8,512]{2,1,0:T(8,128)(2,1)}), bf16[16,8,512]{2,1,0:T(8,128)(2,1)S(1)}, u32[]{:S(2)}, u32[]{:S(2)}) async-start(bf16[16,8,512]{2,1,0:T(8,128)(2,1)} %get-tuple-element.75), calls=%async_computation | async-start | bytes 262144 | tf_op jit(solution)/shard_map/all_to_all | solution.py:504
  10.6 17.3 %collective-permute-start = (bf16[128,512]{1,0:T(8,128)(2,1)}, bf16[128,512]{1,0:T(8,128)(2,1)S(1)}, u32[]{:S(2)}, u32[]{:S(2)}) collective-permute-start(bf16[128,512]{1,0:T(8,128)(2,1)} %get-tuple-element.70), channel_id=1, source_target_pairs={{15,0},{0,1},{1,2},{2,3},{3,4},{4,5},{5,6},{6,7},{7,8},{8,9},{9,10... | collective-permute-start | bytes 393224 | tf_op jit(solution)/shard_map/ppermute | solution.py:496
  11.0 16.9 %collective-permute-start.1 = (bf16[128,512]{1,0:T(8,128)(2,1)}, bf16[128,512]{1,0:T(8,128)(2,1)S(1)}, u32[]{:S(2)}, u32[]{:S(2)}) collective-permute-start(bf16[128,512]{1,0:T(8,128)(2,1)} %get-tuple-element.71), channel_id=1, source_target_pairs={{14,0},{15,1},{0,2},{1,3},{2,4},{3,5},{4,6},{5,7},{6,8},{7,9},{8,1... | collective-permute-start | bytes 393224 | tf_op jit(solution)/shard_map/ppermute | solution.py:496
  12.7 15.2 %collective-permute-start.2 = (bf16[128,512]{1,0:T(8,128)(2,1)}, bf16[128,512]{1,0:T(8,128)(2,1)S(1)}, u32[]{:S(2)}, u32[]{:S(2)}) collective-permute-start(bf16[128,512]{1,0:T(8,128)(2,1)} %get-tuple-element.72), channel_id=1, source_target_pairs={{1,0},{2,1},{3,2},{4,3},{5,4},{6,5},{7,6},{8,7},{9,8},{10,9},{11,1... | collective-permute-start | bytes 393224 | tf_op jit(solution)/shard_map/ppermute | solution.py:496
  16.7 11.2 %collective-permute-start.3 = (bf16[128,512]{1,0:T(8,128)(2,1)}, bf16[128,512]{1,0:T(8,128)(2,1)S(1)}, u32[]{:S(2)}, u32[]{:S(2)}) collective-permute-start(bf16[128,512]{1,0:T(8,128)(2,1)} %get-tuple-element.73), channel_id=1, source_target_pairs={{2,0},{3,1},{4,2},{5,3},{6,4},{7,5},{8,6},{9,7},{10,8},{11,9},{12,... | collective-permute-start | bytes 393224 | tf_op jit(solution)/shard_map/ppermute | solution.py:496
  19.1 0.7 copy-start.12
  23.7 11.8 %all-to-all-start.1 = ((bf16[16,8,512]{2,1,0:T(8,128)(2,1)}), bf16[16,8,512]{2,1,0:T(8,128)(2,1)S(1)}, u32[]{:S(2)}, u32[]{:S(2)}) async-start(bf16[16,8,512]{2,1,0:T(8,128)(2,1)} %get-tuple-element.76), calls=%async_computation.1 | async-start | bytes 262144 | tf_op jit(solution)/shard_map/all_to_all | solution.py:504
  27.9 0.7 copy-start.16
  27.9 0.7 copy-start.18
  27.9 0.7 copy-start.20
  28.0 0.7 copy-start.22
  35.5 0.7 copy-start.13
  42.0 2.6 %collective-permute-start.4 = (bf16[8,96,512]{2,1,0:T(8,128)(2,1)}, bf16[8,96,512]{2,1,0:T(8,128)(2,1)S(1)}, u32[]{:S(2)}, u32[]{:S(2)}) collective-permute-start(bf16[8,96,512]{2,1,0:T(8,128)(2,1)} %get-tuple-element.81), channel_id=1, source_target_pairs={{0,1},{1,0},{2,3},{3,2},{4,5},{5,4},{6,7},{7,6},{8,9},{9,8},{10,11... | collective-permute-start | bytes 2359304 | tf_op jit(solution)/shard_map/ppermute | solution.py:500
  44.5 1.1 copy-start.5
  45.7 1.0 copy-start.7
  46.9 0.8 copy-start.8
  47.7 14.5 %collective-permute-start.5 = (bf16[4,96,512]{2,1,0:T(8,128)(2,1)S(1)}, bf16[4,96,512]{2,1,0:T(8,128)(2,1)S(1)}, u32[]{:S(2)}, u32[]{:S(2)}) collective-permute-start(bf16[4,96,512]{2,1,0:T(8,128)(2,1)S(1)} %get-tuple-element.84), channel_id=1, source_target_pairs={{0,2},{1,3},{2,0},{3,1},{4,6},{5,7},{6,4},{7,5},{8,10},{9,11},{10,... | collective-permute-start | bytes 1179656 | tf_op jit(solution)/shard_map/ppermute | solution.py:500
  49.5 12.7 %all-to-all-start.2 = ((bf16[16,8,512]{2,1,0:T(8,128)(2,1)}), bf16[16,8,512]{2,1,0:T(8,128)(2,1)S(1)}, u32[]{:S(2)}, u32[]{:S(2)}) async-start(bf16[16,8,512]{2,1,0:T(8,128)(2,1)} %get-tuple-element.95), calls=%async_computation.2 | async-start | bytes 262144 | tf_op jit(solution)/shard_map/all_to_all | solution.py:504
  62.2 0.7 copy-start.14
  62.2 0.8 copy-start.9
  63.0 7.3 %copy-start.21 = (bf16[128,512]{1,0:T(8,128)(2,1)S(1)}, bf16[128,512]{1,0:T(8,128)(2,1)}, u32[]{:S(2)}) copy-start(bf16[128,512]{1,0:T(8,128)(2,1)} %get-tuple-element.91) | copy-start | bytes 393220
  63.0 10.5 %copy-start.19 = (bf16[128,512]{1,0:T(8,128)(2,1)S(1)}, bf16[128,512]{1,0:T(8,128)(2,1)}, u32[]{:S(2)}) copy-start(bf16[128,512]{1,0:T(8,128)(2,1)} %get-tuple-element.92) | copy-start | bytes 393220
  63.0 11.1 %copy-start.17 = (bf16[128,512]{1,0:T(8,128)(2,1)S(1)}, bf16[128,512]{1,0:T(8,128)(2,1)}, u32[]{:S(2)}) copy-start(bf16[128,512]{1,0:T(8,128)(2,1)} %get-tuple-element.93) | copy-start | bytes 393220
  63.0 11.1 %copy-start.15 = (bf16[128,512]{1,0:T(8,128)(2,1)S(1)}, bf16[128,512]{1,0:T(8,128)(2,1)}, u32[]{:S(2)}) copy-start(bf16[128,512]{1,0:T(8,128)(2,1)} %get-tuple-element.94) | copy-start | bytes 393220
  63.0 20.2 %copy-start.6 = (f32[256,512]{1,0:T(8,128)S(1)}, f32[256,512]{1,0:T(8,128)}, u32[]{:S(2)}) copy-start(f32[256,512]{1,0:T(8,128)} %get-tuple-element.90.own_ref) | copy-start | bytes 1572868
  63.0 20.1 %copy-start.11 = (s32[1,4,128]{2,1,0:T(4,128)S(1)}, s32[1,4,128]{2,1,0:T(4,128)}, u32[]{:S(2)}) copy-start(s32[1,4,128]{2,1,0:T(4,128)} %param.25) | copy-start | bytes 6148
  70.2 18.1 %collective-permute-start.13 = (bf16[8,144,512]{2,1,0:T(8,128)(2,1)}, bf16[8,144,512]{2,1,0:T(8,128)(2,1)S(1)}, u32[]{:S(2)}, u32[]{:S(2)}) collective-permute-start(bf16[8,144,512]{2,1,0:T(8,128)(2,1)} %get-tuple-element.114), channel_id=1, source_target_pairs={{0,1},{1,0},{2,3},{3,2},{4,5},{5,4},{6,7},{7,6},{8,9},{9,8},{10,11... | collective-permute-start | bytes 3538952 | tf_op jit(solution)/shard_map/ppermute | solution.py:500
  70.3 6.7 %collective-permute-start.6 = (bf16[128,512]{1,0:T(8,128)(2,1)S(1)}, bf16[128,512]{1,0:T(8,128)(2,1)S(1)}, u32[]{:S(2)}, u32[]{:S(2)}) collective-permute-start(bf16[128,512]{1,0:T(8,128)(2,1)S(1)} %copy-done.21), channel_id=1, source_target_pairs={{1,0},{2,1},{3,2},{4,3},{5,4},{6,5},{7,6},{8,7},{9,8},{10,9},{11,1... | collective-permute-start | bytes 393224 | tf_op jit(solution)/shard_map/ppermute | solution.py:496
  73.5 5.0 %collective-permute-start.7 = (bf16[128,512]{1,0:T(8,128)(2,1)S(1)}, bf16[128,512]{1,0:T(8,128)(2,1)S(1)}, u32[]{:S(2)}, u32[]{:S(2)}) collective-permute-start(bf16[128,512]{1,0:T(8,128)(2,1)S(1)} %copy-done.19), channel_id=1, source_target_pairs={{2,0},{3,1},{4,2},{5,3},{6,4},{7,5},{8,6},{9,7},{10,8},{11,9},{12,... | collective-permute-start | bytes 393224 | tf_op jit(solution)/shard_map/ppermute | solution.py:496
  74.1 7.9 %collective-permute-start.8 = (bf16[128,512]{1,0:T(8,128)(2,1)S(1)}, bf16[128,512]{1,0:T(8,128)(2,1)S(1)}, u32[]{:S(2)}, u32[]{:S(2)}) collective-permute-start(bf16[128,512]{1,0:T(8,128)(2,1)S(1)} %copy-done.17), channel_id=1, source_target_pairs={{15,0},{0,1},{1,2},{2,3},{3,4},{4,5},{5,6},{6,7},{7,8},{8,9},{9,10... | collective-permute-start | bytes 393224 | tf_op jit(solution)/shard_map/ppermute | solution.py:496
  74.1 9.1 %collective-permute-start.9 = (bf16[128,512]{1,0:T(8,128)(2,1)S(1)}, bf16[128,512]{1,0:T(8,128)(2,1)S(1)}, u32[]{:S(2)}, u32[]{:S(2)}) collective-permute-start(bf16[128,512]{1,0:T(8,128)(2,1)S(1)} %copy-done.15), channel_id=1, source_target_pairs={{14,0},{15,1},{0,2},{1,3},{2,4},{3,5},{4,6},{5,7},{6,8},{7,9},{8,1... | collective-permute-start | bytes 393224 | tf_op jit(solution)/shard_map/ppermute | solution.py:496
  83.2 1.3 %copy-start = (bf16[8,144,512]{2,1,0:T(8,128)(2,1)S(1)}, bf16[8,144,512]{2,1,0:T(8,128)(2,1)}, u32[]{:S(2)}) copy-start(bf16[8,144,512]{2,1,0:T(8,128)(2,1)} %get-tuple-element.107.refs_4_) | copy-start | bytes 3538948
  84.4 1.5 %copy-start.10 = (bf16[4,96,512]{2,1,0:T(8,128)(2,1)S(1)}, bf16[4,96,512]{2,1,0:T(8,128)(2,1)}, u32[]{:S(2)}) copy-start(bf16[4,96,512]{2,1,0:T(8,128)(2,1)} %copy-done.9) | copy-start | bytes 1179652
  84.8 1.1 copy-start.1
  85.9 1.3 %copy-start.2 = (bf16[8,144,512]{2,1,0:T(8,128)(2,1)S(1)}, bf16[8,144,512]{2,1,0:T(8,128)(2,1)}, u32[]{:S(2)}) copy-start(bf16[8,144,512]{2,1,0:T(8,128)(2,1)} %copy-done.1) | copy-start | bytes 3538948
  87.3 1.1 copy-start.3
  88.3 1.3 %copy-start.4 = (bf16[8,144,512]{2,1,0:T(8,128)(2,1)S(1)}, bf16[8,144,512]{2,1,0:T(8,128)(2,1)}, u32[]{:S(2)}) copy-start(bf16[8,144,512]{2,1,0:T(8,128)(2,1)} %copy-done.3) | copy-start | bytes 3538948
  89.9 16.0 %collective-permute-start.14 = (bf16[4,144,512]{2,1,0:T(8,128)(2,1)S(1)}, bf16[4,144,512]{2,1,0:T(8,128)(2,1)S(1)}, u32[]{:S(2)}, u32[]{:S(2)}) collective-permute-start(bf16[4,144,512]{2,1,0:T(8,128)(2,1)S(1)} %get-tuple-element.117), channel_id=1, source_target_pairs={{0,2},{1,3},{2,0},{3,1},{4,6},{5,7},{6,4},{7,5},{8,10},{9,11},{10,... | collective-permute-start | bytes 1769480 | tf_op jit(solution)/shard_map/ppermute | solution.py:500
  90.0 7.1 %collective-permute-start.10 = (bf16[96,512]{1,0:T(8,128)(2,1)S(1)}, bf16[96,512]{1,0:T(8,128)(2,1)S(1)}, u32[]{:S(2)}, u32[]{:S(2)}) collective-permute-start(bf16[96,512]{1,0:T(8,128)(2,1)S(1)} %get-tuple-element.110), channel_id=1, source_target_pairs={{0,4},{1,5},{2,6},{3,7},{4,0},{5,1},{6,2},{7,3},{8,12},{9,13},{10,... | collective-permute-start | bytes 294920 | tf_op jit(solution)/shard_map/ppermute | solution.py:500
  90.2 11.7 %collective-permute-start.11 = (bf16[96,512]{1,0:T(8,128)(2,1)S(1)}, bf16[96,512]{1,0:T(8,128)(2,1)S(1)}, u32[]{:S(2)}, u32[]{:S(2)}) collective-permute-start(bf16[96,512]{1,0:T(8,128)(2,1)S(1)} %get-tuple-element.111), channel_id=1, source_target_pairs={{0,8},{1,9},{2,10},{3,11},{4,12},{5,13},{6,14},{7,15},{8,0},{9,1},... | collective-permute-start | bytes 294920 | tf_op jit(solution)/shard_map/ppermute | solution.py:500
  94.0 7.9 %collective-permute-start.12 = (bf16[96,512]{1,0:T(8,128)(2,1)S(1)}, bf16[96,512]{1,0:T(8,128)(2,1)S(1)}, u32[]{:S(2)}, u32[]{:S(2)}) collective-permute-start(bf16[96,512]{1,0:T(8,128)(2,1)S(1)} %get-tuple-element.112), channel_id=1, source_target_pairs={{0,12},{1,13},{2,14},{3,15},{4,8},{5,9},{6,10},{7,11},{8,4},{9,5},... | collective-permute-start | bytes 294920 | tf_op jit(solution)/shard_map/ppermute | solution.py:500
  106.0 7.9 %collective-permute-start.15 = (bf16[144,512]{1,0:T(8,128)(2,1)S(1)}, bf16[144,512]{1,0:T(8,128)(2,1)S(1)}, u32[]{:S(2)}, u32[]{:S(2)}) collective-permute-start(bf16[144,512]{1,0:T(8,128)(2,1)S(1)} %get-tuple-element.119), channel_id=1, source_target_pairs={{0,4},{1,5},{2,6},{3,7},{4,0},{5,1},{6,2},{7,3},{8,12},{9,13},{10,... | collective-permute-start | bytes 442376 | tf_op jit(solution)/shard_map/ppermute | solution.py:500
  106.0 14.0 %collective-permute-start.16 = (bf16[144,512]{1,0:T(8,128)(2,1)S(1)}, bf16[144,512]{1,0:T(8,128)(2,1)S(1)}, u32[]{:S(2)}, u32[]{:S(2)}) collective-permute-start(bf16[144,512]{1,0:T(8,128)(2,1)S(1)} %get-tuple-element.120), channel_id=1, source_target_pairs={{0,8},{1,9},{2,10},{3,11},{4,12},{5,13},{6,14},{7,15},{8,0},{9,1},... | collective-permute-start | bytes 442376 | tf_op jit(solution)/shard_map/ppermute | solution.py:500
  108.4 11.7 %collective-permute-start.17 = (bf16[144,512]{1,0:T(8,128)(2,1)S(1)}, bf16[144,512]{1,0:T(8,128)(2,1)S(1)}, u32[]{:S(2)}, u32[]{:S(2)}) collective-permute-start(bf16[144,512]{1,0:T(8,128)(2,1)S(1)} %get-tuple-element.121), channel_id=1, source_target_pairs={{0,12},{1,13},{2,14},{3,15},{4,8},{5,9},{6,10},{7,11},{8,4},{9,5},... | collective-permute-start | bytes 442376 | tf_op jit(solution)/shard_map/ppermute | solution.py:500

commit v5 on v4

--- a/solution.py
+++ b/solution.py
@@ -208,21 +208,28 @@
         by_distance(me_ref[0], spread_ref.shape[0], (g1_ref, g2_ref), kept_ref, given_ref)
 
 
-def fine_backward_kernel(
+def edge_heads_kernel(
     count_ref, recv_ref, dagg_ref, d_ref, gain_ref, std_ref, normed_ref, w2_ref, slope_ref,
-    w1_ref, send_ref, base_ref,
-    out_ref, pre_ref, g_ref, own_ref, *rest, block,
+    w1_ref, send_ref, crecv_ref, all_ref, csend_ref, base_ref,
+    out_ref, pre_ref, g_ref, gc_ref, part_ref, own_ref, *rest, block, fine,
 ):
     piece_refs, space_ref = rest[:-1], rest[-1]
     count, width = d_ref.shape
     own = base_ref.shape[0]
     received = None
-    for start in range(0, count, block):
-        rows = slice(start, start + block)
-        hot_r = one_hot(recv_ref[:, rows], own)
+    for start in list(range(0, fine, block)) + [fine]:
+        rows = slice(start, start + block if start < fine else count)
         d_edges = d_ref[rows, :].astype(F32)
-        place = start + lax.broadcasted_iota(jnp.int32, (block, 1), 0)
-        cotan = jnp.where(place < count_ref[0], d_edges + pick(hot_r, dagg_ref[...]), 0.0)
+        if start < fine:
+            hot_r = one_hot(recv_ref[:, rows], own)
+            hot_s = one_hot(send_ref[:, rows], space_ref.shape[0])
+            place = start + lax.broadcasted_iota(jnp.int32, (block, 1), 0)
+            cotan = jnp.where(place < count_ref[0], d_edges + pick(hot_r, dagg_ref[...]), 0.0)
+        else:
+            table = gathered(all_ref).astype(BF16)
+            hot_r = one_hot(crecv_ref[...], table.shape[0])
+            hot_s = one_hot(csend_ref[...], table.shape[0])
+            cotan = d_edges + pick(hot_r, table)
         back_out, back_pre = head_of_backward(
             cotan, w2_ref[...], gain_ref[...], slope_ref[rows, :].astype(F32),
             normed_ref[rows, :].astype(F32), std_ref[rows, 0:1],
@@ -231,60 +238,44 @@
         pre_ref[rows, :] = back_pre
         out_ref.done(rows)
         pre_ref.done(rows)
-        g_ref[rows, :] = (d_edges + mm_nt(back_pre, w1_ref[0:width, :])).astype(BF16)
-        g_ref.done(rows)
-        dz_send = mm_nt(back_pre, w1_ref[width : 2 * width, :]).astype(BF16)
-        dz_recv = mm_nt(back_pre, w1_ref[2 * width : 3 * width, :]).astype(BF16)
-        sent = mm(one_hot(send_ref[:, rows], space_ref.shape[0]), dz_send)
-        space_ref[...] = sent if start == 0 else space_ref[...] + sent
-        arrived = mm(hot_r, dz_recv)
-        received = arrived if received is None else received + arrived
-    for slot, piece in enumerate(piece_refs):
-        tile = piece.shape[0]
-        piece[...] = space_ref[own + slot * tile : own + (slot + 1) * tile, :].astype(BF16)
-        piece.done()
-    own_ref[...] = base_ref[...] + received + space_ref[0:own, :]
-
-
-def coarse_backward_kernel(
-    me_ref, recv_ref, all_ref, d_ref, gain_ref, std_ref, normed_ref, w2_ref, slope_ref,
-    hidden_ref, out_ref, pre_ref, edges_ref, zs_ref, zr_ref, w1_ref, send_ref,
-    g_ref, *rest, ordered,
+        grads = (d_edges + mm_nt(back_pre, w1_ref[0:width, :])).astype(BF16)
+        sent = mm(hot_s, mm_nt(back_pre, w1_ref[width : 2 * width, :]).astype(BF16))
+        arrived = mm(hot_r, mm_nt(back_pre, w1_ref[2 * width : 3 * width, :]).astype(BF16))
+        if start < fine:
+            g_ref[rows, :] = grads
+            g_ref.done(rows)
+            space_ref[...] = sent if start == 0 else space_ref[...] + sent
+            received = arrived if received is None else received + arrived
+        else:
+            gc_ref[...] = grads
+            part_ref[...] = (sent + arrived).reshape(part_ref.shape).astype(part_ref.dtype)
+        if start + block == fine:
+            for slot, piece in enumerate(piece_refs):
+                tile = piece.shape[0]
+                piece[...] = space_ref[own + slot * tile : own + (slot + 1) * tile, :].astype(BF16)
+                piece.done()
+            own_ref[...] = base_ref[...] + received + space_ref[0:own, :]
+            own_ref.done()
+
+
+def edge_weights_kernel(
+    me_ref, hidden_ref, out_ref, edges_ref, pre_ref, zs_ref, zr_ref, *rest, ordered,
 ):
     if ordered:
-        kept_ref, given_ref, part_ref, g1_ref, g2_ref = rest
+        part_ref, kept_ref, given_ref, g1_ref, g2_ref = rest
     else:
-        part_ref, g1_ref, g2_ref = rest
-    width = d_ref.shape[1]
-    count = hidden_ref.shape[0]
-    rows = slice(count - d_ref.shape[0], count)
-    table = gathered(all_ref).astype(BF16)
-    hot_r = one_hot(recv_ref[...], table.shape[0])
-    d_edges = d_ref[...].astype(F32)
-    cotan = d_edges + pick(hot_r, table)
-    back_out, back_pre = head_of_backward(
-        cotan, w2_ref[...], gain_ref[...], slope_ref[...].astype(F32), normed_ref[...].astype(F32), std_ref[:, 0:1]
-    )
-    out_ref[rows, :] = back_out
-    pre_ref[rows, :] = back_pre
+        g1_ref, g2_ref = rest
+    width = edges_ref.shape[1]
     g2_ref[...] = mm_tn(hidden_ref[...], out_ref[...])
     g1_ref[0:width, :] = mm_tn(edges_ref[...], pre_ref[...])
     g1_ref[width : 2 * width, :] = mm_tn(zs_ref[...], pre_ref[...])
     g1_ref[2 * width : 3 * width, :] = mm_tn(zr_ref[...], pre_ref[...])
-    dz_send = mm_nt(back_pre, w1_ref[width : 2 * width, :]).astype(BF16)
-    dz_recv = mm_nt(back_pre, w1_ref[2 * width : 3 * width, :]).astype(BF16)
-    total = mm(one_hot(send_ref[...], table.shape[0]), dz_send) + mm(hot_r, dz_recv)
     if ordered:
-        part_ref[...] = total
         by_distance(me_ref[0], 2 * kept_ref.shape[0], (g1_ref, g2_ref, part_ref), kept_ref, given_ref)
-        kept_ref.done()
-    else:
-        part_ref[...] = total.reshape(part_ref.shape).astype(BF16)
-    g_ref[...] = (d_edges + mm_nt(back_pre, w1_ref[0:width, :])).astype(BF16)
-
-
-def node_gradient_kernel(own_ref, halo_ref, *refs, slots):
-    piece_refs, out_ref = refs[:slots], refs[len(refs) - 1 - (len(refs) - 1 - slots) // 2]
+
+
+def node_gradient_kernel(own_ref, halo_ref, *refs):
+    piece_refs, out_ref = refs[:-1], refs[-1]
     arrived = None
     for slot, piece in enumerate(piece_refs):
         part = mm(one_hot(halo_ref[slot : slot + 1, :], own_ref.shape[0]), piece[...])
@@ -617,68 +608,77 @@
     dagg_all = exchanged_with_all(dagg_spread, axis)
     if ordered:
         node_taken = exchanged(node_parts[1], axis, 1)
-        node_kept, node_given, base = first_halving(node_parts[0], node_taken, (base,))
-        node_taken = exchanged(node_given, axis, 2)
+        half = shape((peers // 2 // 2,) + node_parts[0].shape[1:], BF16)
+        node_kept, node_given = call(
+            first_halving_kernel, "first_halving", (node_parts[0], node_taken, base), [VM, VM, None], [half, half]
+        )
 
     sum_shapes, sum_scratch = weight_shapes(edge_w1, edge_w2, 16)
     f_zs, f_zr, f_hidden, f_slope, f_normed, f_std = fine_saved
     c_zs, c_zr, c_hidden, c_slope, c_normed, c_std = coarse_saved
-    fine_out, fine_pre, g_fine, own_grad, *pieces = call(
-        functools.partial(fine_backward_kernel, block=block), "fine_backward",
-        (edge_count, fr, dagg, d_fine, eg, f_std, f_normed, edge_w2, f_slope, edge_w1, fs, base),
-        [SM] + [VM] * 8 + [Rows(3), VM, VM],
-        [shape((fine, width), BF16)] * 3 + [shape((own, width), F32)] + [shape((tile, width), BF16)] * slots,
+    pair = [Rows(joined=2), None]
+    edges = fine + coarse
+    rows_out = shape((edges, width), BF16)
+    part = shape((peers * COARSE_DEV, width), F32) if ordered else every
+    out, pre, g_fine, g_coarse, coarse_part, own_grad, *pieces = call(
+        functools.partial(edge_heads_kernel, block=block, fine=fine), "edge_heads",
+        (
+            edge_count, fr, dagg, d_fine, d_coarse, eg, f_std, c_std, f_normed, c_normed, edge_w2, f_slope, c_slope,
+            edge_w1, fs, cr, dagg_all, cs, base,
+        ),
+        [SM, VM, VM] + pair + [VM] + pair * 2 + [VM] + pair + [Rows(3)] + [VM] * 5,
+        [rows_out, rows_out, shape((fine, width), BF16), shape((coarse, width), BF16), part]
+        + [shape((own, width), F32)] + [shape((tile, width), BF16)] * slots,
         scratch=[pltpu.VMEM((space_rows, width), F32)],
-        flops=2 * fine * width * (4 * width + space_rows + 2 * own),
-    )
-    returned = [passed_along(pieces[slot], axis, -offset) for slot, offset in enumerate(offsets)]
-
-    pair = [Rows(joined=2), None]
-    more = [Rows(extra=coarse)]
-    order = (node_taken,) if ordered else ()
-    g_coarse, *edge_parts = call(
-        functools.partial(coarse_backward_kernel, ordered=ordered), "coarse_backward",
+        flops=2 * edges * width * (4 * width + space_rows + 2 * own),
+    )
+    if ordered:
+        node_taken = exchanged(node_given, axis, 2)
+    edge_parts = call(
+        functools.partial(edge_weights_kernel, ordered=ordered), "edge_weights",
         (
-            me, cr, dagg_all, d_coarse, eg, c_std, c_normed, edge_w2, c_slope, f_hidden, c_hidden,
-            fine_out, fine_pre, fine_edges, coarse_edges, f_zs, c_zs, f_zr, c_zr, edge_w1, cs, *order,
+            me, f_hidden, c_hidden, out, fine_edges, coarse_edges, pre, f_zs, c_zs, f_zr, c_zr, coarse_part,
+            *((node_taken,) if ordered else ()),
         ),
-        [SM] + [VM] * 8 + pair + more * 2 + pair * 3 + [Rows(3), VM] + [None] * len(order),
-        [shape((coarse, width), BF16)] + ([] if ordered else [every]) + sum_shapes,
-        scratch=([pltpu.VMEM((peers * COARSE_DEV, width), F32)] if ordered else []) + sum_scratch,
-        flops=2 * width * width * (4 * fine + 12 * coarse),
+        [SM] + pair + [VM] + pair + [VM] + pair * 2 + [VM if ordered else None] + [None] * ordered,
+        sum_shapes,
+        scratch=sum_scratch,
+        flops=2 * edges * width * width * 4,
     )
 
     def rows_of(w):
         return w.shape[0] // peers
 
-    def returned_tiles(passing=()):
-        return small_call(
-            functools.partial(node_gradient_kernel, slots=slots), "node_gradient",
-            (own_grad, halo, *returned), [shape((own, width), F32)], passing,
+    def returned_tiles(pieces):
+        returned = [passed_along(pieces[slot], axis, -offset) for slot, offset in enumerate(offsets)]
+        (total,) = small_call(
+            node_gradient_kernel, "node_gradient", (own_grad, halo, *returned), [shape((own, width), F32)]
         )
+        return total
 
     if ordered:
         edge_kept, edge_given = edge_parts
         edge_taken = exchanged(edge_given, axis, 1)
-        total, edge_kept = returned_tiles((edge_kept,))
-        node_kept, *given, edge_kept = second_halving(node_kept, node_taken, (edge_kept,))
-        node_taken = [exchanged(part, axis, 4 * (k + 1)) for k, part in enumerate(given)]
         edge_kept, edge_given = first_halving(edge_kept, edge_taken)
         edge_taken = exchanged(edge_given, axis, 2)
+        node_kept, *given = second_halving(node_kept, node_taken)
+        node_taken = [exchanged(part, axis, 4 * (k + 1)) for k, part in enumerate(given)]
         g_nw1, g_nw2, edge_kept = last_sum(
             node_kept, node_taken, rows_of(node_w1), rows_of(node_w2), passing=(edge_kept,)
         )
-        edge_kept, *given = second_halving(edge_kept, edge_taken)
+        edge_kept, *given = second_halving(edge_kept, edge_taken, tuple(pieces))
+        given, pieces = given[:-slots], given[-slots:]
         edge_taken = [exchanged(part, axis, 4 * (k + 1)) for k, part in enumerate(given)]
+        total = returned_tiles(pieces)
         g_ew1, g_ew2, g_nodes = last_sum(edge_kept, edge_taken, rows_of(edge_w1), rows_of(edge_w2), total)
     else:
-        coarse_share = exchanged_with_all(edge_parts[0], axis)
+        coarse_share = exchanged_with_all(coarse_part, axis)
         (g_nodes,) = small_call(
-            coarse_gradient_kernel, "coarse_gradient", (*returned_tiles(), coarse_share),
+            coarse_gradient_kernel, "coarse_gradient", (returned_tiles(pieces), coarse_share),
             [shape((own, width), BF16)],
         )
         g_nw1, g_nw2, g_ew1, g_ew2 = [
-            lax.psum_scatter(g, axis, scatter_dimension=0, tiled=True) for g in node_parts + edge_parts[1:]
+            lax.psum_scatter(g, axis, scatter_dimension=0, tiled=True) for g in [*node_parts, *edge_parts]
         ]
     return (new_nodes, new_fine, new_coarse, g_nodes, g_fine, g_coarse, g_ew1, g_ew2, g_nw1, g_nw2)
 

time: 122 us -> 114 us (0.934)
  waiting for transfers between devices: 33.7 us -> 23 us
  local copies, waits for them, and re-layouts: 11.7 us -> 6.38 us
  Pallas kernels: 35.4 us -> 39.2 us
  starting transfers between devices: 38.5 us -> 41.8 us
    ppermute x10, waiting for transfers between devices: 22.6 us -> 12.4 us  [exchanged(): lax.ppermute(block, axis, [(i, i ^ distance) for i in range(lax.axis_size...]
    unnamed x46 -> x36, local copies, waits for them, and re-layouts: 11.7 us -> 6.38 us
    pallas_call x6 -> x7, Pallas kernels: 32.8 us -> 36.7 us  [call(): pl.pallas_call(functools.partial(staged_kernel, kernel, in_specs, out_spe...]
    ppermute x8, starting transfers between devices: 11.7 us -> 13.8 us  [passed_along(): return lax.ppermute(block, axis, route)]
    pallas_call x7 -> x6, Pallas kernels: 2.63 us -> 2.48 us  [small_call(): pl.pallas_call(kernel, out_shape=tuple(outs), input_output_aliases={first...]
  transfers between devices with their start and end apart: 21 -> 21, of which waited for: 12 -> 9; matrix products, arithmetic and copies ran while one was open for 0% -> 0% of each run, Pallas kernels for 15% -> 21%
where the time goes in v5:
time: 114 us; the launch traced here: 112 us
  starting transfers between devices  41.8 us (37%)
  Pallas kernels  39.2 us (34%)
  waiting for transfers between devices  23 us (20%)
  local copies, waits for them, and re-layouts  6.38 us (6%)
  between operations  1.61 us (1%)
    pallas_call x7, Pallas kernels, call(): pl.pallas_call(functools.partial(staged_kernel, kernel, in_specs, out_spe...  36.7 us
    all_to_all x3, starting transfers between devices, exchanged_with_all(): return lax.all_to_all(blocks, axis, 0, 0)  16.8 us
    ppermute x8, starting transfers between devices, passed_along(): return lax.ppermute(block, axis, route)  13.8 us
    ppermute x10, waiting for transfers between devices, exchanged(): lax.ppermute(block, axis, [(i, i ^ distance) for i in range(lax.axis_size...  12.4 us
    ppermute x10, starting transfers between devices, exchanged(): lax.ppermute(block, axis, [(i, i ^ distance) for i in range(lax.axis_size...  11.3 us
    ppermute x8, waiting for transfers between devices, passed_along(): return lax.ppermute(block, axis, route)  6.44 us
    unnamed x36, local copies, waits for them, and re-layouts  6.38 us
    all_to_all x3, waiting for transfers between devices, exchanged_with_all(): return lax.all_to_all(blocks, axis, 0, 0)  4.14 us
  transfers between devices with their start and end apart: 21, of which 9 were waited for; matrix products, arithmetic and copies ran while one was open for 0% of the time, Pallas kernels for 21%

profile of v5, /device:TPU:0, one launch (start us, length us, event | category | flops | bytes accessed | tf_op | source)
XLA Modules:
  0.0 112.0 jit_solution(813178194561763563)
XLA Ops:
  0.6 2.6 %tiles.1 = (bf16[128,512]{1,0:T(8,128)(2,1)}, bf16[128,512]{1,0:T(8,128)(2,1)}, bf16[128,512]{1,0:T(8,128)(2,1)}, bf16[128,512]{1,0:T(8,128)(2,1)}, bf16[16,8,512]{2,1,0:T(8,128)(2,1)}) custom-call(bf16[256,512]{1,0:T(8,128)(2,1)} %refs_1_.5, s32[4,128]{1,0:T(4,128)} %bitcast.8), custom_call_target="tpu_custom_call" | custom-call | bytes 919552 | tf_op jit(solution)/shard_map/tiles/pallas_call | solution.py:456
  3.2 7.4 %all-to-all-start = ((bf16[16,8,512]{2,1,0:T(8,128)(2,1)}), bf16[16,8,512]{2,1,0:T(8,128)(2,1)S(1)}, u32[]{:S(2)}, u32[]{:S(2)}) async-start(bf16[16,8,512]{2,1,0:T(8,128)(2,1)} %get-tuple-element.76), calls=%async_computation | async-start | bytes 262144 | tf_op jit(solution)/shard_map/all_to_all | solution.py:495
  10.6 0.4 collective-permute-start
  11.0 1.7 %collective-permute-start.1 = (bf16[128,512]{1,0:T(8,128)(2,1)}, bf16[128,512]{1,0:T(8,128)(2,1)S(1)}, u32[]{:S(2)}, u32[]{:S(2)}) collective-permute-start(bf16[128,512]{1,0:T(8,128)(2,1)} %get-tuple-element.72), channel_id=1, source_target_pairs={{14,0},{15,1},{0,2},{1,3},{2,4},{3,5},{4,6},{5,7},{6,8},{7,9},{8,1... | collective-permute-start | bytes 393224 | tf_op jit(solution)/shard_map/ppermute | solution.py:487
  12.7 4.0 %collective-permute-start.2 = (bf16[128,512]{1,0:T(8,128)(2,1)}, bf16[128,512]{1,0:T(8,128)(2,1)S(1)}, u32[]{:S(2)}, u32[]{:S(2)}) collective-permute-start(bf16[128,512]{1,0:T(8,128)(2,1)} %get-tuple-element.73), channel_id=1, source_target_pairs={{1,0},{2,1},{3,2},{4,3},{5,4},{6,5},{7,6},{8,7},{9,8},{10,9},{11,1... | collective-permute-start | bytes 393224 | tf_op jit(solution)/shard_map/ppermute | solution.py:487
  16.7 0.3 collective-permute-start.3
  17.0 2.0 %all-to-all-done.refs_0_ = bf16[16,8,512]{2,1,0:T(8,128)(2,1)S(1)} async-done(((bf16[16,8,512]{2,1,0:T(8,128)(2,1)}), bf16[16,8,512]{2,1,0:T(8,128)(2,1)S(1)}, u32[]{:S(2)}, u32[]{:S(2)}) %all-to-all-start) | async-done | bytes 131104 | tf_op jit(solution)/shard_map/all_to_all | solution.py:495
  19.1 0.7 copy-done.11
  19.7 4.0 %coarse_forward.1 = (bf16[128,512]{1,0:T(8,128)(2,1)}, bf16[16,8,512]{2,1,0:T(8,128)(2,1)}, bf16[128,512]{1,0:T(8,128)(2,1)}, bf16[128,512]{1,0:T(8,128)(2,1)}, ...) custom-call(bf16[16,8,512]{2,1,0:T(8,128)(2,1)} %copy-done.11, ...), custom_call_target="tpu_custom_call" | custom-call | flops 268435456 | bytes 3345408 | tf_op jit(solution)/shard_map/coarse_forward/pallas_call | solution.py:456
  23.7 3.5 %all-to-all-start.1 = ((bf16[16,8,512]{2,1,0:T(8,128)(2,1)}), bf16[16,8,512]{2,1,0:T(8,128)(2,1)S(1)}, u32[]{:S(2)}, u32[]{:S(2)}) async-start(bf16[16,8,512]{2,1,0:T(8,128)(2,1)} %get-tuple-element.77), calls=%async_computation.1 | async-start | bytes 262144 | tf_op jit(solution)/shard_map/all_to_all | solution.py:495
  27.9 0.0 collective-permute-done.refs_2_
  27.9 0.0 copy-start.14
  27.9 0.0 copy-start.15
  27.9 0.0 collective-permute-done.2.refs_4_
  27.9 0.0 copy-start.16
  28.0 0.0 copy-start.17
  28.0 0.6 copy-done.14
  28.6 0.0 copy-done.15
  28.6 0.0 copy-done.16
  28.6 0.0 copy-done.17
  28.7 6.8 %fine_forward.1 = (bf16[512,512]{1,0:T(8,128)(2,1)}, f32[256,512]{1,0:T(8,128)}, bf16[512,512]{1,0:T(8,128)(2,1)}, bf16[512,512]{1,0:T(8,128)(2,1)}, bf16[512,51...) custom-call(s32[1]{0:T(128)S(6)} %copy.38.refs_0_, ...), custom_call_target="tpu_custom_call" | custom-call | flops 1879048192 | bytes 7346180 | tf_op jit(solution)/shard_map/fine_forward/pallas_call | solution.py:456
  35.5 0.0 all-to-all-done.1.refs_3_
  35.5 0.0 copy-start.12
  35.5 0.6 copy-done.12
  36.1 5.8 %node_both.1 = (bf16[256,512]{1,0:T(8,128)(2,1)}, f32[256,512]{1,0:T(8,128)}, bf16[256,512]{1,0:T(8,128)(2,1)}, bf16[16,8,512]{2,1,0:T(8,128)(2,1)}, bf16[8,96,5...) custom-call(s32[1]{0:T(128)} %bitcast.refs_0_, bf16[256,512]{1,0:T(8,128)(2,1)} %refs_1_.5, ...), custom_call_target="tpu_custom_call" | custom-call | flops 1207959552 | bytes 5507076 | tf_op jit(solution)/shard_map/node_both/pallas_call | solution.py:456
  42.0 0.4 collective-permute-start.4
  42.3 5.9 %all-to-all-start.2 = ((bf16[16,8,512]{2,1,0:T(8,128)(2,1)}), bf16[16,8,512]{2,1,0:T(8,128)(2,1)S(1)}, u32[]{:S(2)}, u32[]{:S(2)}) async-start(bf16[16,8,512]{2,1,0:T(8,128)(2,1)} %get-tuple-element.99), calls=%async_computation.2 | async-start | bytes 262144 | tf_op jit(solution)/shard_map/all_to_all | solution.py:495
  48.2 0.9 copy-done.10
  49.1 2.9 %first_halving.2 = (bf16[4,96,512]{2,1,0:T(8,128)(2,1)}, bf16[4,96,512]{2,1,0:T(8,128)(2,1)}) custom-call(bf16[8,96,512]{2,1,0:T(8,128)(2,1)} %get-tuple-element.81.refs_0_, bf16[8,96,512]{2,1,0:T(8,128)(2,1)} %copy-done.10, f32[256,512]{1,0:T(8,128)} %get-tuple-element.83.refs_2_.refs_18_), custom_call_target="tpu_custom_call" | custom-call | bytes 2883584 | tf_op jit(solution)/shard_map/first_halving/pallas_call | solution.py:456
  52.1 2.0 %collective-permute-start.5 = (bf16[4,96,512]{2,1,0:T(8,128)(2,1)}, bf16[4,96,512]{2,1,0:T(8,128)(2,1)S(1)}, u32[]{:S(2)}, u32[]{:S(2)}) collective-permute-start(bf16[4,96,512]{2,1,0:T(8,128)(2,1)} %get-tuple-element.85), channel_id=1, source_target_pairs={{0,2},{1,3},{2,0},{3,1},{4,6},{5,7},{6,4},{7,5},{8,10},{9,11},{10,... | collective-permute-start | bytes 1179656 | tf_op jit(solution)/shard_map/ppermute | solution.py:491
  54.1 2.1 %all-to-all-done.2.refs_16_ = bf16[16,8,512]{2,1,0:T(8,128)(2,1)S(1)} async-done(((bf16[16,8,512]{2,1,0:T(8,128)(2,1)}), bf16[16,8,512]{2,1,0:T(8,128)(2,1)S(1)}, u32[]{:S(2)}, u32[]{:S(2)}) %all-to-all-start.2) | async-done | bytes 131104 | tf_op jit(solution)/shard_map/all_to_all | solution.py:495
  56.1 0.7 copy-done.13
  56.8 8.8 %edge_heads.1 = (bf16[640,512]{1,0:T(8,128)(2,1)}, bf16[640,512]{1,0:T(8,128)(2,1)}, bf16[512,512]{1,0:T(8,128)(2,1)}, bf16[128,512]{1,0:T(8,128)(2,1)}, f32[128...) custom-call(s32[1]{0:T(128)S(6)} %copy.38.refs_0_, ...), custom_call_target="tpu_custom_call" | custom-call | flops 2181038080 | bytes 8592388 | tf_op jit(solution)/shard_map/edge_heads/pallas_call | solution.py:456
  65.6 0.0 collective-permute-done.5.taken_ref.refs_12_
  65.6 0.8 copy-done.3
  66.3 5.8 %edge_weights.1 = (bf16[8,144,512]{2,1,0:T(8,128)(2,1)}, bf16[8,144,512]{2,1,0:T(8,128)(2,1)}) custom-call(s32[1]{0:T(128)} %bitcast.refs_0_, bf16[512,512]{1,0:T(8,128)(2,1)} %get-tuple-element.90.refs_1_, bf16[128,512]{1,0:T(8,128)(2,1)} %get-tuple-element.91.refs_2_, bf16[640,512]{1,0:T(8,128)(2,1)} %get-tuple-element.100.refs_3_, ...), custom_call_target="tpu_custom_call" | custom-call | flops 1342177280 | bytes 6946820 | tf_op jit(solution)/shard_map/edge_weights/pallas_call | solution.py:456
  72.2 0.1 collective-permute-start.9
  72.3 3.0 %collective-permute-done.9.taken_ref = bf16[8,144,512]{2,1,0:T(8,128)(2,1)S(1)} collective-permute-done((bf16[8,144,512]{2,1,0:T(8,128)(2,1)}, bf16[8,144,512]{2,1,0:T(8,128)(2,1)S(1)}, u32[]{:S(2)}, u32[]{:S(2)}) %collective-permute-start.9) | collective-permute-done | bytes 1179680 | tf_op jit(solution)/shard_map/ppermute | solution.py:491
  75.3 1.3 %copy-done = bf16[8,144,512]{2,1,0:T(8,128)(2,1)S(1)} copy-done((bf16[8,144,512]{2,1,0:T(8,128)(2,1)S(1)}, bf16[8,144,512]{2,1,0:T(8,128)(2,1)}, u32[]{:S(2)}) %copy-start) | copy-done | bytes 1179672
  76.6 0.3 first_halving.3
  76.9 0.0 copy-start.5
  76.9 0.1 collective-permute-start.10
  77.0 0.6 copy-done.2
  77.6 0.1 copy-done.4
  77.7 0.1 second_halving.2
  77.8 0.7 collective-permute-start.6
  78.5 2.4 %collective-permute-start.7 = (bf16[96,512]{1,0:T(8,128)(2,1)S(1)}, bf16[96,512]{1,0:T(8,128)(2,1)S(1)}, u32[]{:S(2)}, u32[]{:S(2)}) collective-permute-start(bf16[96,512]{1,0:T(8,128)(2,1)S(1)} %get-tuple-element.88), channel_id=1, source_target_pairs={{0,8},{1,9},{2,10},{3,11},{4,12},{5,13},{6,14},{7,15},{8,0},{9,1},... | collective-permute-start | bytes 294920 | tf_op jit(solution)/shard_map/ppermute | solution.py:491
  80.8 1.4 %collective-permute-start.8 = (bf16[96,512]{1,0:T(8,128)(2,1)S(1)}, bf16[96,512]{1,0:T(8,128)(2,1)S(1)}, u32[]{:S(2)}, u32[]{:S(2)}) collective-permute-start(bf16[96,512]{1,0:T(8,128)(2,1)S(1)} %get-tuple-element.89), channel_id=1, source_target_pairs={{0,12},{1,13},{2,14},{3,15},{4,8},{5,9},{6,10},{7,11},{8,4},{9,5},... | collective-permute-start | bytes 294920 | tf_op jit(solution)/shard_map/ppermute | solution.py:491
  82.3 1.8 %collective-permute-done.6.refs_0_ = bf16[96,512]{1,0:T(8,128)(2,1)S(1)} collective-permute-done((bf16[96,512]{1,0:T(8,128)(2,1)S(1)}, bf16[96,512]{1,0:T(8,128)(2,1)S(1)}, u32[]{:S(2)}, u32[]{:S(2)}) %collective-permute-start.6) | collective-permute-done | bytes 98336 | tf_op jit(solution)/shard_map/ppermute | solution.py:491
  84.0 5.0 %collective-permute-done.7.refs_1_ = bf16[96,512]{1,0:T(8,128)(2,1)S(1)} collective-permute-done((bf16[96,512]{1,0:T(8,128)(2,1)S(1)}, bf16[96,512]{1,0:T(8,128)(2,1)S(1)}, u32[]{:S(2)}, u32[]{:S(2)}) %collective-permute-start.7) | collective-permute-done | bytes 98336 | tf_op jit(solution)/shard_map/ppermute | solution.py:491
  89.0 0.0 collective-permute-done.8.refs_2_
  89.0 0.7 last_sum.2
  89.7 2.6 %collective-permute-done.10.taken_ref = bf16[4,144,512]{2,1,0:T(8,128)(2,1)S(1)} collective-permute-done((bf16[4,144,512]{2,1,0:T(8,128)(2,1)S(1)}, bf16[4,144,512]{2,1,0:T(8,128)(2,1)S(1)}, u32[]{:S(2)}, u32[]{:S(2)}) %collective-permute-start.10) | collective-permute-done | bytes 589856 | tf_op jit(solution)/shard_map/ppermute | solution.py:491
  92.4 0.1 second_halving.3
  92.5 1.5 %collective-permute-start.14 = (bf16[128,512]{1,0:T(8,128)(2,1)S(1)}, bf16[128,512]{1,0:T(8,128)(2,1)S(1)}, u32[]{:S(2)}, u32[]{:S(2)}) collective-permute-start(bf16[128,512]{1,0:T(8,128)(2,1)S(1)} %get-tuple-element.121), channel_id=1, source_target_pairs={{1,0},{2,1},{3,2},{4,3},{5,4},{6,5},{7,6},{8,7},{9,8},{10,9},{11,1... | collective-permute-start | bytes 393224 | tf_op jit(solution)/shard_map/ppermute | solution.py:487
  94.0 1.2 %collective-permute-start.15 = (bf16[128,512]{1,0:T(8,128)(2,1)S(1)}, bf16[128,512]{1,0:T(8,128)(2,1)S(1)}, u32[]{:S(2)}, u32[]{:S(2)}) collective-permute-start(bf16[128,512]{1,0:T(8,128)(2,1)S(1)} %get-tuple-element.122), channel_id=1, source_target_pairs={{2,0},{3,1},{4,2},{5,3},{6,4},{7,5},{8,6},{9,7},{10,8},{11,9},{12,... | collective-permute-start | bytes 393224 | tf_op jit(solution)/shard_map/ppermute | solution.py:487
  95.2 1.1 collective-permute-start.12
  96.3 3.3 %collective-permute-start.13 = (bf16[144,512]{1,0:T(8,128)(2,1)S(1)}, bf16[144,512]{1,0:T(8,128)(2,1)S(1)}, u32[]{:S(2)}, u32[]{:S(2)}) collective-permute-start(bf16[144,512]{1,0:T(8,128)(2,1)S(1)} %get-tuple-element.119), channel_id=1, source_target_pairs={{0,12},{1,13},{2,14},{3,15},{4,8},{5,9},{6,10},{7,11},{8,4},{9,5},... | collective-permute-start | bytes 442376 | tf_op jit(solution)/shard_map/ppermute | solution.py:491
  99.6 0.7 collective-permute-done.15.refs_1_
  100.2 4.7 %collective-permute-start.17 = (bf16[128,512]{1,0:T(8,128)(2,1)S(1)}, bf16[128,512]{1,0:T(8,128)(2,1)S(1)}, u32[]{:S(2)}, u32[]{:S(2)}) collective-permute-start(bf16[128,512]{1,0:T(8,128)(2,1)S(1)} %get-tuple-element.124), channel_id=1, source_target_pairs={{14,0},{15,1},{0,2},{1,3},{2,4},{3,5},{4,6},{5,7},{6,8},{7,9},{8,1... | collective-permute-start | bytes 393224 | tf_op jit(solution)/shard_map/ppermute | solution.py:487
  104.9 3.2 %collective-permute-done.16.refs_2_ = bf16[128,512]{1,0:T(8,128)(2,1)S(1)} collective-permute-done((bf16[128,512]{1,0:T(8,128)(2,1)S(1)}, bf16[128,512]{1,0:T(8,128)(2,1)S(1)}, u32[]{:S(2)}, u32[]{:S(2)}) %collective-permute-start.16) | collective-permute-done | bytes 131104 | tf_op jit(solution)/shard_map/ppermute | solution.py:487
  108.1 2.6 %collective-permute-done.17.refs_3_ = bf16[128,512]{1,0:T(8,128)(2,1)S(1)} collective-permute-done((bf16[128,512]{1,0:T(8,128)(2,1)S(1)}, bf16[128,512]{1,0:T(8,128)(2,1)S(1)}, u32[]{:S(2)}, u32[]{:S(2)}) %collective-permute-start.17) | collective-permute-done | bytes 131104 | tf_op jit(solution)/shard_map/ppermute | solution.py:487
  110.7 0.4 node_gradient.1.refs_3_
  111.2 0.9 last_sum.3
  (27 shorter events, 0.1 us)
Async XLA Ops:
  3.2 15.8 %all-to-all-start = ((bf16[16,8,512]{2,1,0:T(8,128)(2,1)}), bf16[16,8,512]{2,1,0:T(8,128)(2,1)S(1)}, u32[]{:S(2)}, u32[]{:S(2)}) async-start(bf16[16,8,512]{2,1,0:T(8,128)(2,1)} %get-tuple-element.76), calls=%async_computation | async-start | bytes 262144 | tf_op jit(solution)/shard_map/all_to_all | solution.py:495
  10.6 17.3 %collective-permute-start = (bf16[128,512]{1,0:T(8,128)(2,1)}, bf16[128,512]{1,0:T(8,128)(2,1)S(1)}, u32[]{:S(2)}, u32[]{:S(2)}) collective-permute-start(bf16[128,512]{1,0:T(8,128)(2,1)} %get-tuple-element.71), channel_id=1, source_target_pairs={{15,0},{0,1},{1,2},{2,3},{3,4},{4,5},{5,6},{6,7},{7,8},{8,9},{9,10... | collective-permute-start | bytes 393224 | tf_op jit(solution)/shard_map/ppermute | solution.py:487
  11.0 16.9 %collective-permute-start.1 = (bf16[128,512]{1,0:T(8,128)(2,1)}, bf16[128,512]{1,0:T(8,128)(2,1)S(1)}, u32[]{:S(2)}, u32[]{:S(2)}) collective-permute-start(bf16[128,512]{1,0:T(8,128)(2,1)} %get-tuple-element.72), channel_id=1, source_target_pairs={{14,0},{15,1},{0,2},{1,3},{2,4},{3,5},{4,6},{5,7},{6,8},{7,9},{8,1... | collective-permute-start | bytes 393224 | tf_op jit(solution)/shard_map/ppermute | solution.py:487
  12.7 15.2 %collective-permute-start.2 = (bf16[128,512]{1,0:T(8,128)(2,1)}, bf16[128,512]{1,0:T(8,128)(2,1)S(1)}, u32[]{:S(2)}, u32[]{:S(2)}) collective-permute-start(bf16[128,512]{1,0:T(8,128)(2,1)} %get-tuple-element.73), channel_id=1, source_target_pairs={{1,0},{2,1},{3,2},{4,3},{5,4},{6,5},{7,6},{8,7},{9,8},{10,9},{11,1... | collective-permute-start | bytes 393224 | tf_op jit(solution)/shard_map/ppermute | solution.py:487
  16.7 11.2 %collective-permute-start.3 = (bf16[128,512]{1,0:T(8,128)(2,1)}, bf16[128,512]{1,0:T(8,128)(2,1)S(1)}, u32[]{:S(2)}, u32[]{:S(2)}) collective-permute-start(bf16[128,512]{1,0:T(8,128)(2,1)} %get-tuple-element.74), channel_id=1, source_target_pairs={{2,0},{3,1},{4,2},{5,3},{6,4},{7,5},{8,6},{9,7},{10,8},{11,9},{12,... | collective-permute-start | bytes 393224 | tf_op jit(solution)/shard_map/ppermute | solution.py:487
  19.1 0.7 copy-start.11
  23.7 11.8 %all-to-all-start.1 = ((bf16[16,8,512]{2,1,0:T(8,128)(2,1)}), bf16[16,8,512]{2,1,0:T(8,128)(2,1)S(1)}, u32[]{:S(2)}, u32[]{:S(2)}) async-start(bf16[16,8,512]{2,1,0:T(8,128)(2,1)} %get-tuple-element.77), calls=%async_computation.1 | async-start | bytes 262144 | tf_op jit(solution)/shard_map/all_to_all | solution.py:495
  27.9 0.7 copy-start.14
  27.9 0.7 copy-start.15
  27.9 0.7 copy-start.16
  28.0 0.7 copy-start.17
  35.5 0.7 copy-start.12
  42.0 6.2 %collective-permute-start.4 = (bf16[8,96,512]{2,1,0:T(8,128)(2,1)}, bf16[8,96,512]{2,1,0:T(8,128)(2,1)S(1)}, u32[]{:S(2)}, u32[]{:S(2)}) collective-permute-start(bf16[8,96,512]{2,1,0:T(8,128)(2,1)} %get-tuple-element.82), channel_id=1, source_target_pairs={{0,1},{1,0},{2,3},{3,2},{4,5},{5,4},{6,7},{7,6},{8,9},{9,8},{10,11... | collective-permute-start | bytes 2359304 | tf_op jit(solution)/shard_map/ppermute | solution.py:491
  42.3 13.8 %all-to-all-start.2 = ((bf16[16,8,512]{2,1,0:T(8,128)(2,1)}), bf16[16,8,512]{2,1,0:T(8,128)(2,1)S(1)}, u32[]{:S(2)}, u32[]{:S(2)}) async-start(bf16[16,8,512]{2,1,0:T(8,128)(2,1)} %get-tuple-element.99), calls=%async_computation.2 | async-start | bytes 262144 | tf_op jit(solution)/shard_map/all_to_all | solution.py:495
  48.2 0.9 copy-start.10
  52.1 13.5 %collective-permute-start.5 = (bf16[4,96,512]{2,1,0:T(8,128)(2,1)}, bf16[4,96,512]{2,1,0:T(8,128)(2,1)S(1)}, u32[]{:S(2)}, u32[]{:S(2)}) collective-permute-start(bf16[4,96,512]{2,1,0:T(8,128)(2,1)} %get-tuple-element.85), channel_id=1, source_target_pairs={{0,2},{1,3},{2,0},{3,1},{4,6},{5,7},{6,4},{7,5},{8,10},{9,11},{10,... | collective-permute-start | bytes 1179656 | tf_op jit(solution)/shard_map/ppermute | solution.py:491
  56.1 0.7 copy-start.13
  65.6 0.8 copy-start.3
  72.2 3.1 %collective-permute-start.9 = (bf16[8,144,512]{2,1,0:T(8,128)(2,1)}, bf16[8,144,512]{2,1,0:T(8,128)(2,1)S(1)}, u32[]{:S(2)}, u32[]{:S(2)}) collective-permute-start(bf16[8,144,512]{2,1,0:T(8,128)(2,1)} %get-tuple-element.108), channel_id=1, source_target_pairs={{0,1},{1,0},{2,3},{3,2},{4,5},{5,4},{6,7},{7,6},{8,9},{9,8},{10,11... | collective-permute-start | bytes 3538952 | tf_op jit(solution)/shard_map/ppermute | solution.py:491
  75.3 1.3 %copy-start = (bf16[8,144,512]{2,1,0:T(8,128)(2,1)S(1)}, bf16[8,144,512]{2,1,0:T(8,128)(2,1)}, u32[]{:S(2)}) copy-start(bf16[8,144,512]{2,1,0:T(8,128)(2,1)} %get-tuple-element.107.kept_ref) | copy-start | bytes 3538948
  76.6 1.0 copy-start.2
  76.6 1.1 copy-start.4
  76.9 15.5 %copy-start.5 = (bf16[128,512]{1,0:T(8,128)(2,1)S(1)}, bf16[128,512]{1,0:T(8,128)(2,1)}, u32[]{:S(2)}) copy-start(bf16[128,512]{1,0:T(8,128)(2,1)} %get-tuple-element.112.refs_0_) | copy-start | bytes 393220
  76.9 15.5 %copy-start.6 = (bf16[128,512]{1,0:T(8,128)(2,1)S(1)}, bf16[128,512]{1,0:T(8,128)(2,1)}, u32[]{:S(2)}) copy-start(bf16[128,512]{1,0:T(8,128)(2,1)} %get-tuple-element.113.refs_1_) | copy-start | bytes 393220
  76.9 15.5 %copy-start.7 = (bf16[128,512]{1,0:T(8,128)(2,1)S(1)}, bf16[128,512]{1,0:T(8,128)(2,1)}, u32[]{:S(2)}) copy-start(bf16[128,512]{1,0:T(8,128)(2,1)} %get-tuple-element.114.refs_2_) | copy-start | bytes 393220
  76.9 15.5 %copy-start.8 = (bf16[128,512]{1,0:T(8,128)(2,1)S(1)}, bf16[128,512]{1,0:T(8,128)(2,1)}, u32[]{:S(2)}) copy-start(bf16[128,512]{1,0:T(8,128)(2,1)} %get-tuple-element.115.refs_3_) | copy-start | bytes 393220
  76.9 15.4 %collective-permute-start.10 = (bf16[4,144,512]{2,1,0:T(8,128)(2,1)S(1)}, bf16[4,144,512]{2,1,0:T(8,128)(2,1)S(1)}, u32[]{:S(2)}, u32[]{:S(2)}) collective-permute-start(bf16[4,144,512]{2,1,0:T(8,128)(2,1)S(1)} %get-tuple-element.111), channel_id=1, source_target_pairs={{0,2},{1,3},{2,0},{3,1},{4,6},{5,7},{6,4},{7,5},{8,10},{9,11},{10,... | collective-permute-start | bytes 1769480 | tf_op jit(solution)/shard_map/ppermute | solution.py:491
  77.8 6.2 %collective-permute-start.6 = (bf16[96,512]{1,0:T(8,128)(2,1)S(1)}, bf16[96,512]{1,0:T(8,128)(2,1)S(1)}, u32[]{:S(2)}, u32[]{:S(2)}) collective-permute-start(bf16[96,512]{1,0:T(8,128)(2,1)S(1)} %get-tuple-element.87), channel_id=1, source_target_pairs={{0,4},{1,5},{2,6},{3,7},{4,0},{5,1},{6,2},{7,3},{8,12},{9,13},{10,... | collective-permute-start | bytes 294920 | tf_op jit(solution)/shard_map/ppermute | solution.py:491
  78.5 10.5 %collective-permute-start.7 = (bf16[96,512]{1,0:T(8,128)(2,1)S(1)}, bf16[96,512]{1,0:T(8,128)(2,1)S(1)}, u32[]{:S(2)}, u32[]{:S(2)}) collective-permute-start(bf16[96,512]{1,0:T(8,128)(2,1)S(1)} %get-tuple-element.88), channel_id=1, source_target_pairs={{0,8},{1,9},{2,10},{3,11},{4,12},{5,13},{6,14},{7,15},{8,0},{9,1},... | collective-permute-start | bytes 294920 | tf_op jit(solution)/shard_map/ppermute | solution.py:491
  80.8 8.2 %collective-permute-start.8 = (bf16[96,512]{1,0:T(8,128)(2,1)S(1)}, bf16[96,512]{1,0:T(8,128)(2,1)S(1)}, u32[]{:S(2)}, u32[]{:S(2)}) collective-permute-start(bf16[96,512]{1,0:T(8,128)(2,1)S(1)} %get-tuple-element.89), channel_id=1, source_target_pairs={{0,12},{1,13},{2,14},{3,15},{4,8},{5,9},{6,10},{7,11},{8,4},{9,5},... | collective-permute-start | bytes 294920 | tf_op jit(solution)/shard_map/ppermute | solution.py:491
  89.0 21.7 %copy-start.1 = (f32[256,512]{1,0:T(8,128)S(1)}, f32[256,512]{1,0:T(8,128)}, u32[]{:S(2)}) copy-start(f32[256,512]{1,0:T(8,128)} %get-tuple-element.120.own_ref) | copy-start | bytes 1572868
  89.0 21.7 %copy-start.9 = (s32[1,4,128]{2,1,0:T(4,128)S(1)}, s32[1,4,128]{2,1,0:T(4,128)}, u32[]{:S(2)}) copy-start(s32[1,4,128]{2,1,0:T(4,128)} %param.25) | copy-start | bytes 6148
  92.5 7.1 %collective-permute-start.14 = (bf16[128,512]{1,0:T(8,128)(2,1)S(1)}, bf16[128,512]{1,0:T(8,128)(2,1)S(1)}, u32[]{:S(2)}, u32[]{:S(2)}) collective-permute-start(bf16[128,512]{1,0:T(8,128)(2,1)S(1)} %get-tuple-element.121), channel_id=1, source_target_pairs={{1,0},{2,1},{3,2},{4,3},{5,4},{6,5},{7,6},{8,7},{9,8},{10,9},{11,1... | collective-permute-start | bytes 393224 | tf_op jit(solution)/shard_map/ppermute | solution.py:487
  94.0 6.2 %collective-permute-start.15 = (bf16[128,512]{1,0:T(8,128)(2,1)S(1)}, bf16[128,512]{1,0:T(8,128)(2,1)S(1)}, u32[]{:S(2)}, u32[]{:S(2)}) collective-permute-start(bf16[128,512]{1,0:T(8,128)(2,1)S(1)} %get-tuple-element.122), channel_id=1, source_target_pairs={{2,0},{3,1},{4,2},{5,3},{6,4},{7,5},{8,6},{9,7},{10,8},{11,9},{12,... | collective-permute-start | bytes 393224 | tf_op jit(solution)/shard_map/ppermute | solution.py:487
  95.2 16.0 %collective-permute-start.11 = (bf16[144,512]{1,0:T(8,128)(2,1)S(1)}, bf16[144,512]{1,0:T(8,128)(2,1)S(1)}, u32[]{:S(2)}, u32[]{:S(2)}) collective-permute-start(bf16[144,512]{1,0:T(8,128)(2,1)S(1)} %get-tuple-element.117), channel_id=1, source_target_pairs={{0,4},{1,5},{2,6},{3,7},{4,0},{5,1},{6,2},{7,3},{8,12},{9,13},{10,... | collective-permute-start | bytes 442376 | tf_op jit(solution)/shard_map/ppermute | solution.py:491
  95.2 16.0 %collective-permute-start.12 = (bf16[144,512]{1,0:T(8,128)(2,1)S(1)}, bf16[144,512]{1,0:T(8,128)(2,1)S(1)}, u32[]{:S(2)}, u32[]{:S(2)}) collective-permute-start(bf16[144,512]{1,0:T(8,128)(2,1)S(1)} %get-tuple-element.118), channel_id=1, source_target_pairs={{0,8},{1,9},{2,10},{3,11},{4,12},{5,13},{6,14},{7,15},{8,0},{9,1},... | collective-permute-start | bytes 442376 | tf_op jit(solution)/shard_map/ppermute | solution.py:491
  96.3 14.9 %collective-permute-start.13 = (bf16[144,512]{1,0:T(8,128)(2,1)S(1)}, bf16[144,512]{1,0:T(8,128)(2,1)S(1)}, u32[]{:S(2)}, u32[]{:S(2)}) collective-permute-start(bf16[144,512]{1,0:T(8,128)(2,1)S(1)} %get-tuple-element.119), channel_id=1, source_target_pairs={{0,12},{1,13},{2,14},{3,15},{4,8},{5,9},{6,10},{7,11},{8,4},{9,5},... | collective-permute-start | bytes 442376 | tf_op jit(solution)/shard_map/ppermute | solution.py:491
  99.6 8.6 %collective-permute-start.16 = (bf16[128,512]{1,0:T(8,128)(2,1)S(1)}, bf16[128,512]{1,0:T(8,128)(2,1)S(1)}, u32[]{:S(2)}, u32[]{:S(2)}) collective-permute-start(bf16[128,512]{1,0:T(8,128)(2,1)S(1)} %get-tuple-element.123), channel_id=1, source_target_pairs={{15,0},{0,1},{1,2},{2,3},{3,4},{4,5},{5,6},{6,7},{7,8},{8,9},{9,10... | collective-permute-start | bytes 393224 | tf_op jit(solution)/shard_map/ppermute | solution.py:487
  100.2 10.5 %collective-permute-start.17 = (bf16[128,512]{1,0:T(8,128)(2,1)S(1)}, bf16[128,512]{1,0:T(8,128)(2,1)S(1)}, u32[]{:S(2)}, u32[]{:S(2)}) collective-permute-start(bf16[128,512]{1,0:T(8,128)(2,1)S(1)} %get-tuple-element.124), channel_id=1, source_target_pairs={{14,0},{15,1},{0,2},{1,3},{2,4},{3,5},{4,6},{5,7},{6,8},{7,9},{8,1... | collective-permute-start | bytes 393224 | tf_op jit(solution)/shard_map/ppermute | solution.py:487

commit v6 on v5

--- a/solution.py
+++ b/solution.py
@@ -38,13 +38,14 @@
     return jnp.where(row == index, 1.0, 0.0).astype(BF16)
 
 
-def pick(hot, table):
-    return mm_tn(hot, table)
-
-
-def pick_wide(hot, table):
-    high, low = halves(table)
-    return mm_tn(hot, high) + mm_tn(hot, low)
+def pick(index, table):
+    entries = index.shape[1]
+    column = jnp.transpose(jnp.broadcast_to(index, (128, entries)))
+    lane = lax.broadcasted_iota(jnp.int32, (entries, 128), 1)
+    parts = []
+    for start in range(0, table.shape[0], 128):
+        parts.append(jnp.where(column == lane + start, 1.0, 0.0).astype(BF16))
+    return mm(jnp.concatenate(parts, 1), table)
 
 
 def put_wide(hot, rows):
@@ -76,15 +77,10 @@
 
 
 def tiles_kernel(nodes_ref, halo_ref, *outs):
-    spread_ref = outs[-1]
     nodes = nodes_ref[...]
-    for slot, out in enumerate(outs[:-1]):
-        hot = one_hot(halo_ref[slot : slot + 1, :], nodes.shape[0])
-        out[...] = pick(hot, nodes).astype(BF16)
+    for slot, out in enumerate(outs):
+        out[...] = pick(halo_ref[slot : slot + 1, :], nodes).astype(BF16)
         out.done()
-    rows = nodes_ref[0:16, :].astype(F32)[:COARSE_DEV].astype(BF16)
-    for peer in range(spread_ref.shape[0]):
-        spread_ref[peer] = rows
 
 
 def gathered(ref):
@@ -98,11 +94,10 @@
 ):
     width = edges_ref.shape[1]
     table = gathered(all_ref).astype(BF16)
-    hot_s = one_hot(send_ref[...], table.shape[0])
     hot_r = one_hot(recv_ref[...], table.shape[0])
     edges = edges_ref[...]
-    zs = pick(hot_s, table).astype(BF16)
-    zr = pick(hot_r, table).astype(BF16)
+    zs = pick(send_ref[...], table).astype(BF16)
+    zr = pick(recv_ref[...], table).astype(BF16)
     pre = (
         mm(edges, w1_ref[0:width, :])
         + mm(zs, w1_ref[width : 2 * width, :])
@@ -136,10 +131,9 @@
     for start in range(0, count, block):
         rows = slice(start, start + block)
         edges = edges_ref[rows, :]
-        hot_s = one_hot(send_ref[:, rows], space_ref.shape[0])
         hot_r = one_hot(recv_ref[:, rows], own)
-        zs = pick(hot_s, space_ref[...]).astype(BF16)
-        zr = pick(hot_r, nodes_ref[...]).astype(BF16)
+        zs = pick(send_ref[:, rows], space_ref[...]).astype(BF16)
+        zr = pick(recv_ref[:, rows], nodes_ref[...]).astype(BF16)
         pre = (
             mm(edges, w1_ref[0:width, :])
             + mm(zs, w1_ref[width : 2 * width, :])
@@ -162,19 +156,22 @@
 
 
 def by_distance(me, peers, sums, kept_ref, given_ref):
+    quarter = peers // 4
     for r in list(range(1, peers, 2)) + list(range(0, peers, 2)):
         if r == 0:
             given_ref.done()
         to = jnp.bitwise_xor(me, r)
         out = given_ref if r % 2 else kept_ref
+        slot = (r // 2 % 2) * quarter + r // 4
         place = 0
         for total in sums:
             rows = total.shape[0] // peers
             part = total[pl.ds(pl.multiple_of(to * rows, 8), rows), :]
             if rows % 16:
                 part = jnp.concatenate([part, jnp.zeros((-rows % 16, part.shape[1]), F32)], 0)
-            out[r // 2, place : place + part.shape[0], :] = part.astype(BF16)
+            out[slot, place : place + part.shape[0], :] = part.astype(BF16)
             place += part.shape[0]
+    kept_ref.done()
 
 
 def node_kernel(
@@ -224,12 +221,12 @@
             hot_r = one_hot(recv_ref[:, rows], own)
             hot_s = one_hot(send_ref[:, rows], space_ref.shape[0])
             place = start + lax.broadcasted_iota(jnp.int32, (block, 1), 0)
-            cotan = jnp.where(place < count_ref[0], d_edges + pick(hot_r, dagg_ref[...]), 0.0)
+            cotan = jnp.where(place < count_ref[0], d_edges + pick(recv_ref[:, rows], dagg_ref[...]), 0.0)
         else:
             table = gathered(all_ref).astype(BF16)
             hot_r = one_hot(crecv_ref[...], table.shape[0])
             hot_s = one_hot(csend_ref[...], table.shape[0])
-            cotan = d_edges + pick(hot_r, table)
+            cotan = d_edges + pick(crecv_ref[...], table)
         back_out, back_pre = head_of_backward(
             cotan, w2_ref[...], gain_ref[...], slope_ref[rows, :].astype(F32),
             normed_ref[rows, :].astype(F32), std_ref[rows, 0:1],
@@ -259,19 +256,21 @@
 
 
 def edge_weights_kernel(
-    me_ref, hidden_ref, out_ref, edges_ref, pre_ref, zs_ref, zr_ref, *rest, ordered,
+    me_ref, edges_ref, pre_ref, zs_ref, zr_ref, hidden_ref, out_ref, *rest, ordered,
 ):
     if ordered:
-        part_ref, kept_ref, given_ref, g1_ref, g2_ref = rest
+        part_ref, kept1_ref, given1_ref, kept2_ref, given2_ref, g1_ref, g2_ref = rest
     else:
         g1_ref, g2_ref = rest
     width = edges_ref.shape[1]
-    g2_ref[...] = mm_tn(hidden_ref[...], out_ref[...])
     g1_ref[0:width, :] = mm_tn(edges_ref[...], pre_ref[...])
     g1_ref[width : 2 * width, :] = mm_tn(zs_ref[...], pre_ref[...])
     g1_ref[2 * width : 3 * width, :] = mm_tn(zr_ref[...], pre_ref[...])
     if ordered:
-        by_distance(me_ref[0], 2 * kept_ref.shape[0], (g1_ref, g2_ref, part_ref), kept_ref, given_ref)
+        by_distance(me_ref[0], 2 * kept1_ref.shape[0], (g1_ref,), kept1_ref, given1_ref)
+    g2_ref[...] = mm_tn(hidden_ref[...], out_ref[...])
+    if ordered:
+        by_distance(me_ref[0], 2 * kept2_ref.shape[0], (g2_ref, part_ref), kept2_ref, given2_ref)
 
 
 def node_gradient_kernel(own_ref, halo_ref, *refs):
@@ -288,15 +287,6 @@
     first = total_ref[0:16, :] + jnp.concatenate([share, jnp.zeros_like(share)], 0)
     g_ref[...] = total_ref[...].astype(BF16)
     g_ref[0:16, :] = first.astype(BF16)
-
-
-def first_halving_kernel(kept_ref, taken_ref, *refs):
-    passing = (len(refs) - 2) // 2
-    keep_ref, give_ref = refs[passing : passing + 2]
-    for j in range(kept_ref.shape[0]):
-        total = (kept_ref[j].astype(F32) + taken_ref[j].astype(F32)).astype(BF16)
-        out = give_ref if j % 2 else keep_ref
-        out[j // 2] = total
 
 
 def second_halving_kernel(kept_ref, taken_ref, *refs, passing):
@@ -309,21 +299,22 @@
             keep_ref[...] = total
 
 
-def last_sum_kernel(kept_ref, *refs, taken, with_nodes, passing):
+def last_sum_kernel(kept_ref, *refs, taken):
     total = kept_ref[...]
     for ref in refs[:taken]:
         total = total + ref[...].astype(F32)
-    if with_nodes:
-        nodes_ref, first_ref, second_ref, g_ref = refs[taken:]
-    else:
-        first_ref, second_ref = refs[taken + passing : len(refs) - passing]
-    cut = first_ref.shape[0]
-    end = cut + second_ref.shape[0]
-    first_ref[...] = total[:cut]
-    second_ref[...] = total[cut:end]
-    if with_nodes:
+    refs = refs[taken:]
+    if refs[0].shape[0] > total.shape[0]:
+        nodes_ref, first_ref, g_ref = refs
+        cut = first_ref.shape[0]
+        first_ref[...] = total[:cut]
         g_ref[...] = nodes_ref[...].astype(BF16)
-        g_ref[0:16, :] = (nodes_ref[0:16, :] + total[end : end + 16]).astype(BF16)
+        g_ref[0:16, :] = (nodes_ref[0:16, :] + total[cut : cut + 16]).astype(BF16)
+        return
+    place = 0
+    for ref in refs:
+        ref[...] = total[place : place + ref.shape[0]]
+        place += ref.shape[0]
 
 
 VM = pl.BlockSpec(memory_space=pltpu.VMEM)
@@ -495,9 +486,10 @@
     return lax.all_to_all(blocks, axis, 0, 0)
 
 
-def first_halving(kept, taken, passing=()):
-    half = shape((kept.shape[0] // 2,) + kept.shape[1:], BF16)
-    return small_call(first_halving_kernel, "first_halving", (kept, taken), [half, half], passing)
+def first_halving(kept, taken):
+    half = kept.shape[0] // 2
+    give = (kept[half:].astype(F32) + taken[half:].astype(F32)).astype(BF16)
+    return kept[:half].astype(F32) + taken[:half].astype(F32), give
 
 
 def second_halving(kept, taken, passing=()):
@@ -507,17 +499,13 @@
     return small_call(kernel, "second_halving", (kept, taken), outs, passing)
 
 
-def last_sum(kept, taken, first_rows, second_rows, nodes=None, passing=()):
-    width = kept.shape[1]
-    outs = [shape((first_rows, width), F32), shape((second_rows, width), F32)]
+def last_sum(kept, taken, sizes, nodes=None):
+    outs = [shape((rows, kept.shape[1]), F32) for rows in sizes]
     ins = (kept, *taken)
     if nodes is not None:
         outs.append(shape(nodes.shape, BF16))
         ins += (nodes,)
-    kernel = functools.partial(
-        last_sum_kernel, taken=len(taken), with_nodes=nodes is not None, passing=len(passing)
-    )
-    return small_call(kernel, "last_sum", ins, outs, passing)
+    return small_call(functools.partial(last_sum_kernel, taken=len(taken)), "last_sum", ins, outs)
 
 
 def local(
@@ -560,10 +548,10 @@
 
     made = call(
         tiles_kernel, "tiles", (nodes, halo), [VM, VM],
-        [shape((tile, width), BF16)] * slots + [every],
+        [shape((tile, width), BF16)] * slots,
     )
     received = [passed_along(made[slot], axis, offset) for slot, offset in enumerate(offsets)]
-    coarse_all = exchanged_with_all(made[-1], axis)
+    coarse_all = exchanged_with_all(jnp.broadcast_to(nodes[:COARSE_DEV][None], every.shape), axis)
 
     def saved_shapes(rows):
         return [
@@ -608,12 +596,13 @@
     dagg_all = exchanged_with_all(dagg_spread, axis)
     if ordered:
         node_taken = exchanged(node_parts[1], axis, 1)
-        half = shape((peers // 2 // 2,) + node_parts[0].shape[1:], BF16)
-        node_kept, node_given = call(
-            first_halving_kernel, "first_halving", (node_parts[0], node_taken, base), [VM, VM, None], [half, half]
-        )
+        node_kept, node_given = first_halving(node_parts[0], node_taken)
 
     sum_shapes, sum_scratch = weight_shapes(edge_w1, edge_w2, 16)
+    if ordered:
+        cut = edge_w1.shape[0] // peers
+        rows = sum_shapes[0].shape[1] - cut
+        sum_shapes = [shape((peers // 2, cut, width), BF16)] * 2 + [shape((peers // 2, rows, width), BF16)] * 2
     f_zs, f_zr, f_hidden, f_slope, f_normed, f_std = fine_saved
     c_zs, c_zr, c_hidden, c_slope, c_normed, c_std = coarse_saved
     pair = [Rows(joined=2), None]
@@ -637,10 +626,10 @@
     edge_parts = call(
         functools.partial(edge_weights_kernel, ordered=ordered), "edge_weights",
         (
-            me, f_hidden, c_hidden, out, fine_edges, coarse_edges, pre, f_zs, c_zs, f_zr, c_zr, coarse_part,
+            me, fine_edges, coarse_edges, pre, f_zs, c_zs, f_zr, c_zr, f_hidden, c_hidden, out, coarse_part,
             *((node_taken,) if ordered else ()),
         ),
-        [SM] + pair + [VM] + pair + [VM] + pair * 2 + [VM if ordered else None] + [None] * ordered,
+        [SM] + pair + [VM] + pair * 3 + [VM] + [VM if ordered else None] + [None] * ordered,
         sum_shapes,
         scratch=sum_scratch,
         flops=2 * edges * width * width * 4,
@@ -657,20 +646,27 @@
         return total
 
     if ordered:
-        edge_kept, edge_given = edge_parts
-        edge_taken = exchanged(edge_given, axis, 1)
-        edge_kept, edge_given = first_halving(edge_kept, edge_taken)
-        edge_taken = exchanged(edge_given, axis, 2)
+
+        def along_z(given):
+            return [exchanged(part, axis, 4 * (k + 1)) for k, part in enumerate(given)]
+
+        kept1, given1, kept2, given2 = edge_parts
+        taken1 = exchanged(given1, axis, 1)
+        taken2 = exchanged(given2, axis, 1)
+        kept1, given1 = first_halving(kept1, taken1)
+        taken1 = exchanged(given1, axis, 2)
+        kept2, given2 = first_halving(kept2, taken2)
+        taken2 = exchanged(given2, axis, 2)
         node_kept, *given = second_halving(node_kept, node_taken)
-        node_taken = [exchanged(part, axis, 4 * (k + 1)) for k, part in enumerate(given)]
-        g_nw1, g_nw2, edge_kept = last_sum(
-            node_kept, node_taken, rows_of(node_w1), rows_of(node_w2), passing=(edge_kept,)
-        )
-        edge_kept, *given = second_halving(edge_kept, edge_taken, tuple(pieces))
+        g_nw1, g_nw2 = last_sum(node_kept, along_z(given), (rows_of(node_w1), rows_of(node_w2)))
+        kept1, *given = second_halving(kept1, taken1, tuple(pieces))
         given, pieces = given[:-slots], given[-slots:]
-        edge_taken = [exchanged(part, axis, 4 * (k + 1)) for k, part in enumerate(given)]
+        taken1 = along_z(given)
+        kept2, *given = second_halving(kept2, taken2)
+        taken2 = along_z(given)
         total = returned_tiles(pieces)
-        g_ew1, g_ew2, g_nodes = last_sum(edge_kept, edge_taken, rows_of(edge_w1), rows_of(edge_w2), total)
+        (g_ew1,) = last_sum(kept1, taken1, (rows_of(edge_w1),))
+        g_ew2, g_nodes = last_sum(kept2, taken2, (rows_of(edge_w2),), total)
     else:
         coarse_share = exchanged_with_all(coarse_part, axis)
         (g_nodes,) = small_call(

time: 114 us -> 111 us (0.974); the launches traced: 112 us -> 110 us
  Pallas kernels: 39.2 us -> 36.1 us
  other arithmetic: 0 us -> 2.87 us
  local copies, waits for them, and re-layouts: 6.38 us -> 4.87 us
    ppermute x8, waiting for transfers between devices: 6.44 us -> 0.02 us  [passed_along(): return lax.ppermute(block, axis, route)]
    ppermute x10 -> x15, starting transfers between devices: 11.3 us -> 16.4 us  [exchanged(): lax.ppermute(block, axis, [(i, i ^ distance) for i in range(lax.axis_size...]
    ppermute x10 -> x15, waiting for transfers between devices: 12.4 us -> 17.4 us  [exchanged(): lax.ppermute(block, axis, [(i, i ^ distance) for i in range(lax.axis_size...]
    ppermute x8, starting transfers between devices: 13.8 us -> 9.2 us  [passed_along(): return lax.ppermute(block, axis, route)]
    pallas_call x7 -> x6, Pallas kernels: 36.7 us -> 33.3 us  [call(): pl.pallas_call(functools.partial(staged_kernel, kernel, in_specs, out_spe...]
    unnamed x36 -> x32, local copies, waits for them, and re-layouts: 6.38 us -> 3.5 us
    convert_element_type x0 -> x2, other arithmetic: none -> 1.51 us  [first_halving(): give = (kept[half:].astype(F32) + taken[half:].astype(F32)).astype(BF16)]
    add x0 -> x1, other arithmetic: none -> 1.37 us  [first_halving(): return (kept[:half].astype(F32) + taken[:half].astype(F32), give)]
  transfers between devices with their start and end apart: 21 -> 26, of which waited for: 9 -> 8; matrix products, arithmetic and copies ran while one was open for 0% -> 3% of each run, Pallas kernels for 21% -> 22%
where the time goes in v6:
time: 111 us; the launch traced here: 110 us
  starting transfers between devices  42.7 us (38%)
  Pallas kernels  36.1 us (33%)
  waiting for transfers between devices  22 us (20%)
  local copies, waits for them, and re-layouts  4.87 us (4%)
  other arithmetic  2.87 us (3%)
  between operations  1.67 us (2%)
    pallas_call x6, Pallas kernels, call(): pl.pallas_call(functools.partial(staged_kernel, kernel, in_specs, out_spe...  33.3 us
    ppermute x15, waiting for transfers between devices, exchanged(): lax.ppermute(block, axis, [(i, i ^ distance) for i in range(lax.axis_size...  17.4 us
    all_to_all x3, starting transfers between devices, exchanged_with_all(): return lax.all_to_all(blocks, axis, 0, 0)  17.2 us
    ppermute x15, starting transfers between devices, exchanged(): lax.ppermute(block, axis, [(i, i ^ distance) for i in range(lax.axis_size...  16.4 us
    ppermute x8, starting transfers between devices, passed_along(): return lax.ppermute(block, axis, route)  9.2 us
    all_to_all x3, waiting for transfers between devices, exchanged_with_all(): return lax.all_to_all(blocks, axis, 0, 0)  4.58 us
    unnamed x32, local copies, waits for them, and re-layouts  3.5 us
    pallas_call x7, Pallas kernels, small_call(): pl.pallas_call(kernel, out_shape=tuple(outs), input_output_aliases={first...  2.81 us
  transfers between devices with their start and end apart: 26, of which 8 were waited for; matrix products, arithmetic and copies ran while one was open for 3% of the time, Pallas kernels for 22%

profile of v6, /device:TPU:0, one launch (start us, length us, event | category | flops | bytes accessed | tf_op | source)
XLA Modules:
  0.0 110.2 jit_solution(12118705915821145378)
XLA Ops:
  0.6 0.7 slice.39
  1.3 0.7 broadcast_in_dim.2
  2.0 7.4 %all-to-all-start = ((bf16[16,8,512]{2,1,0:T(8,128)(2,1)}), bf16[16,8,512]{2,1,0:T(8,128)(2,1)S(1)}, u32[]{:S(2)}, u32[]{:S(2)}) async-start(bf16[16,8,512]{2,1,0:T(8,128)(2,1)} %broadcast_in_dim.2), calls=%async_computation | async-start | bytes 262144 | tf_op jit(solution)/shard_map/all_to_all | solution.py:486
  9.4 2.6 %tiles.1 = (bf16[128,512]{1,0:T(8,128)(2,1)}, bf16[128,512]{1,0:T(8,128)(2,1)}, bf16[128,512]{1,0:T(8,128)(2,1)}, bf16[128,512]{1,0:T(8,128)(2,1)}) custom-call(bf16[256,512]{1,0:T(8,128)(2,1)} %refs_1_.6, s32[4,128]{1,0:T(4,128)} %bitcast.8), custom_call_target="tpu_custom_call" | custom-call | bytes 788480 | tf_op jit(solution)/shard_map/tiles/pallas_call | solution.py:447
  12.0 0.5 collective-permute-start
  12.4 1.7 %collective-permute-start.1 = (bf16[128,512]{1,0:T(8,128)(2,1)}, bf16[128,512]{1,0:T(8,128)(2,1)S(1)}, u32[]{:S(2)}, u32[]{:S(2)}) collective-permute-start(bf16[128,512]{1,0:T(8,128)(2,1)} %get-tuple-element.71), channel_id=1, source_target_pairs={{14,0},{15,1},{0,2},{1,3},{2,4},{3,5},{4,6},{5,7},{6,8},{7,9},{8,1... | collective-permute-start | bytes 393224 | tf_op jit(solution)/shard_map/ppermute | solution.py:478
  14.1 4.0 %collective-permute-start.2 = (bf16[128,512]{1,0:T(8,128)(2,1)}, bf16[128,512]{1,0:T(8,128)(2,1)S(1)}, u32[]{:S(2)}, u32[]{:S(2)}) collective-permute-start(bf16[128,512]{1,0:T(8,128)(2,1)} %get-tuple-element.72), channel_id=1, source_target_pairs={{1,0},{2,1},{3,2},{4,3},{5,4},{6,5},{7,6},{8,7},{9,8},{10,9},{11,1... | collective-permute-start | bytes 393224 | tf_op jit(solution)/shard_map/ppermute | solution.py:478
  18.1 0.3 collective-permute-start.3
  18.4 0.7 copy-done.8
  19.0 4.0 %coarse_forward.1 = (bf16[128,512]{1,0:T(8,128)(2,1)}, bf16[16,8,512]{2,1,0:T(8,128)(2,1)}, bf16[128,512]{1,0:T(8,128)(2,1)}, bf16[128,512]{1,0:T(8,128)(2,1)}, ...) custom-call(bf16[16,8,512]{2,1,0:T(8,128)(2,1)} %copy-done.8, ...), custom_call_target="tpu_custom_call" | custom-call | flops 268435456 | bytes 3345408 | tf_op jit(solution)/shard_map/coarse_forward/pallas_call | solution.py:447
  23.0 4.0 %all-to-all-start.1 = ((bf16[16,8,512]{2,1,0:T(8,128)(2,1)}), bf16[16,8,512]{2,1,0:T(8,128)(2,1)S(1)}, u32[]{:S(2)}, u32[]{:S(2)}) async-start(bf16[16,8,512]{2,1,0:T(8,128)(2,1)} %get-tuple-element.75), calls=%async_computation.1 | async-start | bytes 262144 | tf_op jit(solution)/shard_map/all_to_all | solution.py:486
  27.7 0.0 copy-start.12
  27.8 0.0 copy-start.13
  27.8 0.0 copy-start.14
  27.8 0.6 copy-done.12
  28.4 0.0 copy-done.13
  28.4 0.0 copy-done.14
  28.5 0.0 copy-done.15
  28.5 6.7 %fine_forward.1 = (bf16[512,512]{1,0:T(8,128)(2,1)}, f32[256,512]{1,0:T(8,128)}, bf16[512,512]{1,0:T(8,128)(2,1)}, bf16[512,512]{1,0:T(8,128)(2,1)}, bf16[512,51...) custom-call(s32[1]{0:T(128)S(6)} %copy.36.refs_0_, ...), custom_call_target="tpu_custom_call" | custom-call | flops 1879048192 | bytes 7346180 | tf_op jit(solution)/shard_map/fine_forward/pallas_call | solution.py:447
  35.3 0.0 copy-start.10
  35.3 0.6 copy-done.10
  35.9 5.8 %node_both.1 = (bf16[256,512]{1,0:T(8,128)(2,1)}, f32[256,512]{1,0:T(8,128)}, bf16[256,512]{1,0:T(8,128)(2,1)}, bf16[16,8,512]{2,1,0:T(8,128)(2,1)}, bf16[8,96,5...) custom-call(s32[1]{0:T(128)} %bitcast.refs_0_, bf16[256,512]{1,0:T(8,128)(2,1)} %refs_1_.6, ...), custom_call_target="tpu_custom_call" | custom-call | flops 1207959552 | bytes 5507076 | tf_op jit(solution)/shard_map/node_both/pallas_call | solution.py:447
  41.7 0.5 collective-permute-start.4
  42.2 5.8 %all-to-all-start.2 = ((bf16[16,8,512]{2,1,0:T(8,128)(2,1)}), bf16[16,8,512]{2,1,0:T(8,128)(2,1)S(1)}, u32[]{:S(2)}, u32[]{:S(2)}) async-start(bf16[16,8,512]{2,1,0:T(8,128)(2,1)} %get-tuple-element.86), calls=%async_computation.2 | async-start | bytes 262144 | tf_op jit(solution)/shard_map/all_to_all | solution.py:486
  48.0 1.4 %convert_add_fusion = (f32[4,96,512]{2,1,0:T(8,128)S(1)}, bf16[4,96,512]{2,1,0:T(8,128)(2,1)S(1)}) fusion(bf16[8,96,512]{2,1,0:T(8,128)(2,1)S(1)} %collective-permute-done.4, bf16[8,96,512]{2,1,0:T(8,128)(2,1)} %get-tuple-element.97), kind=kLoop, calls=%fused_computation | loop fusion | flops 1376256 | bytes 2752512 | tf_op jit(solution)/shard_map/add | solution.py:492
  49.4 2.0 %collective-permute-start.5 = (bf16[4,96,512]{2,1,0:T(8,128)(2,1)S(1)}, bf16[4,96,512]{2,1,0:T(8,128)(2,1)S(1)}, u32[]{:S(2)}, u32[]{:S(2)}) collective-permute-start(bf16[4,96,512]{2,1,0:T(8,128)(2,1)S(1)} %get-tuple-element.131), channel_id=1, source_target_pairs={{0,2},{1,3},{2,0},{3,1},{4,6},{5,7},{6,4},{7,5},{8,10},{9,11},{10,... | collective-permute-start | bytes 1179656 | tf_op jit(solution)/shard_map/ppermute | solution.py:482
  51.4 4.6 %all-to-all-done.2.refs_16_ = bf16[16,8,512]{2,1,0:T(8,128)(2,1)S(1)} async-done(((bf16[16,8,512]{2,1,0:T(8,128)(2,1)}), bf16[16,8,512]{2,1,0:T(8,128)(2,1)S(1)}, u32[]{:S(2)}, u32[]{:S(2)}) %all-to-all-start.2) | async-done | bytes 131104 | tf_op jit(solution)/shard_map/all_to_all | solution.py:486
  55.9 0.7 copy-done.11
  56.6 8.8 %edge_heads.1 = (bf16[640,512]{1,0:T(8,128)(2,1)}, bf16[640,512]{1,0:T(8,128)(2,1)}, bf16[512,512]{1,0:T(8,128)(2,1)}, bf16[128,512]{1,0:T(8,128)(2,1)}, f32[128...) custom-call(s32[1]{0:T(128)S(6)} %copy.36.refs_0_, ...), custom_call_target="tpu_custom_call" | custom-call | flops 2181038080 | bytes 8592388 | tf_op jit(solution)/shard_map/edge_heads/pallas_call | solution.py:447
  65.5 0.8 copy-done.1
  66.2 5.4 %edge_weights.1 = (bf16[8,96,512]{2,1,0:T(8,128)(2,1)}, bf16[8,96,512]{2,1,0:T(8,128)(2,1)}, bf16[8,48,512]{2,1,0:T(8,128)(2,1)}, bf16[8,48,512]{2,1,0:T(8,128)(2,1)}) custom-call(s32[1]{0:T(128)} %bitcast.refs_0_, bf16[512,512]{1,0:T(8,128)(2,1)} %refs_1_.7, bf16[128,512]{1,0:T(8,128)(2,1)} %refs_2_.1, bf16[640,512]{1,0:T(8,128)(2,1)} %get-tuple-element.88.refs_3_, ...), custom_call_target="tpu_custom_call" | custom-call | flops 1342177280 | bytes 6946820 | tf_op jit(solution)/shard_map/edge_weights/pallas_call | solution.py:447
  71.6 0.1 collective-permute-start.11
  71.7 0.5 collective-permute-start.6
  72.2 2.0 %collective-permute-done.11 = bf16[8,96,512]{2,1,0:T(8,128)(2,1)S(1)} collective-permute-done((bf16[8,96,512]{2,1,0:T(8,128)(2,1)}, bf16[8,96,512]{2,1,0:T(8,128)(2,1)S(1)}, u32[]{:S(2)}, u32[]{:S(2)}) %collective-permute-start.11) | collective-permute-done | bytes 786464 | tf_op jit(solution)/shard_map/ppermute | solution.py:482
  74.2 1.4 %add_convert_fusion = (bf16[4,96,512]{2,1,0:T(8,128)(2,1)S(1)}, f32[4,96,512]{2,1,0:T(8,128)S(1)}) fusion(bf16[8,96,512]{2,1,0:T(8,128)(2,1)S(1)} %collective-permute-done.11, bf16[8,96,512]{2,1,0:T(8,128)(2,1)} %get-tuple-element.106), kind=kLoop, calls=%fused_computation.1 | loop fusion | flops 1376256 | bytes 2752512 | tf_op jit(solution)/shard_map/convert_element_type | solution.py:491
  75.7 0.1 collective-permute-start.12
  75.8 0.1 add_convert_fusion.2
  75.9 2.1 %collective-permute-start.7 = (bf16[4,48,512]{2,1,0:T(8,128)(2,1)S(1)}, bf16[4,48,512]{2,1,0:T(8,128)(2,1)S(1)}, u32[]{:S(2)}, u32[]{:S(2)}) collective-permute-start(bf16[4,48,512]{2,1,0:T(8,128)(2,1)S(1)} %get-tuple-element.134), channel_id=1, source_target_pairs={{0,2},{1,3},{2,0},{3,1},{4,6},{5,7},{6,4},{7,5},{8,10},{9,11},{10,... | collective-permute-start | bytes 589832 | tf_op jit(solution)/shard_map/ppermute | solution.py:482
  77.9 0.1 second_halving.5
  78.0 0.1 collective-permute-start.20
  78.1 1.3 %collective-permute-start.21 = (bf16[96,512]{1,0:T(8,128)(2,1)S(1)}, bf16[96,512]{1,0:T(8,128)(2,1)S(1)}, u32[]{:S(2)}, u32[]{:S(2)}) collective-permute-start(bf16[96,512]{1,0:T(8,128)(2,1)S(1)} %get-tuple-element.126), channel_id=1, source_target_pairs={{0,8},{1,9},{2,10},{3,11},{4,12},{5,13},{6,14},{7,15},{8,0},{9,1},... | collective-permute-start | bytes 294920 | tf_op jit(solution)/shard_map/ppermute | solution.py:482
  79.4 3.1 %collective-permute-start.22 = (bf16[96,512]{1,0:T(8,128)(2,1)S(1)}, bf16[96,512]{1,0:T(8,128)(2,1)S(1)}, u32[]{:S(2)}, u32[]{:S(2)}) collective-permute-start(bf16[96,512]{1,0:T(8,128)(2,1)S(1)} %get-tuple-element.127), channel_id=1, source_target_pairs={{0,12},{1,13},{2,14},{3,15},{4,8},{5,9},{6,10},{7,11},{8,4},{9,5},... | collective-permute-start | bytes 294920 | tf_op jit(solution)/shard_map/ppermute | solution.py:482
  82.5 5.2 %collective-permute-done.12.taken_ref = bf16[4,96,512]{2,1,0:T(8,128)(2,1)S(1)} collective-permute-done((bf16[4,96,512]{2,1,0:T(8,128)(2,1)S(1)}, bf16[4,96,512]{2,1,0:T(8,128)(2,1)S(1)}, u32[]{:S(2)}, u32[]{:S(2)}) %collective-permute-start.12) | collective-permute-done | bytes 393248 | tf_op jit(solution)/shard_map/ppermute | solution.py:482
  87.7 0.0 copy-start.7
  87.7 0.1 second_halving.4
  87.8 0.1 collective-permute-start.17
  87.9 1.3 %collective-permute-start.18 = (bf16[96,512]{1,0:T(8,128)(2,1)S(1)}, bf16[96,512]{1,0:T(8,128)(2,1)S(1)}, u32[]{:S(2)}, u32[]{:S(2)}) collective-permute-start(bf16[96,512]{1,0:T(8,128)(2,1)S(1)} %get-tuple-element.121), channel_id=1, source_target_pairs={{0,8},{1,9},{2,10},{3,11},{4,12},{5,13},{6,14},{7,15},{8,0},{9,1},... | collective-permute-start | bytes 294920 | tf_op jit(solution)/shard_map/ppermute | solution.py:482
  89.2 0.7 collective-permute-start.13
  89.9 1.9 %collective-permute-start.14 = (bf16[128,512]{1,0:T(8,128)(2,1)S(1)}, bf16[128,512]{1,0:T(8,128)(2,1)S(1)}, u32[]{:S(2)}, u32[]{:S(2)}) collective-permute-start(bf16[128,512]{1,0:T(8,128)(2,1)S(1)} %get-tuple-element.113), channel_id=1, source_target_pairs={{2,0},{3,1},{4,2},{5,3},{6,4},{7,5},{8,6},{9,7},{10,8},{11,9},{12,... | collective-permute-start | bytes 393224 | tf_op jit(solution)/shard_map/ppermute | solution.py:478
  91.7 0.7 collective-permute-start.19
  92.4 0.1 collective-permute-done.17.refs_0_
  92.5 0.0 collective-permute-start.15
  92.6 3.1 %collective-permute-done.18.refs_1_ = bf16[96,512]{1,0:T(8,128)(2,1)S(1)} collective-permute-done((bf16[96,512]{1,0:T(8,128)(2,1)S(1)}, bf16[96,512]{1,0:T(8,128)(2,1)S(1)}, u32[]{:S(2)}, u32[]{:S(2)}) %collective-permute-start.18) | collective-permute-done | bytes 98336 | tf_op jit(solution)/shard_map/ppermute | solution.py:482
  95.7 0.2 collective-permute-start.16
  95.9 5.2 %collective-permute-done.19.refs_2_ = bf16[96,512]{1,0:T(8,128)(2,1)S(1)} collective-permute-done((bf16[96,512]{1,0:T(8,128)(2,1)S(1)}, bf16[96,512]{1,0:T(8,128)(2,1)S(1)}, u32[]{:S(2)}, u32[]{:S(2)}) %collective-permute-start.19) | collective-permute-done | bytes 98336 | tf_op jit(solution)/shard_map/ppermute | solution.py:482
  101.1 2.3 %collective-permute-start.10 = (bf16[48,512]{1,0:T(8,128)(2,1)S(1)}, bf16[48,512]{1,0:T(8,128)(2,1)S(1)}, u32[]{:S(2)}, u32[]{:S(2)}) collective-permute-start(bf16[48,512]{1,0:T(8,128)(2,1)S(1)} %get-tuple-element.104), channel_id=1, source_target_pairs={{0,12},{1,13},{2,14},{3,15},{4,8},{5,9},{6,10},{7,11},{8,4},{9,5},... | collective-permute-start | bytes 147464 | tf_op jit(solution)/shard_map/ppermute | solution.py:482
  103.5 1.0 collective-permute-start.8
  104.4 1.4 %collective-permute-start.9 = (bf16[48,512]{1,0:T(8,128)(2,1)S(1)}, bf16[48,512]{1,0:T(8,128)(2,1)S(1)}, u32[]{:S(2)}, u32[]{:S(2)}) collective-permute-start(bf16[48,512]{1,0:T(8,128)(2,1)S(1)} %get-tuple-element.103), channel_id=1, source_target_pairs={{0,8},{1,9},{2,10},{3,11},{4,12},{5,13},{6,14},{7,15},{8,0},{9,1},... | collective-permute-start | bytes 147464 | tf_op jit(solution)/shard_map/ppermute | solution.py:482
  105.8 0.7 last_sum.5
  106.5 0.7 last_sum.4
  107.3 0.4 node_gradient.1.refs_3_
  107.7 0.3 collective-permute-done.8.refs_0_
  108.0 1.4 %collective-permute-done.9.refs_1_ = bf16[48,512]{1,0:T(8,128)(2,1)S(1)} collective-permute-done((bf16[48,512]{1,0:T(8,128)(2,1)S(1)}, bf16[48,512]{1,0:T(8,128)(2,1)S(1)}, u32[]{:S(2)}, u32[]{:S(2)}) %collective-permute-start.9) | collective-permute-done | bytes 49184 | tf_op jit(solution)/shard_map/ppermute | solution.py:482
  109.4 0.8 last_sum.3
  (38 shorter events, 0.1 us)
Async XLA Ops:
  2.0 16.4 %all-to-all-start = ((bf16[16,8,512]{2,1,0:T(8,128)(2,1)}), bf16[16,8,512]{2,1,0:T(8,128)(2,1)S(1)}, u32[]{:S(2)}, u32[]{:S(2)}) async-start(bf16[16,8,512]{2,1,0:T(8,128)(2,1)} %broadcast_in_dim.2), calls=%async_computation | async-start | bytes 262144 | tf_op jit(solution)/shard_map/all_to_all | solution.py:486
  12.0 15.8 %collective-permute-start = (bf16[128,512]{1,0:T(8,128)(2,1)}, bf16[128,512]{1,0:T(8,128)(2,1)S(1)}, u32[]{:S(2)}, u32[]{:S(2)}) collective-permute-start(bf16[128,512]{1,0:T(8,128)(2,1)} %get-tuple-element.70), channel_id=1, source_target_pairs={{15,0},{0,1},{1,2},{2,3},{3,4},{4,5},{5,6},{6,7},{7,8},{8,9},{9,10... | collective-permute-start | bytes 393224 | tf_op jit(solution)/shard_map/ppermute | solution.py:478
  12.4 15.4 %collective-permute-start.1 = (bf16[128,512]{1,0:T(8,128)(2,1)}, bf16[128,512]{1,0:T(8,128)(2,1)S(1)}, u32[]{:S(2)}, u32[]{:S(2)}) collective-permute-start(bf16[128,512]{1,0:T(8,128)(2,1)} %get-tuple-element.71), channel_id=1, source_target_pairs={{14,0},{15,1},{0,2},{1,3},{2,4},{3,5},{4,6},{5,7},{6,8},{7,9},{8,1... | collective-permute-start | bytes 393224 | tf_op jit(solution)/shard_map/ppermute | solution.py:478
  14.1 13.7 %collective-permute-start.2 = (bf16[128,512]{1,0:T(8,128)(2,1)}, bf16[128,512]{1,0:T(8,128)(2,1)S(1)}, u32[]{:S(2)}, u32[]{:S(2)}) collective-permute-start(bf16[128,512]{1,0:T(8,128)(2,1)} %get-tuple-element.72), channel_id=1, source_target_pairs={{1,0},{2,1},{3,2},{4,3},{5,4},{6,5},{7,6},{8,7},{9,8},{10,9},{11,1... | collective-permute-start | bytes 393224 | tf_op jit(solution)/shard_map/ppermute | solution.py:478
  18.1 9.7 %collective-permute-start.3 = (bf16[128,512]{1,0:T(8,128)(2,1)}, bf16[128,512]{1,0:T(8,128)(2,1)S(1)}, u32[]{:S(2)}, u32[]{:S(2)}) collective-permute-start(bf16[128,512]{1,0:T(8,128)(2,1)} %get-tuple-element.73), channel_id=1, source_target_pairs={{2,0},{3,1},{4,2},{5,3},{6,4},{7,5},{8,6},{9,7},{10,8},{11,9},{12,... | collective-permute-start | bytes 393224 | tf_op jit(solution)/shard_map/ppermute | solution.py:478
  18.4 0.7 copy-start.8
  23.0 12.2 %all-to-all-start.1 = ((bf16[16,8,512]{2,1,0:T(8,128)(2,1)}), bf16[16,8,512]{2,1,0:T(8,128)(2,1)S(1)}, u32[]{:S(2)}, u32[]{:S(2)}) async-start(bf16[16,8,512]{2,1,0:T(8,128)(2,1)} %get-tuple-element.75), calls=%async_computation.1 | async-start | bytes 262144 | tf_op jit(solution)/shard_map/all_to_all | solution.py:486
  27.7 0.7 copy-start.12
  27.8 0.7 copy-start.13
  27.8 0.7 copy-start.14
  27.8 0.7 copy-start.15
  35.3 0.7 copy-start.10
  41.7 6.3 %collective-permute-start.4 = (bf16[8,96,512]{2,1,0:T(8,128)(2,1)}, bf16[8,96,512]{2,1,0:T(8,128)(2,1)S(1)}, u32[]{:S(2)}, u32[]{:S(2)}) collective-permute-start(bf16[8,96,512]{2,1,0:T(8,128)(2,1)} %get-tuple-element.98), channel_id=1, source_target_pairs={{0,1},{1,0},{2,3},{3,2},{4,5},{5,4},{6,7},{7,6},{8,9},{9,8},{10,11... | collective-permute-start | bytes 2359304 | tf_op jit(solution)/shard_map/ppermute | solution.py:482
  42.2 13.7 %all-to-all-start.2 = ((bf16[16,8,512]{2,1,0:T(8,128)(2,1)}), bf16[16,8,512]{2,1,0:T(8,128)(2,1)S(1)}, u32[]{:S(2)}, u32[]{:S(2)}) async-start(bf16[16,8,512]{2,1,0:T(8,128)(2,1)} %get-tuple-element.86), calls=%async_computation.2 | async-start | bytes 262144 | tf_op jit(solution)/shard_map/all_to_all | solution.py:486
  49.4 16.1 %collective-permute-start.5 = (bf16[4,96,512]{2,1,0:T(8,128)(2,1)S(1)}, bf16[4,96,512]{2,1,0:T(8,128)(2,1)S(1)}, u32[]{:S(2)}, u32[]{:S(2)}) collective-permute-start(bf16[4,96,512]{2,1,0:T(8,128)(2,1)S(1)} %get-tuple-element.131), channel_id=1, source_target_pairs={{0,2},{1,3},{2,0},{3,1},{4,6},{5,7},{6,4},{7,5},{8,10},{9,11},{10,... | collective-permute-start | bytes 1179656 | tf_op jit(solution)/shard_map/ppermute | solution.py:482
  55.9 0.7 copy-start.11
  65.5 0.8 copy-start.1
  71.6 4.1 %copy-start.9 = (bf16[8,48,512]{2,1,0:T(8,128)(2,1)S(1)}, bf16[8,48,512]{2,1,0:T(8,128)(2,1)}, u32[]{:S(2)}) copy-start(bf16[8,48,512]{2,1,0:T(8,128)(2,1)} %get-tuple-element.99) | copy-start | bytes 1179652
  71.6 2.6 %collective-permute-start.11 = (bf16[8,96,512]{2,1,0:T(8,128)(2,1)}, bf16[8,96,512]{2,1,0:T(8,128)(2,1)S(1)}, u32[]{:S(2)}, u32[]{:S(2)}) collective-permute-start(bf16[8,96,512]{2,1,0:T(8,128)(2,1)} %get-tuple-element.107), channel_id=1, source_target_pairs={{0,1},{1,0},{2,3},{3,2},{4,5},{5,4},{6,7},{7,6},{8,9},{9,8},{10,11... | collective-permute-start | bytes 2359304 | tf_op jit(solution)/shard_map/ppermute | solution.py:482
  71.7 4.0 %collective-permute-start.6 = (bf16[8,48,512]{2,1,0:T(8,128)(2,1)}, bf16[8,48,512]{2,1,0:T(8,128)(2,1)S(1)}, u32[]{:S(2)}, u32[]{:S(2)}) collective-permute-start(bf16[8,48,512]{2,1,0:T(8,128)(2,1)} %get-tuple-element.100), channel_id=1, source_target_pairs={{0,1},{1,0},{2,3},{3,2},{4,5},{5,4},{6,7},{7,6},{8,9},{9,8},{10,11... | collective-permute-start | bytes 1179656 | tf_op jit(solution)/shard_map/ppermute | solution.py:482
  74.2 3.7 %copy-start.2 = (bf16[4,96,512]{2,1,0:T(8,128)(2,1)S(1)}, bf16[4,96,512]{2,1,0:T(8,128)(2,1)}, u32[]{:S(2)}) copy-start(bf16[4,96,512]{2,1,0:T(8,128)(2,1)} %copy-done.1) | copy-start | bytes 1179652
  75.6 12.1 %copy-start.3 = (bf16[128,512]{1,0:T(8,128)(2,1)S(1)}, bf16[128,512]{1,0:T(8,128)(2,1)}, u32[]{:S(2)}) copy-start(bf16[128,512]{1,0:T(8,128)(2,1)} %get-tuple-element.108.refs_0_) | copy-start | bytes 393220
  75.6 12.1 %copy-start.4 = (bf16[128,512]{1,0:T(8,128)(2,1)S(1)}, bf16[128,512]{1,0:T(8,128)(2,1)}, u32[]{:S(2)}) copy-start(bf16[128,512]{1,0:T(8,128)(2,1)} %get-tuple-element.109.refs_1_) | copy-start | bytes 393220
  75.6 12.1 %copy-start.5 = (bf16[128,512]{1,0:T(8,128)(2,1)S(1)}, bf16[128,512]{1,0:T(8,128)(2,1)}, u32[]{:S(2)}) copy-start(bf16[128,512]{1,0:T(8,128)(2,1)} %get-tuple-element.110.refs_2_) | copy-start | bytes 393220
  75.7 12.0 %copy-start.6 = (bf16[128,512]{1,0:T(8,128)(2,1)S(1)}, bf16[128,512]{1,0:T(8,128)(2,1)}, u32[]{:S(2)}) copy-start(bf16[128,512]{1,0:T(8,128)(2,1)} %get-tuple-element.111.refs_3_) | copy-start | bytes 393220
  75.7 12.0 %collective-permute-start.12 = (bf16[4,96,512]{2,1,0:T(8,128)(2,1)S(1)}, bf16[4,96,512]{2,1,0:T(8,128)(2,1)S(1)}, u32[]{:S(2)}, u32[]{:S(2)}) collective-permute-start(bf16[4,96,512]{2,1,0:T(8,128)(2,1)S(1)} %get-tuple-element.132), channel_id=1, source_target_pairs={{0,2},{1,3},{2,0},{3,1},{4,6},{5,7},{6,4},{7,5},{8,10},{9,11},{10,... | collective-permute-start | bytes 1179656 | tf_op jit(solution)/shard_map/ppermute | solution.py:482
  75.9 15.9 %collective-permute-start.7 = (bf16[4,48,512]{2,1,0:T(8,128)(2,1)S(1)}, bf16[4,48,512]{2,1,0:T(8,128)(2,1)S(1)}, u32[]{:S(2)}, u32[]{:S(2)}) collective-permute-start(bf16[4,48,512]{2,1,0:T(8,128)(2,1)S(1)} %get-tuple-element.134), channel_id=1, source_target_pairs={{0,2},{1,3},{2,0},{3,1},{4,6},{5,7},{6,4},{7,5},{8,10},{9,11},{10,... | collective-permute-start | bytes 589832 | tf_op jit(solution)/shard_map/ppermute | solution.py:482
  78.0 9.9 %collective-permute-start.20 = (bf16[96,512]{1,0:T(8,128)(2,1)S(1)}, bf16[96,512]{1,0:T(8,128)(2,1)S(1)}, u32[]{:S(2)}, u32[]{:S(2)}) collective-permute-start(bf16[96,512]{1,0:T(8,128)(2,1)S(1)} %get-tuple-element.125), channel_id=1, source_target_pairs={{0,4},{1,5},{2,6},{3,7},{4,0},{5,1},{6,2},{7,3},{8,12},{9,13},{10,... | collective-permute-start | bytes 294920 | tf_op jit(solution)/shard_map/ppermute | solution.py:482
  78.1 11.1 %collective-permute-start.21 = (bf16[96,512]{1,0:T(8,128)(2,1)S(1)}, bf16[96,512]{1,0:T(8,128)(2,1)S(1)}, u32[]{:S(2)}, u32[]{:S(2)}) collective-permute-start(bf16[96,512]{1,0:T(8,128)(2,1)S(1)} %get-tuple-element.126), channel_id=1, source_target_pairs={{0,8},{1,9},{2,10},{3,11},{4,12},{5,13},{6,14},{7,15},{8,0},{9,1},... | collective-permute-start | bytes 294920 | tf_op jit(solution)/shard_map/ppermute | solution.py:482
  79.4 10.5 %collective-permute-start.22 = (bf16[96,512]{1,0:T(8,128)(2,1)S(1)}, bf16[96,512]{1,0:T(8,128)(2,1)S(1)}, u32[]{:S(2)}, u32[]{:S(2)}) collective-permute-start(bf16[96,512]{1,0:T(8,128)(2,1)S(1)} %get-tuple-element.127), channel_id=1, source_target_pairs={{0,12},{1,13},{2,14},{3,15},{4,8},{5,9},{6,10},{7,11},{8,4},{9,5},... | collective-permute-start | bytes 294920 | tf_op jit(solution)/shard_map/ppermute | solution.py:482
  87.7 19.6 %copy-start = (f32[256,512]{1,0:T(8,128)S(1)}, f32[256,512]{1,0:T(8,128)}, u32[]{:S(2)}) copy-start(f32[256,512]{1,0:T(8,128)} %get-tuple-element.105.own_ref) | copy-start | bytes 1572868
  87.7 19.6 %copy-start.7 = (s32[1,4,128]{2,1,0:T(4,128)S(1)}, s32[1,4,128]{2,1,0:T(4,128)}, u32[]{:S(2)}) copy-start(s32[1,4,128]{2,1,0:T(4,128)} %param.25) | copy-start | bytes 6148
  87.8 4.7 %collective-permute-start.17 = (bf16[96,512]{1,0:T(8,128)(2,1)S(1)}, bf16[96,512]{1,0:T(8,128)(2,1)S(1)}, u32[]{:S(2)}, u32[]{:S(2)}) collective-permute-start(bf16[96,512]{1,0:T(8,128)(2,1)S(1)} %get-tuple-element.120), channel_id=1, source_target_pairs={{0,4},{1,5},{2,6},{3,7},{4,0},{5,1},{6,2},{7,3},{8,12},{9,13},{10,... | collective-permute-start | bytes 294920 | tf_op jit(solution)/shard_map/ppermute | solution.py:482
  87.9 7.8 %collective-permute-start.18 = (bf16[96,512]{1,0:T(8,128)(2,1)S(1)}, bf16[96,512]{1,0:T(8,128)(2,1)S(1)}, u32[]{:S(2)}, u32[]{:S(2)}) collective-permute-start(bf16[96,512]{1,0:T(8,128)(2,1)S(1)} %get-tuple-element.121), channel_id=1, source_target_pairs={{0,8},{1,9},{2,10},{3,11},{4,12},{5,13},{6,14},{7,15},{8,0},{9,1},... | collective-permute-start | bytes 294920 | tf_op jit(solution)/shard_map/ppermute | solution.py:482
  89.2 14.3 %collective-permute-start.13 = (bf16[128,512]{1,0:T(8,128)(2,1)S(1)}, bf16[128,512]{1,0:T(8,128)(2,1)S(1)}, u32[]{:S(2)}, u32[]{:S(2)}) collective-permute-start(bf16[128,512]{1,0:T(8,128)(2,1)S(1)} %get-tuple-element.112), channel_id=1, source_target_pairs={{1,0},{2,1},{3,2},{4,3},{5,4},{6,5},{7,6},{8,7},{9,8},{10,9},{11,1... | collective-permute-start | bytes 393224 | tf_op jit(solution)/shard_map/ppermute | solution.py:478
  89.9 14.6 %collective-permute-start.14 = (bf16[128,512]{1,0:T(8,128)(2,1)S(1)}, bf16[128,512]{1,0:T(8,128)(2,1)S(1)}, u32[]{:S(2)}, u32[]{:S(2)}) collective-permute-start(bf16[128,512]{1,0:T(8,128)(2,1)S(1)} %get-tuple-element.113), channel_id=1, source_target_pairs={{2,0},{3,1},{4,2},{5,3},{6,4},{7,5},{8,6},{9,7},{10,8},{11,9},{12,... | collective-permute-start | bytes 393224 | tf_op jit(solution)/shard_map/ppermute | solution.py:478
  91.7 9.4 %collective-permute-start.19 = (bf16[96,512]{1,0:T(8,128)(2,1)S(1)}, bf16[96,512]{1,0:T(8,128)(2,1)S(1)}, u32[]{:S(2)}, u32[]{:S(2)}) collective-permute-start(bf16[96,512]{1,0:T(8,128)(2,1)S(1)} %get-tuple-element.122), channel_id=1, source_target_pairs={{0,12},{1,13},{2,14},{3,15},{4,8},{5,9},{6,10},{7,11},{8,4},{9,5},... | collective-permute-start | bytes 294920 | tf_op jit(solution)/shard_map/ppermute | solution.py:482
  92.5 14.7 %collective-permute-start.15 = (bf16[128,512]{1,0:T(8,128)(2,1)S(1)}, bf16[128,512]{1,0:T(8,128)(2,1)S(1)}, u32[]{:S(2)}, u32[]{:S(2)}) collective-permute-start(bf16[128,512]{1,0:T(8,128)(2,1)S(1)} %get-tuple-element.114), channel_id=1, source_target_pairs={{15,0},{0,1},{1,2},{2,3},{3,4},{4,5},{5,6},{6,7},{7,8},{8,9},{9,10... | collective-permute-start | bytes 393224 | tf_op jit(solution)/shard_map/ppermute | solution.py:478
  95.7 11.6 %collective-permute-start.16 = (bf16[128,512]{1,0:T(8,128)(2,1)S(1)}, bf16[128,512]{1,0:T(8,128)(2,1)S(1)}, u32[]{:S(2)}, u32[]{:S(2)}) collective-permute-start(bf16[128,512]{1,0:T(8,128)(2,1)S(1)} %get-tuple-element.115), channel_id=1, source_target_pairs={{14,0},{15,1},{0,2},{1,3},{2,4},{3,5},{4,6},{5,7},{6,8},{7,9},{8,1... | collective-permute-start | bytes 393224 | tf_op jit(solution)/shard_map/ppermute | solution.py:478
  101.1 6.6 %collective-permute-start.10 = (bf16[48,512]{1,0:T(8,128)(2,1)S(1)}, bf16[48,512]{1,0:T(8,128)(2,1)S(1)}, u32[]{:S(2)}, u32[]{:S(2)}) collective-permute-start(bf16[48,512]{1,0:T(8,128)(2,1)S(1)} %get-tuple-element.104), channel_id=1, source_target_pairs={{0,12},{1,13},{2,14},{3,15},{4,8},{5,9},{6,10},{7,11},{8,4},{9,5},... | collective-permute-start | bytes 147464 | tf_op jit(solution)/shard_map/ppermute | solution.py:482
  103.5 4.5 %collective-permute-start.8 = (bf16[48,512]{1,0:T(8,128)(2,1)S(1)}, bf16[48,512]{1,0:T(8,128)(2,1)S(1)}, u32[]{:S(2)}, u32[]{:S(2)}) collective-permute-start(bf16[48,512]{1,0:T(8,128)(2,1)S(1)} %get-tuple-element.102), channel_id=1, source_target_pairs={{0,4},{1,5},{2,6},{3,7},{4,0},{5,1},{6,2},{7,3},{8,12},{9,13},{10,... | collective-permute-start | bytes 147464 | tf_op jit(solution)/shard_map/ppermute | solution.py:482
  104.4 5.0 %collective-permute-start.9 = (bf16[48,512]{1,0:T(8,128)(2,1)S(1)}, bf16[48,512]{1,0:T(8,128)(2,1)S(1)}, u32[]{:S(2)}, u32[]{:S(2)}) collective-permute-start(bf16[48,512]{1,0:T(8,128)(2,1)S(1)} %get-tuple-element.103), channel_id=1, source_target_pairs={{0,8},{1,9},{2,10},{3,11},{4,12},{5,13},{6,14},{7,15},{8,0},{9,1},... | collective-permute-start | bytes 147464 | tf_op jit(solution)/shard_map/ppermute | solution.py:482

commit v7 on v4

--- a/solution.py
+++ b/solution.py
@@ -38,13 +38,14 @@
     return jnp.where(row == index, 1.0, 0.0).astype(BF16)
 
 
-def pick(hot, table):
-    return mm_tn(hot, table)
-
-
-def pick_wide(hot, table):
-    high, low = halves(table)
-    return mm_tn(hot, high) + mm_tn(hot, low)
+def pick(index, table):
+    entries = index.shape[1]
+    column = jnp.transpose(jnp.broadcast_to(index, (128, entries)))
+    lane = lax.broadcasted_iota(jnp.int32, (entries, 128), 1)
+    parts = []
+    for start in range(0, table.shape[0], 128):
+        parts.append(jnp.where(column == lane + start, 1.0, 0.0).astype(BF16))
+    return mm(jnp.concatenate(parts, 1), table)
 
 
 def put_wide(hot, rows):
@@ -76,15 +77,10 @@
 
 
 def tiles_kernel(nodes_ref, halo_ref, *outs):
-    spread_ref = outs[-1]
     nodes = nodes_ref[...]
-    for slot, out in enumerate(outs[:-1]):
-        hot = one_hot(halo_ref[slot : slot + 1, :], nodes.shape[0])
-        out[...] = pick(hot, nodes).astype(BF16)
+    for slot, out in enumerate(outs):
+        out[...] = pick(halo_ref[slot : slot + 1, :], nodes).astype(BF16)
         out.done()
-    rows = nodes_ref[0:16, :].astype(F32)[:COARSE_DEV].astype(BF16)
-    for peer in range(spread_ref.shape[0]):
-        spread_ref[peer] = rows
 
 
 def gathered(ref):
@@ -98,11 +94,10 @@
 ):
     width = edges_ref.shape[1]
     table = gathered(all_ref).astype(BF16)
-    hot_s = one_hot(send_ref[...], table.shape[0])
     hot_r = one_hot(recv_ref[...], table.shape[0])
     edges = edges_ref[...]
-    zs = pick(hot_s, table).astype(BF16)
-    zr = pick(hot_r, table).astype(BF16)
+    zs = pick(send_ref[...], table).astype(BF16)
+    zr = pick(recv_ref[...], table).astype(BF16)
     pre = (
         mm(edges, w1_ref[0:width, :])
         + mm(zs, w1_ref[width : 2 * width, :])
@@ -136,10 +131,9 @@
     for start in range(0, count, block):
         rows = slice(start, start + block)
         edges = edges_ref[rows, :]
-        hot_s = one_hot(send_ref[:, rows], space_ref.shape[0])
         hot_r = one_hot(recv_ref[:, rows], own)
-        zs = pick(hot_s, space_ref[...]).astype(BF16)
-        zr = pick(hot_r, nodes_ref[...]).astype(BF16)
+        zs = pick(send_ref[:, rows], space_ref[...]).astype(BF16)
+        zr = pick(recv_ref[:, rows], nodes_ref[...]).astype(BF16)
         pre = (
             mm(edges, w1_ref[0:width, :])
             + mm(zs, w1_ref[width : 2 * width, :])
@@ -162,19 +156,22 @@
 
 
 def by_distance(me, peers, sums, kept_ref, given_ref):
+    quarter = peers // 4
     for r in list(range(1, peers, 2)) + list(range(0, peers, 2)):
         if r == 0:
             given_ref.done()
         to = jnp.bitwise_xor(me, r)
         out = given_ref if r % 2 else kept_ref
+        slot = (r // 2 % 2) * quarter + r // 4
         place = 0
         for total in sums:
             rows = total.shape[0] // peers
             part = total[pl.ds(pl.multiple_of(to * rows, 8), rows), :]
             if rows % 16:
                 part = jnp.concatenate([part, jnp.zeros((-rows % 16, part.shape[1]), F32)], 0)
-            out[r // 2, place : place + part.shape[0], :] = part.astype(BF16)
+            out[slot, place : place + part.shape[0], :] = part.astype(BF16)
             place += part.shape[0]
+    kept_ref.done()
 
 
 def node_kernel(
@@ -222,7 +219,7 @@
         hot_r = one_hot(recv_ref[:, rows], own)
         d_edges = d_ref[rows, :].astype(F32)
         place = start + lax.broadcasted_iota(jnp.int32, (block, 1), 0)
-        cotan = jnp.where(place < count_ref[0], d_edges + pick(hot_r, dagg_ref[...]), 0.0)
+        cotan = jnp.where(place < count_ref[0], d_edges + pick(recv_ref[:, rows], dagg_ref[...]), 0.0)
         back_out, back_pre = head_of_backward(
             cotan, w2_ref[...], gain_ref[...], slope_ref[rows, :].astype(F32),
             normed_ref[rows, :].astype(F32), std_ref[rows, 0:1],
@@ -248,43 +245,42 @@
 
 def coarse_backward_kernel(
     me_ref, recv_ref, all_ref, d_ref, gain_ref, std_ref, normed_ref, w2_ref, slope_ref,
-    hidden_ref, out_ref, pre_ref, edges_ref, zs_ref, zr_ref, w1_ref, send_ref,
+    edges_ref, pre_ref, zs_ref, zr_ref, hidden_ref, out_ref, w1_ref, send_ref,
     g_ref, *rest, ordered,
 ):
     if ordered:
-        kept_ref, given_ref, part_ref, g1_ref, g2_ref = rest
+        kept1_ref, given1_ref, kept2_ref, given2_ref, part_ref, g1_ref, g2_ref = rest
     else:
         part_ref, g1_ref, g2_ref = rest
     width = d_ref.shape[1]
     count = hidden_ref.shape[0]
     rows = slice(count - d_ref.shape[0], count)
     table = gathered(all_ref).astype(BF16)
-    hot_r = one_hot(recv_ref[...], table.shape[0])
     d_edges = d_ref[...].astype(F32)
-    cotan = d_edges + pick(hot_r, table)
+    cotan = d_edges + pick(recv_ref[...], table)
     back_out, back_pre = head_of_backward(
         cotan, w2_ref[...], gain_ref[...], slope_ref[...].astype(F32), normed_ref[...].astype(F32), std_ref[:, 0:1]
     )
     out_ref[rows, :] = back_out
     pre_ref[rows, :] = back_pre
-    g2_ref[...] = mm_tn(hidden_ref[...], out_ref[...])
     g1_ref[0:width, :] = mm_tn(edges_ref[...], pre_ref[...])
     g1_ref[width : 2 * width, :] = mm_tn(zs_ref[...], pre_ref[...])
     g1_ref[2 * width : 3 * width, :] = mm_tn(zr_ref[...], pre_ref[...])
+    if ordered:
+        by_distance(me_ref[0], 2 * kept1_ref.shape[0], (g1_ref,), kept1_ref, given1_ref)
+    g2_ref[...] = mm_tn(hidden_ref[...], out_ref[...])
     dz_send = mm_nt(back_pre, w1_ref[width : 2 * width, :]).astype(BF16)
     dz_recv = mm_nt(back_pre, w1_ref[2 * width : 3 * width, :]).astype(BF16)
-    total = mm(one_hot(send_ref[...], table.shape[0]), dz_send) + mm(hot_r, dz_recv)
-    if ordered:
-        part_ref[...] = total
-        by_distance(me_ref[0], 2 * kept_ref.shape[0], (g1_ref, g2_ref, part_ref), kept_ref, given_ref)
-        kept_ref.done()
-    else:
-        part_ref[...] = total.reshape(part_ref.shape).astype(BF16)
+    total = mm(one_hot(send_ref[...], table.shape[0]), dz_send) + mm(one_hot(recv_ref[...], table.shape[0]), dz_recv)
+    part_ref[...] = total.reshape(part_ref.shape).astype(part_ref.dtype)
+    if ordered:
+        by_distance(me_ref[0], 2 * kept2_ref.shape[0], (g2_ref, part_ref), kept2_ref, given2_ref)
     g_ref[...] = (d_edges + mm_nt(back_pre, w1_ref[0:width, :])).astype(BF16)
 
 
 def node_gradient_kernel(own_ref, halo_ref, *refs, slots):
-    piece_refs, out_ref = refs[:slots], refs[len(refs) - 1 - (len(refs) - 1 - slots) // 2]
+    passing = (len(refs) - slots - 1) // 2
+    piece_refs, out_ref = refs[:slots], refs[slots + passing]
     arrived = None
     for slot, piece in enumerate(piece_refs):
         part = mm(one_hot(halo_ref[slot : slot + 1, :], own_ref.shape[0]), piece[...])
@@ -297,15 +293,6 @@
     first = total_ref[0:16, :] + jnp.concatenate([share, jnp.zeros_like(share)], 0)
     g_ref[...] = total_ref[...].astype(BF16)
     g_ref[0:16, :] = first.astype(BF16)
-
-
-def first_halving_kernel(kept_ref, taken_ref, *refs):
-    passing = (len(refs) - 2) // 2
-    keep_ref, give_ref = refs[passing : passing + 2]
-    for j in range(kept_ref.shape[0]):
-        total = (kept_ref[j].astype(F32) + taken_ref[j].astype(F32)).astype(BF16)
-        out = give_ref if j % 2 else keep_ref
-        out[j // 2] = total
 
 
 def second_halving_kernel(kept_ref, taken_ref, *refs, passing):
@@ -318,21 +305,27 @@
             keep_ref[...] = total
 
 
-def last_sum_kernel(kept_ref, *refs, taken, with_nodes, passing):
-    total = kept_ref[...]
-    for ref in refs[:taken]:
-        total = total + ref[...].astype(F32)
+def last_sum_kernel(*refs, counts, sizes, with_nodes):
+    place = 0
+    totals = []
+    for count in counts:
+        total = refs[place][...]
+        for ref in refs[place + 1 : place + count]:
+            total = total + ref[...].astype(F32)
+        totals.append(total)
+        place += count
     if with_nodes:
-        nodes_ref, first_ref, second_ref, g_ref = refs[taken:]
-    else:
-        first_ref, second_ref = refs[taken + passing : len(refs) - passing]
-    cut = first_ref.shape[0]
-    end = cut + second_ref.shape[0]
-    first_ref[...] = total[:cut]
-    second_ref[...] = total[cut:end]
+        nodes_ref, g_ref = refs[place], refs[-1]
+        place += 1
+    for total, rows in zip(totals, sizes):
+        start = 0
+        for count in rows:
+            refs[place][...] = total[start : start + count]
+            start += count
+            place += 1
     if with_nodes:
         g_ref[...] = nodes_ref[...].astype(BF16)
-        g_ref[0:16, :] = (nodes_ref[0:16, :] + total[end : end + 16]).astype(BF16)
+        g_ref[0:16, :] = (nodes_ref[0:16, :] + totals[-1][start : start + 16]).astype(BF16)
 
 
 VM = pl.BlockSpec(memory_space=pltpu.VMEM)
@@ -504,9 +497,10 @@
     return lax.all_to_all(blocks, axis, 0, 0)
 
 
-def first_halving(kept, taken, passing=()):
-    half = shape((kept.shape[0] // 2,) + kept.shape[1:], BF16)
-    return small_call(first_halving_kernel, "first_halving", (kept, taken), [half, half], passing)
+def first_halving(kept, taken):
+    half = kept.shape[0] // 2
+    give = (kept[half:].astype(F32) + taken[half:].astype(F32)).astype(BF16)
+    return kept[:half].astype(F32) + taken[:half].astype(F32), give
 
 
 def second_halving(kept, taken, passing=()):
@@ -516,17 +510,18 @@
     return small_call(kernel, "second_halving", (kept, taken), outs, passing)
 
 
-def last_sum(kept, taken, first_rows, second_rows, nodes=None, passing=()):
-    width = kept.shape[1]
-    outs = [shape((first_rows, width), F32), shape((second_rows, width), F32)]
-    ins = (kept, *taken)
+def last_sum(groups, sizes, nodes=None):
+    ins, outs = [], []
+    for (kept, taken), rows in zip(groups, sizes):
+        ins += [kept, *taken]
+        outs += [shape((count, kept.shape[1]), F32) for count in rows]
     if nodes is not None:
+        ins.append(nodes)
         outs.append(shape(nodes.shape, BF16))
-        ins += (nodes,)
     kernel = functools.partial(
-        last_sum_kernel, taken=len(taken), with_nodes=nodes is not None, passing=len(passing)
-    )
-    return small_call(kernel, "last_sum", ins, outs, passing)
+        last_sum_kernel, counts=[1 + len(taken) for _, taken in groups], sizes=sizes, with_nodes=nodes is not None
+    )
+    return small_call(kernel, "last_sum", ins, outs)
 
 
 def local(
@@ -569,10 +564,10 @@
 
     made = call(
         tiles_kernel, "tiles", (nodes, halo), [VM, VM],
-        [shape((tile, width), BF16)] * slots + [every],
+        [shape((tile, width), BF16)] * slots,
     )
     received = [passed_along(made[slot], axis, offset) for slot, offset in enumerate(offsets)]
-    coarse_all = exchanged_with_all(made[-1], axis)
+    coarse_all = exchanged_with_all(jnp.broadcast_to(nodes[:COARSE_DEV][None], every.shape), axis)
 
     def saved_shapes(rows):
         return [
@@ -617,10 +612,13 @@
     dagg_all = exchanged_with_all(dagg_spread, axis)
     if ordered:
         node_taken = exchanged(node_parts[1], axis, 1)
-        node_kept, node_given, base = first_halving(node_parts[0], node_taken, (base,))
-        node_taken = exchanged(node_given, axis, 2)
+        node_kept, node_given = first_halving(node_parts[0], node_taken)
 
     sum_shapes, sum_scratch = weight_shapes(edge_w1, edge_w2, 16)
+    if ordered:
+        cut = edge_w1.shape[0] // peers
+        rows = sum_shapes[0].shape[1] - cut
+        sum_shapes = [shape((peers // 2, cut, width), BF16)] * 2 + [shape((peers // 2, rows, width), BF16)] * 2
     f_zs, f_zr, f_hidden, f_slope, f_normed, f_std = fine_saved
     c_zs, c_zr, c_hidden, c_slope, c_normed, c_std = coarse_saved
     fine_out, fine_pre, g_fine, own_grad, *pieces = call(
@@ -632,17 +630,18 @@
         flops=2 * fine * width * (4 * width + space_rows + 2 * own),
     )
     returned = [passed_along(pieces[slot], axis, -offset) for slot, offset in enumerate(offsets)]
-
+    if ordered:
+        node_taken = exchanged(node_given, axis, 2)
     pair = [Rows(joined=2), None]
     more = [Rows(extra=coarse)]
     order = (node_taken,) if ordered else ()
     g_coarse, *edge_parts = call(
         functools.partial(coarse_backward_kernel, ordered=ordered), "coarse_backward",
         (
-            me, cr, dagg_all, d_coarse, eg, c_std, c_normed, edge_w2, c_slope, f_hidden, c_hidden,
-            fine_out, fine_pre, fine_edges, coarse_edges, f_zs, c_zs, f_zr, c_zr, edge_w1, cs, *order,
+            me, cr, dagg_all, d_coarse, eg, c_std, c_normed, edge_w2, c_slope, fine_edges, coarse_edges,
+            fine_pre, f_zs, c_zs, f_zr, c_zr, f_hidden, c_hidden, fine_out, edge_w1, cs, *order,
         ),
-        [SM] + [VM] * 8 + pair + more * 2 + pair * 3 + [Rows(3), VM] + [None] * len(order),
+        [SM] + [VM] * 8 + pair + more + pair * 3 + more + [Rows(3), VM] + [None] * len(order),
         [shape((coarse, width), BF16)] + ([] if ordered else [every]) + sum_shapes,
         scratch=([pltpu.VMEM((peers * COARSE_DEV, width), F32)] if ordered else []) + sum_scratch,
         flops=2 * width * width * (4 * fine + 12 * coarse),
@@ -658,19 +657,25 @@
         )
 
     if ordered:
-        edge_kept, edge_given = edge_parts
-        edge_taken = exchanged(edge_given, axis, 1)
-        total, edge_kept = returned_tiles((edge_kept,))
-        node_kept, *given, edge_kept = second_halving(node_kept, node_taken, (edge_kept,))
-        node_taken = [exchanged(part, axis, 4 * (k + 1)) for k, part in enumerate(given)]
-        edge_kept, edge_given = first_halving(edge_kept, edge_taken)
-        edge_taken = exchanged(edge_given, axis, 2)
-        g_nw1, g_nw2, edge_kept = last_sum(
-            node_kept, node_taken, rows_of(node_w1), rows_of(node_w2), passing=(edge_kept,)
+
+        def along_z(given):
+            return [exchanged(part, axis, 4 * (k + 1)) for k, part in enumerate(given)]
+
+        kept1, given1, kept2, given2 = edge_parts
+        total, given1 = returned_tiles((given1,))
+        taken1 = exchanged(given1, axis, 1)
+        taken2 = exchanged(given2, axis, 1)
+        kept1, given1 = first_halving(kept1, taken1)
+        taken1 = exchanged(given1, axis, 2)
+        kept2, given2 = first_halving(kept2, taken2)
+        taken2 = exchanged(given2, axis, 2)
+        node_kept, *given = second_halving(node_kept, node_taken)
+        g_nw1, g_nw2 = last_sum([(node_kept, along_z(given))], [(rows_of(node_w1), rows_of(node_w2))])
+        kept1, *given1 = second_halving(kept1, taken1)
+        kept2, *given2 = second_halving(kept2, taken2)
+        g_ew1, g_ew2, g_nodes = last_sum(
+            [(kept1, along_z(given1)), (kept2, along_z(given2))], [(rows_of(edge_w1),), (rows_of(edge_w2),)], total
         )
-        edge_kept, *given = second_halving(edge_kept, edge_taken)
-        edge_taken = [exchanged(part, axis, 4 * (k + 1)) for k, part in enumerate(given)]
-        g_ew1, g_ew2, g_nodes = last_sum(edge_kept, edge_taken, rows_of(edge_w1), rows_of(edge_w2), total)
     else:
         coarse_share = exchanged_with_all(edge_parts[0], axis)
         (g_nodes,) = small_call(
@@ -678,7 +683,7 @@
             [shape((own, width), BF16)],
         )
         g_nw1, g_nw2, g_ew1, g_ew2 = [
-            lax.psum_scatter(g, axis, scatter_dimension=0, tiled=True) for g in node_parts + edge_parts[1:]
+            lax.psum_scatter(g, axis, scatter_dimension=0, tiled=True) for g in [*node_parts, *edge_parts[1:]]
         ]
     return (new_nodes, new_fine, new_coarse, g_nodes, g_fine, g_coarse, g_ew1, g_ew2, g_nw1, g_nw2)
 

time: 122 us -> 112 us (0.918)
  waiting for transfers between devices: 33.7 us -> 21.1 us
  starting transfers between devices: 38.5 us -> 47 us
  local copies, waits for them, and re-layouts: 11.7 us -> 5.33 us
  other arithmetic: 0 us -> 1.62 us
    unnamed x46 -> x30, local copies, waits for them, and re-layouts: 11.7 us -> 3.97 us
    ppermute x8, waiting for transfers between devices: 7.55 us -> 0.11 us  [passed_along(): return lax.ppermute(block, axis, route)]
    ppermute x10 -> x15, starting transfers between devices: 11.2 us -> 18.1 us  [exchanged(): lax.ppermute(block, axis, [(i, i ^ distance) for i in range(lax.axis_size...]
    all_to_all x3, waiting for transfers between devices: 3.58 us -> 0.01 us  [exchanged_with_all(): return lax.all_to_all(blocks, axis, 0, 0)]
    ppermute x10 -> x15, waiting for transfers between devices: 22.6 us -> 21 us  [exchanged(): lax.ppermute(block, axis, [(i, i ^ distance) for i in range(lax.axis_size...]
    add x0 -> x1, other arithmetic: none -> 1.31 us  [first_halving(): return (kept[:half].astype(F32) + taken[:half].astype(F32), give)]
    ppermute x8, starting transfers between devices: 11.7 us -> 12.9 us  [passed_along(): return lax.ppermute(block, axis, route)]
    pallas_call x7 -> x6, Pallas kernels: 2.63 us -> 2.14 us  [small_call(): pl.pallas_call(kernel, out_shape=tuple(outs), input_output_aliases={first...]
  transfers between devices with their start and end apart: 21 -> 26, of which waited for: 12 -> 6; matrix products, arithmetic and copies ran while one was open for 0% -> 0% of each run, Pallas kernels for 15% -> 25%
where the time goes in v7:
time: 112 us; the launch traced here: 111 us
  starting transfers between devices  47 us (42%)
  Pallas kernels  34.4 us (31%)
  waiting for transfers between devices  21.1 us (19%)
  local copies, waits for them, and re-layouts  5.33 us (5%)
  other arithmetic  1.62 us (1%)
  between operations  1.61 us (1%)
    pallas_call x6, Pallas kernels, call(): pl.pallas_call(functools.partial(staged_kernel, kernel, in_specs, out_spe...  32.3 us
    ppermute x15, waiting for transfers between devices, exchanged(): lax.ppermute(block, axis, [(i, i ^ distance) for i in range(lax.axis_size...  21 us
    ppermute x15, starting transfers between devices, exchanged(): lax.ppermute(block, axis, [(i, i ^ distance) for i in range(lax.axis_size...  18.1 us
    all_to_all x3, starting transfers between devices, exchanged_with_all(): return lax.all_to_all(blocks, axis, 0, 0)  16.1 us
    ppermute x8, starting transfers between devices, passed_along(): return lax.ppermute(block, axis, route)  12.9 us
    unnamed x30, local copies, waits for them, and re-layouts  3.97 us
  transfers between devices with their start and end apart: 26, of which 6 were waited for; matrix products, arithmetic and copies ran while one was open for 0% of the time, Pallas kernels for 25%

profile of v7, /device:TPU:0, one launch (start us, length us, event | category | flops | bytes accessed | tf_op | source)
XLA Modules:
  0.0 111.1 jit_solution(12854421328212553108)
XLA Ops:
  0.6 0.7 slice.39
  1.3 0.7 broadcast_in_dim.2
  2.0 7.4 %all-to-all-start = ((bf16[16,8,512]{2,1,0:T(8,128)(2,1)}), bf16[16,8,512]{2,1,0:T(8,128)(2,1)S(1)}, u32[]{:S(2)}, u32[]{:S(2)}) async-start(bf16[16,8,512]{2,1,0:T(8,128)(2,1)} %broadcast_in_dim.2), calls=%async_computation | async-start | bytes 262144 | tf_op jit(solution)/shard_map/all_to_all | solution.py:497
  9.4 2.6 %tiles.1 = (bf16[128,512]{1,0:T(8,128)(2,1)}, bf16[128,512]{1,0:T(8,128)(2,1)}, bf16[128,512]{1,0:T(8,128)(2,1)}, bf16[128,512]{1,0:T(8,128)(2,1)}) custom-call(bf16[256,512]{1,0:T(8,128)(2,1)} %refs_1_.5, s32[4,128]{1,0:T(4,128)} %bitcast.8), custom_call_target="tpu_custom_call" | custom-call | bytes 788480 | tf_op jit(solution)/shard_map/tiles/pallas_call | solution.py:458
  12.0 0.5 collective-permute-start
  12.4 1.7 %collective-permute-start.1 = (bf16[128,512]{1,0:T(8,128)(2,1)}, bf16[128,512]{1,0:T(8,128)(2,1)S(1)}, u32[]{:S(2)}, u32[]{:S(2)}) collective-permute-start(bf16[128,512]{1,0:T(8,128)(2,1)} %get-tuple-element.69), channel_id=1, source_target_pairs={{14,0},{15,1},{0,2},{1,3},{2,4},{3,5},{4,6},{5,7},{6,8},{7,9},{8,1... | collective-permute-start | bytes 393224 | tf_op jit(solution)/shard_map/ppermute | solution.py:489
  14.1 4.0 %collective-permute-start.2 = (bf16[128,512]{1,0:T(8,128)(2,1)}, bf16[128,512]{1,0:T(8,128)(2,1)S(1)}, u32[]{:S(2)}, u32[]{:S(2)}) collective-permute-start(bf16[128,512]{1,0:T(8,128)(2,1)} %get-tuple-element.70), channel_id=1, source_target_pairs={{1,0},{2,1},{3,2},{4,3},{5,4},{6,5},{7,6},{8,7},{9,8},{10,9},{11,1... | collective-permute-start | bytes 393224 | tf_op jit(solution)/shard_map/ppermute | solution.py:489
  18.1 0.3 collective-permute-start.3
  18.4 0.7 copy-done.6
  19.0 4.0 %coarse_forward.1 = (bf16[128,512]{1,0:T(8,128)(2,1)}, bf16[16,8,512]{2,1,0:T(8,128)(2,1)}, bf16[128,512]{1,0:T(8,128)(2,1)}, bf16[128,512]{1,0:T(8,128)(2,1)}, ...) custom-call(bf16[16,8,512]{2,1,0:T(8,128)(2,1)} %copy-done.6, ...), custom_call_target="tpu_custom_call" | custom-call | flops 268435456 | bytes 3345408 | tf_op jit(solution)/shard_map/coarse_forward/pallas_call | solution.py:458
  23.0 4.0 %all-to-all-start.1 = ((bf16[16,8,512]{2,1,0:T(8,128)(2,1)}), bf16[16,8,512]{2,1,0:T(8,128)(2,1)S(1)}, u32[]{:S(2)}, u32[]{:S(2)}) async-start(bf16[16,8,512]{2,1,0:T(8,128)(2,1)} %get-tuple-element.73), calls=%async_computation.1 | async-start | bytes 262144 | tf_op jit(solution)/shard_map/all_to_all | solution.py:497
  27.7 0.0 collective-permute-done.refs_2_
  27.7 0.0 copy-start.11
  27.8 0.0 collective-permute-done.1.refs_3_
  27.8 0.0 copy-start.12
  27.8 0.0 copy-start.13
  27.8 0.0 collective-permute-done.3.refs_5_
  27.8 0.0 copy-start.14
  27.8 0.6 copy-done.11
  28.4 0.0 copy-done.12
  28.4 0.0 copy-done.13
  28.5 0.0 copy-done.14
  28.5 6.7 %fine_forward.1 = (bf16[512,512]{1,0:T(8,128)(2,1)}, f32[256,512]{1,0:T(8,128)}, bf16[512,512]{1,0:T(8,128)(2,1)}, bf16[512,512]{1,0:T(8,128)(2,1)}, bf16[512,51...) custom-call(s32[1]{0:T(128)S(6)} %copy.30.refs_0_, ...), custom_call_target="tpu_custom_call" | custom-call | flops 1879048192 | bytes 7346180 | tf_op jit(solution)/shard_map/fine_forward/pallas_call | solution.py:458
  35.3 0.0 copy-start.9
  35.3 0.6 copy-done.9
  35.9 5.8 %node_both.1 = (bf16[256,512]{1,0:T(8,128)(2,1)}, f32[256,512]{1,0:T(8,128)}, bf16[256,512]{1,0:T(8,128)(2,1)}, bf16[16,8,512]{2,1,0:T(8,128)(2,1)}, bf16[8,96,5...) custom-call(s32[1]{0:T(128)} %bitcast.refs_0_, bf16[256,512]{1,0:T(8,128)(2,1)} %refs_1_.5, ...), custom_call_target="tpu_custom_call" | custom-call | flops 1207959552 | bytes 5507076 | tf_op jit(solution)/shard_map/node_both/pallas_call | solution.py:458
  41.7 0.5 collective-permute-start.4
  42.2 2.1 %collective-permute-done.4 = bf16[8,96,512]{2,1,0:T(8,128)(2,1)S(1)} collective-permute-done((bf16[8,96,512]{2,1,0:T(8,128)(2,1)}, bf16[8,96,512]{2,1,0:T(8,128)(2,1)S(1)}, u32[]{:S(2)}, u32[]{:S(2)}) %collective-permute-start.4) | collective-permute-done | bytes 786464 | tf_op jit(solution)/shard_map/ppermute | solution.py:493
  44.4 1.3 %convert_add_fusion = (f32[4,96,512]{2,1,0:T(8,128)S(1)}, bf16[4,96,512]{2,1,0:T(8,128)(2,1)S(1)}) fusion(bf16[8,96,512]{2,1,0:T(8,128)(2,1)S(1)} %collective-permute-done.4, bf16[8,96,512]{2,1,0:T(8,128)(2,1)} %get-tuple-element.94), kind=kLoop, calls=%fused_computation | loop fusion | flops 1376256 | bytes 2752512 | tf_op jit(solution)/shard_map/add | solution.py:503
  45.7 1.9 %collective-permute-start.5 = (bf16[4,96,512]{2,1,0:T(8,128)(2,1)S(1)}, bf16[4,96,512]{2,1,0:T(8,128)(2,1)S(1)}, u32[]{:S(2)}, u32[]{:S(2)}) collective-permute-start(bf16[4,96,512]{2,1,0:T(8,128)(2,1)S(1)} %get-tuple-element.127), channel_id=1, source_target_pairs={{0,2},{1,3},{2,0},{3,1},{4,6},{5,7},{6,4},{7,5},{8,10},{9,11},{10,... | collective-permute-start | bytes 1179656 | tf_op jit(solution)/shard_map/ppermute | solution.py:493
  47.6 4.7 %all-to-all-start.2 = ((bf16[16,8,512]{2,1,0:T(8,128)(2,1)}), bf16[16,8,512]{2,1,0:T(8,128)(2,1)S(1)}, u32[]{:S(2)}, u32[]{:S(2)}) async-start(bf16[16,8,512]{2,1,0:T(8,128)(2,1)} %get-tuple-element.77), calls=%async_computation.2 | async-start | bytes 262144 | tf_op jit(solution)/shard_map/all_to_all | solution.py:497
  52.3 6.4 %fine_backward.1 = (bf16[512,512]{1,0:T(8,128)(2,1)}, bf16[512,512]{1,0:T(8,128)(2,1)}, bf16[512,512]{1,0:T(8,128)(2,1)}, f32[256,512]{1,0:T(8,128)}, bf16[128,5...) custom-call(s32[1]{0:T(128)S(6)} %copy.30.refs_0_, ...), custom_call_target="tpu_custom_call" | custom-call | flops 1744830464 | bytes 7346180 | tf_op jit(solution)/shard_map/fine_backward/pallas_call | solution.py:458
  58.7 4.4 %collective-permute-start.6 = (bf16[128,512]{1,0:T(8,128)(2,1)}, bf16[128,512]{1,0:T(8,128)(2,1)S(1)}, u32[]{:S(2)}, u32[]{:S(2)}) collective-permute-start(bf16[128,512]{1,0:T(8,128)(2,1)} %get-tuple-element.98), channel_id=1, source_target_pairs={{1,0},{2,1},{3,2},{4,3},{5,4},{6,5},{7,6},{8,7},{9,8},{10,9},{11,1... | collective-permute-start | bytes 393224 | tf_op jit(solution)/shard_map/ppermute | solution.py:489
  63.1 0.6 collective-permute-start.7
  63.7 1.5 %collective-permute-start.9 = (bf16[128,512]{1,0:T(8,128)(2,1)}, bf16[128,512]{1,0:T(8,128)(2,1)S(1)}, u32[]{:S(2)}, u32[]{:S(2)}) collective-permute-start(bf16[128,512]{1,0:T(8,128)(2,1)} %get-tuple-element.101), channel_id=1, source_target_pairs={{14,0},{15,1},{0,2},{1,3},{2,4},{3,5},{4,6},{5,7},{6,8},{7,9},{8,1... | collective-permute-start | bytes 393224 | tf_op jit(solution)/shard_map/ppermute | solution.py:489
  65.2 0.6 copy-done.8
  65.8 0.1 copy-done.2
  66.0 6.8 %coarse_backward.1 = (bf16[128,512]{1,0:T(8,128)(2,1)}, bf16[8,96,512]{2,1,0:T(8,128)(2,1)}, bf16[8,96,512]{2,1,0:T(8,128)(2,1)}, bf16[8,48,512]{2,1,0:T(8,128)(2,1)}, bf16[8,48,512]{2,1,0:T(8,128)(2,1)}) custom-call(s32[1]{0:T(128)} %bitcast.refs_0_, s32[1,128]{1,0:T(1,128)} %bitcast.17, bf16[16,8,512]{2,1,0:T(8,128)(2,1)} %copy-done.8, ...), custom_call_target="tpu_custom_call" | custom-call | flops 1879048192 | bytes 9243652 | tf_op jit(solution)/shard_map/coarse_backward/pallas_call | solution.py:458
  72.8 0.1 collective-permute-done.9.refs_3_
  72.9 1.1 %copy-done = bf16[8,96,512]{2,1,0:T(8,128)(2,1)S(1)} copy-done((bf16[8,96,512]{2,1,0:T(8,128)(2,1)S(1)}, bf16[8,96,512]{2,1,0:T(8,128)(2,1)}, u32[]{:S(2)}) %copy-start) | copy-done | bytes 786456
  74.1 0.4 node_gradient.1
  74.5 0.7 collective-permute-start.10
  75.3 0.5 collective-permute-start.15
  75.8 1.4 %collective-permute-done.10 = bf16[8,96,512]{2,1,0:T(8,128)(2,1)S(1)} collective-permute-done((bf16[8,96,512]{2,1,0:T(8,128)(2,1)S(1)}, bf16[8,96,512]{2,1,0:T(8,128)(2,1)S(1)}, u32[]{:S(2)}, u32[]{:S(2)}) %collective-permute-start.10) | collective-permute-done | bytes 786464 | tf_op jit(solution)/shard_map/ppermute | solution.py:493
  77.2 0.2 add_convert_fusion
  77.4 0.1 collective-permute-start.11
  77.5 0.3 collective-permute-done.15
  77.7 0.1 add_convert_fusion.2
  77.8 1.8 %collective-permute-start.16 = (bf16[4,48,512]{2,1,0:T(8,128)(2,1)S(1)}, bf16[4,48,512]{2,1,0:T(8,128)(2,1)S(1)}, u32[]{:S(2)}, u32[]{:S(2)}) collective-permute-start(bf16[4,48,512]{2,1,0:T(8,128)(2,1)S(1)} %get-tuple-element.130), channel_id=1, source_target_pairs={{0,2},{1,3},{2,0},{3,1},{4,6},{5,7},{6,4},{7,5},{8,10},{9,11},{10,... | collective-permute-start | bytes 589832 | tf_op jit(solution)/shard_map/ppermute | solution.py:493
  79.7 0.1 second_halving.5
  79.7 0.1 collective-permute-start.20
  79.8 3.4 %collective-permute-start.21 = (bf16[96,512]{1,0:T(8,128)(2,1)S(1)}, bf16[96,512]{1,0:T(8,128)(2,1)S(1)}, u32[]{:S(2)}, u32[]{:S(2)}) collective-permute-start(bf16[96,512]{1,0:T(8,128)(2,1)S(1)} %get-tuple-element.122), channel_id=1, source_target_pairs={{0,8},{1,9},{2,10},{3,11},{4,12},{5,13},{6,14},{7,15},{8,0},{9,1},... | collective-permute-start | bytes 294920 | tf_op jit(solution)/shard_map/ppermute | solution.py:493
  83.3 0.9 collective-permute-start.22
  84.2 8.9 %collective-permute-done.16.taken_ref = bf16[4,48,512]{2,1,0:T(8,128)(2,1)S(1)} collective-permute-done((bf16[4,48,512]{2,1,0:T(8,128)(2,1)S(1)}, bf16[4,48,512]{2,1,0:T(8,128)(2,1)S(1)}, u32[]{:S(2)}, u32[]{:S(2)}) %collective-permute-start.16) | collective-permute-done | bytes 196640 | tf_op jit(solution)/shard_map/ppermute | solution.py:493
  93.1 0.1 collective-permute-start.17
  93.2 0.1 second_halving.3
  93.3 2.1 %collective-permute-start.12 = (bf16[96,512]{1,0:T(8,128)(2,1)S(1)}, bf16[96,512]{1,0:T(8,128)(2,1)S(1)}, u32[]{:S(2)}, u32[]{:S(2)}) collective-permute-start(bf16[96,512]{1,0:T(8,128)(2,1)S(1)} %get-tuple-element.105), channel_id=1, source_target_pairs={{0,4},{1,5},{2,6},{3,7},{4,0},{5,1},{6,2},{7,3},{8,12},{9,13},{10,... | collective-permute-start | bytes 294920 | tf_op jit(solution)/shard_map/ppermute | solution.py:493
  95.3 1.5 %collective-permute-start.13 = (bf16[96,512]{1,0:T(8,128)(2,1)S(1)}, bf16[96,512]{1,0:T(8,128)(2,1)S(1)}, u32[]{:S(2)}, u32[]{:S(2)}) collective-permute-start(bf16[96,512]{1,0:T(8,128)(2,1)S(1)} %get-tuple-element.106), channel_id=1, source_target_pairs={{0,8},{1,9},{2,10},{3,11},{4,12},{5,13},{6,14},{7,15},{8,0},{9,1},... | collective-permute-start | bytes 294920 | tf_op jit(solution)/shard_map/ppermute | solution.py:493
  96.9 1.4 %collective-permute-start.14 = (bf16[96,512]{1,0:T(8,128)(2,1)S(1)}, bf16[96,512]{1,0:T(8,128)(2,1)S(1)}, u32[]{:S(2)}, u32[]{:S(2)}) collective-permute-start(bf16[96,512]{1,0:T(8,128)(2,1)S(1)} %get-tuple-element.107), channel_id=1, source_target_pairs={{0,12},{1,13},{2,14},{3,15},{4,8},{5,9},{6,10},{7,11},{8,4},{9,5},... | collective-permute-start | bytes 294920 | tf_op jit(solution)/shard_map/ppermute | solution.py:493
  98.3 2.0 %collective-permute-start.18 = (bf16[48,512]{1,0:T(8,128)(2,1)S(1)}, bf16[48,512]{1,0:T(8,128)(2,1)S(1)}, u32[]{:S(2)}, u32[]{:S(2)}) collective-permute-start(bf16[48,512]{1,0:T(8,128)(2,1)S(1)} %get-tuple-element.112), channel_id=1, source_target_pairs={{0,8},{1,9},{2,10},{3,11},{4,12},{5,13},{6,14},{7,15},{8,0},{9,1},... | collective-permute-start | bytes 147464 | tf_op jit(solution)/shard_map/ppermute | solution.py:493
  100.3 1.0 collective-permute-start.19
  101.2 0.7 last_sum.3
  101.9 8.3 %collective-permute-done.18.refs_6_ = bf16[48,512]{1,0:T(8,128)(2,1)S(1)} collective-permute-done((bf16[48,512]{1,0:T(8,128)(2,1)S(1)}, bf16[48,512]{1,0:T(8,128)(2,1)S(1)}, u32[]{:S(2)}, u32[]{:S(2)}) %collective-permute-start.18) | collective-permute-done | bytes 49184 | tf_op jit(solution)/shard_map/ppermute | solution.py:493
  110.3 0.9 last_sum.2
  (35 shorter events, 0.1 us)
Async XLA Ops:
  2.0 16.4 %all-to-all-start = ((bf16[16,8,512]{2,1,0:T(8,128)(2,1)}), bf16[16,8,512]{2,1,0:T(8,128)(2,1)S(1)}, u32[]{:S(2)}, u32[]{:S(2)}) async-start(bf16[16,8,512]{2,1,0:T(8,128)(2,1)} %broadcast_in_dim.2), calls=%async_computation | async-start | bytes 262144 | tf_op jit(solution)/shard_map/all_to_all | solution.py:497
  12.0 15.8 %collective-permute-start = (bf16[128,512]{1,0:T(8,128)(2,1)}, bf16[128,512]{1,0:T(8,128)(2,1)S(1)}, u32[]{:S(2)}, u32[]{:S(2)}) collective-permute-start(bf16[128,512]{1,0:T(8,128)(2,1)} %get-tuple-element.68), channel_id=1, source_target_pairs={{15,0},{0,1},{1,2},{2,3},{3,4},{4,5},{5,6},{6,7},{7,8},{8,9},{9,10... | collective-permute-start | bytes 393224 | tf_op jit(solution)/shard_map/ppermute | solution.py:489
  12.4 15.4 %collective-permute-start.1 = (bf16[128,512]{1,0:T(8,128)(2,1)}, bf16[128,512]{1,0:T(8,128)(2,1)S(1)}, u32[]{:S(2)}, u32[]{:S(2)}) collective-permute-start(bf16[128,512]{1,0:T(8,128)(2,1)} %get-tuple-element.69), channel_id=1, source_target_pairs={{14,0},{15,1},{0,2},{1,3},{2,4},{3,5},{4,6},{5,7},{6,8},{7,9},{8,1... | collective-permute-start | bytes 393224 | tf_op jit(solution)/shard_map/ppermute | solution.py:489
  14.1 13.7 %collective-permute-start.2 = (bf16[128,512]{1,0:T(8,128)(2,1)}, bf16[128,512]{1,0:T(8,128)(2,1)S(1)}, u32[]{:S(2)}, u32[]{:S(2)}) collective-permute-start(bf16[128,512]{1,0:T(8,128)(2,1)} %get-tuple-element.70), channel_id=1, source_target_pairs={{1,0},{2,1},{3,2},{4,3},{5,4},{6,5},{7,6},{8,7},{9,8},{10,9},{11,1... | collective-permute-start | bytes 393224 | tf_op jit(solution)/shard_map/ppermute | solution.py:489
  18.1 9.7 %collective-permute-start.3 = (bf16[128,512]{1,0:T(8,128)(2,1)}, bf16[128,512]{1,0:T(8,128)(2,1)S(1)}, u32[]{:S(2)}, u32[]{:S(2)}) collective-permute-start(bf16[128,512]{1,0:T(8,128)(2,1)} %get-tuple-element.71), channel_id=1, source_target_pairs={{2,0},{3,1},{4,2},{5,3},{6,4},{7,5},{8,6},{9,7},{10,8},{11,9},{12,... | collective-permute-start | bytes 393224 | tf_op jit(solution)/shard_map/ppermute | solution.py:489
  18.4 0.7 copy-start.6
  23.0 12.2 %all-to-all-start.1 = ((bf16[16,8,512]{2,1,0:T(8,128)(2,1)}), bf16[16,8,512]{2,1,0:T(8,128)(2,1)S(1)}, u32[]{:S(2)}, u32[]{:S(2)}) async-start(bf16[16,8,512]{2,1,0:T(8,128)(2,1)} %get-tuple-element.73), calls=%async_computation.1 | async-start | bytes 262144 | tf_op jit(solution)/shard_map/all_to_all | solution.py:497
  27.7 0.7 copy-start.11
  27.8 0.7 copy-start.12
  27.8 0.7 copy-start.13
  27.8 0.7 copy-start.14
  35.3 0.7 copy-start.9
  41.7 2.6 %collective-permute-start.4 = (bf16[8,96,512]{2,1,0:T(8,128)(2,1)}, bf16[8,96,512]{2,1,0:T(8,128)(2,1)S(1)}, u32[]{:S(2)}, u32[]{:S(2)}) collective-permute-start(bf16[8,96,512]{2,1,0:T(8,128)(2,1)} %get-tuple-element.95), channel_id=1, source_target_pairs={{0,1},{1,0},{2,3},{3,2},{4,5},{5,4},{6,7},{7,6},{8,9},{9,8},{10,11... | collective-permute-start | bytes 2359304 | tf_op jit(solution)/shard_map/ppermute | solution.py:493
  45.7 19.5 %collective-permute-start.5 = (bf16[4,96,512]{2,1,0:T(8,128)(2,1)S(1)}, bf16[4,96,512]{2,1,0:T(8,128)(2,1)S(1)}, u32[]{:S(2)}, u32[]{:S(2)}) collective-permute-start(bf16[4,96,512]{2,1,0:T(8,128)(2,1)S(1)} %get-tuple-element.127), channel_id=1, source_target_pairs={{0,2},{1,3},{2,0},{3,1},{4,6},{5,7},{6,4},{7,5},{8,10},{9,11},{10,... | collective-permute-start | bytes 1179656 | tf_op jit(solution)/shard_map/ppermute | solution.py:493
  47.6 17.6 %all-to-all-start.2 = ((bf16[16,8,512]{2,1,0:T(8,128)(2,1)}), bf16[16,8,512]{2,1,0:T(8,128)(2,1)S(1)}, u32[]{:S(2)}, u32[]{:S(2)}) async-start(bf16[16,8,512]{2,1,0:T(8,128)(2,1)} %get-tuple-element.77), calls=%async_computation.2 | async-start | bytes 262144 | tf_op jit(solution)/shard_map/all_to_all | solution.py:497
  58.7 14.1 %collective-permute-start.6 = (bf16[128,512]{1,0:T(8,128)(2,1)}, bf16[128,512]{1,0:T(8,128)(2,1)S(1)}, u32[]{:S(2)}, u32[]{:S(2)}) collective-permute-start(bf16[128,512]{1,0:T(8,128)(2,1)} %get-tuple-element.98), channel_id=1, source_target_pairs={{1,0},{2,1},{3,2},{4,3},{5,4},{6,5},{7,6},{8,7},{9,8},{10,9},{11,1... | collective-permute-start | bytes 393224 | tf_op jit(solution)/shard_map/ppermute | solution.py:489
  63.1 9.7 %collective-permute-start.7 = (bf16[128,512]{1,0:T(8,128)(2,1)}, bf16[128,512]{1,0:T(8,128)(2,1)S(1)}, u32[]{:S(2)}, u32[]{:S(2)}) collective-permute-start(bf16[128,512]{1,0:T(8,128)(2,1)} %get-tuple-element.99), channel_id=1, source_target_pairs={{2,0},{3,1},{4,2},{5,3},{6,4},{7,5},{8,6},{9,7},{10,8},{11,9},{12,... | collective-permute-start | bytes 393224 | tf_op jit(solution)/shard_map/ppermute | solution.py:489
  63.7 9.2 %collective-permute-start.8 = (bf16[128,512]{1,0:T(8,128)(2,1)}, bf16[128,512]{1,0:T(8,128)(2,1)S(1)}, u32[]{:S(2)}, u32[]{:S(2)}) collective-permute-start(bf16[128,512]{1,0:T(8,128)(2,1)} %get-tuple-element.100), channel_id=1, source_target_pairs={{15,0},{0,1},{1,2},{2,3},{3,4},{4,5},{5,6},{6,7},{7,8},{8,9},{9,10... | collective-permute-start | bytes 393224 | tf_op jit(solution)/shard_map/ppermute | solution.py:489
  63.7 9.3 %collective-permute-start.9 = (bf16[128,512]{1,0:T(8,128)(2,1)}, bf16[128,512]{1,0:T(8,128)(2,1)S(1)}, u32[]{:S(2)}, u32[]{:S(2)}) collective-permute-start(bf16[128,512]{1,0:T(8,128)(2,1)} %get-tuple-element.101), channel_id=1, source_target_pairs={{14,0},{15,1},{0,2},{1,3},{2,4},{3,5},{4,6},{5,7},{6,8},{7,9},{8,1... | collective-permute-start | bytes 393224 | tf_op jit(solution)/shard_map/ppermute | solution.py:489
  65.2 0.7 copy-start.8
  65.2 0.8 copy-start.2
  66.0 7.0 %copy-start.1 = (f32[256,512]{1,0:T(8,128)S(1)}, f32[256,512]{1,0:T(8,128)}, u32[]{:S(2)}) copy-start(f32[256,512]{1,0:T(8,128)} %get-tuple-element.97.own_ref) | copy-start | bytes 1572868
  66.0 7.0 %copy-start.4 = (s32[1,4,128]{2,1,0:T(4,128)S(1)}, s32[1,4,128]{2,1,0:T(4,128)}, u32[]{:S(2)}) copy-start(s32[1,4,128]{2,1,0:T(4,128)} %param.25) | copy-start | bytes 6148
  72.9 1.1 %copy-start = (bf16[8,96,512]{2,1,0:T(8,128)(2,1)S(1)}, bf16[8,96,512]{2,1,0:T(8,128)(2,1)}, u32[]{:S(2)}) copy-start(bf16[8,96,512]{2,1,0:T(8,128)(2,1)} %get-tuple-element.102.refs_4_) | copy-start | bytes 2359300
  74.1 1.2 %copy-start.10 = (bf16[8,48,512]{2,1,0:T(8,128)(2,1)S(1)}, bf16[8,48,512]{2,1,0:T(8,128)(2,1)}, u32[]{:S(2)}) copy-start(bf16[8,48,512]{2,1,0:T(8,128)(2,1)} %get-tuple-element.109) | copy-start | bytes 1179652
  74.1 3.1 %copy-start.5 = (bf16[8,96,512]{2,1,0:T(8,128)(2,1)S(1)}, bf16[8,96,512]{2,1,0:T(8,128)(2,1)}, u32[]{:S(2)}) copy-start(bf16[8,96,512]{2,1,0:T(8,128)(2,1)} %get-tuple-element.96) | copy-start | bytes 2359300
  74.5 3.2 %copy-start.7 = (bf16[8,48,512]{2,1,0:T(8,128)(2,1)S(1)}, bf16[8,48,512]{2,1,0:T(8,128)(2,1)}, u32[]{:S(2)}) copy-start(bf16[8,48,512]{2,1,0:T(8,128)(2,1)} %get-tuple-element.108) | copy-start | bytes 1179652
  74.5 2.7 %collective-permute-start.10 = (bf16[8,96,512]{2,1,0:T(8,128)(2,1)S(1)}, bf16[8,96,512]{2,1,0:T(8,128)(2,1)S(1)}, u32[]{:S(2)}, u32[]{:S(2)}) collective-permute-start(bf16[8,96,512]{2,1,0:T(8,128)(2,1)S(1)} %get-tuple-element.103), channel_id=1, source_target_pairs={{0,1},{1,0},{2,3},{3,2},{4,5},{5,4},{6,7},{7,6},{8,9},{9,8},{10,11... | collective-permute-start | bytes 2359304 | tf_op jit(solution)/shard_map/ppermute | solution.py:493
  75.3 2.5 %collective-permute-start.15 = (bf16[8,48,512]{2,1,0:T(8,128)(2,1)S(1)}, bf16[8,48,512]{2,1,0:T(8,128)(2,1)S(1)}, u32[]{:S(2)}, u32[]{:S(2)}) collective-permute-start(bf16[8,48,512]{2,1,0:T(8,128)(2,1)S(1)} %copy-done.10), channel_id=1, source_target_pairs={{0,1},{1,0},{2,3},{3,2},{4,5},{5,4},{6,7},{7,6},{8,9},{9,8},{10,11... | collective-permute-start | bytes 1179656 | tf_op jit(solution)/shard_map/ppermute | solution.py:493
  77.2 2.5 %copy-start.3 = (bf16[4,96,512]{2,1,0:T(8,128)(2,1)S(1)}, bf16[4,96,512]{2,1,0:T(8,128)(2,1)}, u32[]{:S(2)}) copy-start(bf16[4,96,512]{2,1,0:T(8,128)(2,1)} %copy-done.2) | copy-start | bytes 1179652
  77.4 15.8 %collective-permute-start.11 = (bf16[4,96,512]{2,1,0:T(8,128)(2,1)S(1)}, bf16[4,96,512]{2,1,0:T(8,128)(2,1)S(1)}, u32[]{:S(2)}, u32[]{:S(2)}) collective-permute-start(bf16[4,96,512]{2,1,0:T(8,128)(2,1)S(1)} %get-tuple-element.128), channel_id=1, source_target_pairs={{0,2},{1,3},{2,0},{3,1},{4,6},{5,7},{6,4},{7,5},{8,10},{9,11},{10,... | collective-permute-start | bytes 1179656 | tf_op jit(solution)/shard_map/ppermute | solution.py:493
  77.8 15.2 %collective-permute-start.16 = (bf16[4,48,512]{2,1,0:T(8,128)(2,1)S(1)}, bf16[4,48,512]{2,1,0:T(8,128)(2,1)S(1)}, u32[]{:S(2)}, u32[]{:S(2)}) collective-permute-start(bf16[4,48,512]{2,1,0:T(8,128)(2,1)S(1)} %get-tuple-element.130), channel_id=1, source_target_pairs={{0,2},{1,3},{2,0},{3,1},{4,6},{5,7},{6,4},{7,5},{8,10},{9,11},{10,... | collective-permute-start | bytes 589832 | tf_op jit(solution)/shard_map/ppermute | solution.py:493
  79.7 15.6 %collective-permute-start.20 = (bf16[96,512]{1,0:T(8,128)(2,1)S(1)}, bf16[96,512]{1,0:T(8,128)(2,1)S(1)}, u32[]{:S(2)}, u32[]{:S(2)}) collective-permute-start(bf16[96,512]{1,0:T(8,128)(2,1)S(1)} %get-tuple-element.121), channel_id=1, source_target_pairs={{0,4},{1,5},{2,6},{3,7},{4,0},{5,1},{6,2},{7,3},{8,12},{9,13},{10,... | collective-permute-start | bytes 294920 | tf_op jit(solution)/shard_map/ppermute | solution.py:493
  79.8 17.0 %collective-permute-start.21 = (bf16[96,512]{1,0:T(8,128)(2,1)S(1)}, bf16[96,512]{1,0:T(8,128)(2,1)S(1)}, u32[]{:S(2)}, u32[]{:S(2)}) collective-permute-start(bf16[96,512]{1,0:T(8,128)(2,1)S(1)} %get-tuple-element.122), channel_id=1, source_target_pairs={{0,8},{1,9},{2,10},{3,11},{4,12},{5,13},{6,14},{7,15},{8,0},{9,1},... | collective-permute-start | bytes 294920 | tf_op jit(solution)/shard_map/ppermute | solution.py:493
  83.3 15.0 %collective-permute-start.22 = (bf16[96,512]{1,0:T(8,128)(2,1)S(1)}, bf16[96,512]{1,0:T(8,128)(2,1)S(1)}, u32[]{:S(2)}, u32[]{:S(2)}) collective-permute-start(bf16[96,512]{1,0:T(8,128)(2,1)S(1)} %get-tuple-element.123), channel_id=1, source_target_pairs={{0,12},{1,13},{2,14},{3,15},{4,8},{5,9},{6,10},{7,11},{8,4},{9,5},... | collective-permute-start | bytes 294920 | tf_op jit(solution)/shard_map/ppermute | solution.py:493
  93.1 7.2 %collective-permute-start.17 = (bf16[48,512]{1,0:T(8,128)(2,1)S(1)}, bf16[48,512]{1,0:T(8,128)(2,1)S(1)}, u32[]{:S(2)}, u32[]{:S(2)}) collective-permute-start(bf16[48,512]{1,0:T(8,128)(2,1)S(1)} %get-tuple-element.111), channel_id=1, source_target_pairs={{0,4},{1,5},{2,6},{3,7},{4,0},{5,1},{6,2},{7,3},{8,12},{9,13},{10,... | collective-permute-start | bytes 147464 | tf_op jit(solution)/shard_map/ppermute | solution.py:493
  93.3 17.0 %collective-permute-start.12 = (bf16[96,512]{1,0:T(8,128)(2,1)S(1)}, bf16[96,512]{1,0:T(8,128)(2,1)S(1)}, u32[]{:S(2)}, u32[]{:S(2)}) collective-permute-start(bf16[96,512]{1,0:T(8,128)(2,1)S(1)} %get-tuple-element.105), channel_id=1, source_target_pairs={{0,4},{1,5},{2,6},{3,7},{4,0},{5,1},{6,2},{7,3},{8,12},{9,13},{10,... | collective-permute-start | bytes 294920 | tf_op jit(solution)/shard_map/ppermute | solution.py:493
  95.3 14.9 %collective-permute-start.13 = (bf16[96,512]{1,0:T(8,128)(2,1)S(1)}, bf16[96,512]{1,0:T(8,128)(2,1)S(1)}, u32[]{:S(2)}, u32[]{:S(2)}) collective-permute-start(bf16[96,512]{1,0:T(8,128)(2,1)S(1)} %get-tuple-element.106), channel_id=1, source_target_pairs={{0,8},{1,9},{2,10},{3,11},{4,12},{5,13},{6,14},{7,15},{8,0},{9,1},... | collective-permute-start | bytes 294920 | tf_op jit(solution)/shard_map/ppermute | solution.py:493
  96.9 13.4 %collective-permute-start.14 = (bf16[96,512]{1,0:T(8,128)(2,1)S(1)}, bf16[96,512]{1,0:T(8,128)(2,1)S(1)}, u32[]{:S(2)}, u32[]{:S(2)}) collective-permute-start(bf16[96,512]{1,0:T(8,128)(2,1)S(1)} %get-tuple-element.107), channel_id=1, source_target_pairs={{0,12},{1,13},{2,14},{3,15},{4,8},{5,9},{6,10},{7,11},{8,4},{9,5},... | collective-permute-start | bytes 294920 | tf_op jit(solution)/shard_map/ppermute | solution.py:493
  98.3 11.9 %collective-permute-start.18 = (bf16[48,512]{1,0:T(8,128)(2,1)S(1)}, bf16[48,512]{1,0:T(8,128)(2,1)S(1)}, u32[]{:S(2)}, u32[]{:S(2)}) collective-permute-start(bf16[48,512]{1,0:T(8,128)(2,1)S(1)} %get-tuple-element.112), channel_id=1, source_target_pairs={{0,8},{1,9},{2,10},{3,11},{4,12},{5,13},{6,14},{7,15},{8,0},{9,1},... | collective-permute-start | bytes 147464 | tf_op jit(solution)/shard_map/ppermute | solution.py:493
  100.3 10.0 %collective-permute-start.19 = (bf16[48,512]{1,0:T(8,128)(2,1)S(1)}, bf16[48,512]{1,0:T(8,128)(2,1)S(1)}, u32[]{:S(2)}, u32[]{:S(2)}) collective-permute-start(bf16[48,512]{1,0:T(8,128)(2,1)S(1)} %get-tuple-element.113), channel_id=1, source_target_pairs={{0,12},{1,13},{2,14},{3,15},{4,8},{5,9},{6,10},{7,11},{8,4},{9,5},... | collective-permute-start | bytes 147464 | tf_op jit(solution)/shard_map/ppermute | solution.py:493

commit v8 on v7

--- a/solution.py
+++ b/solution.py
@@ -156,13 +156,15 @@
 
 
 def by_distance(me, peers, sums, kept_ref, given_ref):
-    quarter = peers // 4
     for r in list(range(1, peers, 2)) + list(range(0, peers, 2)):
         if r == 0:
             given_ref.done()
         to = jnp.bitwise_xor(me, r)
         out = given_ref if r % 2 else kept_ref
-        slot = (r // 2 % 2) * quarter + r // 4
+        slot, rest, span = 0, r // 2, peers // 4
+        while span:
+            slot += rest % 2 * span
+            rest, span = rest // 2, span // 2
         place = 0
         for total in sums:
             rows = total.shape[0] // peers
@@ -278,9 +280,8 @@
     g_ref[...] = (d_edges + mm_nt(back_pre, w1_ref[0:width, :])).astype(BF16)
 
 
-def node_gradient_kernel(own_ref, halo_ref, *refs, slots):
-    passing = (len(refs) - slots - 1) // 2
-    piece_refs, out_ref = refs[:slots], refs[slots + passing]
+def node_gradient_kernel(own_ref, halo_ref, *refs):
+    piece_refs, out_ref = refs[:-1], refs[-1]
     arrived = None
     for slot, piece in enumerate(piece_refs):
         part = mm(one_hot(halo_ref[slot : slot + 1, :], own_ref.shape[0]), piece[...])
@@ -295,25 +296,21 @@
     g_ref[0:16, :] = first.astype(BF16)
 
 
-def second_halving_kernel(kept_ref, taken_ref, *refs, passing):
-    keep_ref, give_refs = refs[passing], refs[passing + 1 : len(refs) - passing]
-    for j in range(kept_ref.shape[0]):
-        total = kept_ref[j].astype(F32) + taken_ref[j].astype(F32)
-        if j:
-            give_refs[j - 1][...] = total.astype(BF16)
-        else:
-            keep_ref[...] = total
-
-
-def last_sum_kernel(*refs, counts, sizes, with_nodes):
-    place = 0
-    totals = []
-    for count in counts:
-        total = refs[place][...]
-        for ref in refs[place + 1 : place + count]:
-            total = total + ref[...].astype(F32)
-        totals.append(total)
-        place += count
+def order_kernel(*refs):
+    pass
+
+
+def halving_kernel(kept_ref, taken_ref, keep_ref, give_ref):
+    half = keep_ref.shape[0]
+    for j in range(half):
+        give_ref[j] = (kept_ref[half + j] + taken_ref[half + j].astype(F32)).astype(BF16)
+    for j in range(half):
+        keep_ref[j] = kept_ref[j] + taken_ref[j].astype(F32)
+
+
+def last_sum_kernel(*refs, sizes, with_nodes):
+    place = 2 * len(sizes)
+    totals = [refs[2 * i][0] + refs[2 * i + 1][0].astype(F32) for i in range(len(sizes))]
     if with_nodes:
         nodes_ref, g_ref = refs[place], refs[-1]
         place += 1
@@ -503,25 +500,22 @@
     return kept[:half].astype(F32) + taken[:half].astype(F32), give
 
 
-def second_halving(kept, taken, passing=()):
-    block = kept.shape[1:]
-    outs = [shape(block, F32)] + [shape(block, BF16)] * (kept.shape[0] - 1)
-    kernel = functools.partial(second_halving_kernel, passing=len(passing))
-    return small_call(kernel, "second_halving", (kept, taken), outs, passing)
+def halving(kept, taken):
+    half = (kept.shape[0] // 2,) + kept.shape[1:]
+    return small_call(halving_kernel, "halving", (kept, taken), [shape(half, F32), shape(half, BF16)])
 
 
 def last_sum(groups, sizes, nodes=None):
     ins, outs = [], []
     for (kept, taken), rows in zip(groups, sizes):
-        ins += [kept, *taken]
-        outs += [shape((count, kept.shape[1]), F32) for count in rows]
+        ins += [kept, taken]
+        outs += [shape((count, kept.shape[2]), F32) for count in rows]
     if nodes is not None:
         ins.append(nodes)
         outs.append(shape(nodes.shape, BF16))
-    kernel = functools.partial(
-        last_sum_kernel, counts=[1 + len(taken) for _, taken in groups], sizes=sizes, with_nodes=nodes is not None
-    )
-    return small_call(kernel, "last_sum", ins, outs)
+    return small_call(
+        functools.partial(last_sum_kernel, sizes=sizes, with_nodes=nodes is not None), "last_sum", ins, outs
+    )
 
 
 def local(
@@ -650,37 +644,38 @@
     def rows_of(w):
         return w.shape[0] // peers
 
-    def returned_tiles(passing=()):
-        return small_call(
-            functools.partial(node_gradient_kernel, slots=slots), "node_gradient",
-            (own_grad, halo, *returned), [shape((own, width), F32)], passing,
+    def tile_gradient():
+        (total,) = small_call(
+            node_gradient_kernel, "node_gradient", (own_grad, halo, *returned), [shape((own, width), F32)]
         )
-
-    if ordered:
-
-        def along_z(given):
-            return [exchanged(part, axis, 4 * (k + 1)) for k, part in enumerate(given)]
-
+        return total
+
+    if ordered:
         kept1, given1, kept2, given2 = edge_parts
-        total, given1 = returned_tiles((given1,))
+        given1, *returned = small_call(order_kernel, "order", (), [], (given1, *returned))
         taken1 = exchanged(given1, axis, 1)
         taken2 = exchanged(given2, axis, 1)
         kept1, given1 = first_halving(kept1, taken1)
         taken1 = exchanged(given1, axis, 2)
         kept2, given2 = first_halving(kept2, taken2)
         taken2 = exchanged(given2, axis, 2)
-        node_kept, *given = second_halving(node_kept, node_taken)
-        g_nw1, g_nw2 = last_sum([(node_kept, along_z(given))], [(rows_of(node_w1), rows_of(node_w2))])
-        kept1, *given1 = second_halving(kept1, taken1)
-        kept2, *given2 = second_halving(kept2, taken2)
+        distance = 4
+        while distance < peers:
+            node_kept, given = halving(node_kept, node_taken)
+            node_taken = exchanged(given, axis, distance)
+            kept1, given1 = halving(kept1, taken1)
+            taken1 = exchanged(given1, axis, distance)
+            kept2, given2 = halving(kept2, taken2)
+            taken2 = exchanged(given2, axis, distance)
+            distance *= 2
+        g_nw1, g_nw2 = last_sum([(node_kept, node_taken)], [(rows_of(node_w1), rows_of(node_w2))])
         g_ew1, g_ew2, g_nodes = last_sum(
-            [(kept1, along_z(given1)), (kept2, along_z(given2))], [(rows_of(edge_w1),), (rows_of(edge_w2),)], total
+            [(kept1, taken1), (kept2, taken2)], [(rows_of(edge_w1),), (rows_of(edge_w2),)], tile_gradient()
         )
     else:
         coarse_share = exchanged_with_all(edge_parts[0], axis)
         (g_nodes,) = small_call(
-            coarse_gradient_kernel, "coarse_gradient", (*returned_tiles(), coarse_share),
-            [shape((own, width), BF16)],
+            coarse_gradient_kernel, "coarse_gradient", (tile_gradient(), coarse_share), [shape((own, width), BF16)],
         )
         g_nw1, g_nw2, g_ew1, g_ew2 = [
             lax.psum_scatter(g, axis, scatter_dimension=0, tiled=True) for g in [*node_parts, *edge_parts[1:]]

time: 112 us -> 109 us (0.973)
  starting transfers between devices: 47 us -> 39.1 us
  waiting for transfers between devices: 21.1 us -> 26 us
    ppermute x15 -> x12, starting transfers between devices: 18.1 us -> 10.2 us  [exchanged(): lax.ppermute(block, axis, [(i, i ^ distance) for i in range(lax.axis_size...]
    ppermute x15 -> x12, waiting for transfers between devices: 21 us -> 25.8 us  [exchanged(): lax.ppermute(block, axis, [(i, i ^ distance) for i in range(lax.axis_size...]
    unnamed x30 -> x28, local copies, waits for them, and re-layouts: 3.97 us -> 3.97 us
  transfers between devices with their start and end apart: 26 -> 23, of which waited for: 6 -> 9; matrix products, arithmetic and copies ran while one was open for 0% -> 0% of each run, Pallas kernels for 25% -> 26%
where the time goes in v8:
time: 109 us; the launch traced here: 108 us
  starting transfers between devices  39.1 us (36%)
  Pallas kernels  34.4 us (32%)
  waiting for transfers between devices  26 us (24%)
  local copies, waits for them, and re-layouts  5.34 us (5%)
  other arithmetic  1.62 us (1%)
  between operations  1.6 us (1%)
    pallas_call x6, Pallas kernels, call(): pl.pallas_call(functools.partial(staged_kernel, kernel, in_specs, out_spe...  32.2 us
    ppermute x12, waiting for transfers between devices, exchanged(): lax.ppermute(block, axis, [(i, i ^ distance) for i in range(lax.axis_size...  25.8 us
    all_to_all x3, starting transfers between devices, exchanged_with_all(): return lax.all_to_all(blocks, axis, 0, 0)  16.1 us
    ppermute x8, starting transfers between devices, passed_along(): return lax.ppermute(block, axis, route)  12.9 us
    ppermute x12, starting transfers between devices, exchanged(): lax.ppermute(block, axis, [(i, i ^ distance) for i in range(lax.axis_size...  10.2 us
    unnamed x28, local copies, waits for them, and re-layouts  3.97 us
    pallas_call x10, Pallas kernels, small_call(): pl.pallas_call(kernel, out_shape=tuple(outs), input_output_aliases={first...  2.18 us
  transfers between devices with their start and end apart: 23, of which 9 were waited for; matrix products, arithmetic and copies ran while one was open for 0% of the time, Pallas kernels for 26%

profile of v8, /device:TPU:0, one launch (start us, length us, event | category | flops | bytes accessed | tf_op | source)
XLA Modules:
  0.0 108.1 jit_solution(5586026819392689368)
XLA Ops:
  0.6 0.7 slice.39
  1.3 0.7 broadcast_in_dim.2
  2.0 7.4 %all-to-all-start = ((bf16[16,8,512]{2,1,0:T(8,128)(2,1)}), bf16[16,8,512]{2,1,0:T(8,128)(2,1)S(1)}, u32[]{:S(2)}, u32[]{:S(2)}) async-start(bf16[16,8,512]{2,1,0:T(8,128)(2,1)} %broadcast_in_dim.2), calls=%async_computation | async-start | bytes 262144 | tf_op jit(solution)/shard_map/all_to_all | solution.py:494
  9.4 2.6 %tiles.1 = (bf16[128,512]{1,0:T(8,128)(2,1)}, bf16[128,512]{1,0:T(8,128)(2,1)}, bf16[128,512]{1,0:T(8,128)(2,1)}, bf16[128,512]{1,0:T(8,128)(2,1)}) custom-call(bf16[256,512]{1,0:T(8,128)(2,1)} %refs_1_.5, s32[4,128]{1,0:T(4,128)} %bitcast.8), custom_call_target="tpu_custom_call" | custom-call | bytes 788480 | tf_op jit(solution)/shard_map/tiles/pallas_call | solution.py:455
  12.0 0.5 collective-permute-start
  12.4 1.7 %collective-permute-start.1 = (bf16[128,512]{1,0:T(8,128)(2,1)}, bf16[128,512]{1,0:T(8,128)(2,1)S(1)}, u32[]{:S(2)}, u32[]{:S(2)}) collective-permute-start(bf16[128,512]{1,0:T(8,128)(2,1)} %get-tuple-element.72), channel_id=1, source_target_pairs={{14,0},{15,1},{0,2},{1,3},{2,4},{3,5},{4,6},{5,7},{6,8},{7,9},{8,1... | collective-permute-start | bytes 393224 | tf_op jit(solution)/shard_map/ppermute | solution.py:486
  14.1 4.0 %collective-permute-start.2 = (bf16[128,512]{1,0:T(8,128)(2,1)}, bf16[128,512]{1,0:T(8,128)(2,1)S(1)}, u32[]{:S(2)}, u32[]{:S(2)}) collective-permute-start(bf16[128,512]{1,0:T(8,128)(2,1)} %get-tuple-element.73), channel_id=1, source_target_pairs={{1,0},{2,1},{3,2},{4,3},{5,4},{6,5},{7,6},{8,7},{9,8},{10,9},{11,1... | collective-permute-start | bytes 393224 | tf_op jit(solution)/shard_map/ppermute | solution.py:486
  18.1 0.3 collective-permute-start.3
  18.4 0.7 copy-done.6
  19.0 4.0 %coarse_forward.1 = (bf16[128,512]{1,0:T(8,128)(2,1)}, bf16[16,8,512]{2,1,0:T(8,128)(2,1)}, bf16[128,512]{1,0:T(8,128)(2,1)}, bf16[128,512]{1,0:T(8,128)(2,1)}, ...) custom-call(bf16[16,8,512]{2,1,0:T(8,128)(2,1)} %copy-done.6, ...), custom_call_target="tpu_custom_call" | custom-call | flops 268435456 | bytes 3345408 | tf_op jit(solution)/shard_map/coarse_forward/pallas_call | solution.py:455
  23.0 4.0 %all-to-all-start.1 = ((bf16[16,8,512]{2,1,0:T(8,128)(2,1)}), bf16[16,8,512]{2,1,0:T(8,128)(2,1)S(1)}, u32[]{:S(2)}, u32[]{:S(2)}) async-start(bf16[16,8,512]{2,1,0:T(8,128)(2,1)} %get-tuple-element.76), calls=%async_computation.1 | async-start | bytes 262144 | tf_op jit(solution)/shard_map/all_to_all | solution.py:494
  27.7 0.0 collective-permute-done.refs_2_
  27.7 0.0 copy-start.10
  27.8 0.0 collective-permute-done.1.refs_3_
  27.8 0.0 copy-start.11
  27.8 0.0 copy-start.12
  27.8 0.0 collective-permute-done.3.refs_5_
  27.8 0.0 copy-start.13
  27.8 0.6 copy-done.10
  28.4 0.0 copy-done.11
  28.4 0.0 copy-done.12
  28.5 0.0 copy-done.13
  28.5 6.7 %fine_forward.1 = (bf16[512,512]{1,0:T(8,128)(2,1)}, f32[256,512]{1,0:T(8,128)}, bf16[512,512]{1,0:T(8,128)(2,1)}, bf16[512,512]{1,0:T(8,128)(2,1)}, bf16[512,51...) custom-call(s32[1]{0:T(128)S(6)} %copy.38.refs_0_, ...), custom_call_target="tpu_custom_call" | custom-call | flops 1879048192 | bytes 7346180 | tf_op jit(solution)/shard_map/fine_forward/pallas_call | solution.py:455
  35.3 0.0 copy-start.9
  35.3 0.6 copy-done.9
  35.9 5.8 %node_both.1 = (bf16[256,512]{1,0:T(8,128)(2,1)}, f32[256,512]{1,0:T(8,128)}, bf16[256,512]{1,0:T(8,128)(2,1)}, bf16[16,8,512]{2,1,0:T(8,128)(2,1)}, bf16[8,96,5...) custom-call(s32[1]{0:T(128)} %bitcast.refs_0_, bf16[256,512]{1,0:T(8,128)(2,1)} %refs_1_.5, ...), custom_call_target="tpu_custom_call" | custom-call | flops 1207959552 | bytes 5507076 | tf_op jit(solution)/shard_map/node_both/pallas_call | solution.py:455
  41.7 0.5 collective-permute-start.4
  42.2 2.1 %collective-permute-done.4 = bf16[8,96,512]{2,1,0:T(8,128)(2,1)S(1)} collective-permute-done((bf16[8,96,512]{2,1,0:T(8,128)(2,1)}, bf16[8,96,512]{2,1,0:T(8,128)(2,1)S(1)}, u32[]{:S(2)}, u32[]{:S(2)}) %collective-permute-start.4) | collective-permute-done | bytes 786464 | tf_op jit(solution)/shard_map/ppermute | solution.py:490
  44.4 1.3 %convert_add_fusion = (f32[4,96,512]{2,1,0:T(8,128)S(1)}, bf16[4,96,512]{2,1,0:T(8,128)(2,1)S(1)}) fusion(bf16[8,96,512]{2,1,0:T(8,128)(2,1)S(1)} %collective-permute-done.4, bf16[8,96,512]{2,1,0:T(8,128)(2,1)} %get-tuple-element.97), kind=kLoop, calls=%fused_computation | loop fusion | flops 1376256 | bytes 2752512 | tf_op jit(solution)/shard_map/add | solution.py:500
  45.7 1.9 %collective-permute-start.5 = (bf16[4,96,512]{2,1,0:T(8,128)(2,1)S(1)}, bf16[4,96,512]{2,1,0:T(8,128)(2,1)S(1)}, u32[]{:S(2)}, u32[]{:S(2)}) collective-permute-start(bf16[4,96,512]{2,1,0:T(8,128)(2,1)S(1)} %get-tuple-element.133), channel_id=1, source_target_pairs={{0,2},{1,3},{2,0},{3,1},{4,6},{5,7},{6,4},{7,5},{8,10},{9,11},{10,... | collective-permute-start | bytes 1179656 | tf_op jit(solution)/shard_map/ppermute | solution.py:490
  47.6 4.7 %all-to-all-start.2 = ((bf16[16,8,512]{2,1,0:T(8,128)(2,1)}), bf16[16,8,512]{2,1,0:T(8,128)(2,1)S(1)}, u32[]{:S(2)}, u32[]{:S(2)}) async-start(bf16[16,8,512]{2,1,0:T(8,128)(2,1)} %get-tuple-element.80), calls=%async_computation.2 | async-start | bytes 262144 | tf_op jit(solution)/shard_map/all_to_all | solution.py:494
  52.3 6.4 %fine_backward.1 = (bf16[512,512]{1,0:T(8,128)(2,1)}, bf16[512,512]{1,0:T(8,128)(2,1)}, bf16[512,512]{1,0:T(8,128)(2,1)}, f32[256,512]{1,0:T(8,128)}, bf16[128,5...) custom-call(s32[1]{0:T(128)S(6)} %copy.38.refs_0_, ...), custom_call_target="tpu_custom_call" | custom-call | flops 1744830464 | bytes 7346180 | tf_op jit(solution)/shard_map/fine_backward/pallas_call | solution.py:455
  58.7 4.4 %collective-permute-start.6 = (bf16[128,512]{1,0:T(8,128)(2,1)}, bf16[128,512]{1,0:T(8,128)(2,1)S(1)}, u32[]{:S(2)}, u32[]{:S(2)}) collective-permute-start(bf16[128,512]{1,0:T(8,128)(2,1)} %get-tuple-element.101), channel_id=1, source_target_pairs={{1,0},{2,1},{3,2},{4,3},{5,4},{6,5},{7,6},{8,7},{9,8},{10,9},{11,1... | collective-permute-start | bytes 393224 | tf_op jit(solution)/shard_map/ppermute | solution.py:486
  63.1 0.6 collective-permute-start.7
  63.7 1.5 %collective-permute-start.9 = (bf16[128,512]{1,0:T(8,128)(2,1)}, bf16[128,512]{1,0:T(8,128)(2,1)S(1)}, u32[]{:S(2)}, u32[]{:S(2)}) collective-permute-start(bf16[128,512]{1,0:T(8,128)(2,1)} %get-tuple-element.104), channel_id=1, source_target_pairs={{14,0},{15,1},{0,2},{1,3},{2,4},{3,5},{4,6},{5,7},{6,8},{7,9},{8,1... | collective-permute-start | bytes 393224 | tf_op jit(solution)/shard_map/ppermute | solution.py:486
  65.2 0.6 copy-done.8
  65.8 0.1 copy-done.2
  66.0 6.8 %coarse_backward.1 = (bf16[128,512]{1,0:T(8,128)(2,1)}, bf16[8,96,512]{2,1,0:T(8,128)(2,1)}, bf16[8,96,512]{2,1,0:T(8,128)(2,1)}, bf16[8,48,512]{2,1,0:T(8,128)(2,1)}, bf16[8,48,512]{2,1,0:T(8,128)(2,1)}) custom-call(s32[1]{0:T(128)} %bitcast.refs_0_, s32[1,128]{1,0:T(1,128)} %bitcast.17, bf16[16,8,512]{2,1,0:T(8,128)(2,1)} %copy-done.8, ...), custom_call_target="tpu_custom_call" | custom-call | flops 1879048192 | bytes 9243652 | tf_op jit(solution)/shard_map/coarse_backward/pallas_call | solution.py:455
  72.8 0.1 collective-permute-done.9.refs_4_
  72.9 1.1 %copy-done = bf16[8,96,512]{2,1,0:T(8,128)(2,1)S(1)} copy-done((bf16[8,96,512]{2,1,0:T(8,128)(2,1)S(1)}, bf16[8,96,512]{2,1,0:T(8,128)(2,1)}, u32[]{:S(2)}) %copy-start) | copy-done | bytes 786456
  74.1 0.7 collective-permute-start.10
  74.7 0.1 collective-permute-start.14
  74.8 2.3 %collective-permute-done.10 = bf16[8,96,512]{2,1,0:T(8,128)(2,1)S(1)} collective-permute-done((bf16[8,96,512]{2,1,0:T(8,128)(2,1)S(1)}, bf16[8,96,512]{2,1,0:T(8,128)(2,1)S(1)}, u32[]{:S(2)}, u32[]{:S(2)}) %collective-permute-start.10) | collective-permute-done | bytes 786464 | tf_op jit(solution)/shard_map/ppermute | solution.py:490
  77.1 0.2 add_convert_fusion
  77.3 0.1 collective-permute-start.11
  77.4 0.1 collective-permute-done.14
  77.4 0.1 add_convert_fusion.2
  77.5 2.0 %collective-permute-start.15 = (bf16[4,48,512]{2,1,0:T(8,128)(2,1)S(1)}, bf16[4,48,512]{2,1,0:T(8,128)(2,1)S(1)}, u32[]{:S(2)}, u32[]{:S(2)}) collective-permute-start(bf16[4,48,512]{2,1,0:T(8,128)(2,1)S(1)} %get-tuple-element.136), channel_id=1, source_target_pairs={{0,2},{1,3},{2,0},{3,1},{4,6},{5,7},{6,4},{7,5},{8,10},{9,11},{10,... | collective-permute-start | bytes 589832 | tf_op jit(solution)/shard_map/ppermute | solution.py:490
  79.6 0.1 halving.10
  79.6 0.1 collective-permute-start.18
  79.7 9.6 %collective-permute-done.11.taken_ref = bf16[4,96,512]{2,1,0:T(8,128)(2,1)S(1)} collective-permute-done((bf16[4,96,512]{2,1,0:T(8,128)(2,1)S(1)}, bf16[4,96,512]{2,1,0:T(8,128)(2,1)S(1)}, u32[]{:S(2)}, u32[]{:S(2)}) %collective-permute-start.11) | collective-permute-done | bytes 393248 | tf_op jit(solution)/shard_map/ppermute | solution.py:490
  89.3 0.1 halving.6
  89.4 0.1 collective-permute-start.12
  89.5 3.5 %collective-permute-done.15.taken_ref = bf16[4,48,512]{2,1,0:T(8,128)(2,1)S(1)} collective-permute-done((bf16[4,48,512]{2,1,0:T(8,128)(2,1)S(1)}, bf16[4,48,512]{2,1,0:T(8,128)(2,1)S(1)}, u32[]{:S(2)}, u32[]{:S(2)}) %collective-permute-start.15) | collective-permute-done | bytes 196640 | tf_op jit(solution)/shard_map/ppermute | solution.py:490
  93.0 0.1 collective-permute-start.16
  93.1 3.4 %collective-permute-start.19 = (bf16[1,96,512]{2,1,0:T(8,128)(2,1)S(1)}, bf16[1,96,512]{2,1,0:T(8,128)(2,1)S(1)}, u32[]{:S(2)}, u32[]{:S(2)}) collective-permute-start(bf16[1,96,512]{2,1,0:T(8,128)(2,1)S(1)} %get-tuple-element.129), channel_id=1, source_target_pairs={{0,8},{1,9},{2,10},{3,11},{4,12},{5,13},{6,14},{7,15},{8,0},{9,1},... | collective-permute-start | bytes 294920 | tf_op jit(solution)/shard_map/ppermute | solution.py:490
  96.6 0.4 collective-permute-start.13
  97.0 2.3 %collective-permute-done.16.taken_ref = bf16[2,48,512]{2,1,0:T(8,128)(2,1)S(1)} collective-permute-done((bf16[2,48,512]{2,1,0:T(8,128)(2,1)S(1)}, bf16[2,48,512]{2,1,0:T(8,128)(2,1)S(1)}, u32[]{:S(2)}, u32[]{:S(2)}) %collective-permute-start.16) | collective-permute-done | bytes 98336 | tf_op jit(solution)/shard_map/ppermute | solution.py:490
  99.4 0.8 collective-permute-start.17
  100.2 0.4 node_gradient.1.refs_4_
  100.6 4.0 %collective-permute-done.19.refs_1_ = bf16[1,96,512]{2,1,0:T(8,128)(2,1)S(1)} collective-permute-done((bf16[1,96,512]{2,1,0:T(8,128)(2,1)S(1)}, bf16[1,96,512]{2,1,0:T(8,128)(2,1)S(1)}, u32[]{:S(2)}, u32[]{:S(2)}) %collective-permute-start.19) | collective-permute-done | bytes 98336 | tf_op jit(solution)/shard_map/ppermute | solution.py:490
  104.6 0.7 last_sum.3
  105.3 1.9 %collective-permute-done.17.refs_3_ = bf16[1,48,512]{2,1,0:T(8,128)(2,1)S(1)} collective-permute-done((bf16[1,48,512]{2,1,0:T(8,128)(2,1)S(1)}, bf16[1,48,512]{2,1,0:T(8,128)(2,1)S(1)}, u32[]{:S(2)}, u32[]{:S(2)}) %collective-permute-start.17) | collective-permute-done | bytes 49184 | tf_op jit(solution)/shard_map/ppermute | solution.py:490
  107.2 0.8 last_sum.2
  (31 shorter events, 0.2 us)
Async XLA Ops:
  2.0 16.4 %all-to-all-start = ((bf16[16,8,512]{2,1,0:T(8,128)(2,1)}), bf16[16,8,512]{2,1,0:T(8,128)(2,1)S(1)}, u32[]{:S(2)}, u32[]{:S(2)}) async-start(bf16[16,8,512]{2,1,0:T(8,128)(2,1)} %broadcast_in_dim.2), calls=%async_computation | async-start | bytes 262144 | tf_op jit(solution)/shard_map/all_to_all | solution.py:494
  12.0 15.8 %collective-permute-start = (bf16[128,512]{1,0:T(8,128)(2,1)}, bf16[128,512]{1,0:T(8,128)(2,1)S(1)}, u32[]{:S(2)}, u32[]{:S(2)}) collective-permute-start(bf16[128,512]{1,0:T(8,128)(2,1)} %get-tuple-element.71), channel_id=1, source_target_pairs={{15,0},{0,1},{1,2},{2,3},{3,4},{4,5},{5,6},{6,7},{7,8},{8,9},{9,10... | collective-permute-start | bytes 393224 | tf_op jit(solution)/shard_map/ppermute | solution.py:486
  12.4 15.4 %collective-permute-start.1 = (bf16[128,512]{1,0:T(8,128)(2,1)}, bf16[128,512]{1,0:T(8,128)(2,1)S(1)}, u32[]{:S(2)}, u32[]{:S(2)}) collective-permute-start(bf16[128,512]{1,0:T(8,128)(2,1)} %get-tuple-element.72), channel_id=1, source_target_pairs={{14,0},{15,1},{0,2},{1,3},{2,4},{3,5},{4,6},{5,7},{6,8},{7,9},{8,1... | collective-permute-start | bytes 393224 | tf_op jit(solution)/shard_map/ppermute | solution.py:486
  14.1 13.7 %collective-permute-start.2 = (bf16[128,512]{1,0:T(8,128)(2,1)}, bf16[128,512]{1,0:T(8,128)(2,1)S(1)}, u32[]{:S(2)}, u32[]{:S(2)}) collective-permute-start(bf16[128,512]{1,0:T(8,128)(2,1)} %get-tuple-element.73), channel_id=1, source_target_pairs={{1,0},{2,1},{3,2},{4,3},{5,4},{6,5},{7,6},{8,7},{9,8},{10,9},{11,1... | collective-permute-start | bytes 393224 | tf_op jit(solution)/shard_map/ppermute | solution.py:486
  18.1 9.7 %collective-permute-start.3 = (bf16[128,512]{1,0:T(8,128)(2,1)}, bf16[128,512]{1,0:T(8,128)(2,1)S(1)}, u32[]{:S(2)}, u32[]{:S(2)}) collective-permute-start(bf16[128,512]{1,0:T(8,128)(2,1)} %get-tuple-element.74), channel_id=1, source_target_pairs={{2,0},{3,1},{4,2},{5,3},{6,4},{7,5},{8,6},{9,7},{10,8},{11,9},{12,... | collective-permute-start | bytes 393224 | tf_op jit(solution)/shard_map/ppermute | solution.py:486
  18.4 0.7 copy-start.6
  23.0 12.2 %all-to-all-start.1 = ((bf16[16,8,512]{2,1,0:T(8,128)(2,1)}), bf16[16,8,512]{2,1,0:T(8,128)(2,1)S(1)}, u32[]{:S(2)}, u32[]{:S(2)}) async-start(bf16[16,8,512]{2,1,0:T(8,128)(2,1)} %get-tuple-element.76), calls=%async_computation.1 | async-start | bytes 262144 | tf_op jit(solution)/shard_map/all_to_all | solution.py:494
  27.7 0.7 copy-start.10
  27.8 0.7 copy-start.11
  27.8 0.7 copy-start.12
  27.8 0.7 copy-start.13
  35.3 0.7 copy-start.9
  41.7 2.6 %collective-permute-start.4 = (bf16[8,96,512]{2,1,0:T(8,128)(2,1)}, bf16[8,96,512]{2,1,0:T(8,128)(2,1)S(1)}, u32[]{:S(2)}, u32[]{:S(2)}) collective-permute-start(bf16[8,96,512]{2,1,0:T(8,128)(2,1)} %get-tuple-element.98), channel_id=1, source_target_pairs={{0,1},{1,0},{2,3},{3,2},{4,5},{5,4},{6,7},{7,6},{8,9},{9,8},{10,11... | collective-permute-start | bytes 2359304 | tf_op jit(solution)/shard_map/ppermute | solution.py:490
  45.7 19.5 %collective-permute-start.5 = (bf16[4,96,512]{2,1,0:T(8,128)(2,1)S(1)}, bf16[4,96,512]{2,1,0:T(8,128)(2,1)S(1)}, u32[]{:S(2)}, u32[]{:S(2)}) collective-permute-start(bf16[4,96,512]{2,1,0:T(8,128)(2,1)S(1)} %get-tuple-element.133), channel_id=1, source_target_pairs={{0,2},{1,3},{2,0},{3,1},{4,6},{5,7},{6,4},{7,5},{8,10},{9,11},{10,... | collective-permute-start | bytes 1179656 | tf_op jit(solution)/shard_map/ppermute | solution.py:490
  47.6 17.6 %all-to-all-start.2 = ((bf16[16,8,512]{2,1,0:T(8,128)(2,1)}), bf16[16,8,512]{2,1,0:T(8,128)(2,1)S(1)}, u32[]{:S(2)}, u32[]{:S(2)}) async-start(bf16[16,8,512]{2,1,0:T(8,128)(2,1)} %get-tuple-element.80), calls=%async_computation.2 | async-start | bytes 262144 | tf_op jit(solution)/shard_map/all_to_all | solution.py:494
  58.7 14.1 %collective-permute-start.6 = (bf16[128,512]{1,0:T(8,128)(2,1)}, bf16[128,512]{1,0:T(8,128)(2,1)S(1)}, u32[]{:S(2)}, u32[]{:S(2)}) collective-permute-start(bf16[128,512]{1,0:T(8,128)(2,1)} %get-tuple-element.101), channel_id=1, source_target_pairs={{1,0},{2,1},{3,2},{4,3},{5,4},{6,5},{7,6},{8,7},{9,8},{10,9},{11,1... | collective-permute-start | bytes 393224 | tf_op jit(solution)/shard_map/ppermute | solution.py:486
  63.1 9.7 %collective-permute-start.7 = (bf16[128,512]{1,0:T(8,128)(2,1)}, bf16[128,512]{1,0:T(8,128)(2,1)S(1)}, u32[]{:S(2)}, u32[]{:S(2)}) collective-permute-start(bf16[128,512]{1,0:T(8,128)(2,1)} %get-tuple-element.102), channel_id=1, source_target_pairs={{2,0},{3,1},{4,2},{5,3},{6,4},{7,5},{8,6},{9,7},{10,8},{11,9},{12,... | collective-permute-start | bytes 393224 | tf_op jit(solution)/shard_map/ppermute | solution.py:486
  63.7 9.1 %collective-permute-start.8 = (bf16[128,512]{1,0:T(8,128)(2,1)}, bf16[128,512]{1,0:T(8,128)(2,1)S(1)}, u32[]{:S(2)}, u32[]{:S(2)}) collective-permute-start(bf16[128,512]{1,0:T(8,128)(2,1)} %get-tuple-element.103), channel_id=1, source_target_pairs={{15,0},{0,1},{1,2},{2,3},{3,4},{4,5},{5,6},{6,7},{7,8},{8,9},{9,10... | collective-permute-start | bytes 393224 | tf_op jit(solution)/shard_map/ppermute | solution.py:486
  63.7 9.3 %collective-permute-start.9 = (bf16[128,512]{1,0:T(8,128)(2,1)}, bf16[128,512]{1,0:T(8,128)(2,1)S(1)}, u32[]{:S(2)}, u32[]{:S(2)}) collective-permute-start(bf16[128,512]{1,0:T(8,128)(2,1)} %get-tuple-element.104), channel_id=1, source_target_pairs={{14,0},{15,1},{0,2},{1,3},{2,4},{3,5},{4,6},{5,7},{6,8},{7,9},{8,1... | collective-permute-start | bytes 393224 | tf_op jit(solution)/shard_map/ppermute | solution.py:486
  65.2 0.7 copy-start.8
  65.2 0.8 copy-start.2
  72.9 1.1 %copy-start = (bf16[8,96,512]{2,1,0:T(8,128)(2,1)S(1)}, bf16[8,96,512]{2,1,0:T(8,128)(2,1)}, u32[]{:S(2)}) copy-start(bf16[8,96,512]{2,1,0:T(8,128)(2,1)} %get-tuple-element.100.refs_0_) | copy-start | bytes 2359300
  74.1 3.0 %copy-start.5 = (bf16[8,96,512]{2,1,0:T(8,128)(2,1)S(1)}, bf16[8,96,512]{2,1,0:T(8,128)(2,1)}, u32[]{:S(2)}) copy-start(bf16[8,96,512]{2,1,0:T(8,128)(2,1)} %get-tuple-element.99) | copy-start | bytes 2359300
  74.1 3.4 %copy-start.7 = (bf16[8,48,512]{2,1,0:T(8,128)(2,1)S(1)}, bf16[8,48,512]{2,1,0:T(8,128)(2,1)}, u32[]{:S(2)}) copy-start(bf16[8,48,512]{2,1,0:T(8,128)(2,1)} %get-tuple-element.110) | copy-start | bytes 1179652
  74.1 3.0 %collective-permute-start.10 = (bf16[8,96,512]{2,1,0:T(8,128)(2,1)S(1)}, bf16[8,96,512]{2,1,0:T(8,128)(2,1)S(1)}, u32[]{:S(2)}, u32[]{:S(2)}) collective-permute-start(bf16[8,96,512]{2,1,0:T(8,128)(2,1)S(1)} %get-tuple-element.105), channel_id=1, source_target_pairs={{0,1},{1,0},{2,3},{3,2},{4,5},{5,4},{6,7},{7,6},{8,9},{9,8},{10,11... | collective-permute-start | bytes 2359304 | tf_op jit(solution)/shard_map/ppermute | solution.py:490
  74.7 2.7 %collective-permute-start.14 = (bf16[8,48,512]{2,1,0:T(8,128)(2,1)}, bf16[8,48,512]{2,1,0:T(8,128)(2,1)S(1)}, u32[]{:S(2)}, u32[]{:S(2)}) collective-permute-start(bf16[8,48,512]{2,1,0:T(8,128)(2,1)} %get-tuple-element.111), channel_id=1, source_target_pairs={{0,1},{1,0},{2,3},{3,2},{4,5},{5,4},{6,7},{7,6},{8,9},{9,8},{10,11... | collective-permute-start | bytes 1179656 | tf_op jit(solution)/shard_map/ppermute | solution.py:490
  77.1 2.5 %copy-start.3 = (bf16[4,96,512]{2,1,0:T(8,128)(2,1)S(1)}, bf16[4,96,512]{2,1,0:T(8,128)(2,1)}, u32[]{:S(2)}) copy-start(bf16[4,96,512]{2,1,0:T(8,128)(2,1)} %copy-done.2) | copy-start | bytes 1179652
  77.3 12.0 %collective-permute-start.11 = (bf16[4,96,512]{2,1,0:T(8,128)(2,1)S(1)}, bf16[4,96,512]{2,1,0:T(8,128)(2,1)S(1)}, u32[]{:S(2)}, u32[]{:S(2)}) collective-permute-start(bf16[4,96,512]{2,1,0:T(8,128)(2,1)S(1)} %get-tuple-element.134), channel_id=1, source_target_pairs={{0,2},{1,3},{2,0},{3,1},{4,6},{5,7},{6,4},{7,5},{8,10},{9,11},{10,... | collective-permute-start | bytes 1179656 | tf_op jit(solution)/shard_map/ppermute | solution.py:490
  77.5 15.4 %collective-permute-start.15 = (bf16[4,48,512]{2,1,0:T(8,128)(2,1)S(1)}, bf16[4,48,512]{2,1,0:T(8,128)(2,1)S(1)}, u32[]{:S(2)}, u32[]{:S(2)}) collective-permute-start(bf16[4,48,512]{2,1,0:T(8,128)(2,1)S(1)} %get-tuple-element.136), channel_id=1, source_target_pairs={{0,2},{1,3},{2,0},{3,1},{4,6},{5,7},{6,4},{7,5},{8,10},{9,11},{10,... | collective-permute-start | bytes 589832 | tf_op jit(solution)/shard_map/ppermute | solution.py:490
  79.6 13.4 %collective-permute-start.18 = (bf16[2,96,512]{2,1,0:T(8,128)(2,1)S(1)}, bf16[2,96,512]{2,1,0:T(8,128)(2,1)S(1)}, u32[]{:S(2)}, u32[]{:S(2)}) collective-permute-start(bf16[2,96,512]{2,1,0:T(8,128)(2,1)S(1)} %get-tuple-element.127), channel_id=1, source_target_pairs={{0,4},{1,5},{2,6},{3,7},{4,0},{5,1},{6,2},{7,3},{8,12},{9,13},{10,... | collective-permute-start | bytes 589832 | tf_op jit(solution)/shard_map/ppermute | solution.py:490
  89.3 10.9 %copy-start.1 = (f32[256,512]{1,0:T(8,128)S(1)}, f32[256,512]{1,0:T(8,128)}, u32[]{:S(2)}) copy-start(f32[256,512]{1,0:T(8,128)} %get-tuple-element.116.own_ref) | copy-start | bytes 1572868
  89.3 10.9 %copy-start.4 = (s32[1,4,128]{2,1,0:T(4,128)S(1)}, s32[1,4,128]{2,1,0:T(4,128)}, u32[]{:S(2)}) copy-start(s32[1,4,128]{2,1,0:T(4,128)} %param.25) | copy-start | bytes 6148
  89.4 7.2 %collective-permute-start.12 = (bf16[2,96,512]{2,1,0:T(8,128)(2,1)S(1)}, bf16[2,96,512]{2,1,0:T(8,128)(2,1)S(1)}, u32[]{:S(2)}, u32[]{:S(2)}) collective-permute-start(bf16[2,96,512]{2,1,0:T(8,128)(2,1)S(1)} %get-tuple-element.107), channel_id=1, source_target_pairs={{0,4},{1,5},{2,6},{3,7},{4,0},{5,1},{6,2},{7,3},{8,12},{9,13},{10,... | collective-permute-start | bytes 589832 | tf_op jit(solution)/shard_map/ppermute | solution.py:490
  93.0 6.3 %collective-permute-start.16 = (bf16[2,48,512]{2,1,0:T(8,128)(2,1)S(1)}, bf16[2,48,512]{2,1,0:T(8,128)(2,1)S(1)}, u32[]{:S(2)}, u32[]{:S(2)}) collective-permute-start(bf16[2,48,512]{2,1,0:T(8,128)(2,1)S(1)} %get-tuple-element.113), channel_id=1, source_target_pairs={{0,4},{1,5},{2,6},{3,7},{4,0},{5,1},{6,2},{7,3},{8,12},{9,13},{10,... | collective-permute-start | bytes 294920 | tf_op jit(solution)/shard_map/ppermute | solution.py:490
  93.1 11.5 %collective-permute-start.19 = (bf16[1,96,512]{2,1,0:T(8,128)(2,1)S(1)}, bf16[1,96,512]{2,1,0:T(8,128)(2,1)S(1)}, u32[]{:S(2)}, u32[]{:S(2)}) collective-permute-start(bf16[1,96,512]{2,1,0:T(8,128)(2,1)S(1)} %get-tuple-element.129), channel_id=1, source_target_pairs={{0,8},{1,9},{2,10},{3,11},{4,12},{5,13},{6,14},{7,15},{8,0},{9,1},... | collective-permute-start | bytes 294920 | tf_op jit(solution)/shard_map/ppermute | solution.py:490
  96.6 10.6 %collective-permute-start.13 = (bf16[1,96,512]{2,1,0:T(8,128)(2,1)S(1)}, bf16[1,96,512]{2,1,0:T(8,128)(2,1)S(1)}, u32[]{:S(2)}, u32[]{:S(2)}) collective-permute-start(bf16[1,96,512]{2,1,0:T(8,128)(2,1)S(1)} %get-tuple-element.109), channel_id=1, source_target_pairs={{0,8},{1,9},{2,10},{3,11},{4,12},{5,13},{6,14},{7,15},{8,0},{9,1},... | collective-permute-start | bytes 294920 | tf_op jit(solution)/shard_map/ppermute | solution.py:490
  99.4 7.9 %collective-permute-start.17 = (bf16[1,48,512]{2,1,0:T(8,128)(2,1)S(1)}, bf16[1,48,512]{2,1,0:T(8,128)(2,1)S(1)}, u32[]{:S(2)}, u32[]{:S(2)}) collective-permute-start(bf16[1,48,512]{2,1,0:T(8,128)(2,1)S(1)} %get-tuple-element.115), channel_id=1, source_target_pairs={{0,8},{1,9},{2,10},{3,11},{4,12},{5,13},{6,14},{7,15},{8,0},{9,1},... | collective-permute-start | bytes 147464 | tf_op jit(solution)/shard_map/ppermute | solution.py:490

commit v9 on v8

--- a/solution.py
+++ b/solution.py
@@ -155,16 +155,24 @@
             ref.done(rows)
 
 
-def by_distance(me, peers, sums, kept_ref, given_ref):
+def x_first(peers):
+    return [1 << bit for bit in range(1, peers.bit_length() - 1)]
+
+
+def x_last(peers):
+    steps = x_first(peers)
+    return steps[1:] + steps[:1]
+
+
+def by_distance(me, peers, steps, sums, kept_ref, given_ref):
     for r in list(range(1, peers, 2)) + list(range(0, peers, 2)):
         if r == 0:
             given_ref.done()
         to = jnp.bitwise_xor(me, r)
         out = given_ref if r % 2 else kept_ref
-        slot, rest, span = 0, r // 2, peers // 4
-        while span:
-            slot += rest % 2 * span
-            rest, span = rest // 2, span // 2
+        slot = 0
+        for distance in steps:
+            slot = 2 * slot + r // distance % 2
         place = 0
         for total in sums:
             rows = total.shape[0] // peers
@@ -204,7 +212,18 @@
     g1_ref[width : 2 * width, :] = mm_tn(agg, back_pre)
     g2_ref[...] = mm_tn(hidden, back_out)
     if ordered:
-        by_distance(me_ref[0], spread_ref.shape[0], (g1_ref, g2_ref), kept_ref, given_ref)
+        by_distance(me_ref[0], spread_ref.shape[0], x_first(spread_ref.shape[0]), (g1_ref, g2_ref), kept_ref, given_ref)
+
+
+def fine_and_node_kernel(count_ref, me_ref, nodes_ref, *refs, slots, block, ordered):
+    edge_ins, node_ins = refs[: slots + 6], refs[slots + 6 : slots + 11]
+    edge_outs, node_outs = refs[slots + 11 : slots + 18], refs[slots + 18 : slots + 24]
+    space_ref, agg_ref, *scratch = refs[slots + 24 :]
+    fine_forward_kernel(
+        count_ref, nodes_ref, *edge_ins, edge_outs[0], agg_ref, *edge_outs[1:], space_ref, slots=slots, block=block
+    )
+    share_ref, *node_ins = node_ins
+    node_kernel(me_ref, nodes_ref, agg_ref, share_ref, *node_ins, *node_outs, *scratch, ordered=ordered)
 
 
 def fine_backward_kernel(
@@ -269,14 +288,15 @@
     g1_ref[width : 2 * width, :] = mm_tn(zs_ref[...], pre_ref[...])
     g1_ref[2 * width : 3 * width, :] = mm_tn(zr_ref[...], pre_ref[...])
     if ordered:
-        by_distance(me_ref[0], 2 * kept1_ref.shape[0], (g1_ref,), kept1_ref, given1_ref)
+        peers = 2 * kept1_ref.shape[0]
+        by_distance(me_ref[0], peers, x_first(peers), (g1_ref,), kept1_ref, given1_ref)
     g2_ref[...] = mm_tn(hidden_ref[...], out_ref[...])
     dz_send = mm_nt(back_pre, w1_ref[width : 2 * width, :]).astype(BF16)
     dz_recv = mm_nt(back_pre, w1_ref[2 * width : 3 * width, :]).astype(BF16)
     total = mm(one_hot(send_ref[...], table.shape[0]), dz_send) + mm(one_hot(recv_ref[...], table.shape[0]), dz_recv)
     part_ref[...] = total.reshape(part_ref.shape).astype(part_ref.dtype)
     if ordered:
-        by_distance(me_ref[0], 2 * kept2_ref.shape[0], (g2_ref, part_ref), kept2_ref, given2_ref)
+        by_distance(me_ref[0], peers, x_last(peers), (g2_ref, part_ref), kept2_ref, given2_ref)
     g_ref[...] = (d_edges + mm_nt(back_pre, w1_ref[0:width, :])).astype(BF16)
 
 
@@ -300,7 +320,9 @@
     pass
 
 
-def halving_kernel(kept_ref, taken_ref, keep_ref, give_ref):
+def halving_kernel(kept_ref, taken_ref, *refs):
+    passing = (len(refs) - 2) // 2
+    keep_ref, give_ref = refs[passing : passing + 2]
     half = keep_ref.shape[0]
     for j in range(half):
         give_ref[j] = (kept_ref[half + j] + taken_ref[half + j].astype(F32)).astype(BF16)
@@ -500,9 +522,9 @@
     return kept[:half].astype(F32) + taken[:half].astype(F32), give
 
 
-def halving(kept, taken):
+def halving(kept, taken, passing=()):
     half = (kept.shape[0] // 2,) + kept.shape[1:]
-    return small_call(halving_kernel, "halving", (kept, taken), [shape(half, F32), shape(half, BF16)])
+    return small_call(halving_kernel, "halving", (kept, taken), [shape(half, F32), shape(half, BF16)], passing)
 
 
 def last_sum(groups, sizes, nodes=None):
@@ -579,15 +601,6 @@
 
     block = 256 if fine % 256 == 0 else fine
     space_rows = own + slots * tile
-    new_fine, fine_agg, *fine_saved = call(
-        functools.partial(fine_forward_kernel, slots=slots, block=block), "fine_forward",
-        (edge_count, nodes, *received, fine_edges, fs, fr, edge_w1, edge_w2, eg),
-        [SM] + [VM] * (slots + 4) + [Rows(3), VM, VM],
-        [shape((fine, width), BF16), shape((own, width), F32)] + saved_shapes(fine),
-        scratch=[pltpu.VMEM((space_rows, width), BF16)],
-        flops=2 * fine * width * (4 * width + space_rows + 3 * own),
-    )
-
     def weight_shapes(w1, w2, more):
         if not ordered:
             return [shape(w1.shape, F32), shape(w2.shape, F32)], []
@@ -596,13 +609,19 @@
         return outs, [pltpu.VMEM(w1.shape, F32), pltpu.VMEM(w2.shape, F32)]
 
     sum_shapes, sum_scratch = weight_shapes(node_w1, node_w2, 0)
-    new_nodes, base, dagg, dagg_spread, *node_parts = call(
-        functools.partial(node_kernel, ordered=ordered), "node_both",
-        (me, nodes, fine_agg, share, d_nodes, node_w1, node_w2, ng), [SM] + [VM] * 4 + [Rows(2), VM, VM],
-        [shape((own, width), BF16), shape((own, width), F32), shape((own, width), BF16), every] + sum_shapes,
-        scratch=[pltpu.VMEM((own, width), F32)] + sum_scratch,
-        flops=2 * own * width * width * 9,
-    )
+    new_fine, *made = call(
+        functools.partial(fine_and_node_kernel, slots=slots, block=block, ordered=ordered), "fine_and_node",
+        (
+            edge_count, me, nodes, *received, fine_edges, fs, fr, edge_w1, edge_w2, eg,
+            share, d_nodes, node_w1, node_w2, ng,
+        ),
+        [SM, SM] + [VM] * (slots + 4) + [Rows(3)] + [VM] * 4 + [Rows(2), VM, VM],
+        [shape((fine, width), BF16)] + saved_shapes(fine)
+        + [shape((own, width), BF16), shape((own, width), F32), shape((own, width), BF16), every] + sum_shapes,
+        scratch=[pltpu.VMEM((space_rows, width), BF16)] + [pltpu.VMEM((own, width), F32)] * 2 + sum_scratch,
+        flops=2 * fine * width * (4 * width + space_rows + 3 * own) + 2 * own * width * width * 9,
+    )
+    fine_saved, (new_nodes, base, dagg, dagg_spread), node_parts = made[:6], made[6:10], made[10:]
     dagg_all = exchanged_with_all(dagg_spread, axis)
     if ordered:
         node_taken = exchanged(node_parts[1], axis, 1)
@@ -655,19 +674,19 @@
         given1, *returned = small_call(order_kernel, "order", (), [], (given1, *returned))
         taken1 = exchanged(given1, axis, 1)
         taken2 = exchanged(given2, axis, 1)
+        steps1, steps2 = x_first(peers), x_last(peers)
         kept1, given1 = first_halving(kept1, taken1)
-        taken1 = exchanged(given1, axis, 2)
+        taken1 = exchanged(given1, axis, steps1[0])
         kept2, given2 = first_halving(kept2, taken2)
-        taken2 = exchanged(given2, axis, 2)
-        distance = 4
-        while distance < peers:
-            node_kept, given = halving(node_kept, node_taken)
-            node_taken = exchanged(given, axis, distance)
-            kept1, given1 = halving(kept1, taken1)
-            taken1 = exchanged(given1, axis, distance)
-            kept2, given2 = halving(kept2, taken2)
-            taken2 = exchanged(given2, axis, distance)
-            distance *= 2
+        taken2 = exchanged(given2, axis, steps2[0])
+        for k in range(1, len(steps1)):
+            passing = (kept1,) if k > 1 else ()
+            node_kept, given, *passing = halving(node_kept, node_taken, passing)
+            node_taken = exchanged(given, axis, steps1[k])
+            kept2, given2, *passing = halving(kept2, taken2, tuple(passing))
+            taken2 = exchanged(given2, axis, steps2[k])
+            kept1, given1 = halving(passing[0] if passing else kept1, taken1)
+            taken1 = exchanged(given1, axis, steps1[k])
         g_nw1, g_nw2 = last_sum([(node_kept, node_taken)], [(rows_of(node_w1), rows_of(node_w2))])
         g_ew1, g_ew2, g_nodes = last_sum(
             [(kept1, taken1), (kept2, taken2)], [(rows_of(edge_w1),), (rows_of(edge_w2),)], tile_gradient()

time: 109 us -> 114 us (1.046)
  blocking collectives: 0 us -> 15.2 us
  starting transfers between devices: 39.1 us -> 29.5 us
  waiting for transfers between devices: 26 us -> 30.4 us
  Pallas kernels: 34.4 us -> 31.4 us
  local copies, waits for them, and re-layouts: 5.34 us -> 3.31 us
    all_to_all x0 -> x1, blocking collectives: none -> 15.2 us  [exchanged_with_all(): return lax.all_to_all(blocks, axis, 0, 0)]
    all_to_all x3 -> x2, starting transfers between devices: 16.1 us -> 8.23 us  [exchanged_with_all(): return lax.all_to_all(blocks, axis, 0, 0)]
    ppermute x8, waiting for transfers between devices: 0.16 us -> 7.49 us  [passed_along(): return lax.ppermute(block, axis, route)]
    pallas_call x6 -> x5, Pallas kernels: 32.2 us -> 29.2 us  [call(): pl.pallas_call(functools.partial(staged_kernel, kernel, in_specs, out_spe...]
    ppermute x12, waiting for transfers between devices: 25.8 us -> 22.9 us  [exchanged(): lax.ppermute(block, axis, [(i, i ^ distance) for i in range(lax.axis_size...]
    ppermute x12, starting transfers between devices: 10.2 us -> 8.42 us  [exchanged(): lax.ppermute(block, axis, [(i, i ^ distance) for i in range(lax.axis_size...]
    unnamed x28 -> x26, local copies, waits for them, and re-layouts: 3.97 us -> 2.59 us
  transfers between devices with their start and end apart: 23 -> 22, of which waited for: 9 -> 12; matrix products, arithmetic and copies ran while one was open for 0% -> 0% of each run, Pallas kernels for 26% -> 15%
where the time goes in v9:
time: 114 us; the launch traced here: 113 us
  Pallas kernels  31.4 us (28%)
  waiting for transfers between devices  30.4 us (27%)
  starting transfers between devices  29.5 us (26%)
  blocking collectives  15.2 us (13%)
  local copies, waits for them, and re-layouts  3.31 us (3%)
  other arithmetic  1.63 us (1%)
  between operations  1.54 us (1%)
    pallas_call x5, Pallas kernels, call(): pl.pallas_call(functools.partial(staged_kernel, kernel, in_specs, out_spe...  29.2 us
    ppermute x12, waiting for transfers between devices, exchanged(): lax.ppermute(block, axis, [(i, i ^ distance) for i in range(lax.axis_size...  22.9 us
    all_to_all x1, blocking collectives, exchanged_with_all(): return lax.all_to_all(blocks, axis, 0, 0)  15.2 us
    ppermute x8, starting transfers between devices, passed_along(): return lax.ppermute(block, axis, route)  12.9 us
    ppermute x12, starting transfers between devices, exchanged(): lax.ppermute(block, axis, [(i, i ^ distance) for i in range(lax.axis_size...  8.42 us
    all_to_all x2, starting transfers between devices, exchanged_with_all(): return lax.all_to_all(blocks, axis, 0, 0)  8.23 us
    ppermute x8, waiting for transfers between devices, passed_along(): return lax.ppermute(block, axis, route)  7.49 us
    unnamed x26, local copies, waits for them, and re-layouts  2.59 us
  transfers between devices with their start and end apart: 22, of which 12 were waited for; matrix products, arithmetic and copies ran while one was open for 0% of the time, Pallas kernels for 15%

profile of v9, /device:TPU:0, one launch (start us, length us, event | category | flops | bytes accessed | tf_op | source)
XLA Modules:
  0.0 112.9 jit_solution(6454329561284907841)
XLA Ops:
  0.6 0.7 slice.39
  1.4 15.2 %all_to_all.15.refs_0_ = bf16[16,8,512]{2,1,0:T(8,128)(2,1)} all-to-all(bf16[16,8,512]{2,1,0:T(8,128)(2,1)S(1)} %broadcast_in_dim.2), channel_id=1, replica_groups=mesh['groups'=2,'patch'=16] {'patch'}, dimensions={0} | all-to-all | bytes 262144 | tf_op jit(solution)/shard_map/all_to_all | solution.py:516
  16.6 4.0 %coarse_forward.1 = (bf16[128,512]{1,0:T(8,128)(2,1)}, bf16[16,8,512]{2,1,0:T(8,128)(2,1)}, bf16[128,512]{1,0:T(8,128)(2,1)}, bf16[128,512]{1,0:T(8,128)(2,1)}, ...) custom-call(bf16[16,8,512]{2,1,0:T(8,128)(2,1)} %all_to_all.15.refs_0_, ...), custom_call_target="tpu_custom_call" | custom-call | flops 268435456 | bytes 3345408 | tf_op jit(solution)/shard_map/coarse_forward/pallas_call | solution.py:477
  20.6 3.5 %all-to-all-start.1 = ((bf16[16,8,512]{2,1,0:T(8,128)(2,1)}), bf16[16,8,512]{2,1,0:T(8,128)(2,1)S(1)}, u32[]{:S(2)}, u32[]{:S(2)}) async-start(bf16[16,8,512]{2,1,0:T(8,128)(2,1)} %get-tuple-element.76), calls=%async_computation.1 | async-start | bytes 262144 | tf_op jit(solution)/shard_map/all_to_all | solution.py:516
  24.1 2.6 %tiles.1 = (bf16[128,512]{1,0:T(8,128)(2,1)}, bf16[128,512]{1,0:T(8,128)(2,1)}, bf16[128,512]{1,0:T(8,128)(2,1)}, bf16[128,512]{1,0:T(8,128)(2,1)}) custom-call(bf16[256,512]{1,0:T(8,128)(2,1)} %refs_2_.1, s32[4,128]{1,0:T(4,128)} %bitcast.8), custom_call_target="tpu_custom_call" | custom-call | bytes 788480 | tf_op jit(solution)/shard_map/tiles/pallas_call | solution.py:477
  26.7 0.3 collective-permute-start
  27.0 1.7 %collective-permute-start.1 = (bf16[128,512]{1,0:T(8,128)(2,1)}, bf16[128,512]{1,0:T(8,128)(2,1)S(1)}, u32[]{:S(2)}, u32[]{:S(2)}) collective-permute-start(bf16[128,512]{1,0:T(8,128)(2,1)} %get-tuple-element.73), channel_id=1, source_target_pairs={{14,0},{15,1},{0,2},{1,3},{2,4},{3,5},{4,6},{5,7},{6,8},{7,9},{8,1... | collective-permute-start | bytes 393224 | tf_op jit(solution)/shard_map/ppermute | solution.py:508
  28.7 4.0 %collective-permute-start.2 = (bf16[128,512]{1,0:T(8,128)(2,1)}, bf16[128,512]{1,0:T(8,128)(2,1)S(1)}, u32[]{:S(2)}, u32[]{:S(2)}) collective-permute-start(bf16[128,512]{1,0:T(8,128)(2,1)} %get-tuple-element.74), channel_id=1, source_target_pairs={{1,0},{2,1},{3,2},{4,3},{5,4},{6,5},{7,6},{8,7},{9,8},{10,9},{11,1... | collective-permute-start | bytes 393224 | tf_op jit(solution)/shard_map/ppermute | solution.py:508
  32.7 0.4 collective-permute-start.3
  33.7 1.0 collective-permute-done.refs_3_
  34.7 1.7 %collective-permute-done.1.refs_4_ = bf16[128,512]{1,0:T(8,128)(2,1)S(1)} collective-permute-done((bf16[128,512]{1,0:T(8,128)(2,1)}, bf16[128,512]{1,0:T(8,128)(2,1)S(1)}, u32[]{:S(2)}, u32[]{:S(2)}) %collective-permute-start.1) | collective-permute-done | bytes 131104 | tf_op jit(solution)/shard_map/ppermute | solution.py:508
  36.4 0.0 collective-permute-done.2.refs_5_
  36.4 4.7 %collective-permute-done.3.refs_6_ = bf16[128,512]{1,0:T(8,128)(2,1)S(1)} collective-permute-done((bf16[128,512]{1,0:T(8,128)(2,1)}, bf16[128,512]{1,0:T(8,128)(2,1)S(1)}, u32[]{:S(2)}, u32[]{:S(2)}) %collective-permute-start.3) | collective-permute-done | bytes 131104 | tf_op jit(solution)/shard_map/ppermute | solution.py:508
  41.0 0.0 all-to-all-done.1.refs_13_
  41.1 0.6 copy-done.12
  41.7 0.0 copy-done.7
  41.7 9.4 %fine_and_node.1 = (bf16[512,512]{1,0:T(8,128)(2,1)}, bf16[512,512]{1,0:T(8,128)(2,1)}, bf16[512,512]{1,0:T(8,128)(2,1)}, bf16[512,512]{1,0:T(8,128)(2,1)}, bf16...) custom-call(s32[1]{0:T(128)S(6)} %copy.42.refs_0_, ...), custom_call_target="tpu_custom_call" | custom-call | flops 3087007744 | bytes 11542536 | tf_op jit(solution)/shard_map/fine_and_node/pallas_call | solution.py:477
  51.1 0.1 collective-permute-start.4
  51.2 2.5 %collective-permute-done.4 = bf16[8,96,512]{2,1,0:T(8,128)(2,1)S(1)} collective-permute-done((bf16[8,96,512]{2,1,0:T(8,128)(2,1)}, bf16[8,96,512]{2,1,0:T(8,128)(2,1)S(1)}, u32[]{:S(2)}, u32[]{:S(2)}) %collective-permute-start.4) | collective-permute-done | bytes 786464 | tf_op jit(solution)/shard_map/ppermute | solution.py:512
  53.7 1.3 %convert_add_fusion.1 = (f32[4,96,512]{2,1,0:T(8,128)S(1)}, bf16[4,96,512]{2,1,0:T(8,128)(2,1)S(1)}) fusion(bf16[8,96,512]{2,1,0:T(8,128)(2,1)S(1)} %collective-permute-done.4, bf16[8,96,512]{2,1,0:T(8,128)(2,1)} %get-tuple-element.97), kind=kLoop, calls=%fused_computation.2 | loop fusion | flops 1376256 | bytes 2752512 | tf_op jit(solution)/shard_map/add | solution.py:522
  55.0 0.1 collective-permute-start.5
  55.1 4.7 %all-to-all-start.2 = ((bf16[16,8,512]{2,1,0:T(8,128)(2,1)}), bf16[16,8,512]{2,1,0:T(8,128)(2,1)S(1)}, u32[]{:S(2)}, u32[]{:S(2)}) async-start(bf16[16,8,512]{2,1,0:T(8,128)(2,1)} %get-tuple-element.80), calls=%async_computation.2 | async-start | bytes 262144 | tf_op jit(solution)/shard_map/all_to_all | solution.py:516
  59.8 6.4 %fine_backward.1 = (bf16[512,512]{1,0:T(8,128)(2,1)}, bf16[512,512]{1,0:T(8,128)(2,1)}, bf16[512,512]{1,0:T(8,128)(2,1)}, f32[256,512]{1,0:T(8,128)}, bf16[128,5...) custom-call(s32[1]{0:T(128)S(6)} %copy.42.refs_0_, ...), custom_call_target="tpu_custom_call" | custom-call | flops 1744830464 | bytes 7346180 | tf_op jit(solution)/shard_map/fine_backward/pallas_call | solution.py:477
  66.2 4.4 %collective-permute-start.10 = (bf16[128,512]{1,0:T(8,128)(2,1)}, bf16[128,512]{1,0:T(8,128)(2,1)S(1)}, u32[]{:S(2)}, u32[]{:S(2)}) collective-permute-start(bf16[128,512]{1,0:T(8,128)(2,1)} %get-tuple-element.107), channel_id=1, source_target_pairs={{1,0},{2,1},{3,2},{4,3},{5,4},{6,5},{7,6},{8,7},{9,8},{10,9},{11,1... | collective-permute-start | bytes 393224 | tf_op jit(solution)/shard_map/ppermute | solution.py:508
  70.7 0.6 collective-permute-start.11
  71.2 0.0 collective-permute-start.12
  71.2 1.5 %collective-permute-start.13 = (bf16[128,512]{1,0:T(8,128)(2,1)}, bf16[128,512]{1,0:T(8,128)(2,1)S(1)}, u32[]{:S(2)}, u32[]{:S(2)}) collective-permute-start(bf16[128,512]{1,0:T(8,128)(2,1)} %get-tuple-element.110), channel_id=1, source_target_pairs={{14,0},{15,1},{0,2},{1,3},{2,4},{3,5},{4,6},{5,7},{6,8},{7,9},{8,1... | collective-permute-start | bytes 393224 | tf_op jit(solution)/shard_map/ppermute | solution.py:508
  72.7 0.0 all-to-all-done.2.refs_2_
  72.7 0.0 collective-permute-done.5.refs_21_.taken_ref
  72.7 0.6 copy-done.8
  73.4 0.1 copy-done.2
  73.5 6.8 %coarse_backward.1 = (bf16[128,512]{1,0:T(8,128)(2,1)}, bf16[8,96,512]{2,1,0:T(8,128)(2,1)}, bf16[8,96,512]{2,1,0:T(8,128)(2,1)}, bf16[8,48,512]{2,1,0:T(8,128)(2,1)}, bf16[8,48,512]{2,1,0:T(8,128)(2,1)}) custom-call(s32[1]{0:T(128)} %bitcast.refs_1_.refs_0_, s32[1,128]{1,0:T(1,128)} %bitcast.17, bf16[16,8,512]{2,1,0:T(8,128)(2,1)} %copy-done.8, ...), custom_call_target="tpu_custom_call" | custom-call | flops 1879048192 | bytes 9243652 | tf_op jit(solution)/shard_map/coarse_backward/pallas_call | solution.py:477
  80.3 0.0 collective-permute-done.11.refs_2_
  80.3 0.0 collective-permute-done.12.refs_3_
  80.3 0.2 collective-permute-done.13.refs_4_
  80.5 1.1 %copy-done = bf16[8,96,512]{2,1,0:T(8,128)(2,1)S(1)} copy-done((bf16[8,96,512]{2,1,0:T(8,128)(2,1)S(1)}, bf16[8,96,512]{2,1,0:T(8,128)(2,1)}, u32[]{:S(2)}) %copy-start) | copy-done | bytes 786456
  81.6 0.7 collective-permute-start.14
  82.3 0.1 collective-permute-start.6
  82.4 2.3 %collective-permute-done.14 = bf16[8,96,512]{2,1,0:T(8,128)(2,1)S(1)} collective-permute-done((bf16[8,96,512]{2,1,0:T(8,128)(2,1)S(1)}, bf16[8,96,512]{2,1,0:T(8,128)(2,1)S(1)}, u32[]{:S(2)}, u32[]{:S(2)}) %collective-permute-start.14) | collective-permute-done | bytes 786464 | tf_op jit(solution)/shard_map/ppermute | solution.py:512
  84.6 0.2 add_convert_fusion
  84.9 0.1 collective-permute-start.15
  84.9 0.0 collective-permute-done.6
  85.0 0.1 add_convert_fusion.2
  85.1 1.0 collective-permute-start.7
  86.1 0.1 halving.7
  86.1 1.2 %collective-permute-start.9 = (bf16[2,96,512]{2,1,0:T(8,128)(2,1)S(1)}, bf16[2,96,512]{2,1,0:T(8,128)(2,1)S(1)}, u32[]{:S(2)}, u32[]{:S(2)}) collective-permute-start(bf16[2,96,512]{2,1,0:T(8,128)(2,1)S(1)} %get-tuple-element.104), channel_id=1, source_target_pairs={{0,4},{1,5},{2,6},{3,7},{4,0},{5,1},{6,2},{7,3},{8,12},{9,13},{10,... | collective-permute-start | bytes 589832 | tf_op jit(solution)/shard_map/ppermute | solution.py:512
  87.3 9.0 %collective-permute-done.15.taken_ref = bf16[4,96,512]{2,1,0:T(8,128)(2,1)S(1)} collective-permute-done((bf16[4,96,512]{2,1,0:T(8,128)(2,1)S(1)}, bf16[4,96,512]{2,1,0:T(8,128)(2,1)S(1)}, u32[]{:S(2)}, u32[]{:S(2)}) %collective-permute-start.15) | collective-permute-done | bytes 393248 | tf_op jit(solution)/shard_map/ppermute | solution.py:512
  96.3 0.1 halving.8
  96.4 0.0 copy-start.4
  96.4 0.1 collective-permute-start.16
  96.5 0.0 collective-permute-done.7.taken_ref
  96.6 3.4 %collective-permute-start.8 = (bf16[2,48,512]{2,1,0:T(8,128)(2,1)S(1)}, bf16[2,48,512]{2,1,0:T(8,128)(2,1)S(1)}, u32[]{:S(2)}, u32[]{:S(2)}) collective-permute-start(bf16[2,48,512]{2,1,0:T(8,128)(2,1)S(1)} %get-tuple-element.102), channel_id=1, source_target_pairs={{0,8},{1,9},{2,10},{3,11},{4,12},{5,13},{6,14},{7,15},{8,0},{9,1},... | collective-permute-start | bytes 294920 | tf_op jit(solution)/shard_map/ppermute | solution.py:512
  100.0 0.0 collective-permute-done.9.taken_ref
  100.0 0.1 collective-permute-start.19
  100.1 3.8 %collective-permute-done.8.taken_ref = bf16[2,48,512]{2,1,0:T(8,128)(2,1)S(1)} collective-permute-done((bf16[2,48,512]{2,1,0:T(8,128)(2,1)S(1)}, bf16[2,48,512]{2,1,0:T(8,128)(2,1)S(1)}, u32[]{:S(2)}, u32[]{:S(2)}) %collective-permute-start.8) | collective-permute-done | bytes 98336 | tf_op jit(solution)/shard_map/ppermute | solution.py:512
  103.9 2.5 %collective-permute-done.16.taken_ref = bf16[2,96,512]{2,1,0:T(8,128)(2,1)S(1)} collective-permute-done((bf16[2,96,512]{2,1,0:T(8,128)(2,1)S(1)}, bf16[2,96,512]{2,1,0:T(8,128)(2,1)S(1)}, u32[]{:S(2)}, u32[]{:S(2)}) %collective-permute-start.16) | collective-permute-done | bytes 196640 | tf_op jit(solution)/shard_map/ppermute | solution.py:512
  106.4 1.0 collective-permute-start.17
  107.4 0.7 collective-permute-start.18
  108.1 0.4 node_gradient.1.refs_4_
  108.6 2.0 %collective-permute-done.19.refs_1_ = bf16[1,96,512]{2,1,0:T(8,128)(2,1)S(1)} collective-permute-done((bf16[1,96,512]{2,1,0:T(8,128)(2,1)S(1)}, bf16[1,96,512]{2,1,0:T(8,128)(2,1)S(1)}, u32[]{:S(2)}, u32[]{:S(2)}) %collective-permute-start.19) | collective-permute-done | bytes 98336 | tf_op jit(solution)/shard_map/ppermute | solution.py:512
  110.6 0.7 last_sum.3
  111.3 0.3 collective-permute-done.18.refs_3_
  111.5 0.6 collective-permute-done.17.refs_1_
  112.1 0.8 last_sum.2
  (27 shorter events, 0.2 us)
Async XLA Ops:
  20.6 20.5 %all-to-all-start.1 = ((bf16[16,8,512]{2,1,0:T(8,128)(2,1)}), bf16[16,8,512]{2,1,0:T(8,128)(2,1)S(1)}, u32[]{:S(2)}, u32[]{:S(2)}) async-start(bf16[16,8,512]{2,1,0:T(8,128)(2,1)} %get-tuple-element.76), calls=%async_computation.1 | async-start | bytes 262144 | tf_op jit(solution)/shard_map/all_to_all | solution.py:516
  26.7 8.0 %collective-permute-start = (bf16[128,512]{1,0:T(8,128)(2,1)}, bf16[128,512]{1,0:T(8,128)(2,1)S(1)}, u32[]{:S(2)}, u32[]{:S(2)}) collective-permute-start(bf16[128,512]{1,0:T(8,128)(2,1)} %get-tuple-element.72), channel_id=1, source_target_pairs={{15,0},{0,1},{1,2},{2,3},{3,4},{4,5},{5,6},{6,7},{7,8},{8,9},{9,10... | collective-permute-start | bytes 393224 | tf_op jit(solution)/shard_map/ppermute | solution.py:508
  27.0 9.4 %collective-permute-start.1 = (bf16[128,512]{1,0:T(8,128)(2,1)}, bf16[128,512]{1,0:T(8,128)(2,1)S(1)}, u32[]{:S(2)}, u32[]{:S(2)}) collective-permute-start(bf16[128,512]{1,0:T(8,128)(2,1)} %get-tuple-element.73), channel_id=1, source_target_pairs={{14,0},{15,1},{0,2},{1,3},{2,4},{3,5},{4,6},{5,7},{6,8},{7,9},{8,1... | collective-permute-start | bytes 393224 | tf_op jit(solution)/shard_map/ppermute | solution.py:508
  28.7 7.7 %collective-permute-start.2 = (bf16[128,512]{1,0:T(8,128)(2,1)}, bf16[128,512]{1,0:T(8,128)(2,1)S(1)}, u32[]{:S(2)}, u32[]{:S(2)}) collective-permute-start(bf16[128,512]{1,0:T(8,128)(2,1)} %get-tuple-element.74), channel_id=1, source_target_pairs={{1,0},{2,1},{3,2},{4,3},{5,4},{6,5},{7,6},{8,7},{9,8},{10,9},{11,1... | collective-permute-start | bytes 393224 | tf_op jit(solution)/shard_map/ppermute | solution.py:508
  32.7 8.4 %collective-permute-start.3 = (bf16[128,512]{1,0:T(8,128)(2,1)}, bf16[128,512]{1,0:T(8,128)(2,1)S(1)}, u32[]{:S(2)}, u32[]{:S(2)}) collective-permute-start(bf16[128,512]{1,0:T(8,128)(2,1)} %get-tuple-element.75), channel_id=1, source_target_pairs={{2,0},{3,1},{4,2},{5,3},{6,4},{7,5},{8,6},{9,7},{10,8},{11,9},{12,... | collective-permute-start | bytes 393224 | tf_op jit(solution)/shard_map/ppermute | solution.py:508
  34.7 6.4 %copy-start.9 = (bf16[128,512]{1,0:T(8,128)(2,1)}, bf16[128,512]{1,0:T(8,128)(2,1)S(1)}, u32[]{:S(2)}) copy-start(bf16[128,512]{1,0:T(8,128)(2,1)S(1)} %collective-permute-done.refs_3_) | copy-start | bytes 393220
  36.4 4.7 %copy-start.10 = (bf16[128,512]{1,0:T(8,128)(2,1)}, bf16[128,512]{1,0:T(8,128)(2,1)S(1)}, u32[]{:S(2)}) copy-start(bf16[128,512]{1,0:T(8,128)(2,1)S(1)} %collective-permute-done.1.refs_4_) | copy-start | bytes 393220
  36.4 4.7 %copy-start.11 = (bf16[128,512]{1,0:T(8,128)(2,1)}, bf16[128,512]{1,0:T(8,128)(2,1)S(1)}, u32[]{:S(2)}) copy-start(bf16[128,512]{1,0:T(8,128)(2,1)S(1)} %collective-permute-done.2.refs_5_) | copy-start | bytes 393220
  41.0 0.7 copy-start.12
  41.1 0.7 copy-start.7
  51.1 2.6 %collective-permute-start.4 = (bf16[8,96,512]{2,1,0:T(8,128)(2,1)}, bf16[8,96,512]{2,1,0:T(8,128)(2,1)S(1)}, u32[]{:S(2)}, u32[]{:S(2)}) collective-permute-start(bf16[8,96,512]{2,1,0:T(8,128)(2,1)} %get-tuple-element.98), channel_id=1, source_target_pairs={{0,1},{1,0},{2,3},{3,2},{4,5},{5,4},{6,7},{7,6},{8,9},{9,8},{10,11... | collective-permute-start | bytes 2359304 | tf_op jit(solution)/shard_map/ppermute | solution.py:512
  55.0 17.7 %collective-permute-start.5 = (bf16[4,96,512]{2,1,0:T(8,128)(2,1)S(1)}, bf16[4,96,512]{2,1,0:T(8,128)(2,1)S(1)}, u32[]{:S(2)}, u32[]{:S(2)}) collective-permute-start(bf16[4,96,512]{2,1,0:T(8,128)(2,1)S(1)} %get-tuple-element.137), channel_id=1, source_target_pairs={{0,2},{1,3},{2,0},{3,1},{4,6},{5,7},{6,4},{7,5},{8,10},{9,11},{10,... | collective-permute-start | bytes 1179656 | tf_op jit(solution)/shard_map/ppermute | solution.py:512
  55.1 17.6 %all-to-all-start.2 = ((bf16[16,8,512]{2,1,0:T(8,128)(2,1)}), bf16[16,8,512]{2,1,0:T(8,128)(2,1)S(1)}, u32[]{:S(2)}, u32[]{:S(2)}) async-start(bf16[16,8,512]{2,1,0:T(8,128)(2,1)} %get-tuple-element.80), calls=%async_computation.2 | async-start | bytes 262144 | tf_op jit(solution)/shard_map/all_to_all | solution.py:516
  66.2 14.1 %collective-permute-start.10 = (bf16[128,512]{1,0:T(8,128)(2,1)}, bf16[128,512]{1,0:T(8,128)(2,1)S(1)}, u32[]{:S(2)}, u32[]{:S(2)}) collective-permute-start(bf16[128,512]{1,0:T(8,128)(2,1)} %get-tuple-element.107), channel_id=1, source_target_pairs={{1,0},{2,1},{3,2},{4,3},{5,4},{6,5},{7,6},{8,7},{9,8},{10,9},{11,1... | collective-permute-start | bytes 393224 | tf_op jit(solution)/shard_map/ppermute | solution.py:508
  70.7 9.6 %collective-permute-start.11 = (bf16[128,512]{1,0:T(8,128)(2,1)}, bf16[128,512]{1,0:T(8,128)(2,1)S(1)}, u32[]{:S(2)}, u32[]{:S(2)}) collective-permute-start(bf16[128,512]{1,0:T(8,128)(2,1)} %get-tuple-element.108), channel_id=1, source_target_pairs={{2,0},{3,1},{4,2},{5,3},{6,4},{7,5},{8,6},{9,7},{10,8},{11,9},{12,... | collective-permute-start | bytes 393224 | tf_op jit(solution)/shard_map/ppermute | solution.py:508
  71.2 9.1 %collective-permute-start.12 = (bf16[128,512]{1,0:T(8,128)(2,1)}, bf16[128,512]{1,0:T(8,128)(2,1)S(1)}, u32[]{:S(2)}, u32[]{:S(2)}) collective-permute-start(bf16[128,512]{1,0:T(8,128)(2,1)} %get-tuple-element.109), channel_id=1, source_target_pairs={{15,0},{0,1},{1,2},{2,3},{3,4},{4,5},{5,6},{6,7},{7,8},{8,9},{9,10... | collective-permute-start | bytes 393224 | tf_op jit(solution)/shard_map/ppermute | solution.py:508
  71.2 9.3 %collective-permute-start.13 = (bf16[128,512]{1,0:T(8,128)(2,1)}, bf16[128,512]{1,0:T(8,128)(2,1)S(1)}, u32[]{:S(2)}, u32[]{:S(2)}) collective-permute-start(bf16[128,512]{1,0:T(8,128)(2,1)} %get-tuple-element.110), channel_id=1, source_target_pairs={{14,0},{15,1},{0,2},{1,3},{2,4},{3,5},{4,6},{5,7},{6,8},{7,9},{8,1... | collective-permute-start | bytes 393224 | tf_op jit(solution)/shard_map/ppermute | solution.py:508
  72.7 0.7 copy-start.8
  72.7 0.8 copy-start.2
  80.5 1.1 %copy-start = (bf16[8,96,512]{2,1,0:T(8,128)(2,1)S(1)}, bf16[8,96,512]{2,1,0:T(8,128)(2,1)}, u32[]{:S(2)}) copy-start(bf16[8,96,512]{2,1,0:T(8,128)(2,1)} %get-tuple-element.106.refs_0_) | copy-start | bytes 2359300
  81.6 3.0 %copy-start.5 = (bf16[8,96,512]{2,1,0:T(8,128)(2,1)S(1)}, bf16[8,96,512]{2,1,0:T(8,128)(2,1)}, u32[]{:S(2)}) copy-start(bf16[8,96,512]{2,1,0:T(8,128)(2,1)} %get-tuple-element.105) | copy-start | bytes 2359300
  81.6 3.4 %copy-start.6 = (bf16[8,48,512]{2,1,0:T(8,128)(2,1)S(1)}, bf16[8,48,512]{2,1,0:T(8,128)(2,1)}, u32[]{:S(2)}) copy-start(bf16[8,48,512]{2,1,0:T(8,128)(2,1)} %get-tuple-element.99) | copy-start | bytes 1179652
  81.6 3.0 %collective-permute-start.14 = (bf16[8,96,512]{2,1,0:T(8,128)(2,1)S(1)}, bf16[8,96,512]{2,1,0:T(8,128)(2,1)S(1)}, u32[]{:S(2)}, u32[]{:S(2)}) collective-permute-start(bf16[8,96,512]{2,1,0:T(8,128)(2,1)S(1)} %get-tuple-element.111), channel_id=1, source_target_pairs={{0,1},{1,0},{2,3},{3,2},{4,5},{5,4},{6,7},{7,6},{8,9},{9,8},{10,11... | collective-permute-start | bytes 2359304 | tf_op jit(solution)/shard_map/ppermute | solution.py:512
  82.3 2.7 %collective-permute-start.6 = (bf16[8,48,512]{2,1,0:T(8,128)(2,1)}, bf16[8,48,512]{2,1,0:T(8,128)(2,1)S(1)}, u32[]{:S(2)}, u32[]{:S(2)}) collective-permute-start(bf16[8,48,512]{2,1,0:T(8,128)(2,1)} %get-tuple-element.100), channel_id=1, source_target_pairs={{0,1},{1,0},{2,3},{3,2},{4,5},{5,4},{6,7},{7,6},{8,9},{9,8},{10,11... | collective-permute-start | bytes 1179656 | tf_op jit(solution)/shard_map/ppermute | solution.py:512
  84.6 1.5 %copy-start.3 = (bf16[4,96,512]{2,1,0:T(8,128)(2,1)S(1)}, bf16[4,96,512]{2,1,0:T(8,128)(2,1)}, u32[]{:S(2)}) copy-start(bf16[4,96,512]{2,1,0:T(8,128)(2,1)} %copy-done.2) | copy-start | bytes 1179652
  84.9 11.5 %collective-permute-start.15 = (bf16[4,96,512]{2,1,0:T(8,128)(2,1)S(1)}, bf16[4,96,512]{2,1,0:T(8,128)(2,1)S(1)}, u32[]{:S(2)}, u32[]{:S(2)}) collective-permute-start(bf16[4,96,512]{2,1,0:T(8,128)(2,1)S(1)} %get-tuple-element.134), channel_id=1, source_target_pairs={{0,2},{1,3},{2,0},{3,1},{4,6},{5,7},{6,4},{7,5},{8,10},{9,11},{10,... | collective-permute-start | bytes 1179656 | tf_op jit(solution)/shard_map/ppermute | solution.py:512
  85.1 11.4 %collective-permute-start.7 = (bf16[4,48,512]{2,1,0:T(8,128)(2,1)S(1)}, bf16[4,48,512]{2,1,0:T(8,128)(2,1)S(1)}, u32[]{:S(2)}, u32[]{:S(2)}) collective-permute-start(bf16[4,48,512]{2,1,0:T(8,128)(2,1)S(1)} %get-tuple-element.138), channel_id=1, source_target_pairs={{0,4},{1,5},{2,6},{3,7},{4,0},{5,1},{6,2},{7,3},{8,12},{9,13},{10,... | collective-permute-start | bytes 589832 | tf_op jit(solution)/shard_map/ppermute | solution.py:512
  86.1 13.8 %collective-permute-start.9 = (bf16[2,96,512]{2,1,0:T(8,128)(2,1)S(1)}, bf16[2,96,512]{2,1,0:T(8,128)(2,1)S(1)}, u32[]{:S(2)}, u32[]{:S(2)}) collective-permute-start(bf16[2,96,512]{2,1,0:T(8,128)(2,1)S(1)} %get-tuple-element.104), channel_id=1, source_target_pairs={{0,4},{1,5},{2,6},{3,7},{4,0},{5,1},{6,2},{7,3},{8,12},{9,13},{10,... | collective-permute-start | bytes 589832 | tf_op jit(solution)/shard_map/ppermute | solution.py:512
  96.4 11.7 %copy-start.1 = (f32[256,512]{1,0:T(8,128)S(1)}, f32[256,512]{1,0:T(8,128)}, u32[]{:S(2)}) copy-start(f32[256,512]{1,0:T(8,128)} %get-tuple-element.120.own_ref) | copy-start | bytes 1572868
  96.4 11.7 %copy-start.4 = (s32[1,4,128]{2,1,0:T(4,128)S(1)}, s32[1,4,128]{2,1,0:T(4,128)}, u32[]{:S(2)}) copy-start(s32[1,4,128]{2,1,0:T(4,128)} %param.25) | copy-start | bytes 6148
  96.4 10.0 %collective-permute-start.16 = (bf16[2,96,512]{2,1,0:T(8,128)(2,1)S(1)}, bf16[2,96,512]{2,1,0:T(8,128)(2,1)S(1)}, u32[]{:S(2)}, u32[]{:S(2)}) collective-permute-start(bf16[2,96,512]{2,1,0:T(8,128)(2,1)S(1)} %get-tuple-element.115), channel_id=1, source_target_pairs={{0,4},{1,5},{2,6},{3,7},{4,0},{5,1},{6,2},{7,3},{8,12},{9,13},{10,... | collective-permute-start | bytes 589832 | tf_op jit(solution)/shard_map/ppermute | solution.py:512
  96.6 7.3 %collective-permute-start.8 = (bf16[2,48,512]{2,1,0:T(8,128)(2,1)S(1)}, bf16[2,48,512]{2,1,0:T(8,128)(2,1)S(1)}, u32[]{:S(2)}, u32[]{:S(2)}) collective-permute-start(bf16[2,48,512]{2,1,0:T(8,128)(2,1)S(1)} %get-tuple-element.102), channel_id=1, source_target_pairs={{0,8},{1,9},{2,10},{3,11},{4,12},{5,13},{6,14},{7,15},{8,0},{9,1},... | collective-permute-start | bytes 294920 | tf_op jit(solution)/shard_map/ppermute | solution.py:512
  100.0 10.6 %collective-permute-start.19 = (bf16[1,96,512]{2,1,0:T(8,128)(2,1)S(1)}, bf16[1,96,512]{2,1,0:T(8,128)(2,1)S(1)}, u32[]{:S(2)}, u32[]{:S(2)}) collective-permute-start(bf16[1,96,512]{2,1,0:T(8,128)(2,1)S(1)} %get-tuple-element.131), channel_id=1, source_target_pairs={{0,8},{1,9},{2,10},{3,11},{4,12},{5,13},{6,14},{7,15},{8,0},{9,1},... | collective-permute-start | bytes 294920 | tf_op jit(solution)/shard_map/ppermute | solution.py:512
  106.4 5.7 %collective-permute-start.17 = (bf16[1,96,512]{2,1,0:T(8,128)(2,1)S(1)}, bf16[1,96,512]{2,1,0:T(8,128)(2,1)S(1)}, u32[]{:S(2)}, u32[]{:S(2)}) collective-permute-start(bf16[1,96,512]{2,1,0:T(8,128)(2,1)S(1)} %get-tuple-element.117), channel_id=1, source_target_pairs={{0,8},{1,9},{2,10},{3,11},{4,12},{5,13},{6,14},{7,15},{8,0},{9,1},... | collective-permute-start | bytes 294920 | tf_op jit(solution)/shard_map/ppermute | solution.py:512
  107.4 4.1 %collective-permute-start.18 = (bf16[1,48,512]{2,1,0:T(8,128)(2,1)S(1)}, bf16[1,48,512]{2,1,0:T(8,128)(2,1)S(1)}, u32[]{:S(2)}, u32[]{:S(2)}) collective-permute-start(bf16[1,48,512]{2,1,0:T(8,128)(2,1)S(1)} %get-tuple-element.119), channel_id=1, source_target_pairs={{0,2},{1,3},{2,0},{3,1},{4,6},{5,7},{6,4},{7,5},{8,10},{9,11},{10,... | collective-permute-start | bytes 147464 | tf_op jit(solution)/shard_map/ppermute | solution.py:512

commit v10 on v9

--- a/solution.py
+++ b/solution.py
@@ -164,6 +164,11 @@
     return steps[1:] + steps[:1]
 
 
+def x_then_far(peers):
+    steps = x_first(peers)
+    return steps[:1] + steps[:0:-1]
+
+
 def by_distance(me, peers, steps, sums, kept_ref, given_ref):
     for r in list(range(1, peers, 2)) + list(range(0, peers, 2)):
         if r == 0:
@@ -212,18 +217,7 @@
     g1_ref[width : 2 * width, :] = mm_tn(agg, back_pre)
     g2_ref[...] = mm_tn(hidden, back_out)
     if ordered:
-        by_distance(me_ref[0], spread_ref.shape[0], x_first(spread_ref.shape[0]), (g1_ref, g2_ref), kept_ref, given_ref)
-
-
-def fine_and_node_kernel(count_ref, me_ref, nodes_ref, *refs, slots, block, ordered):
-    edge_ins, node_ins = refs[: slots + 6], refs[slots + 6 : slots + 11]
-    edge_outs, node_outs = refs[slots + 11 : slots + 18], refs[slots + 18 : slots + 24]
-    space_ref, agg_ref, *scratch = refs[slots + 24 :]
-    fine_forward_kernel(
-        count_ref, nodes_ref, *edge_ins, edge_outs[0], agg_ref, *edge_outs[1:], space_ref, slots=slots, block=block
-    )
-    share_ref, *node_ins = node_ins
-    node_kernel(me_ref, nodes_ref, agg_ref, share_ref, *node_ins, *node_outs, *scratch, ordered=ordered)
+        by_distance(me_ref[0], spread_ref.shape[0], x_then_far(spread_ref.shape[0]), (g1_ref, g2_ref), kept_ref, given_ref)
 
 
 def fine_backward_kernel(
@@ -601,6 +595,15 @@
 
     block = 256 if fine % 256 == 0 else fine
     space_rows = own + slots * tile
+    new_fine, fine_agg, *fine_saved = call(
+        functools.partial(fine_forward_kernel, slots=slots, block=block), "fine_forward",
+        (edge_count, nodes, *received, fine_edges, fs, fr, edge_w1, edge_w2, eg),
+        [SM] + [VM] * (slots + 4) + [Rows(3), VM, VM],
+        [shape((fine, width), BF16), shape((own, width), F32)] + saved_shapes(fine),
+        scratch=[pltpu.VMEM((space_rows, width), BF16)],
+        flops=2 * fine * width * (4 * width + space_rows + 3 * own),
+    )
+
     def weight_shapes(w1, w2, more):
         if not ordered:
             return [shape(w1.shape, F32), shape(w2.shape, F32)], []
@@ -609,19 +612,13 @@
         return outs, [pltpu.VMEM(w1.shape, F32), pltpu.VMEM(w2.shape, F32)]
 
     sum_shapes, sum_scratch = weight_shapes(node_w1, node_w2, 0)
-    new_fine, *made = call(
-        functools.partial(fine_and_node_kernel, slots=slots, block=block, ordered=ordered), "fine_and_node",
-        (
-            edge_count, me, nodes, *received, fine_edges, fs, fr, edge_w1, edge_w2, eg,
-            share, d_nodes, node_w1, node_w2, ng,
-        ),
-        [SM, SM] + [VM] * (slots + 4) + [Rows(3)] + [VM] * 4 + [Rows(2), VM, VM],
-        [shape((fine, width), BF16)] + saved_shapes(fine)
-        + [shape((own, width), BF16), shape((own, width), F32), shape((own, width), BF16), every] + sum_shapes,
-        scratch=[pltpu.VMEM((space_rows, width), BF16)] + [pltpu.VMEM((own, width), F32)] * 2 + sum_scratch,
-        flops=2 * fine * width * (4 * width + space_rows + 3 * own) + 2 * own * width * width * 9,
-    )
-    fine_saved, (new_nodes, base, dagg, dagg_spread), node_parts = made[:6], made[6:10], made[10:]
+    new_nodes, base, dagg, dagg_spread, *node_parts = call(
+        functools.partial(node_kernel, ordered=ordered), "node_both",
+        (me, nodes, fine_agg, share, d_nodes, node_w1, node_w2, ng), [SM] + [VM] * 4 + [Rows(2), VM, VM],
+        [shape((own, width), BF16), shape((own, width), F32), shape((own, width), BF16), every] + sum_shapes,
+        scratch=[pltpu.VMEM((own, width), F32)] + sum_scratch,
+        flops=2 * own * width * width * 9,
+    )
     dagg_all = exchanged_with_all(dagg_spread, axis)
     if ordered:
         node_taken = exchanged(node_parts[1], axis, 1)
@@ -674,15 +671,15 @@
         given1, *returned = small_call(order_kernel, "order", (), [], (given1, *returned))
         taken1 = exchanged(given1, axis, 1)
         taken2 = exchanged(given2, axis, 1)
-        steps1, steps2 = x_first(peers), x_last(peers)
+        steps1, steps2, node_steps = x_first(peers), x_last(peers), x_then_far(peers)
         kept1, given1 = first_halving(kept1, taken1)
         taken1 = exchanged(given1, axis, steps1[0])
         kept2, given2 = first_halving(kept2, taken2)
         taken2 = exchanged(given2, axis, steps2[0])
         for k in range(1, len(steps1)):
-            passing = (kept1,) if k > 1 else ()
+            passing = (kept1,) if k == 1 else ()
             node_kept, given, *passing = halving(node_kept, node_taken, passing)
-            node_taken = exchanged(given, axis, steps1[k])
+            node_taken = exchanged(given, axis, node_steps[k])
             kept2, given2, *passing = halving(kept2, taken2, tuple(passing))
             taken2 = exchanged(given2, axis, steps2[k])
             kept1, given1 = halving(passing[0] if passing else kept1, taken1)

time: 114 us -> 106 us (0.930)
  blocking collectives: 15.2 us -> 0 us
  starting transfers between devices: 29.5 us -> 42.9 us
  waiting for transfers between devices: 30.4 us -> 20 us
  Pallas kernels: 31.4 us -> 34.5 us
  local copies, waits for them, and re-layouts: 3.31 us -> 5.34 us
    all_to_all x1 -> x0, blocking collectives: 15.2 us -> none  [exchanged_with_all(): return lax.all_to_all(blocks, axis, 0, 0)]
    all_to_all x2 -> x3, starting transfers between devices: 8.23 us -> 16.1 us  [exchanged_with_all(): return lax.all_to_all(blocks, axis, 0, 0)]
    ppermute x8, waiting for transfers between devices: 7.49 us -> 0.16 us  [passed_along(): return lax.ppermute(block, axis, route)]
    ppermute x12, starting transfers between devices: 8.42 us -> 13.9 us  [exchanged(): lax.ppermute(block, axis, [(i, i ^ distance) for i in range(lax.axis_size...]
    pallas_call x5 -> x6, Pallas kernels: 29.2 us -> 32.2 us  [call(): pl.pallas_call(functools.partial(staged_kernel, kernel, in_specs, out_spe...]
    ppermute x12, waiting for transfers between devices: 22.9 us -> 19.9 us  [exchanged(): lax.ppermute(block, axis, [(i, i ^ distance) for i in range(lax.axis_size...]
    unnamed x26 -> x28, local copies, waits for them, and re-layouts: 2.59 us -> 3.97 us
  transfers between devices with their start and end apart: 22 -> 23, of which waited for: 12 -> 9; matrix products, arithmetic and copies ran while one was open for 0% -> 0% of each run, Pallas kernels for 15% -> 26%
where the time goes in v10:
time: 106 us
  starting transfers between devices  42.9 us (40%)
  Pallas kernels  34.5 us (33%)
  waiting for transfers between devices  20 us (19%)
  local copies, waits for them, and re-layouts  5.34 us (5%)
  other arithmetic  1.6 us (2%)
  between operations  1.6 us (2%)
    pallas_call x6, Pallas kernels, call(): pl.pallas_call(functools.partial(staged_kernel, kernel, in_specs, out_spe...  32.2 us
    ppermute x12, waiting for transfers between devices, exchanged(): lax.ppermute(block, axis, [(i, i ^ distance) for i in range(lax.axis_size...  19.9 us
    all_to_all x3, starting transfers between devices, exchanged_with_all(): return lax.all_to_all(blocks, axis, 0, 0)  16.1 us
    ppermute x12, starting transfers between devices, exchanged(): lax.ppermute(block, axis, [(i, i ^ distance) for i in range(lax.axis_size...  13.9 us
    ppermute x8, starting transfers between devices, passed_along(): return lax.ppermute(block, axis, route)  12.9 us
    unnamed x28, local copies, waits for them, and re-layouts  3.97 us
    pallas_call x10, Pallas kernels, small_call(): pl.pallas_call(kernel, out_shape=tuple(outs), input_output_aliases={first...  2.21 us
  transfers between devices with their start and end apart: 23, of which 9 were waited for; matrix products, arithmetic and copies ran while one was open for 0% of the time, Pallas kernels for 26%

profile of v10, /device:TPU:0, one launch (start us, length us, event | category | flops | bytes accessed | tf_op | source)
XLA Modules:
  0.0 105.9 jit_solution(7918672204022272893)
XLA Ops:
  0.6 0.7 slice.39
  1.3 0.7 broadcast_in_dim.2
  2.0 7.4 %all-to-all-start = ((bf16[16,8,512]{2,1,0:T(8,128)(2,1)}), bf16[16,8,512]{2,1,0:T(8,128)(2,1)S(1)}, u32[]{:S(2)}, u32[]{:S(2)}) async-start(bf16[16,8,512]{2,1,0:T(8,128)(2,1)} %broadcast_in_dim.2), calls=%async_computation | async-start | bytes 262144 | tf_op jit(solution)/shard_map/all_to_all | solution.py:510
  9.4 2.6 %tiles.1 = (bf16[128,512]{1,0:T(8,128)(2,1)}, bf16[128,512]{1,0:T(8,128)(2,1)}, bf16[128,512]{1,0:T(8,128)(2,1)}, bf16[128,512]{1,0:T(8,128)(2,1)}) custom-call(bf16[256,512]{1,0:T(8,128)(2,1)} %refs_1_.5, s32[4,128]{1,0:T(4,128)} %bitcast.8), custom_call_target="tpu_custom_call" | custom-call | bytes 788480 | tf_op jit(solution)/shard_map/tiles/pallas_call | solution.py:471
  12.0 0.5 collective-permute-start
  12.4 1.7 %collective-permute-start.1 = (bf16[128,512]{1,0:T(8,128)(2,1)}, bf16[128,512]{1,0:T(8,128)(2,1)S(1)}, u32[]{:S(2)}, u32[]{:S(2)}) collective-permute-start(bf16[128,512]{1,0:T(8,128)(2,1)} %get-tuple-element.74), channel_id=1, source_target_pairs={{14,0},{15,1},{0,2},{1,3},{2,4},{3,5},{4,6},{5,7},{6,8},{7,9},{8,1... | collective-permute-start | bytes 393224 | tf_op jit(solution)/shard_map/ppermute | solution.py:502
  14.1 4.0 %collective-permute-start.2 = (bf16[128,512]{1,0:T(8,128)(2,1)}, bf16[128,512]{1,0:T(8,128)(2,1)S(1)}, u32[]{:S(2)}, u32[]{:S(2)}) collective-permute-start(bf16[128,512]{1,0:T(8,128)(2,1)} %get-tuple-element.75), channel_id=1, source_target_pairs={{1,0},{2,1},{3,2},{4,3},{5,4},{6,5},{7,6},{8,7},{9,8},{10,9},{11,1... | collective-permute-start | bytes 393224 | tf_op jit(solution)/shard_map/ppermute | solution.py:502
  18.1 0.3 collective-permute-start.3
  18.4 0.0 all-to-all-done.refs_0_
  18.4 0.7 copy-done.6
  19.0 4.0 %coarse_forward.1 = (bf16[128,512]{1,0:T(8,128)(2,1)}, bf16[16,8,512]{2,1,0:T(8,128)(2,1)}, bf16[128,512]{1,0:T(8,128)(2,1)}, bf16[128,512]{1,0:T(8,128)(2,1)}, ...) custom-call(bf16[16,8,512]{2,1,0:T(8,128)(2,1)} %copy-done.6, ...), custom_call_target="tpu_custom_call" | custom-call | flops 268435456 | bytes 3345408 | tf_op jit(solution)/shard_map/coarse_forward/pallas_call | solution.py:471
  23.0 4.0 %all-to-all-start.1 = ((bf16[16,8,512]{2,1,0:T(8,128)(2,1)}), bf16[16,8,512]{2,1,0:T(8,128)(2,1)S(1)}, u32[]{:S(2)}, u32[]{:S(2)}) async-start(bf16[16,8,512]{2,1,0:T(8,128)(2,1)} %get-tuple-element.78), calls=%async_computation.1 | async-start | bytes 262144 | tf_op jit(solution)/shard_map/all_to_all | solution.py:510
  27.7 0.0 copy-start.10
  27.8 0.0 collective-permute-done.1.refs_3_
  27.8 0.0 copy-start.11
  27.8 0.0 copy-start.12
  27.8 0.0 copy-start.13
  27.8 0.6 copy-done.10
  28.4 0.0 copy-done.11
  28.4 0.0 copy-done.12
  28.5 0.0 copy-done.13
  28.5 6.7 %fine_forward.1 = (bf16[512,512]{1,0:T(8,128)(2,1)}, f32[256,512]{1,0:T(8,128)}, bf16[512,512]{1,0:T(8,128)(2,1)}, bf16[512,512]{1,0:T(8,128)(2,1)}, bf16[512,51...) custom-call(s32[1]{0:T(128)S(6)} %copy.42.refs_0_, ...), custom_call_target="tpu_custom_call" | custom-call | flops 1879048192 | bytes 7346180 | tf_op jit(solution)/shard_map/fine_forward/pallas_call | solution.py:471
  35.3 0.0 copy-start.9
  35.3 0.6 copy-done.9
  35.9 5.8 %node_both.1 = (bf16[256,512]{1,0:T(8,128)(2,1)}, f32[256,512]{1,0:T(8,128)}, bf16[256,512]{1,0:T(8,128)(2,1)}, bf16[16,8,512]{2,1,0:T(8,128)(2,1)}, bf16[8,96,5...) custom-call(s32[1]{0:T(128)} %bitcast.refs_0_, bf16[256,512]{1,0:T(8,128)(2,1)} %refs_1_.5, ...), custom_call_target="tpu_custom_call" | custom-call | flops 1207959552 | bytes 5507076 | tf_op jit(solution)/shard_map/node_both/pallas_call | solution.py:471
  41.7 0.5 collective-permute-start.4
  42.2 2.1 %collective-permute-done.4 = bf16[8,96,512]{2,1,0:T(8,128)(2,1)S(1)} collective-permute-done((bf16[8,96,512]{2,1,0:T(8,128)(2,1)}, bf16[8,96,512]{2,1,0:T(8,128)(2,1)S(1)}, u32[]{:S(2)}, u32[]{:S(2)}) %collective-permute-start.4) | collective-permute-done | bytes 786464 | tf_op jit(solution)/shard_map/ppermute | solution.py:506
  44.4 1.3 %convert_add_fusion.1 = (f32[4,96,512]{2,1,0:T(8,128)S(1)}, bf16[4,96,512]{2,1,0:T(8,128)(2,1)S(1)}) fusion(bf16[8,96,512]{2,1,0:T(8,128)(2,1)S(1)} %collective-permute-done.4, bf16[8,96,512]{2,1,0:T(8,128)(2,1)} %get-tuple-element.99), kind=kLoop, calls=%fused_computation.2 | loop fusion | flops 1376256 | bytes 2752512 | tf_op jit(solution)/shard_map/add | solution.py:516
  45.7 1.9 %collective-permute-start.5 = (bf16[4,96,512]{2,1,0:T(8,128)(2,1)S(1)}, bf16[4,96,512]{2,1,0:T(8,128)(2,1)S(1)}, u32[]{:S(2)}, u32[]{:S(2)}) collective-permute-start(bf16[4,96,512]{2,1,0:T(8,128)(2,1)S(1)} %get-tuple-element.139), channel_id=1, source_target_pairs={{0,2},{1,3},{2,0},{3,1},{4,6},{5,7},{6,4},{7,5},{8,10},{9,11},{10,... | collective-permute-start | bytes 1179656 | tf_op jit(solution)/shard_map/ppermute | solution.py:506
  47.6 4.7 %all-to-all-start.2 = ((bf16[16,8,512]{2,1,0:T(8,128)(2,1)}), bf16[16,8,512]{2,1,0:T(8,128)(2,1)S(1)}, u32[]{:S(2)}, u32[]{:S(2)}) async-start(bf16[16,8,512]{2,1,0:T(8,128)(2,1)} %get-tuple-element.82), calls=%async_computation.2 | async-start | bytes 262144 | tf_op jit(solution)/shard_map/all_to_all | solution.py:510
  52.3 6.4 %fine_backward.1 = (bf16[512,512]{1,0:T(8,128)(2,1)}, bf16[512,512]{1,0:T(8,128)(2,1)}, bf16[512,512]{1,0:T(8,128)(2,1)}, f32[256,512]{1,0:T(8,128)}, bf16[128,5...) custom-call(s32[1]{0:T(128)S(6)} %copy.42.refs_0_, ...), custom_call_target="tpu_custom_call" | custom-call | flops 1744830464 | bytes 7346180 | tf_op jit(solution)/shard_map/fine_backward/pallas_call | solution.py:471
  58.7 4.4 %collective-permute-start.8 = (bf16[128,512]{1,0:T(8,128)(2,1)}, bf16[128,512]{1,0:T(8,128)(2,1)S(1)}, u32[]{:S(2)}, u32[]{:S(2)}) collective-permute-start(bf16[128,512]{1,0:T(8,128)(2,1)} %get-tuple-element.105), channel_id=1, source_target_pairs={{1,0},{2,1},{3,2},{4,3},{5,4},{6,5},{7,6},{8,7},{9,8},{10,9},{11,1... | collective-permute-start | bytes 393224 | tf_op jit(solution)/shard_map/ppermute | solution.py:502
  63.1 0.6 collective-permute-start.9
  63.7 1.5 %collective-permute-start.11 = (bf16[128,512]{1,0:T(8,128)(2,1)}, bf16[128,512]{1,0:T(8,128)(2,1)S(1)}, u32[]{:S(2)}, u32[]{:S(2)}) collective-permute-start(bf16[128,512]{1,0:T(8,128)(2,1)} %get-tuple-element.108), channel_id=1, source_target_pairs={{14,0},{15,1},{0,2},{1,3},{2,4},{3,5},{4,6},{5,7},{6,8},{7,9},{8,1... | collective-permute-start | bytes 393224 | tf_op jit(solution)/shard_map/ppermute | solution.py:502
  65.2 0.6 copy-done.8
  65.8 0.1 copy-done.2
  66.0 6.8 %coarse_backward.1 = (bf16[128,512]{1,0:T(8,128)(2,1)}, bf16[8,96,512]{2,1,0:T(8,128)(2,1)}, bf16[8,96,512]{2,1,0:T(8,128)(2,1)}, bf16[8,48,512]{2,1,0:T(8,128)(2,1)}, bf16[8,48,512]{2,1,0:T(8,128)(2,1)}) custom-call(s32[1]{0:T(128)} %bitcast.refs_0_, s32[1,128]{1,0:T(1,128)} %bitcast.17, bf16[16,8,512]{2,1,0:T(8,128)(2,1)} %copy-done.8, ...), custom_call_target="tpu_custom_call" | custom-call | flops 1879048192 | bytes 9243652 | tf_op jit(solution)/shard_map/coarse_backward/pallas_call | solution.py:471
  72.8 0.1 collective-permute-done.11.refs_4_
  72.9 1.1 %copy-done = bf16[8,96,512]{2,1,0:T(8,128)(2,1)S(1)} copy-done((bf16[8,96,512]{2,1,0:T(8,128)(2,1)S(1)}, bf16[8,96,512]{2,1,0:T(8,128)(2,1)}, u32[]{:S(2)}) %copy-start) | copy-done | bytes 786456
  74.1 0.7 collective-permute-start.12
  74.7 0.1 collective-permute-start.6
  74.8 2.3 %collective-permute-done.12 = bf16[8,96,512]{2,1,0:T(8,128)(2,1)S(1)} collective-permute-done((bf16[8,96,512]{2,1,0:T(8,128)(2,1)S(1)}, bf16[8,96,512]{2,1,0:T(8,128)(2,1)S(1)}, u32[]{:S(2)}, u32[]{:S(2)}) %collective-permute-start.12) | collective-permute-done | bytes 786464 | tf_op jit(solution)/shard_map/ppermute | solution.py:506
  77.1 0.2 add_convert_fusion
  77.3 0.1 collective-permute-start.13
  77.4 0.1 collective-permute-done.6
  77.4 0.1 add_convert_fusion.2
  77.5 1.0 collective-permute-start.7
  78.5 0.1 halving.6
  78.6 3.9 %collective-permute-start.18 = (bf16[2,96,512]{2,1,0:T(8,128)(2,1)S(1)}, bf16[2,96,512]{2,1,0:T(8,128)(2,1)S(1)}, u32[]{:S(2)}, u32[]{:S(2)}) collective-permute-start(bf16[2,96,512]{2,1,0:T(8,128)(2,1)S(1)} %get-tuple-element.131), channel_id=1, source_target_pairs={{0,8},{1,9},{2,10},{3,11},{4,12},{5,13},{6,14},{7,15},{8,0},{9,1},... | collective-permute-start | bytes 589832 | tf_op jit(solution)/shard_map/ppermute | solution.py:506
  82.5 6.1 %collective-permute-done.7.taken_ref = bf16[4,48,512]{2,1,0:T(8,128)(2,1)S(1)} collective-permute-done((bf16[4,48,512]{2,1,0:T(8,128)(2,1)S(1)}, bf16[4,48,512]{2,1,0:T(8,128)(2,1)S(1)}, u32[]{:S(2)}, u32[]{:S(2)}) %collective-permute-start.7) | collective-permute-done | bytes 196640 | tf_op jit(solution)/shard_map/ppermute | solution.py:506
  88.7 0.0 copy-start.4
  88.7 0.1 collective-permute-done.13.taken_ref
  88.7 0.1 halving.8
  88.8 0.1 collective-permute-start.14
  88.9 3.4 %collective-permute-start.16 = (bf16[2,48,512]{2,1,0:T(8,128)(2,1)S(1)}, bf16[2,48,512]{2,1,0:T(8,128)(2,1)S(1)}, u32[]{:S(2)}, u32[]{:S(2)}) collective-permute-start(bf16[2,48,512]{2,1,0:T(8,128)(2,1)S(1)} %get-tuple-element.117), channel_id=1, source_target_pairs={{0,8},{1,9},{2,10},{3,11},{4,12},{5,13},{6,14},{7,15},{8,0},{9,1},... | collective-permute-start | bytes 294920 | tf_op jit(solution)/shard_map/ppermute | solution.py:506
  92.3 0.1 collective-permute-start.19
  92.5 6.3 %collective-permute-done.14.taken_ref = bf16[2,96,512]{2,1,0:T(8,128)(2,1)S(1)} collective-permute-done((bf16[2,96,512]{2,1,0:T(8,128)(2,1)S(1)}, bf16[2,96,512]{2,1,0:T(8,128)(2,1)S(1)}, u32[]{:S(2)}, u32[]{:S(2)}) %collective-permute-start.14) | collective-permute-done | bytes 196640 | tf_op jit(solution)/shard_map/ppermute | solution.py:506
  98.8 0.7 collective-permute-start.15
  99.5 1.5 %collective-permute-start.17 = (bf16[1,48,512]{2,1,0:T(8,128)(2,1)S(1)}, bf16[1,48,512]{2,1,0:T(8,128)(2,1)S(1)}, u32[]{:S(2)}, u32[]{:S(2)}) collective-permute-start(bf16[1,48,512]{2,1,0:T(8,128)(2,1)S(1)} %get-tuple-element.119), channel_id=1, source_target_pairs={{0,2},{1,3},{2,0},{3,1},{4,6},{5,7},{6,4},{7,5},{8,10},{9,11},{10,... | collective-permute-start | bytes 147464 | tf_op jit(solution)/shard_map/ppermute | solution.py:506
  101.0 0.4 node_gradient.1.refs_4_
  101.4 0.7 last_sum.3
  102.1 1.6 %collective-permute-done.17.refs_3_ = bf16[1,48,512]{2,1,0:T(8,128)(2,1)S(1)} collective-permute-done((bf16[1,48,512]{2,1,0:T(8,128)(2,1)S(1)}, bf16[1,48,512]{2,1,0:T(8,128)(2,1)S(1)}, u32[]{:S(2)}, u32[]{:S(2)}) %collective-permute-start.17) | collective-permute-done | bytes 49184 | tf_op jit(solution)/shard_map/ppermute | solution.py:506
  103.7 1.4 %collective-permute-done.15.refs_1_ = bf16[1,96,512]{2,1,0:T(8,128)(2,1)S(1)} collective-permute-done((bf16[1,96,512]{2,1,0:T(8,128)(2,1)S(1)}, bf16[1,96,512]{2,1,0:T(8,128)(2,1)S(1)}, u32[]{:S(2)}, u32[]{:S(2)}) %collective-permute-start.15) | collective-permute-done | bytes 98336 | tf_op jit(solution)/shard_map/ppermute | solution.py:506
  105.1 0.8 last_sum.2
  (31 shorter events, 0.2 us)
Async XLA Ops:
  2.0 16.4 %all-to-all-start = ((bf16[16,8,512]{2,1,0:T(8,128)(2,1)}), bf16[16,8,512]{2,1,0:T(8,128)(2,1)S(1)}, u32[]{:S(2)}, u32[]{:S(2)}) async-start(bf16[16,8,512]{2,1,0:T(8,128)(2,1)} %broadcast_in_dim.2), calls=%async_computation | async-start | bytes 262144 | tf_op jit(solution)/shard_map/all_to_all | solution.py:510
  12.0 15.8 %collective-permute-start = (bf16[128,512]{1,0:T(8,128)(2,1)}, bf16[128,512]{1,0:T(8,128)(2,1)S(1)}, u32[]{:S(2)}, u32[]{:S(2)}) collective-permute-start(bf16[128,512]{1,0:T(8,128)(2,1)} %get-tuple-element.73), channel_id=1, source_target_pairs={{15,0},{0,1},{1,2},{2,3},{3,4},{4,5},{5,6},{6,7},{7,8},{8,9},{9,10... | collective-permute-start | bytes 393224 | tf_op jit(solution)/shard_map/ppermute | solution.py:502
  12.4 15.4 %collective-permute-start.1 = (bf16[128,512]{1,0:T(8,128)(2,1)}, bf16[128,512]{1,0:T(8,128)(2,1)S(1)}, u32[]{:S(2)}, u32[]{:S(2)}) collective-permute-start(bf16[128,512]{1,0:T(8,128)(2,1)} %get-tuple-element.74), channel_id=1, source_target_pairs={{14,0},{15,1},{0,2},{1,3},{2,4},{3,5},{4,6},{5,7},{6,8},{7,9},{8,1... | collective-permute-start | bytes 393224 | tf_op jit(solution)/shard_map/ppermute | solution.py:502
  14.1 13.7 %collective-permute-start.2 = (bf16[128,512]{1,0:T(8,128)(2,1)}, bf16[128,512]{1,0:T(8,128)(2,1)S(1)}, u32[]{:S(2)}, u32[]{:S(2)}) collective-permute-start(bf16[128,512]{1,0:T(8,128)(2,1)} %get-tuple-element.75), channel_id=1, source_target_pairs={{1,0},{2,1},{3,2},{4,3},{5,4},{6,5},{7,6},{8,7},{9,8},{10,9},{11,1... | collective-permute-start | bytes 393224 | tf_op jit(solution)/shard_map/ppermute | solution.py:502
  18.1 9.7 %collective-permute-start.3 = (bf16[128,512]{1,0:T(8,128)(2,1)}, bf16[128,512]{1,0:T(8,128)(2,1)S(1)}, u32[]{:S(2)}, u32[]{:S(2)}) collective-permute-start(bf16[128,512]{1,0:T(8,128)(2,1)} %get-tuple-element.76), channel_id=1, source_target_pairs={{2,0},{3,1},{4,2},{5,3},{6,4},{7,5},{8,6},{9,7},{10,8},{11,9},{12,... | collective-permute-start | bytes 393224 | tf_op jit(solution)/shard_map/ppermute | solution.py:502
  18.4 0.7 copy-start.6
  23.0 12.2 %all-to-all-start.1 = ((bf16[16,8,512]{2,1,0:T(8,128)(2,1)}), bf16[16,8,512]{2,1,0:T(8,128)(2,1)S(1)}, u32[]{:S(2)}, u32[]{:S(2)}) async-start(bf16[16,8,512]{2,1,0:T(8,128)(2,1)} %get-tuple-element.78), calls=%async_computation.1 | async-start | bytes 262144 | tf_op jit(solution)/shard_map/all_to_all | solution.py:510
  27.7 0.7 copy-start.10
  27.8 0.7 copy-start.11
  27.8 0.7 copy-start.12
  27.8 0.7 copy-start.13
  35.3 0.7 copy-start.9
  41.7 2.6 %collective-permute-start.4 = (bf16[8,96,512]{2,1,0:T(8,128)(2,1)}, bf16[8,96,512]{2,1,0:T(8,128)(2,1)S(1)}, u32[]{:S(2)}, u32[]{:S(2)}) collective-permute-start(bf16[8,96,512]{2,1,0:T(8,128)(2,1)} %get-tuple-element.100), channel_id=1, source_target_pairs={{0,1},{1,0},{2,3},{3,2},{4,5},{5,4},{6,7},{7,6},{8,9},{9,8},{10,11... | collective-permute-start | bytes 2359304 | tf_op jit(solution)/shard_map/ppermute | solution.py:506
  45.7 19.5 %collective-permute-start.5 = (bf16[4,96,512]{2,1,0:T(8,128)(2,1)S(1)}, bf16[4,96,512]{2,1,0:T(8,128)(2,1)S(1)}, u32[]{:S(2)}, u32[]{:S(2)}) collective-permute-start(bf16[4,96,512]{2,1,0:T(8,128)(2,1)S(1)} %get-tuple-element.139), channel_id=1, source_target_pairs={{0,2},{1,3},{2,0},{3,1},{4,6},{5,7},{6,4},{7,5},{8,10},{9,11},{10,... | collective-permute-start | bytes 1179656 | tf_op jit(solution)/shard_map/ppermute | solution.py:506
  47.6 17.6 %all-to-all-start.2 = ((bf16[16,8,512]{2,1,0:T(8,128)(2,1)}), bf16[16,8,512]{2,1,0:T(8,128)(2,1)S(1)}, u32[]{:S(2)}, u32[]{:S(2)}) async-start(bf16[16,8,512]{2,1,0:T(8,128)(2,1)} %get-tuple-element.82), calls=%async_computation.2 | async-start | bytes 262144 | tf_op jit(solution)/shard_map/all_to_all | solution.py:510
  58.7 14.1 %collective-permute-start.8 = (bf16[128,512]{1,0:T(8,128)(2,1)}, bf16[128,512]{1,0:T(8,128)(2,1)S(1)}, u32[]{:S(2)}, u32[]{:S(2)}) collective-permute-start(bf16[128,512]{1,0:T(8,128)(2,1)} %get-tuple-element.105), channel_id=1, source_target_pairs={{1,0},{2,1},{3,2},{4,3},{5,4},{6,5},{7,6},{8,7},{9,8},{10,9},{11,1... | collective-permute-start | bytes 393224 | tf_op jit(solution)/shard_map/ppermute | solution.py:502
  63.1 9.7 %collective-permute-start.9 = (bf16[128,512]{1,0:T(8,128)(2,1)}, bf16[128,512]{1,0:T(8,128)(2,1)S(1)}, u32[]{:S(2)}, u32[]{:S(2)}) collective-permute-start(bf16[128,512]{1,0:T(8,128)(2,1)} %get-tuple-element.106), channel_id=1, source_target_pairs={{2,0},{3,1},{4,2},{5,3},{6,4},{7,5},{8,6},{9,7},{10,8},{11,9},{12,... | collective-permute-start | bytes 393224 | tf_op jit(solution)/shard_map/ppermute | solution.py:502
  63.7 9.1 %collective-permute-start.10 = (bf16[128,512]{1,0:T(8,128)(2,1)}, bf16[128,512]{1,0:T(8,128)(2,1)S(1)}, u32[]{:S(2)}, u32[]{:S(2)}) collective-permute-start(bf16[128,512]{1,0:T(8,128)(2,1)} %get-tuple-element.107), channel_id=1, source_target_pairs={{15,0},{0,1},{1,2},{2,3},{3,4},{4,5},{5,6},{6,7},{7,8},{8,9},{9,10... | collective-permute-start | bytes 393224 | tf_op jit(solution)/shard_map/ppermute | solution.py:502
  63.7 9.3 %collective-permute-start.11 = (bf16[128,512]{1,0:T(8,128)(2,1)}, bf16[128,512]{1,0:T(8,128)(2,1)S(1)}, u32[]{:S(2)}, u32[]{:S(2)}) collective-permute-start(bf16[128,512]{1,0:T(8,128)(2,1)} %get-tuple-element.108), channel_id=1, source_target_pairs={{14,0},{15,1},{0,2},{1,3},{2,4},{3,5},{4,6},{5,7},{6,8},{7,9},{8,1... | collective-permute-start | bytes 393224 | tf_op jit(solution)/shard_map/ppermute | solution.py:502
  65.2 0.7 copy-start.8
  65.2 0.8 copy-start.2
  72.9 1.1 %copy-start = (bf16[8,96,512]{2,1,0:T(8,128)(2,1)S(1)}, bf16[8,96,512]{2,1,0:T(8,128)(2,1)}, u32[]{:S(2)}) copy-start(bf16[8,96,512]{2,1,0:T(8,128)(2,1)} %get-tuple-element.104.refs_0_) | copy-start | bytes 2359300
  74.1 3.0 %copy-start.5 = (bf16[8,96,512]{2,1,0:T(8,128)(2,1)S(1)}, bf16[8,96,512]{2,1,0:T(8,128)(2,1)}, u32[]{:S(2)}) copy-start(bf16[8,96,512]{2,1,0:T(8,128)(2,1)} %get-tuple-element.103) | copy-start | bytes 2359300
  74.1 3.4 %copy-start.7 = (bf16[8,48,512]{2,1,0:T(8,128)(2,1)S(1)}, bf16[8,48,512]{2,1,0:T(8,128)(2,1)}, u32[]{:S(2)}) copy-start(bf16[8,48,512]{2,1,0:T(8,128)(2,1)} %get-tuple-element.101) | copy-start | bytes 1179652
  74.1 3.0 %collective-permute-start.12 = (bf16[8,96,512]{2,1,0:T(8,128)(2,1)S(1)}, bf16[8,96,512]{2,1,0:T(8,128)(2,1)S(1)}, u32[]{:S(2)}, u32[]{:S(2)}) collective-permute-start(bf16[8,96,512]{2,1,0:T(8,128)(2,1)S(1)} %get-tuple-element.109), channel_id=1, source_target_pairs={{0,1},{1,0},{2,3},{3,2},{4,5},{5,4},{6,7},{7,6},{8,9},{9,8},{10,11... | collective-permute-start | bytes 2359304 | tf_op jit(solution)/shard_map/ppermute | solution.py:506
  74.7 2.7 %collective-permute-start.6 = (bf16[8,48,512]{2,1,0:T(8,128)(2,1)}, bf16[8,48,512]{2,1,0:T(8,128)(2,1)S(1)}, u32[]{:S(2)}, u32[]{:S(2)}) collective-permute-start(bf16[8,48,512]{2,1,0:T(8,128)(2,1)} %get-tuple-element.102), channel_id=1, source_target_pairs={{0,1},{1,0},{2,3},{3,2},{4,5},{5,4},{6,7},{7,6},{8,9},{9,8},{10,11... | collective-permute-start | bytes 1179656 | tf_op jit(solution)/shard_map/ppermute | solution.py:506
  77.1 1.4 %copy-start.3 = (bf16[4,96,512]{2,1,0:T(8,128)(2,1)S(1)}, bf16[4,96,512]{2,1,0:T(8,128)(2,1)}, u32[]{:S(2)}) copy-start(bf16[4,96,512]{2,1,0:T(8,128)(2,1)} %copy-done.2) | copy-start | bytes 1179652
  77.3 11.5 %collective-permute-start.13 = (bf16[4,96,512]{2,1,0:T(8,128)(2,1)S(1)}, bf16[4,96,512]{2,1,0:T(8,128)(2,1)S(1)}, u32[]{:S(2)}, u32[]{:S(2)}) collective-permute-start(bf16[4,96,512]{2,1,0:T(8,128)(2,1)S(1)} %get-tuple-element.136), channel_id=1, source_target_pairs={{0,2},{1,3},{2,0},{3,1},{4,6},{5,7},{6,4},{7,5},{8,10},{9,11},{10,... | collective-permute-start | bytes 1179656 | tf_op jit(solution)/shard_map/ppermute | solution.py:506
  77.5 11.1 %collective-permute-start.7 = (bf16[4,48,512]{2,1,0:T(8,128)(2,1)S(1)}, bf16[4,48,512]{2,1,0:T(8,128)(2,1)S(1)}, u32[]{:S(2)}, u32[]{:S(2)}) collective-permute-start(bf16[4,48,512]{2,1,0:T(8,128)(2,1)S(1)} %get-tuple-element.140), channel_id=1, source_target_pairs={{0,4},{1,5},{2,6},{3,7},{4,0},{5,1},{6,2},{7,3},{8,12},{9,13},{10,... | collective-permute-start | bytes 589832 | tf_op jit(solution)/shard_map/ppermute | solution.py:506
  78.6 13.7 %collective-permute-start.18 = (bf16[2,96,512]{2,1,0:T(8,128)(2,1)S(1)}, bf16[2,96,512]{2,1,0:T(8,128)(2,1)S(1)}, u32[]{:S(2)}, u32[]{:S(2)}) collective-permute-start(bf16[2,96,512]{2,1,0:T(8,128)(2,1)S(1)} %get-tuple-element.131), channel_id=1, source_target_pairs={{0,8},{1,9},{2,10},{3,11},{4,12},{5,13},{6,14},{7,15},{8,0},{9,1},... | collective-permute-start | bytes 589832 | tf_op jit(solution)/shard_map/ppermute | solution.py:506
  88.7 12.3 %copy-start.1 = (f32[256,512]{1,0:T(8,128)S(1)}, f32[256,512]{1,0:T(8,128)}, u32[]{:S(2)}) copy-start(f32[256,512]{1,0:T(8,128)} %get-tuple-element.120.own_ref) | copy-start | bytes 1572868
  88.7 12.3 %copy-start.4 = (s32[1,4,128]{2,1,0:T(4,128)S(1)}, s32[1,4,128]{2,1,0:T(4,128)}, u32[]{:S(2)}) copy-start(s32[1,4,128]{2,1,0:T(4,128)} %param.25) | copy-start | bytes 6148
  88.8 9.9 %collective-permute-start.14 = (bf16[2,96,512]{2,1,0:T(8,128)(2,1)S(1)}, bf16[2,96,512]{2,1,0:T(8,128)(2,1)S(1)}, u32[]{:S(2)}, u32[]{:S(2)}) collective-permute-start(bf16[2,96,512]{2,1,0:T(8,128)(2,1)S(1)} %get-tuple-element.113), channel_id=1, source_target_pairs={{0,4},{1,5},{2,6},{3,7},{4,0},{5,1},{6,2},{7,3},{8,12},{9,13},{10,... | collective-permute-start | bytes 589832 | tf_op jit(solution)/shard_map/ppermute | solution.py:506
  88.9 10.6 %collective-permute-start.16 = (bf16[2,48,512]{2,1,0:T(8,128)(2,1)S(1)}, bf16[2,48,512]{2,1,0:T(8,128)(2,1)S(1)}, u32[]{:S(2)}, u32[]{:S(2)}) collective-permute-start(bf16[2,48,512]{2,1,0:T(8,128)(2,1)S(1)} %get-tuple-element.117), channel_id=1, source_target_pairs={{0,8},{1,9},{2,10},{3,11},{4,12},{5,13},{6,14},{7,15},{8,0},{9,1},... | collective-permute-start | bytes 294920 | tf_op jit(solution)/shard_map/ppermute | solution.py:506
  92.3 9.1 %collective-permute-start.19 = (bf16[1,96,512]{2,1,0:T(8,128)(2,1)S(1)}, bf16[1,96,512]{2,1,0:T(8,128)(2,1)S(1)}, u32[]{:S(2)}, u32[]{:S(2)}) collective-permute-start(bf16[1,96,512]{2,1,0:T(8,128)(2,1)S(1)} %get-tuple-element.133), channel_id=1, source_target_pairs={{0,4},{1,5},{2,6},{3,7},{4,0},{5,1},{6,2},{7,3},{8,12},{9,13},{10,... | collective-permute-start | bytes 294920 | tf_op jit(solution)/shard_map/ppermute | solution.py:506
  98.8 6.3 %collective-permute-start.15 = (bf16[1,96,512]{2,1,0:T(8,128)(2,1)S(1)}, bf16[1,96,512]{2,1,0:T(8,128)(2,1)S(1)}, u32[]{:S(2)}, u32[]{:S(2)}) collective-permute-start(bf16[1,96,512]{2,1,0:T(8,128)(2,1)S(1)} %get-tuple-element.115), channel_id=1, source_target_pairs={{0,8},{1,9},{2,10},{3,11},{4,12},{5,13},{6,14},{7,15},{8,0},{9,1},... | collective-permute-start | bytes 294920 | tf_op jit(solution)/shard_map/ppermute | solution.py:506
  99.5 4.2 %collective-permute-start.17 = (bf16[1,48,512]{2,1,0:T(8,128)(2,1)S(1)}, bf16[1,48,512]{2,1,0:T(8,128)(2,1)S(1)}, u32[]{:S(2)}, u32[]{:S(2)}) collective-permute-start(bf16[1,48,512]{2,1,0:T(8,128)(2,1)S(1)} %get-tuple-element.119), channel_id=1, source_target_pairs={{0,2},{1,3},{2,0},{3,1},{4,6},{5,7},{6,4},{7,5},{8,10},{9,11},{10,... | collective-permute-start | bytes 147464 | tf_op jit(solution)/shard_map/ppermute | solution.py:506

commit v11 on v10

--- a/solution.py
+++ b/solution.py
@@ -164,9 +164,8 @@
     return steps[1:] + steps[:1]
 
 
-def x_then_far(peers):
-    steps = x_first(peers)
-    return steps[:1] + steps[:0:-1]
+def first_rows(rows):
+    return rows * 5 // 6 // 16 * 16
 
 
 def by_distance(me, peers, steps, sums, kept_ref, given_ref):
@@ -179,9 +178,10 @@
         for distance in steps:
             slot = 2 * slot + r // distance % 2
         place = 0
-        for total in sums:
-            rows = total.shape[0] // peers
-            part = total[pl.ds(pl.multiple_of(to * rows, 8), rows), :]
+        for total, first, last in sums:
+            whole = total.shape[0] // peers
+            rows = last - first
+            part = total[pl.ds(pl.multiple_of(to * whole + first, 8), rows), :]
             if rows % 16:
                 part = jnp.concatenate([part, jnp.zeros((-rows % 16, part.shape[1]), F32)], 0)
             out[slot, place : place + part.shape[0], :] = part.astype(BF16)
@@ -217,7 +217,12 @@
     g1_ref[width : 2 * width, :] = mm_tn(agg, back_pre)
     g2_ref[...] = mm_tn(hidden, back_out)
     if ordered:
-        by_distance(me_ref[0], spread_ref.shape[0], x_then_far(spread_ref.shape[0]), (g1_ref, g2_ref), kept_ref, given_ref)
+        peers = spread_ref.shape[0]
+
+        def share(ref):
+            return ref, 0, ref.shape[0] // peers
+
+        by_distance(me_ref[0], peers, x_last(peers), (share(g1_ref), share(g2_ref)), kept_ref, given_ref)
 
 
 def fine_backward_kernel(
@@ -283,14 +288,19 @@
     g1_ref[2 * width : 3 * width, :] = mm_tn(zr_ref[...], pre_ref[...])
     if ordered:
         peers = 2 * kept1_ref.shape[0]
-        by_distance(me_ref[0], peers, x_first(peers), (g1_ref,), kept1_ref, given1_ref)
+        by_distance(me_ref[0], peers, x_first(peers), ((g1_ref, 0, kept1_ref.shape[1]),), kept1_ref, given1_ref)
     g2_ref[...] = mm_tn(hidden_ref[...], out_ref[...])
     dz_send = mm_nt(back_pre, w1_ref[width : 2 * width, :]).astype(BF16)
     dz_recv = mm_nt(back_pre, w1_ref[2 * width : 3 * width, :]).astype(BF16)
     total = mm(one_hot(send_ref[...], table.shape[0]), dz_send) + mm(one_hot(recv_ref[...], table.shape[0]), dz_recv)
     part_ref[...] = total.reshape(part_ref.shape).astype(part_ref.dtype)
     if ordered:
-        by_distance(me_ref[0], peers, x_last(peers), (g2_ref, part_ref), kept2_ref, given2_ref)
+        sums = (
+            (g1_ref, kept1_ref.shape[1], g1_ref.shape[0] // peers),
+            (g2_ref, 0, g2_ref.shape[0] // peers),
+            (part_ref, 0, part_ref.shape[0] // peers),
+        )
+        by_distance(me_ref[0], peers, x_last(peers), sums, kept2_ref, given2_ref)
     g_ref[...] = (d_edges + mm_nt(back_pre, w1_ref[0:width, :])).astype(BF16)
 
 
@@ -324,21 +334,25 @@
         keep_ref[j] = kept_ref[j] + taken_ref[j].astype(F32)
 
 
-def last_sum_kernel(*refs, sizes, with_nodes):
-    place = 2 * len(sizes)
-    totals = [refs[2 * i][0] + refs[2 * i + 1][0].astype(F32) for i in range(len(sizes))]
+def last_sum_kernel(*refs, groups, with_nodes):
+    place = 2 * groups
+    totals = [refs[2 * i][0] + refs[2 * i + 1][0].astype(F32) for i in range(groups)]
     if with_nodes:
         nodes_ref, g_ref = refs[place], refs[-1]
-        place += 1
-    for total, rows in zip(totals, sizes):
-        start = 0
-        for count in rows:
-            refs[place][...] = total[start : start + count]
-            start += count
-            place += 1
-    if with_nodes:
-        g_ref[...] = nodes_ref[...].astype(BF16)
-        g_ref[0:16, :] = (nodes_ref[0:16, :] + totals[-1][start : start + 16]).astype(BF16)
+    first_ref, second_ref = refs[place + with_nodes :][:2]
+    done = totals[0].shape[0]
+    cut = first_ref.shape[0]
+    if groups == 1:
+        first_ref[...] = totals[0][:cut]
+        second_ref[...] = totals[0][cut:]
+        return
+    rest = totals[1]
+    first_ref[0:done, :] = totals[0]
+    first_ref[done:cut, :] = rest[: cut - done]
+    start = cut - done + second_ref.shape[0]
+    second_ref[...] = rest[cut - done : start]
+    g_ref[...] = nodes_ref[...].astype(BF16)
+    g_ref[0:16, :] = (nodes_ref[0:16, :] + rest[start : start + 16]).astype(BF16)
 
 
 VM = pl.BlockSpec(memory_space=pltpu.VMEM)
@@ -522,16 +536,13 @@
 
 
 def last_sum(groups, sizes, nodes=None):
-    ins, outs = [], []
-    for (kept, taken), rows in zip(groups, sizes):
-        ins += [kept, taken]
-        outs += [shape((count, kept.shape[2]), F32) for count in rows]
+    ins = [array for group in groups for array in group]
+    outs = [shape((count, ins[0].shape[2]), F32) for count in sizes]
     if nodes is not None:
         ins.append(nodes)
         outs.append(shape(nodes.shape, BF16))
-    return small_call(
-        functools.partial(last_sum_kernel, sizes=sizes, with_nodes=nodes is not None), "last_sum", ins, outs
-    )
+    kernel = functools.partial(last_sum_kernel, groups=len(groups), with_nodes=nodes is not None)
+    return small_call(kernel, "last_sum", ins, outs)
 
 
 def local(
@@ -626,7 +637,7 @@
 
     sum_shapes, sum_scratch = weight_shapes(edge_w1, edge_w2, 16)
     if ordered:
-        cut = edge_w1.shape[0] // peers
+        cut = first_rows(edge_w1.shape[0] // peers)
         rows = sum_shapes[0].shape[1] - cut
         sum_shapes = [shape((peers // 2, cut, width), BF16)] * 2 + [shape((peers // 2, rows, width), BF16)] * 2
     f_zs, f_zr, f_hidden, f_slope, f_normed, f_std = fine_saved
@@ -641,17 +652,16 @@
     )
     returned = [passed_along(pieces[slot], axis, -offset) for slot, offset in enumerate(offsets)]
     if ordered:
-        node_taken = exchanged(node_given, axis, 2)
+        node_taken = exchanged(node_given, axis, 4)
     pair = [Rows(joined=2), None]
     more = [Rows(extra=coarse)]
-    order = (node_taken,) if ordered else ()
     g_coarse, *edge_parts = call(
         functools.partial(coarse_backward_kernel, ordered=ordered), "coarse_backward",
         (
             me, cr, dagg_all, d_coarse, eg, c_std, c_normed, edge_w2, c_slope, fine_edges, coarse_edges,
-            fine_pre, f_zs, c_zs, f_zr, c_zr, f_hidden, c_hidden, fine_out, edge_w1, cs, *order,
+            fine_pre, f_zs, c_zs, f_zr, c_zr, f_hidden, c_hidden, fine_out, edge_w1, cs,
         ),
-        [SM] + [VM] * 8 + pair + more + pair * 3 + more + [Rows(3), VM] + [None] * len(order),
+        [SM] + [VM] * 8 + pair + more + pair * 3 + more + [Rows(3), VM],
         [shape((coarse, width), BF16)] + ([] if ordered else [every]) + sum_shapes,
         scratch=([pltpu.VMEM((peers * COARSE_DEV, width), F32)] if ordered else []) + sum_scratch,
         flops=2 * width * width * (4 * fine + 12 * coarse),
@@ -668,10 +678,12 @@
 
     if ordered:
         kept1, given1, kept2, given2 = edge_parts
-        given1, *returned = small_call(order_kernel, "order", (), [], (given1, *returned))
+        given1, node_taken, *returned = small_call(
+            order_kernel, "order", (), [], (given1, node_taken, *returned)
+        )
         taken1 = exchanged(given1, axis, 1)
         taken2 = exchanged(given2, axis, 1)
-        steps1, steps2, node_steps = x_first(peers), x_last(peers), x_then_far(peers)
+        steps1, steps2 = x_first(peers), x_last(peers)
         kept1, given1 = first_halving(kept1, taken1)
         taken1 = exchanged(given1, axis, steps1[0])
         kept2, given2 = first_halving(kept2, taken2)
@@ -679,14 +691,14 @@
         for k in range(1, len(steps1)):
             passing = (kept1,) if k == 1 else ()
             node_kept, given, *passing = halving(node_kept, node_taken, passing)
-            node_taken = exchanged(given, axis, node_steps[k])
+            node_taken = exchanged(given, axis, steps2[k])
             kept2, given2, *passing = halving(kept2, taken2, tuple(passing))
             taken2 = exchanged(given2, axis, steps2[k])
             kept1, given1 = halving(passing[0] if passing else kept1, taken1)
             taken1 = exchanged(given1, axis, steps1[k])
-        g_nw1, g_nw2 = last_sum([(node_kept, node_taken)], [(rows_of(node_w1), rows_of(node_w2))])
+        g_nw1, g_nw2 = last_sum([(node_kept, node_taken)], (rows_of(node_w1), rows_of(node_w2)))
         g_ew1, g_ew2, g_nodes = last_sum(
-            [(kept1, taken1), (kept2, taken2)], [(rows_of(edge_w1),), (rows_of(edge_w2),)], tile_gradient()
+            [(kept1, taken1), (kept2, taken2)], (rows_of(edge_w1), rows_of(edge_w2)), tile_gradient()
         )
     else:
         coarse_share = exchanged_with_all(edge_parts[0], axis)

time: 106 us -> 103 us (0.972)
  waiting for transfers between devices: 20 us -> 16.4 us
    ppermute x12, waiting for transfers between devices: 19.9 us -> 15.9 us  [exchanged(): lax.ppermute(block, axis, [(i, i ^ distance) for i in range(lax.axis_size...]
    ppermute x8, starting transfers between devices: 12.9 us -> 11.3 us  [passed_along(): return lax.ppermute(block, axis, route)]
    add x1 -> x0, other arithmetic: 1.31 us -> none  [first_halving(): return (kept[:half].astype(F32) + taken[:half].astype(F32), give)]
    convert_element_type x2 -> x3, other arithmetic: 0.29 us -> 1.6 us  [first_halving(): give = (kept[half:].astype(F32) + taken[half:].astype(F32)).astype(BF16)]
    all_to_all x3, starting transfers between devices: 16.1 us -> 17.1 us  [exchanged_with_all(): return lax.all_to_all(blocks, axis, 0, 0)]
    unnamed x28 -> x24, local copies, waits for them, and re-layouts: 3.97 us -> 3.79 us
  transfers between devices with their start and end apart: 23 -> 23, of which waited for: 9 -> 6; matrix products, arithmetic and copies ran while one was open for 0% -> 2% of each run, Pallas kernels for 26% -> 27%
where the time goes in v11:
time: 103 us; the launch traced here: 102 us
  starting transfers between devices  43.3 us (42%)
  Pallas kernels  34.4 us (33%)
  waiting for transfers between devices  16.4 us (16%)
  local copies, waits for them, and re-layouts  5.15 us (5%)
  other arithmetic  1.6 us (2%)
  between operations  1.59 us (2%)
    pallas_call x6, Pallas kernels, call(): pl.pallas_call(functools.partial(staged_kernel, kernel, in_specs, out_spe...  32.2 us
    all_to_all x3, starting transfers between devices, exchanged_with_all(): return lax.all_to_all(blocks, axis, 0, 0)  17.1 us
    ppermute x12, waiting for transfers between devices, exchanged(): lax.ppermute(block, axis, [(i, i ^ distance) for i in range(lax.axis_size...  15.9 us
    ppermute x12, starting transfers between devices, exchanged(): lax.ppermute(block, axis, [(i, i ^ distance) for i in range(lax.axis_size...  14.9 us
    ppermute x8, starting transfers between devices, passed_along(): return lax.ppermute(block, axis, route)  11.3 us
    unnamed x24, local copies, waits for them, and re-layouts  3.79 us
    pallas_call x10, Pallas kernels, small_call(): pl.pallas_call(kernel, out_shape=tuple(outs), input_output_aliases={first...  2.19 us
  transfers between devices with their start and end apart: 23, of which 6 were waited for; matrix products, arithmetic and copies ran while one was open for 2% of the time, Pallas kernels for 27%

profile of v11, /device:TPU:0, one launch (start us, length us, event | category | flops | bytes accessed | tf_op | source)
XLA Modules:
  0.0 102.5 jit_solution(6906568935101563033)
XLA Ops:
  0.6 0.7 slice.39
  1.3 0.7 broadcast_in_dim.2
  2.0 7.4 %all-to-all-start = ((bf16[16,8,512]{2,1,0:T(8,128)(2,1)}), bf16[16,8,512]{2,1,0:T(8,128)(2,1)S(1)}, u32[]{:S(2)}, u32[]{:S(2)}) async-start(bf16[16,8,512]{2,1,0:T(8,128)(2,1)} %broadcast_in_dim.2), calls=%async_computation | async-start | bytes 262144 | tf_op jit(solution)/shard_map/all_to_all | solution.py:524
  9.4 2.6 %tiles.1 = (bf16[128,512]{1,0:T(8,128)(2,1)}, bf16[128,512]{1,0:T(8,128)(2,1)}, bf16[128,512]{1,0:T(8,128)(2,1)}, bf16[128,512]{1,0:T(8,128)(2,1)}) custom-call(bf16[256,512]{1,0:T(8,128)(2,1)} %refs_1_.5, s32[4,128]{1,0:T(4,128)} %bitcast.8), custom_call_target="tpu_custom_call" | custom-call | bytes 788480 | tf_op jit(solution)/shard_map/tiles/pallas_call | solution.py:485
  12.0 0.5 collective-permute-start
  12.4 1.7 %collective-permute-start.1 = (bf16[128,512]{1,0:T(8,128)(2,1)}, bf16[128,512]{1,0:T(8,128)(2,1)S(1)}, u32[]{:S(2)}, u32[]{:S(2)}) collective-permute-start(bf16[128,512]{1,0:T(8,128)(2,1)} %get-tuple-element.75), channel_id=1, source_target_pairs={{14,0},{15,1},{0,2},{1,3},{2,4},{3,5},{4,6},{5,7},{6,8},{7,9},{8,1... | collective-permute-start | bytes 393224 | tf_op jit(solution)/shard_map/ppermute | solution.py:516
  14.1 4.0 %collective-permute-start.2 = (bf16[128,512]{1,0:T(8,128)(2,1)}, bf16[128,512]{1,0:T(8,128)(2,1)S(1)}, u32[]{:S(2)}, u32[]{:S(2)}) collective-permute-start(bf16[128,512]{1,0:T(8,128)(2,1)} %get-tuple-element.76), channel_id=1, source_target_pairs={{1,0},{2,1},{3,2},{4,3},{5,4},{6,5},{7,6},{8,7},{9,8},{10,9},{11,1... | collective-permute-start | bytes 393224 | tf_op jit(solution)/shard_map/ppermute | solution.py:516
  18.1 0.3 collective-permute-start.3
  18.4 0.7 copy-done.5
  19.0 4.0 %coarse_forward.1 = (bf16[128,512]{1,0:T(8,128)(2,1)}, bf16[16,8,512]{2,1,0:T(8,128)(2,1)}, bf16[128,512]{1,0:T(8,128)(2,1)}, bf16[128,512]{1,0:T(8,128)(2,1)}, ...) custom-call(bf16[16,8,512]{2,1,0:T(8,128)(2,1)} %copy-done.5, ...), custom_call_target="tpu_custom_call" | custom-call | flops 268435456 | bytes 3345408 | tf_op jit(solution)/shard_map/coarse_forward/pallas_call | solution.py:485
  23.0 4.0 %all-to-all-start.1 = ((bf16[16,8,512]{2,1,0:T(8,128)(2,1)}), bf16[16,8,512]{2,1,0:T(8,128)(2,1)S(1)}, u32[]{:S(2)}, u32[]{:S(2)}) async-start(bf16[16,8,512]{2,1,0:T(8,128)(2,1)} %get-tuple-element.79), calls=%async_computation.1 | async-start | bytes 262144 | tf_op jit(solution)/shard_map/all_to_all | solution.py:524
  27.7 0.0 collective-permute-done.refs_2_
  27.7 0.0 copy-start.8
  27.8 0.0 collective-permute-done.1.refs_3_
  27.8 0.0 copy-start.9
  27.8 0.0 copy-start.10
  27.8 0.0 collective-permute-done.3.refs_5_
  27.8 0.0 copy-start.11
  27.8 0.6 copy-done.8
  28.4 0.0 copy-done.9
  28.4 0.0 copy-done.10
  28.5 0.0 copy-done.11
  28.5 6.7 %fine_forward.1 = (bf16[512,512]{1,0:T(8,128)(2,1)}, f32[256,512]{1,0:T(8,128)}, bf16[512,512]{1,0:T(8,128)(2,1)}, bf16[512,512]{1,0:T(8,128)(2,1)}, bf16[512,51...) custom-call(s32[1]{0:T(128)S(6)} %copy.44.refs_0_, ...), custom_call_target="tpu_custom_call" | custom-call | flops 1879048192 | bytes 7346180 | tf_op jit(solution)/shard_map/fine_forward/pallas_call | solution.py:485
  35.3 0.0 copy-start.7
  35.3 0.6 copy-done.7
  35.9 5.8 %node_both.1 = (bf16[256,512]{1,0:T(8,128)(2,1)}, f32[256,512]{1,0:T(8,128)}, bf16[256,512]{1,0:T(8,128)(2,1)}, bf16[16,8,512]{2,1,0:T(8,128)(2,1)}, bf16[8,96,5...) custom-call(s32[1]{0:T(128)} %bitcast.refs_0_, bf16[256,512]{1,0:T(8,128)(2,1)} %refs_1_.5, ...), custom_call_target="tpu_custom_call" | custom-call | flops 1207959552 | bytes 5507076 | tf_op jit(solution)/shard_map/node_both/pallas_call | solution.py:485
  41.7 0.5 collective-permute-start.6
  42.2 5.8 %all-to-all-start.2 = ((bf16[16,8,512]{2,1,0:T(8,128)(2,1)}), bf16[16,8,512]{2,1,0:T(8,128)(2,1)S(1)}, u32[]{:S(2)}, u32[]{:S(2)}) async-start(bf16[16,8,512]{2,1,0:T(8,128)(2,1)} %get-tuple-element.83), calls=%async_computation.2 | async-start | bytes 262144 | tf_op jit(solution)/shard_map/all_to_all | solution.py:524
  48.0 0.0 collective-permute-done.6
  48.0 1.3 %add_convert_fusion = (bf16[4,96,512]{2,1,0:T(8,128)(2,1)S(1)}, f32[4,96,512]{2,1,0:T(8,128)S(1)}) fusion(bf16[8,96,512]{2,1,0:T(8,128)(2,1)S(1)} %collective-permute-done.6, bf16[8,96,512]{2,1,0:T(8,128)(2,1)} %get-tuple-element.102), kind=kLoop, calls=%fused_computation | loop fusion | flops 1376256 | bytes 2752512 | tf_op jit(solution)/shard_map/convert_element_type | solution.py:529
  49.3 2.0 %collective-permute-start.7 = (bf16[4,96,512]{2,1,0:T(8,128)(2,1)S(1)}, bf16[4,96,512]{2,1,0:T(8,128)(2,1)S(1)}, u32[]{:S(2)}, u32[]{:S(2)}) collective-permute-start(bf16[4,96,512]{2,1,0:T(8,128)(2,1)S(1)} %get-tuple-element.138), channel_id=1, source_target_pairs={{0,4},{1,5},{2,6},{3,7},{4,0},{5,1},{6,2},{7,3},{8,12},{9,13},{10,... | collective-permute-start | bytes 1179656 | tf_op jit(solution)/shard_map/ppermute | solution.py:520
  51.3 6.4 %fine_backward.1 = (bf16[512,512]{1,0:T(8,128)(2,1)}, bf16[512,512]{1,0:T(8,128)(2,1)}, bf16[512,512]{1,0:T(8,128)(2,1)}, f32[256,512]{1,0:T(8,128)}, bf16[128,5...) custom-call(s32[1]{0:T(128)S(6)} %copy.44.refs_0_, ...), custom_call_target="tpu_custom_call" | custom-call | flops 1744830464 | bytes 7346180 | tf_op jit(solution)/shard_map/fine_backward/pallas_call | solution.py:485
  57.7 2.8 %collective-permute-start.8 = (bf16[128,512]{1,0:T(8,128)(2,1)}, bf16[128,512]{1,0:T(8,128)(2,1)S(1)}, u32[]{:S(2)}, u32[]{:S(2)}) collective-permute-start(bf16[128,512]{1,0:T(8,128)(2,1)} %get-tuple-element.105), channel_id=1, source_target_pairs={{1,0},{2,1},{3,2},{4,3},{5,4},{6,5},{7,6},{8,7},{9,8},{10,9},{11,1... | collective-permute-start | bytes 393224 | tf_op jit(solution)/shard_map/ppermute | solution.py:516
  60.5 0.6 collective-permute-start.9
  61.1 0.2 collective-permute-start.10
  61.2 1.3 %collective-permute-start.11 = (bf16[128,512]{1,0:T(8,128)(2,1)}, bf16[128,512]{1,0:T(8,128)(2,1)S(1)}, u32[]{:S(2)}, u32[]{:S(2)}) collective-permute-start(bf16[128,512]{1,0:T(8,128)(2,1)} %get-tuple-element.108), channel_id=1, source_target_pairs={{14,0},{15,1},{0,2},{1,3},{2,4},{3,5},{4,6},{5,7},{6,8},{7,9},{8,1... | collective-permute-start | bytes 393224 | tf_op jit(solution)/shard_map/ppermute | solution.py:516
  62.6 0.7 copy-done.6
  63.2 6.8 %coarse_backward.1 = (bf16[128,512]{1,0:T(8,128)(2,1)}, bf16[8,80,512]{2,1,0:T(8,128)(2,1)}, bf16[8,80,512]{2,1,0:T(8,128)(2,1)}, bf16[8,64,512]{2,1,0:T(8,128)(2,1)}, bf16[8,64,512]{2,1,0:T(8,128)(2,1)}) custom-call(s32[1]{0:T(128)} %bitcast.refs_0_, s32[1,128]{1,0:T(1,128)} %bitcast.17, bf16[16,8,512]{2,1,0:T(8,128)(2,1)} %copy-done.6, ...), custom_call_target="tpu_custom_call" | custom-call | flops 1879048192 | bytes 8850436 | tf_op jit(solution)/shard_map/coarse_backward/pallas_call | solution.py:485
  70.0 0.5 collective-permute-done.11.refs_5_
  70.5 1.1 %copy-done = bf16[8,80,512]{2,1,0:T(8,128)(2,1)S(1)} copy-done((bf16[8,80,512]{2,1,0:T(8,128)(2,1)S(1)}, bf16[8,80,512]{2,1,0:T(8,128)(2,1)}, u32[]{:S(2)}) %copy-start) | copy-done | bytes 655384
  71.6 0.5 collective-permute-start.12
  72.1 0.1 collective-permute-start.4
  72.2 1.9 %collective-permute-done.12 = bf16[8,80,512]{2,1,0:T(8,128)(2,1)S(1)} collective-permute-done((bf16[8,80,512]{2,1,0:T(8,128)(2,1)S(1)}, bf16[8,80,512]{2,1,0:T(8,128)(2,1)S(1)}, u32[]{:S(2)}, u32[]{:S(2)}) %collective-permute-start.12) | collective-permute-done | bytes 655392 | tf_op jit(solution)/shard_map/ppermute | solution.py:520
  74.1 0.2 add_convert_fusion.1
  74.2 0.8 collective-permute-start.13
  75.0 0.1 add_convert_fusion.2
  75.2 0.5 collective-permute-start.5
  75.7 0.1 halving.6
  75.7 3.9 %collective-permute-start.18 = (bf16[2,96,512]{2,1,0:T(8,128)(2,1)S(1)}, bf16[2,96,512]{2,1,0:T(8,128)(2,1)S(1)}, u32[]{:S(2)}, u32[]{:S(2)}) collective-permute-start(bf16[2,96,512]{2,1,0:T(8,128)(2,1)S(1)} %get-tuple-element.133), channel_id=1, source_target_pairs={{0,8},{1,9},{2,10},{3,11},{4,12},{5,13},{6,14},{7,15},{8,0},{9,1},... | collective-permute-start | bytes 589832 | tf_op jit(solution)/shard_map/ppermute | solution.py:520
  79.6 8.2 %collective-permute-done.5.taken_ref = bf16[4,64,512]{2,1,0:T(8,128)(2,1)S(1)} collective-permute-done((bf16[4,64,512]{2,1,0:T(8,128)(2,1)S(1)}, bf16[4,64,512]{2,1,0:T(8,128)(2,1)S(1)}, u32[]{:S(2)}, u32[]{:S(2)}) %collective-permute-start.5) | collective-permute-done | bytes 262176 | tf_op jit(solution)/shard_map/ppermute | solution.py:520
  87.8 0.1 halving.7
  87.9 0.0 copy-start.2
  87.9 0.1 halving.8
  87.9 0.1 collective-permute-start.14
  88.0 4.2 %collective-permute-start.16 = (bf16[2,64,512]{2,1,0:T(8,128)(2,1)S(1)}, bf16[2,64,512]{2,1,0:T(8,128)(2,1)S(1)}, u32[]{:S(2)}, u32[]{:S(2)}) collective-permute-start(bf16[2,64,512]{2,1,0:T(8,128)(2,1)S(1)} %get-tuple-element.119), channel_id=1, source_target_pairs={{0,8},{1,9},{2,10},{3,11},{4,12},{5,13},{6,14},{7,15},{8,0},{9,1},... | collective-permute-start | bytes 393224 | tf_op jit(solution)/shard_map/ppermute | solution.py:520
  92.3 0.8 collective-permute-start.19
  93.1 3.1 %collective-permute-done.14.taken_ref = bf16[2,80,512]{2,1,0:T(8,128)(2,1)S(1)} collective-permute-done((bf16[2,80,512]{2,1,0:T(8,128)(2,1)S(1)}, bf16[2,80,512]{2,1,0:T(8,128)(2,1)S(1)}, u32[]{:S(2)}, u32[]{:S(2)}) %collective-permute-start.14) | collective-permute-done | bytes 163872 | tf_op jit(solution)/shard_map/ppermute | solution.py:520
  96.2 0.2 collective-permute-start.15
  96.5 1.3 %collective-permute-start.17 = (bf16[1,64,512]{2,1,0:T(8,128)(2,1)S(1)}, bf16[1,64,512]{2,1,0:T(8,128)(2,1)S(1)}, u32[]{:S(2)}, u32[]{:S(2)}) collective-permute-start(bf16[1,64,512]{2,1,0:T(8,128)(2,1)S(1)} %get-tuple-element.121), channel_id=1, source_target_pairs={{0,2},{1,3},{2,0},{3,1},{4,6},{5,7},{6,4},{7,5},{8,10},{9,11},{10,... | collective-permute-start | bytes 196616 | tf_op jit(solution)/shard_map/ppermute | solution.py:520
  97.8 0.4 node_gradient.1.refs_4_
  98.3 0.7 last_sum.3
  99.0 1.9 %collective-permute-done.17.refs_3_ = bf16[1,64,512]{2,1,0:T(8,128)(2,1)S(1)} collective-permute-done((bf16[1,64,512]{2,1,0:T(8,128)(2,1)S(1)}, bf16[1,64,512]{2,1,0:T(8,128)(2,1)S(1)}, u32[]{:S(2)}, u32[]{:S(2)}) %collective-permute-start.17) | collective-permute-done | bytes 65568 | tf_op jit(solution)/shard_map/ppermute | solution.py:520
  100.8 0.8 collective-permute-done.15.refs_1_
  101.7 0.8 last_sum.2
  (27 shorter events, 0.1 us)
Async XLA Ops:
  2.0 16.4 %all-to-all-start = ((bf16[16,8,512]{2,1,0:T(8,128)(2,1)}), bf16[16,8,512]{2,1,0:T(8,128)(2,1)S(1)}, u32[]{:S(2)}, u32[]{:S(2)}) async-start(bf16[16,8,512]{2,1,0:T(8,128)(2,1)} %broadcast_in_dim.2), calls=%async_computation | async-start | bytes 262144 | tf_op jit(solution)/shard_map/all_to_all | solution.py:524
  12.0 15.8 %collective-permute-start = (bf16[128,512]{1,0:T(8,128)(2,1)}, bf16[128,512]{1,0:T(8,128)(2,1)S(1)}, u32[]{:S(2)}, u32[]{:S(2)}) collective-permute-start(bf16[128,512]{1,0:T(8,128)(2,1)} %get-tuple-element.74), channel_id=1, source_target_pairs={{15,0},{0,1},{1,2},{2,3},{3,4},{4,5},{5,6},{6,7},{7,8},{8,9},{9,10... | collective-permute-start | bytes 393224 | tf_op jit(solution)/shard_map/ppermute | solution.py:516
  12.4 15.4 %collective-permute-start.1 = (bf16[128,512]{1,0:T(8,128)(2,1)}, bf16[128,512]{1,0:T(8,128)(2,1)S(1)}, u32[]{:S(2)}, u32[]{:S(2)}) collective-permute-start(bf16[128,512]{1,0:T(8,128)(2,1)} %get-tuple-element.75), channel_id=1, source_target_pairs={{14,0},{15,1},{0,2},{1,3},{2,4},{3,5},{4,6},{5,7},{6,8},{7,9},{8,1... | collective-permute-start | bytes 393224 | tf_op jit(solution)/shard_map/ppermute | solution.py:516
  14.1 13.7 %collective-permute-start.2 = (bf16[128,512]{1,0:T(8,128)(2,1)}, bf16[128,512]{1,0:T(8,128)(2,1)S(1)}, u32[]{:S(2)}, u32[]{:S(2)}) collective-permute-start(bf16[128,512]{1,0:T(8,128)(2,1)} %get-tuple-element.76), channel_id=1, source_target_pairs={{1,0},{2,1},{3,2},{4,3},{5,4},{6,5},{7,6},{8,7},{9,8},{10,9},{11,1... | collective-permute-start | bytes 393224 | tf_op jit(solution)/shard_map/ppermute | solution.py:516
  18.1 9.7 %collective-permute-start.3 = (bf16[128,512]{1,0:T(8,128)(2,1)}, bf16[128,512]{1,0:T(8,128)(2,1)S(1)}, u32[]{:S(2)}, u32[]{:S(2)}) collective-permute-start(bf16[128,512]{1,0:T(8,128)(2,1)} %get-tuple-element.77), channel_id=1, source_target_pairs={{2,0},{3,1},{4,2},{5,3},{6,4},{7,5},{8,6},{9,7},{10,8},{11,9},{12,... | collective-permute-start | bytes 393224 | tf_op jit(solution)/shard_map/ppermute | solution.py:516
  18.4 0.7 copy-start.5
  23.0 12.2 %all-to-all-start.1 = ((bf16[16,8,512]{2,1,0:T(8,128)(2,1)}), bf16[16,8,512]{2,1,0:T(8,128)(2,1)S(1)}, u32[]{:S(2)}, u32[]{:S(2)}) async-start(bf16[16,8,512]{2,1,0:T(8,128)(2,1)} %get-tuple-element.79), calls=%async_computation.1 | async-start | bytes 262144 | tf_op jit(solution)/shard_map/all_to_all | solution.py:524
  27.7 0.7 copy-start.8
  27.8 0.7 copy-start.9
  27.8 0.7 copy-start.10
  27.8 0.7 copy-start.11
  35.3 0.7 copy-start.7
  41.7 6.3 %collective-permute-start.6 = (bf16[8,96,512]{2,1,0:T(8,128)(2,1)}, bf16[8,96,512]{2,1,0:T(8,128)(2,1)S(1)}, u32[]{:S(2)}, u32[]{:S(2)}) collective-permute-start(bf16[8,96,512]{2,1,0:T(8,128)(2,1)} %get-tuple-element.103), channel_id=1, source_target_pairs={{0,1},{1,0},{2,3},{3,2},{4,5},{5,4},{6,7},{7,6},{8,9},{9,8},{10,11... | collective-permute-start | bytes 2359304 | tf_op jit(solution)/shard_map/ppermute | solution.py:520
  42.2 20.3 %all-to-all-start.2 = ((bf16[16,8,512]{2,1,0:T(8,128)(2,1)}), bf16[16,8,512]{2,1,0:T(8,128)(2,1)S(1)}, u32[]{:S(2)}, u32[]{:S(2)}) async-start(bf16[16,8,512]{2,1,0:T(8,128)(2,1)} %get-tuple-element.83), calls=%async_computation.2 | async-start | bytes 262144 | tf_op jit(solution)/shard_map/all_to_all | solution.py:524
  49.3 21.2 %collective-permute-start.7 = (bf16[4,96,512]{2,1,0:T(8,128)(2,1)S(1)}, bf16[4,96,512]{2,1,0:T(8,128)(2,1)S(1)}, u32[]{:S(2)}, u32[]{:S(2)}) collective-permute-start(bf16[4,96,512]{2,1,0:T(8,128)(2,1)S(1)} %get-tuple-element.138), channel_id=1, source_target_pairs={{0,4},{1,5},{2,6},{3,7},{4,0},{5,1},{6,2},{7,3},{8,12},{9,13},{10,... | collective-permute-start | bytes 1179656 | tf_op jit(solution)/shard_map/ppermute | solution.py:520
  57.7 12.3 %collective-permute-start.8 = (bf16[128,512]{1,0:T(8,128)(2,1)}, bf16[128,512]{1,0:T(8,128)(2,1)S(1)}, u32[]{:S(2)}, u32[]{:S(2)}) collective-permute-start(bf16[128,512]{1,0:T(8,128)(2,1)} %get-tuple-element.105), channel_id=1, source_target_pairs={{1,0},{2,1},{3,2},{4,3},{5,4},{6,5},{7,6},{8,7},{9,8},{10,9},{11,1... | collective-permute-start | bytes 393224 | tf_op jit(solution)/shard_map/ppermute | solution.py:516
  60.5 9.5 %collective-permute-start.9 = (bf16[128,512]{1,0:T(8,128)(2,1)}, bf16[128,512]{1,0:T(8,128)(2,1)S(1)}, u32[]{:S(2)}, u32[]{:S(2)}) collective-permute-start(bf16[128,512]{1,0:T(8,128)(2,1)} %get-tuple-element.106), channel_id=1, source_target_pairs={{2,0},{3,1},{4,2},{5,3},{6,4},{7,5},{8,6},{9,7},{10,8},{11,9},{12,... | collective-permute-start | bytes 393224 | tf_op jit(solution)/shard_map/ppermute | solution.py:516
  61.1 8.9 %collective-permute-start.10 = (bf16[128,512]{1,0:T(8,128)(2,1)}, bf16[128,512]{1,0:T(8,128)(2,1)S(1)}, u32[]{:S(2)}, u32[]{:S(2)}) collective-permute-start(bf16[128,512]{1,0:T(8,128)(2,1)} %get-tuple-element.107), channel_id=1, source_target_pairs={{15,0},{0,1},{1,2},{2,3},{3,4},{4,5},{5,6},{6,7},{7,8},{8,9},{9,10... | collective-permute-start | bytes 393224 | tf_op jit(solution)/shard_map/ppermute | solution.py:516
  61.2 9.2 %collective-permute-start.11 = (bf16[128,512]{1,0:T(8,128)(2,1)}, bf16[128,512]{1,0:T(8,128)(2,1)S(1)}, u32[]{:S(2)}, u32[]{:S(2)}) collective-permute-start(bf16[128,512]{1,0:T(8,128)(2,1)} %get-tuple-element.108), channel_id=1, source_target_pairs={{14,0},{15,1},{0,2},{1,3},{2,4},{3,5},{4,6},{5,7},{6,8},{7,9},{8,1... | collective-permute-start | bytes 393224 | tf_op jit(solution)/shard_map/ppermute | solution.py:516
  62.6 0.7 copy-start.6
  70.5 1.1 %copy-start = (bf16[8,80,512]{2,1,0:T(8,128)(2,1)S(1)}, bf16[8,80,512]{2,1,0:T(8,128)(2,1)}, u32[]{:S(2)}) copy-start(bf16[8,80,512]{2,1,0:T(8,128)(2,1)} %get-tuple-element.104.refs_0_) | copy-start | bytes 1966084
  71.6 2.5 %copy-start.3 = (bf16[8,80,512]{2,1,0:T(8,128)(2,1)S(1)}, bf16[8,80,512]{2,1,0:T(8,128)(2,1)}, u32[]{:S(2)}) copy-start(bf16[8,80,512]{2,1,0:T(8,128)(2,1)} %get-tuple-element.110) | copy-start | bytes 1966084
  71.6 3.5 %copy-start.4 = (bf16[8,64,512]{2,1,0:T(8,128)(2,1)S(1)}, bf16[8,64,512]{2,1,0:T(8,128)(2,1)}, u32[]{:S(2)}) copy-start(bf16[8,64,512]{2,1,0:T(8,128)(2,1)} %get-tuple-element.100) | copy-start | bytes 1572868
  71.6 2.5 %collective-permute-start.12 = (bf16[8,80,512]{2,1,0:T(8,128)(2,1)S(1)}, bf16[8,80,512]{2,1,0:T(8,128)(2,1)S(1)}, u32[]{:S(2)}, u32[]{:S(2)}) collective-permute-start(bf16[8,80,512]{2,1,0:T(8,128)(2,1)S(1)} %get-tuple-element.111), channel_id=1, source_target_pairs={{0,1},{1,0},{2,3},{3,2},{4,5},{5,4},{6,7},{7,6},{8,9},{9,8},{10,11... | collective-permute-start | bytes 1966088 | tf_op jit(solution)/shard_map/ppermute | solution.py:520
  72.1 2.9 %collective-permute-start.4 = (bf16[8,64,512]{2,1,0:T(8,128)(2,1)}, bf16[8,64,512]{2,1,0:T(8,128)(2,1)S(1)}, u32[]{:S(2)}, u32[]{:S(2)}) collective-permute-start(bf16[8,64,512]{2,1,0:T(8,128)(2,1)} %get-tuple-element.101), channel_id=1, source_target_pairs={{0,1},{1,0},{2,3},{3,2},{4,5},{5,4},{6,7},{7,6},{8,9},{9,8},{10,11... | collective-permute-start | bytes 1572872 | tf_op jit(solution)/shard_map/ppermute | solution.py:520
  74.2 13.6 %collective-permute-start.13 = (bf16[4,80,512]{2,1,0:T(8,128)(2,1)S(1)}, bf16[4,80,512]{2,1,0:T(8,128)(2,1)S(1)}, u32[]{:S(2)}, u32[]{:S(2)}) collective-permute-start(bf16[4,80,512]{2,1,0:T(8,128)(2,1)S(1)} %get-tuple-element.140), channel_id=1, source_target_pairs={{0,2},{1,3},{2,0},{3,1},{4,6},{5,7},{6,4},{7,5},{8,10},{9,11},{10,... | collective-permute-start | bytes 983048 | tf_op jit(solution)/shard_map/ppermute | solution.py:520
  75.2 12.6 %collective-permute-start.5 = (bf16[4,64,512]{2,1,0:T(8,128)(2,1)S(1)}, bf16[4,64,512]{2,1,0:T(8,128)(2,1)S(1)}, u32[]{:S(2)}, u32[]{:S(2)}) collective-permute-start(bf16[4,64,512]{2,1,0:T(8,128)(2,1)S(1)} %get-tuple-element.142), channel_id=1, source_target_pairs={{0,4},{1,5},{2,6},{3,7},{4,0},{5,1},{6,2},{7,3},{8,12},{9,13},{10,... | collective-permute-start | bytes 786440 | tf_op jit(solution)/shard_map/ppermute | solution.py:520
  75.7 16.5 %collective-permute-start.18 = (bf16[2,96,512]{2,1,0:T(8,128)(2,1)S(1)}, bf16[2,96,512]{2,1,0:T(8,128)(2,1)S(1)}, u32[]{:S(2)}, u32[]{:S(2)}) collective-permute-start(bf16[2,96,512]{2,1,0:T(8,128)(2,1)S(1)} %get-tuple-element.133), channel_id=1, source_target_pairs={{0,8},{1,9},{2,10},{3,11},{4,12},{5,13},{6,14},{7,15},{8,0},{9,1},... | collective-permute-start | bytes 589832 | tf_op jit(solution)/shard_map/ppermute | solution.py:520
  87.8 10.0 %copy-start.1 = (f32[256,512]{1,0:T(8,128)S(1)}, f32[256,512]{1,0:T(8,128)}, u32[]{:S(2)}) copy-start(f32[256,512]{1,0:T(8,128)} %get-tuple-element.122.own_ref) | copy-start | bytes 1572868
  87.9 10.0 %copy-start.2 = (s32[1,4,128]{2,1,0:T(4,128)S(1)}, s32[1,4,128]{2,1,0:T(4,128)}, u32[]{:S(2)}) copy-start(s32[1,4,128]{2,1,0:T(4,128)} %param.25) | copy-start | bytes 6148
  87.9 8.3 %collective-permute-start.14 = (bf16[2,80,512]{2,1,0:T(8,128)(2,1)S(1)}, bf16[2,80,512]{2,1,0:T(8,128)(2,1)S(1)}, u32[]{:S(2)}, u32[]{:S(2)}) collective-permute-start(bf16[2,80,512]{2,1,0:T(8,128)(2,1)S(1)} %get-tuple-element.115), channel_id=1, source_target_pairs={{0,4},{1,5},{2,6},{3,7},{4,0},{5,1},{6,2},{7,3},{8,12},{9,13},{10,... | collective-permute-start | bytes 491528 | tf_op jit(solution)/shard_map/ppermute | solution.py:520
  88.0 8.5 %collective-permute-start.16 = (bf16[2,64,512]{2,1,0:T(8,128)(2,1)S(1)}, bf16[2,64,512]{2,1,0:T(8,128)(2,1)S(1)}, u32[]{:S(2)}, u32[]{:S(2)}) collective-permute-start(bf16[2,64,512]{2,1,0:T(8,128)(2,1)S(1)} %get-tuple-element.119), channel_id=1, source_target_pairs={{0,8},{1,9},{2,10},{3,11},{4,12},{5,13},{6,14},{7,15},{8,0},{9,1},... | collective-permute-start | bytes 393224 | tf_op jit(solution)/shard_map/ppermute | solution.py:520
  92.3 6.0 %collective-permute-start.19 = (bf16[1,96,512]{2,1,0:T(8,128)(2,1)S(1)}, bf16[1,96,512]{2,1,0:T(8,128)(2,1)S(1)}, u32[]{:S(2)}, u32[]{:S(2)}) collective-permute-start(bf16[1,96,512]{2,1,0:T(8,128)(2,1)S(1)} %get-tuple-element.135), channel_id=1, source_target_pairs={{0,2},{1,3},{2,0},{3,1},{4,6},{5,7},{6,4},{7,5},{8,10},{9,11},{10,... | collective-permute-start | bytes 294920 | tf_op jit(solution)/shard_map/ppermute | solution.py:520
  96.2 5.4 %collective-permute-start.15 = (bf16[1,80,512]{2,1,0:T(8,128)(2,1)S(1)}, bf16[1,80,512]{2,1,0:T(8,128)(2,1)S(1)}, u32[]{:S(2)}, u32[]{:S(2)}) collective-permute-start(bf16[1,80,512]{2,1,0:T(8,128)(2,1)S(1)} %get-tuple-element.117), channel_id=1, source_target_pairs={{0,8},{1,9},{2,10},{3,11},{4,12},{5,13},{6,14},{7,15},{8,0},{9,1},... | collective-permute-start | bytes 245768 | tf_op jit(solution)/shard_map/ppermute | solution.py:520
  96.5 4.3 %collective-permute-start.17 = (bf16[1,64,512]{2,1,0:T(8,128)(2,1)S(1)}, bf16[1,64,512]{2,1,0:T(8,128)(2,1)S(1)}, u32[]{:S(2)}, u32[]{:S(2)}) collective-permute-start(bf16[1,64,512]{2,1,0:T(8,128)(2,1)S(1)} %get-tuple-element.121), channel_id=1, source_target_pairs={{0,2},{1,3},{2,0},{3,1},{4,6},{5,7},{6,4},{7,5},{8,10},{9,11},{10,... | collective-permute-start | bytes 196616 | tf_op jit(solution)/shard_map/ppermute | solution.py:520

commit v12 on v11

--- a/solution.py
+++ b/solution.py
@@ -324,9 +324,7 @@
     pass
 
 
-def halving_kernel(kept_ref, taken_ref, *refs):
-    passing = (len(refs) - 2) // 2
-    keep_ref, give_ref = refs[passing : passing + 2]
+def halving_kernel(kept_ref, taken_ref, keep_ref, give_ref):
     half = keep_ref.shape[0]
     for j in range(half):
         give_ref[j] = (kept_ref[half + j] + taken_ref[half + j].astype(F32)).astype(BF16)
@@ -494,7 +492,7 @@
     )(*ins)
 
 
-def small_call(kernel, name, ins, outs, passing=()):
+def small_call(kernel, name, ins, outs, passing=(), limit=SMALL_LIMIT):
     first = len(ins)
     last = len(outs)
     outs = list(outs) + [shape(a.shape, a.dtype) for a in passing]
@@ -506,7 +504,7 @@
         out_specs=tuple([VM] * last + [ANY] * len(passing)),
         name=name,
         cost_estimate=cost(ins, outs, 0),
-        compiler_params=pltpu.CompilerParams(vmem_limit_bytes=SMALL_LIMIT),
+        compiler_params=pltpu.CompilerParams(vmem_limit_bytes=limit),
     )(*ins, *passing)
 
 
@@ -530,9 +528,9 @@
     return kept[:half].astype(F32) + taken[:half].astype(F32), give
 
 
-def halving(kept, taken, passing=()):
+def halving(kept, taken):
     half = (kept.shape[0] // 2,) + kept.shape[1:]
-    return small_call(halving_kernel, "halving", (kept, taken), [shape(half, F32), shape(half, BF16)], passing)
+    return small_call(halving_kernel, "halving", (kept, taken), [shape(half, F32), shape(half, BF16)])
 
 
 def last_sum(groups, sizes, nodes=None):
@@ -588,7 +586,8 @@
         [shape((tile, width), BF16)] * slots,
     )
     received = [passed_along(made[slot], axis, offset) for slot, offset in enumerate(offsets)]
-    coarse_all = exchanged_with_all(jnp.broadcast_to(nodes[:COARSE_DEV][None], every.shape), axis)
+    spread = jnp.maximum(jnp.broadcast_to(nodes[:COARSE_DEV][None], every.shape), jnp.asarray(-1000.0, BF16))
+    coarse_all = exchanged_with_all(spread, axis)
 
     def saved_shapes(rows):
         return [
@@ -679,7 +678,7 @@
     if ordered:
         kept1, given1, kept2, given2 = edge_parts
         given1, node_taken, *returned = small_call(
-            order_kernel, "order", (), [], (given1, node_taken, *returned)
+            order_kernel, "order", (), [], (given1, node_taken, *returned), VMEM_LIMIT
         )
         taken1 = exchanged(given1, axis, 1)
         taken2 = exchanged(given2, axis, 1)
@@ -689,13 +688,12 @@
         kept2, given2 = first_halving(kept2, taken2)
         taken2 = exchanged(given2, axis, steps2[0])
         for k in range(1, len(steps1)):
-            passing = (kept1,) if k == 1 else ()
-            node_kept, given, *passing = halving(node_kept, node_taken, passing)
+            node_kept, given = halving(node_kept, node_taken)
             node_taken = exchanged(given, axis, steps2[k])
-            kept2, given2, *passing = halving(kept2, taken2, tuple(passing))
+            kept1, given1 = halving(kept1, taken1)
+            taken1 = exchanged(given1, axis, steps1[k])
+            kept2, given2 = halving(kept2, taken2)
             taken2 = exchanged(given2, axis, steps2[k])
-            kept1, given1 = halving(passing[0] if passing else kept1, taken1)
-            taken1 = exchanged(given1, axis, steps1[k])
         g_nw1, g_nw2 = last_sum([(node_kept, node_taken)], (rows_of(node_w1), rows_of(node_w2)))
         g_ew1, g_ew2, g_nodes = last_sum(
             [(kept1, taken1), (kept2, taken2)], (rows_of(edge_w1), rows_of(edge_w2)), tile_gradient()

time: 103 us -> 105 us (1.019)
  waiting for transfers between devices: 16.4 us -> 21 us
  starting transfers between devices: 43.3 us -> 41.3 us
    ppermute x12, waiting for transfers between devices: 15.9 us -> 20.6 us  [exchanged(): lax.ppermute(block, axis, [(i, i ^ distance) for i in range(lax.axis_size...]
    ppermute x12, starting transfers between devices: 14.9 us -> 12.8 us  [exchanged(): lax.ppermute(block, axis, [(i, i ^ distance) for i in range(lax.axis_size...]
    add x0 -> x1, other arithmetic: none -> 1.32 us  [first_halving(): return (kept[:half].astype(F32) + taken[:half].astype(F32), give)]
    convert_element_type x3 -> x2, other arithmetic: 1.6 us -> 0.29 us  [first_halving(): give = (kept[half:].astype(F32) + taken[half:].astype(F32)).astype(BF16)]
    unnamed x24 -> x44, local copies, waits for them, and re-layouts: 3.79 us -> 3.52 us
  transfers between devices with their start and end apart: 23 -> 23, of which waited for: 6 -> 7; matrix products, arithmetic and copies ran while one was open for 2% -> 2% of each run, Pallas kernels for 27% -> 26%
where the time goes in v12:
time: 105 us
  starting transfers between devices  41.3 us (39%)
  Pallas kernels  34.5 us (33%)
  waiting for transfers between devices  21 us (20%)
  local copies, waits for them, and re-layouts  4.19 us (4%)
  other arithmetic  2.31 us (2%)
  between operations  1.67 us (2%)
    pallas_call x6, Pallas kernels, call(): pl.pallas_call(functools.partial(staged_kernel, kernel, in_specs, out_spe...  32.3 us
    ppermute x12, waiting for transfers between devices, exchanged(): lax.ppermute(block, axis, [(i, i ^ distance) for i in range(lax.axis_size...  20.6 us
    all_to_all x3, starting transfers between devices, exchanged_with_all(): return lax.all_to_all(blocks, axis, 0, 0)  17.2 us
    ppermute x12, starting transfers between devices, exchanged(): lax.ppermute(block, axis, [(i, i ^ distance) for i in range(lax.axis_size...  12.8 us
    ppermute x8, starting transfers between devices, passed_along(): return lax.ppermute(block, axis, route)  11.3 us
    unnamed x44, local copies, waits for them, and re-layouts  3.52 us
    pallas_call x10, Pallas kernels, small_call(): pl.pallas_call(kernel, out_shape=tuple(outs), input_output_aliases={first...  2.2 us
  transfers between devices with their start and end apart: 23, of which 7 were waited for; matrix products, arithmetic and copies ran while one was open for 2% of the time, Pallas kernels for 26%

profile of v12, /device:TPU:0, one launch (start us, length us, event | category | flops | bytes accessed | tf_op | source)
XLA Modules:
  0.0 104.9 jit_solution(7724523929274338898)
XLA Ops:
  0.6 0.7 slice_maximum_fusion
  1.3 0.7 broadcast_in_dim.2
  2.0 7.4 %all-to-all-start = ((bf16[16,8,512]{2,1,0:T(8,128)(2,1)}), bf16[16,8,512]{2,1,0:T(8,128)(2,1)S(1)}, u32[]{:S(2)}, u32[]{:S(2)}) async-start(bf16[16,8,512]{2,1,0:T(8,128)(2,1)} %broadcast_in_dim.2), calls=%async_computation | async-start | bytes 262144 | tf_op jit(solution)/shard_map/all_to_all | solution.py:522
  9.4 2.6 %tiles.1 = (bf16[128,512]{1,0:T(8,128)(2,1)}, bf16[128,512]{1,0:T(8,128)(2,1)}, bf16[128,512]{1,0:T(8,128)(2,1)}, bf16[128,512]{1,0:T(8,128)(2,1)}) custom-call(bf16[256,512]{1,0:T(8,128)(2,1)} %refs_1_.5, s32[4,128]{1,0:T(4,128)} %bitcast.8), custom_call_target="tpu_custom_call" | custom-call | bytes 788480 | tf_op jit(solution)/shard_map/tiles/pallas_call | solution.py:483
  12.0 0.5 collective-permute-start
  12.4 1.7 %collective-permute-start.1 = (bf16[128,512]{1,0:T(8,128)(2,1)}, bf16[128,512]{1,0:T(8,128)(2,1)S(1)}, u32[]{:S(2)}, u32[]{:S(2)}) collective-permute-start(bf16[128,512]{1,0:T(8,128)(2,1)} %get-tuple-element.73), channel_id=1, source_target_pairs={{14,0},{15,1},{0,2},{1,3},{2,4},{3,5},{4,6},{5,7},{6,8},{7,9},{8,1... | collective-permute-start | bytes 393224 | tf_op jit(solution)/shard_map/ppermute | solution.py:514
  14.1 4.0 %collective-permute-start.2 = (bf16[128,512]{1,0:T(8,128)(2,1)}, bf16[128,512]{1,0:T(8,128)(2,1)S(1)}, u32[]{:S(2)}, u32[]{:S(2)}) collective-permute-start(bf16[128,512]{1,0:T(8,128)(2,1)} %get-tuple-element.74), channel_id=1, source_target_pairs={{1,0},{2,1},{3,2},{4,3},{5,4},{6,5},{7,6},{8,7},{9,8},{10,9},{11,1... | collective-permute-start | bytes 393224 | tf_op jit(solution)/shard_map/ppermute | solution.py:514
  18.1 0.3 collective-permute-start.3
  18.4 0.7 copy-done.14
  19.0 4.0 %coarse_forward.1 = (bf16[128,512]{1,0:T(8,128)(2,1)}, bf16[16,8,512]{2,1,0:T(8,128)(2,1)}, bf16[128,512]{1,0:T(8,128)(2,1)}, bf16[128,512]{1,0:T(8,128)(2,1)}, ...) custom-call(bf16[16,8,512]{2,1,0:T(8,128)(2,1)} %copy-done.14, ...), custom_call_target="tpu_custom_call" | custom-call | flops 268435456 | bytes 3345408 | tf_op jit(solution)/shard_map/coarse_forward/pallas_call | solution.py:483
  23.0 4.0 %all-to-all-start.1 = ((bf16[16,8,512]{2,1,0:T(8,128)(2,1)}), bf16[16,8,512]{2,1,0:T(8,128)(2,1)S(1)}, u32[]{:S(2)}, u32[]{:S(2)}) async-start(bf16[16,8,512]{2,1,0:T(8,128)(2,1)} %get-tuple-element.77), calls=%async_computation.1 | async-start | bytes 262144 | tf_op jit(solution)/shard_map/all_to_all | solution.py:522
  27.8 0.0 copy-start.19
  27.8 0.0 copy-start.21
  27.8 0.6 copy-done.18
  28.4 0.0 copy-done.19
  28.5 0.0 copy-done.20
  28.5 0.0 copy-done.21
  28.5 6.7 %fine_forward.1 = (bf16[512,512]{1,0:T(8,128)(2,1)}, f32[256,512]{1,0:T(8,128)}, bf16[512,512]{1,0:T(8,128)(2,1)}, bf16[512,512]{1,0:T(8,128)(2,1)}, bf16[512,51...) custom-call(s32[1]{0:T(128)S(6)} %copy.40.refs_0_, ...), custom_call_target="tpu_custom_call" | custom-call | flops 1879048192 | bytes 7346180 | tf_op jit(solution)/shard_map/fine_forward/pallas_call | solution.py:483
  35.3 0.6 copy-done.16
  35.9 5.8 %node_both.1 = (bf16[256,512]{1,0:T(8,128)(2,1)}, f32[256,512]{1,0:T(8,128)}, bf16[256,512]{1,0:T(8,128)(2,1)}, bf16[16,8,512]{2,1,0:T(8,128)(2,1)}, bf16[8,96,5...) custom-call(s32[1]{0:T(128)} %bitcast.refs_0_, bf16[256,512]{1,0:T(8,128)(2,1)} %refs_1_.5, ...), custom_call_target="tpu_custom_call" | custom-call | flops 1207959552 | bytes 5507076 | tf_op jit(solution)/shard_map/node_both/pallas_call | solution.py:483
  41.8 0.5 collective-permute-start.4
  42.2 5.8 %all-to-all-start.2 = ((bf16[16,8,512]{2,1,0:T(8,128)(2,1)}), bf16[16,8,512]{2,1,0:T(8,128)(2,1)S(1)}, u32[]{:S(2)}, u32[]{:S(2)}) async-start(bf16[16,8,512]{2,1,0:T(8,128)(2,1)} %get-tuple-element.81), calls=%async_computation.2 | async-start | bytes 262144 | tf_op jit(solution)/shard_map/all_to_all | solution.py:522
  48.0 1.3 %convert_add_fusion = (f32[4,96,512]{2,1,0:T(8,128)S(1)}, bf16[4,96,512]{2,1,0:T(8,128)(2,1)S(1)}) fusion(bf16[8,96,512]{2,1,0:T(8,128)(2,1)S(1)} %collective-permute-done.4, bf16[8,96,512]{2,1,0:T(8,128)(2,1)} %get-tuple-element.100), kind=kLoop, calls=%fused_computation | loop fusion | flops 1376256 | bytes 2752512 | tf_op jit(solution)/shard_map/add | solution.py:528
  49.3 2.0 %collective-permute-start.5 = (bf16[4,96,512]{2,1,0:T(8,128)(2,1)S(1)}, bf16[4,96,512]{2,1,0:T(8,128)(2,1)S(1)}, u32[]{:S(2)}, u32[]{:S(2)}) collective-permute-start(bf16[4,96,512]{2,1,0:T(8,128)(2,1)S(1)} %get-tuple-element.135), channel_id=1, source_target_pairs={{0,4},{1,5},{2,6},{3,7},{4,0},{5,1},{6,2},{7,3},{8,12},{9,13},{10,... | collective-permute-start | bytes 1179656 | tf_op jit(solution)/shard_map/ppermute | solution.py:518
  51.3 6.4 %fine_backward.1 = (bf16[512,512]{1,0:T(8,128)(2,1)}, bf16[512,512]{1,0:T(8,128)(2,1)}, bf16[512,512]{1,0:T(8,128)(2,1)}, f32[256,512]{1,0:T(8,128)}, bf16[128,5...) custom-call(s32[1]{0:T(128)S(6)} %copy.40.refs_0_, ...), custom_call_target="tpu_custom_call" | custom-call | flops 1744830464 | bytes 7346180 | tf_op jit(solution)/shard_map/fine_backward/pallas_call | solution.py:483
  57.7 2.8 %collective-permute-start.6 = (bf16[128,512]{1,0:T(8,128)(2,1)}, bf16[128,512]{1,0:T(8,128)(2,1)S(1)}, u32[]{:S(2)}, u32[]{:S(2)}) collective-permute-start(bf16[128,512]{1,0:T(8,128)(2,1)} %get-tuple-element.102), channel_id=1, source_target_pairs={{1,0},{2,1},{3,2},{4,3},{5,4},{6,5},{7,6},{8,7},{9,8},{10,9},{11,1... | collective-permute-start | bytes 393224 | tf_op jit(solution)/shard_map/ppermute | solution.py:514
  60.5 0.6 collective-permute-start.7
  61.1 0.2 collective-permute-start.8
  61.3 1.3 %collective-permute-start.9 = (bf16[128,512]{1,0:T(8,128)(2,1)}, bf16[128,512]{1,0:T(8,128)(2,1)S(1)}, u32[]{:S(2)}, u32[]{:S(2)}) collective-permute-start(bf16[128,512]{1,0:T(8,128)(2,1)} %get-tuple-element.105), channel_id=1, source_target_pairs={{14,0},{15,1},{0,2},{1,3},{2,4},{3,5},{4,6},{5,7},{6,8},{7,9},{8,1... | collective-permute-start | bytes 393224 | tf_op jit(solution)/shard_map/ppermute | solution.py:514
  62.6 0.7 copy-done.15
  63.2 6.8 %coarse_backward.1 = (bf16[128,512]{1,0:T(8,128)(2,1)}, bf16[8,80,512]{2,1,0:T(8,128)(2,1)}, bf16[8,80,512]{2,1,0:T(8,128)(2,1)}, bf16[8,64,512]{2,1,0:T(8,128)(2,1)}, bf16[8,64,512]{2,1,0:T(8,128)(2,1)}) custom-call(s32[1]{0:T(128)} %bitcast.refs_0_, s32[1,128]{1,0:T(1,128)} %bitcast.17, bf16[16,8,512]{2,1,0:T(8,128)(2,1)} %copy-done.15, ...), custom_call_target="tpu_custom_call" | custom-call | flops 1879048192 | bytes 8850436 | tf_op jit(solution)/shard_map/coarse_backward/pallas_call | solution.py:483
  70.1 0.0 copy-start.4
  70.1 0.0 copy-start.6
  70.1 0.4 collective-permute-done.9.refs_5_
  70.5 0.2 copy-done.2
  70.7 0.0 copy-done.4
  70.7 0.0 copy-done.6
  70.8 0.4 copy-done.8
  71.2 0.1 copy-done
  71.3 0.5 collective-permute-start.10
  71.8 0.1 collective-permute-start.14
  71.9 2.1 %collective-permute-done.10 = bf16[8,80,512]{2,1,0:T(8,128)(2,1)S(1)} collective-permute-done((bf16[8,80,512]{2,1,0:T(8,128)(2,1)}, bf16[8,80,512]{2,1,0:T(8,128)(2,1)S(1)}, u32[]{:S(2)}, u32[]{:S(2)}) %collective-permute-start.10) | collective-permute-done | bytes 655392 | tf_op jit(solution)/shard_map/ppermute | solution.py:518
  74.0 0.2 add_convert_fusion.1
  74.1 0.8 collective-permute-start.11
  74.9 0.1 add_convert_fusion.2
  75.1 0.5 collective-permute-start.15
  75.6 0.1 halving.10
  75.7 3.9 %collective-permute-start.18 = (bf16[2,96,512]{2,1,0:T(8,128)(2,1)S(1)}, bf16[2,96,512]{2,1,0:T(8,128)(2,1)S(1)}, u32[]{:S(2)}, u32[]{:S(2)}) collective-permute-start(bf16[2,96,512]{2,1,0:T(8,128)(2,1)S(1)} %get-tuple-element.129), channel_id=1, source_target_pairs={{0,8},{1,9},{2,10},{3,11},{4,12},{5,13},{6,14},{7,15},{8,0},{9,1},... | collective-permute-start | bytes 589832 | tf_op jit(solution)/shard_map/ppermute | solution.py:518
  79.5 4.7 %collective-permute-done.11.taken_ref = bf16[4,80,512]{2,1,0:T(8,128)(2,1)S(1)} collective-permute-done((bf16[4,80,512]{2,1,0:T(8,128)(2,1)S(1)}, bf16[4,80,512]{2,1,0:T(8,128)(2,1)S(1)}, u32[]{:S(2)}, u32[]{:S(2)}) %collective-permute-start.11) | collective-permute-done | bytes 327712 | tf_op jit(solution)/shard_map/ppermute | solution.py:518
  84.2 0.0 copy-start.11
  84.2 0.1 halving.6
  84.3 0.1 collective-permute-start.12
  84.4 4.1 %collective-permute-done.15.taken_ref = bf16[4,64,512]{2,1,0:T(8,128)(2,1)S(1)} collective-permute-done((bf16[4,64,512]{2,1,0:T(8,128)(2,1)S(1)}, bf16[4,64,512]{2,1,0:T(8,128)(2,1)S(1)}, u32[]{:S(2)}, u32[]{:S(2)}) %collective-permute-start.15) | collective-permute-done | bytes 262176 | tf_op jit(solution)/shard_map/ppermute | solution.py:518
  88.5 0.1 halving.8
  88.6 1.8 %collective-permute-start.16 = (bf16[2,64,512]{2,1,0:T(8,128)(2,1)S(1)}, bf16[2,64,512]{2,1,0:T(8,128)(2,1)S(1)}, u32[]{:S(2)}, u32[]{:S(2)}) collective-permute-start(bf16[2,64,512]{2,1,0:T(8,128)(2,1)S(1)} %get-tuple-element.114), channel_id=1, source_target_pairs={{0,8},{1,9},{2,10},{3,11},{4,12},{5,13},{6,14},{7,15},{8,0},{9,1},... | collective-permute-start | bytes 393224 | tf_op jit(solution)/shard_map/ppermute | solution.py:518
  90.5 0.1 collective-permute-start.19
  90.5 2.0 %collective-permute-done.12.taken_ref = bf16[2,80,512]{2,1,0:T(8,128)(2,1)S(1)} collective-permute-done((bf16[2,80,512]{2,1,0:T(8,128)(2,1)S(1)}, bf16[2,80,512]{2,1,0:T(8,128)(2,1)S(1)}, u32[]{:S(2)}, u32[]{:S(2)}) %collective-permute-start.12) | collective-permute-done | bytes 163872 | tf_op jit(solution)/shard_map/ppermute | solution.py:518
  92.6 1.9 %collective-permute-start.13 = (bf16[1,80,512]{2,1,0:T(8,128)(2,1)S(1)}, bf16[1,80,512]{2,1,0:T(8,128)(2,1)S(1)}, u32[]{:S(2)}, u32[]{:S(2)}) collective-permute-start(bf16[1,80,512]{2,1,0:T(8,128)(2,1)S(1)} %get-tuple-element.110), channel_id=1, source_target_pairs={{0,8},{1,9},{2,10},{3,11},{4,12},{5,13},{6,14},{7,15},{8,0},{9,1},... | collective-permute-start | bytes 245768 | tf_op jit(solution)/shard_map/ppermute | solution.py:518
  94.5 5.2 %collective-permute-done.16.taken_ref = bf16[2,64,512]{2,1,0:T(8,128)(2,1)S(1)} collective-permute-done((bf16[2,64,512]{2,1,0:T(8,128)(2,1)S(1)}, bf16[2,64,512]{2,1,0:T(8,128)(2,1)S(1)}, u32[]{:S(2)}, u32[]{:S(2)}) %collective-permute-start.16) | collective-permute-done | bytes 131104 | tf_op jit(solution)/shard_map/ppermute | solution.py:518
  99.7 0.7 collective-permute-start.17
  100.5 0.4 node_gradient.1.refs_4_
  100.9 0.7 last_sum.3
  101.6 2.4 %collective-permute-done.17.refs_3_ = bf16[1,64,512]{2,1,0:T(8,128)(2,1)S(1)} collective-permute-done((bf16[1,64,512]{2,1,0:T(8,128)(2,1)S(1)}, bf16[1,64,512]{2,1,0:T(8,128)(2,1)S(1)}, u32[]{:S(2)}, u32[]{:S(2)}) %collective-permute-start.17) | collective-permute-done | bytes 65568 | tf_op jit(solution)/shard_map/ppermute | solution.py:518
  104.0 0.8 last_sum.2
  (47 shorter events, 0.2 us)
Async XLA Ops:
  2.0 16.4 %all-to-all-start = ((bf16[16,8,512]{2,1,0:T(8,128)(2,1)}), bf16[16,8,512]{2,1,0:T(8,128)(2,1)S(1)}, u32[]{:S(2)}, u32[]{:S(2)}) async-start(bf16[16,8,512]{2,1,0:T(8,128)(2,1)} %broadcast_in_dim.2), calls=%async_computation | async-start | bytes 262144 | tf_op jit(solution)/shard_map/all_to_all | solution.py:522
  12.0 15.8 %collective-permute-start = (bf16[128,512]{1,0:T(8,128)(2,1)}, bf16[128,512]{1,0:T(8,128)(2,1)S(1)}, u32[]{:S(2)}, u32[]{:S(2)}) collective-permute-start(bf16[128,512]{1,0:T(8,128)(2,1)} %get-tuple-element.72), channel_id=1, source_target_pairs={{15,0},{0,1},{1,2},{2,3},{3,4},{4,5},{5,6},{6,7},{7,8},{8,9},{9,10... | collective-permute-start | bytes 393224 | tf_op jit(solution)/shard_map/ppermute | solution.py:514
  12.4 15.4 %collective-permute-start.1 = (bf16[128,512]{1,0:T(8,128)(2,1)}, bf16[128,512]{1,0:T(8,128)(2,1)S(1)}, u32[]{:S(2)}, u32[]{:S(2)}) collective-permute-start(bf16[128,512]{1,0:T(8,128)(2,1)} %get-tuple-element.73), channel_id=1, source_target_pairs={{14,0},{15,1},{0,2},{1,3},{2,4},{3,5},{4,6},{5,7},{6,8},{7,9},{8,1... | collective-permute-start | bytes 393224 | tf_op jit(solution)/shard_map/ppermute | solution.py:514
  14.1 13.7 %collective-permute-start.2 = (bf16[128,512]{1,0:T(8,128)(2,1)}, bf16[128,512]{1,0:T(8,128)(2,1)S(1)}, u32[]{:S(2)}, u32[]{:S(2)}) collective-permute-start(bf16[128,512]{1,0:T(8,128)(2,1)} %get-tuple-element.74), channel_id=1, source_target_pairs={{1,0},{2,1},{3,2},{4,3},{5,4},{6,5},{7,6},{8,7},{9,8},{10,9},{11,1... | collective-permute-start | bytes 393224 | tf_op jit(solution)/shard_map/ppermute | solution.py:514
  18.1 9.7 %collective-permute-start.3 = (bf16[128,512]{1,0:T(8,128)(2,1)}, bf16[128,512]{1,0:T(8,128)(2,1)S(1)}, u32[]{:S(2)}, u32[]{:S(2)}) collective-permute-start(bf16[128,512]{1,0:T(8,128)(2,1)} %get-tuple-element.75), channel_id=1, source_target_pairs={{2,0},{3,1},{4,2},{5,3},{6,4},{7,5},{8,6},{9,7},{10,8},{11,9},{12,... | collective-permute-start | bytes 393224 | tf_op jit(solution)/shard_map/ppermute | solution.py:514
  18.4 0.7 copy-start.14
  23.0 12.2 %all-to-all-start.1 = ((bf16[16,8,512]{2,1,0:T(8,128)(2,1)}), bf16[16,8,512]{2,1,0:T(8,128)(2,1)S(1)}, u32[]{:S(2)}, u32[]{:S(2)}) async-start(bf16[16,8,512]{2,1,0:T(8,128)(2,1)} %get-tuple-element.77), calls=%async_computation.1 | async-start | bytes 262144 | tf_op jit(solution)/shard_map/all_to_all | solution.py:522
  27.7 0.7 copy-start.18
  27.8 0.7 copy-start.19
  27.8 0.7 copy-start.20
  27.8 0.7 copy-start.21
  35.3 0.7 copy-start.16
  41.8 6.2 %collective-permute-start.4 = (bf16[8,96,512]{2,1,0:T(8,128)(2,1)}, bf16[8,96,512]{2,1,0:T(8,128)(2,1)S(1)}, u32[]{:S(2)}, u32[]{:S(2)}) collective-permute-start(bf16[8,96,512]{2,1,0:T(8,128)(2,1)} %get-tuple-element.101), channel_id=1, source_target_pairs={{0,1},{1,0},{2,3},{3,2},{4,5},{5,4},{6,7},{7,6},{8,9},{9,8},{10,11... | collective-permute-start | bytes 2359304 | tf_op jit(solution)/shard_map/ppermute | solution.py:518
  42.2 20.4 %all-to-all-start.2 = ((bf16[16,8,512]{2,1,0:T(8,128)(2,1)}), bf16[16,8,512]{2,1,0:T(8,128)(2,1)S(1)}, u32[]{:S(2)}, u32[]{:S(2)}) async-start(bf16[16,8,512]{2,1,0:T(8,128)(2,1)} %get-tuple-element.81), calls=%async_computation.2 | async-start | bytes 262144 | tf_op jit(solution)/shard_map/all_to_all | solution.py:522
  49.3 21.2 %collective-permute-start.5 = (bf16[4,96,512]{2,1,0:T(8,128)(2,1)S(1)}, bf16[4,96,512]{2,1,0:T(8,128)(2,1)S(1)}, u32[]{:S(2)}, u32[]{:S(2)}) collective-permute-start(bf16[4,96,512]{2,1,0:T(8,128)(2,1)S(1)} %get-tuple-element.135), channel_id=1, source_target_pairs={{0,4},{1,5},{2,6},{3,7},{4,0},{5,1},{6,2},{7,3},{8,12},{9,13},{10,... | collective-permute-start | bytes 1179656 | tf_op jit(solution)/shard_map/ppermute | solution.py:518
  57.7 12.3 %collective-permute-start.6 = (bf16[128,512]{1,0:T(8,128)(2,1)}, bf16[128,512]{1,0:T(8,128)(2,1)S(1)}, u32[]{:S(2)}, u32[]{:S(2)}) collective-permute-start(bf16[128,512]{1,0:T(8,128)(2,1)} %get-tuple-element.102), channel_id=1, source_target_pairs={{1,0},{2,1},{3,2},{4,3},{5,4},{6,5},{7,6},{8,7},{9,8},{10,9},{11,1... | collective-permute-start | bytes 393224 | tf_op jit(solution)/shard_map/ppermute | solution.py:514
  60.5 9.5 %collective-permute-start.7 = (bf16[128,512]{1,0:T(8,128)(2,1)}, bf16[128,512]{1,0:T(8,128)(2,1)S(1)}, u32[]{:S(2)}, u32[]{:S(2)}) collective-permute-start(bf16[128,512]{1,0:T(8,128)(2,1)} %get-tuple-element.103), channel_id=1, source_target_pairs={{2,0},{3,1},{4,2},{5,3},{6,4},{7,5},{8,6},{9,7},{10,8},{11,9},{12,... | collective-permute-start | bytes 393224 | tf_op jit(solution)/shard_map/ppermute | solution.py:514
  61.1 9.0 %collective-permute-start.8 = (bf16[128,512]{1,0:T(8,128)(2,1)}, bf16[128,512]{1,0:T(8,128)(2,1)S(1)}, u32[]{:S(2)}, u32[]{:S(2)}) collective-permute-start(bf16[128,512]{1,0:T(8,128)(2,1)} %get-tuple-element.104), channel_id=1, source_target_pairs={{15,0},{0,1},{1,2},{2,3},{3,4},{4,5},{5,6},{6,7},{7,8},{8,9},{9,10... | collective-permute-start | bytes 393224 | tf_op jit(solution)/shard_map/ppermute | solution.py:514
  61.3 9.2 %collective-permute-start.9 = (bf16[128,512]{1,0:T(8,128)(2,1)}, bf16[128,512]{1,0:T(8,128)(2,1)S(1)}, u32[]{:S(2)}, u32[]{:S(2)}) collective-permute-start(bf16[128,512]{1,0:T(8,128)(2,1)} %get-tuple-element.105), channel_id=1, source_target_pairs={{14,0},{15,1},{0,2},{1,3},{2,4},{3,5},{4,6},{5,7},{6,8},{7,9},{8,1... | collective-permute-start | bytes 393224 | tf_op jit(solution)/shard_map/ppermute | solution.py:514
  62.6 0.7 copy-start.15
  70.0 1.8 %copy-start.17 = (bf16[8,64,512]{2,1,0:T(8,128)(2,1)S(1)}, bf16[8,64,512]{2,1,0:T(8,128)(2,1)}, u32[]{:S(2)}) copy-start(bf16[8,64,512]{2,1,0:T(8,128)(2,1)} %get-tuple-element.112) | copy-start | bytes 1572868
  70.0 4.0 %copy-start.12 = (bf16[8,80,512]{2,1,0:T(8,128)(2,1)S(1)}, bf16[8,80,512]{2,1,0:T(8,128)(2,1)}, u32[]{:S(2)}) copy-start(bf16[8,80,512]{2,1,0:T(8,128)(2,1)} %get-tuple-element.98) | copy-start | bytes 1966084
  70.0 0.7 copy-start.2
  70.1 0.7 copy-start.4
  70.1 0.7 copy-start.6
  70.5 0.7 copy-start.8
  70.5 0.8 copy-start
  71.3 3.6 %copy-start.13 = (bf16[8,64,512]{2,1,0:T(8,128)(2,1)S(1)}, bf16[8,64,512]{2,1,0:T(8,128)(2,1)}, u32[]{:S(2)}) copy-start(bf16[8,64,512]{2,1,0:T(8,128)(2,1)} %get-tuple-element.111) | copy-start | bytes 1572868
  71.3 2.7 %collective-permute-start.10 = (bf16[8,80,512]{2,1,0:T(8,128)(2,1)}, bf16[8,80,512]{2,1,0:T(8,128)(2,1)S(1)}, u32[]{:S(2)}, u32[]{:S(2)}) collective-permute-start(bf16[8,80,512]{2,1,0:T(8,128)(2,1)} %get-tuple-element.106), channel_id=1, source_target_pairs={{0,1},{1,0},{2,3},{3,2},{4,5},{5,4},{6,7},{7,6},{8,9},{9,8},{10,11... | collective-permute-start | bytes 1966088 | tf_op jit(solution)/shard_map/ppermute | solution.py:518
  71.8 3.1 %collective-permute-start.14 = (bf16[8,64,512]{2,1,0:T(8,128)(2,1)S(1)}, bf16[8,64,512]{2,1,0:T(8,128)(2,1)S(1)}, u32[]{:S(2)}, u32[]{:S(2)}) collective-permute-start(bf16[8,64,512]{2,1,0:T(8,128)(2,1)S(1)} %copy-done.17), channel_id=1, source_target_pairs={{0,1},{1,0},{2,3},{3,2},{4,5},{5,4},{6,7},{7,6},{8,9},{9,8},{10,11... | collective-permute-start | bytes 1572872 | tf_op jit(solution)/shard_map/ppermute | solution.py:518
  74.0 1.6 %copy-start.1 = (bf16[4,96,512]{2,1,0:T(8,128)(2,1)S(1)}, bf16[4,96,512]{2,1,0:T(8,128)(2,1)}, u32[]{:S(2)}) copy-start(bf16[4,96,512]{2,1,0:T(8,128)(2,1)} %get-tuple-element.127.taken_ref) | copy-start | bytes 1179652
  74.1 10.1 %collective-permute-start.11 = (bf16[4,80,512]{2,1,0:T(8,128)(2,1)S(1)}, bf16[4,80,512]{2,1,0:T(8,128)(2,1)S(1)}, u32[]{:S(2)}, u32[]{:S(2)}) collective-permute-start(bf16[4,80,512]{2,1,0:T(8,128)(2,1)S(1)} %get-tuple-element.136), channel_id=1, source_target_pairs={{0,2},{1,3},{2,0},{3,1},{4,6},{5,7},{6,4},{7,5},{8,10},{9,11},{10,... | collective-permute-start | bytes 983048 | tf_op jit(solution)/shard_map/ppermute | solution.py:518
  75.1 13.4 %collective-permute-start.15 = (bf16[4,64,512]{2,1,0:T(8,128)(2,1)S(1)}, bf16[4,64,512]{2,1,0:T(8,128)(2,1)S(1)}, u32[]{:S(2)}, u32[]{:S(2)}) collective-permute-start(bf16[4,64,512]{2,1,0:T(8,128)(2,1)S(1)} %get-tuple-element.138), channel_id=1, source_target_pairs={{0,4},{1,5},{2,6},{3,7},{4,0},{5,1},{6,2},{7,3},{8,12},{9,13},{10,... | collective-permute-start | bytes 786440 | tf_op jit(solution)/shard_map/ppermute | solution.py:518
  75.7 14.8 %collective-permute-start.18 = (bf16[2,96,512]{2,1,0:T(8,128)(2,1)S(1)}, bf16[2,96,512]{2,1,0:T(8,128)(2,1)S(1)}, u32[]{:S(2)}, u32[]{:S(2)}) collective-permute-start(bf16[2,96,512]{2,1,0:T(8,128)(2,1)S(1)} %get-tuple-element.129), channel_id=1, source_target_pairs={{0,8},{1,9},{2,10},{3,11},{4,12},{5,13},{6,14},{7,15},{8,0},{9,1},... | collective-permute-start | bytes 589832 | tf_op jit(solution)/shard_map/ppermute | solution.py:518
  84.2 16.2 %copy-start.3 = (bf16[128,512]{1,0:T(8,128)(2,1)S(1)}, bf16[128,512]{1,0:T(8,128)(2,1)}, u32[]{:S(2)}) copy-start(bf16[128,512]{1,0:T(8,128)(2,1)} %get-tuple-element.118.refs_0_) | copy-start | bytes 393220
  84.2 16.2 %copy-start.5 = (bf16[128,512]{1,0:T(8,128)(2,1)S(1)}, bf16[128,512]{1,0:T(8,128)(2,1)}, u32[]{:S(2)}) copy-start(bf16[128,512]{1,0:T(8,128)(2,1)} %get-tuple-element.119.refs_1_) | copy-start | bytes 393220
  84.2 16.2 %copy-start.7 = (bf16[128,512]{1,0:T(8,128)(2,1)S(1)}, bf16[128,512]{1,0:T(8,128)(2,1)}, u32[]{:S(2)}) copy-start(bf16[128,512]{1,0:T(8,128)(2,1)} %get-tuple-element.120.refs_2_) | copy-start | bytes 393220
  84.2 16.2 %copy-start.9 = (bf16[128,512]{1,0:T(8,128)(2,1)S(1)}, bf16[128,512]{1,0:T(8,128)(2,1)}, u32[]{:S(2)}) copy-start(bf16[128,512]{1,0:T(8,128)(2,1)} %get-tuple-element.121.refs_3_) | copy-start | bytes 393220
  84.2 16.2 %copy-start.10 = (f32[256,512]{1,0:T(8,128)S(1)}, f32[256,512]{1,0:T(8,128)}, u32[]{:S(2)}) copy-start(f32[256,512]{1,0:T(8,128)} %get-tuple-element.117.own_ref) | copy-start | bytes 1572868
  84.2 16.2 %copy-start.11 = (s32[1,4,128]{2,1,0:T(4,128)S(1)}, s32[1,4,128]{2,1,0:T(4,128)}, u32[]{:S(2)}) copy-start(s32[1,4,128]{2,1,0:T(4,128)} %param.25) | copy-start | bytes 6148
  84.3 8.3 %collective-permute-start.12 = (bf16[2,80,512]{2,1,0:T(8,128)(2,1)S(1)}, bf16[2,80,512]{2,1,0:T(8,128)(2,1)S(1)}, u32[]{:S(2)}, u32[]{:S(2)}) collective-permute-start(bf16[2,80,512]{2,1,0:T(8,128)(2,1)S(1)} %get-tuple-element.108), channel_id=1, source_target_pairs={{0,4},{1,5},{2,6},{3,7},{4,0},{5,1},{6,2},{7,3},{8,12},{9,13},{10,... | collective-permute-start | bytes 491528 | tf_op jit(solution)/shard_map/ppermute | solution.py:518
  88.6 11.1 %collective-permute-start.16 = (bf16[2,64,512]{2,1,0:T(8,128)(2,1)S(1)}, bf16[2,64,512]{2,1,0:T(8,128)(2,1)S(1)}, u32[]{:S(2)}, u32[]{:S(2)}) collective-permute-start(bf16[2,64,512]{2,1,0:T(8,128)(2,1)S(1)} %get-tuple-element.114), channel_id=1, source_target_pairs={{0,8},{1,9},{2,10},{3,11},{4,12},{5,13},{6,14},{7,15},{8,0},{9,1},... | collective-permute-start | bytes 393224 | tf_op jit(solution)/shard_map/ppermute | solution.py:518
  90.5 10.4 %collective-permute-start.19 = (bf16[1,96,512]{2,1,0:T(8,128)(2,1)S(1)}, bf16[1,96,512]{2,1,0:T(8,128)(2,1)S(1)}, u32[]{:S(2)}, u32[]{:S(2)}) collective-permute-start(bf16[1,96,512]{2,1,0:T(8,128)(2,1)S(1)} %get-tuple-element.131), channel_id=1, source_target_pairs={{0,2},{1,3},{2,0},{3,1},{4,6},{5,7},{6,4},{7,5},{8,10},{9,11},{10,... | collective-permute-start | bytes 294920 | tf_op jit(solution)/shard_map/ppermute | solution.py:518
  92.6 11.4 %collective-permute-start.13 = (bf16[1,80,512]{2,1,0:T(8,128)(2,1)S(1)}, bf16[1,80,512]{2,1,0:T(8,128)(2,1)S(1)}, u32[]{:S(2)}, u32[]{:S(2)}) collective-permute-start(bf16[1,80,512]{2,1,0:T(8,128)(2,1)S(1)} %get-tuple-element.110), channel_id=1, source_target_pairs={{0,8},{1,9},{2,10},{3,11},{4,12},{5,13},{6,14},{7,15},{8,0},{9,1},... | collective-permute-start | bytes 245768 | tf_op jit(solution)/shard_map/ppermute | solution.py:518
  99.7 4.3 %collective-permute-start.17 = (bf16[1,64,512]{2,1,0:T(8,128)(2,1)S(1)}, bf16[1,64,512]{2,1,0:T(8,128)(2,1)S(1)}, u32[]{:S(2)}, u32[]{:S(2)}) collective-permute-start(bf16[1,64,512]{2,1,0:T(8,128)(2,1)S(1)} %get-tuple-element.116), channel_id=1, source_target_pairs={{0,2},{1,3},{2,0},{3,1},{4,6},{5,7},{6,4},{7,5},{8,10},{9,11},{10,... | collective-permute-start | bytes 196616 | tf_op jit(solution)/shard_map/ppermute | solution.py:518

commit v13 on v12

--- a/solution.py
+++ b/solution.py
@@ -222,21 +222,22 @@
         def share(ref):
             return ref, 0, ref.shape[0] // peers
 
-        by_distance(me_ref[0], peers, x_last(peers), (share(g1_ref), share(g2_ref)), kept_ref, given_ref)
+        by_distance(me_ref[0], peers, x_first(peers), (share(g1_ref), share(g2_ref)), kept_ref, given_ref)
 
 
 def fine_backward_kernel(
     count_ref, recv_ref, dagg_ref, d_ref, gain_ref, std_ref, normed_ref, w2_ref, slope_ref,
     w1_ref, send_ref, base_ref,
-    out_ref, pre_ref, g_ref, own_ref, *rest, block,
+    out_ref, pre_ref, g_ref, own_ref, order_ref, *rest, block,
 ):
-    piece_refs, space_ref = rest[:-1], rest[-1]
+    piece_refs, (send_dz_ref, recv_dz_ref) = rest[:-2], rest[-2:]
     count, width = d_ref.shape
     own = base_ref.shape[0]
-    received = None
+    tile = piece_refs[0].shape[0]
+    order_ref[...] = jnp.zeros(order_ref.shape, F32)
+    order_ref.done()
     for start in range(0, count, block):
         rows = slice(start, start + block)
-        hot_r = one_hot(recv_ref[:, rows], own)
         d_edges = d_ref[rows, :].astype(F32)
         place = start + lax.broadcasted_iota(jnp.int32, (block, 1), 0)
         cotan = jnp.where(place < count_ref[0], d_edges + pick(recv_ref[:, rows], dagg_ref[...]), 0.0)
@@ -250,17 +251,15 @@
         pre_ref.done(rows)
         g_ref[rows, :] = (d_edges + mm_nt(back_pre, w1_ref[0:width, :])).astype(BF16)
         g_ref.done(rows)
-        dz_send = mm_nt(back_pre, w1_ref[width : 2 * width, :]).astype(BF16)
-        dz_recv = mm_nt(back_pre, w1_ref[2 * width : 3 * width, :]).astype(BF16)
-        sent = mm(one_hot(send_ref[:, rows], space_ref.shape[0]), dz_send)
-        space_ref[...] = sent if start == 0 else space_ref[...] + sent
-        arrived = mm(hot_r, dz_recv)
-        received = arrived if received is None else received + arrived
+        send_dz_ref[rows, :] = mm_nt(back_pre, w1_ref[width : 2 * width, :]).astype(BF16)
+        recv_dz_ref[rows, :] = mm_nt(back_pre, w1_ref[2 * width : 3 * width, :]).astype(BF16)
+    send = send_ref[...]
     for slot, piece in enumerate(piece_refs):
-        tile = piece.shape[0]
-        piece[...] = space_ref[own + slot * tile : own + (slot + 1) * tile, :].astype(BF16)
+        piece[...] = mm(one_hot(send - (own + slot * tile), tile), send_dz_ref[...]).astype(BF16)
         piece.done()
-    own_ref[...] = base_ref[...] + received + space_ref[0:own, :]
+    own_ref[...] = (
+        base_ref[...] + (mm(one_hot(recv_ref[...], own), recv_dz_ref[...]) + mm(one_hot(send, own), send_dz_ref[...]))
+    )
 
 
 def coarse_backward_kernel(
@@ -324,7 +323,8 @@
     pass
 
 
-def halving_kernel(kept_ref, taken_ref, keep_ref, give_ref):
+def halving_kernel(kept_ref, taken_ref, *refs):
+    keep_ref, give_ref = refs if len(refs) == 2 else refs[1:3]
     half = keep_ref.shape[0]
     for j in range(half):
         give_ref[j] = (kept_ref[half + j] + taken_ref[half + j].astype(F32)).astype(BF16)
@@ -528,9 +528,9 @@
     return kept[:half].astype(F32) + taken[:half].astype(F32), give
 
 
-def halving(kept, taken):
+def halving(kept, taken, passing=()):
     half = (kept.shape[0] // 2,) + kept.shape[1:]
-    return small_call(halving_kernel, "halving", (kept, taken), [shape(half, F32), shape(half, BF16)])
+    return small_call(halving_kernel, "halving", (kept, taken), [shape(half, F32), shape(half, BF16)], passing)
 
 
 def last_sum(groups, sizes, nodes=None):
@@ -586,8 +586,7 @@
         [shape((tile, width), BF16)] * slots,
     )
     received = [passed_along(made[slot], axis, offset) for slot, offset in enumerate(offsets)]
-    spread = jnp.maximum(jnp.broadcast_to(nodes[:COARSE_DEV][None], every.shape), jnp.asarray(-1000.0, BF16))
-    coarse_all = exchanged_with_all(spread, axis)
+    coarse_all = exchanged_with_all(jnp.broadcast_to(nodes[:COARSE_DEV][None], every.shape), axis)
 
     def saved_shapes(rows):
         return [
@@ -641,16 +640,19 @@
         sum_shapes = [shape((peers // 2, cut, width), BF16)] * 2 + [shape((peers // 2, rows, width), BF16)] * 2
     f_zs, f_zr, f_hidden, f_slope, f_normed, f_std = fine_saved
     c_zs, c_zr, c_hidden, c_slope, c_normed, c_std = coarse_saved
-    fine_out, fine_pre, g_fine, own_grad, *pieces = call(
+    fine_out, fine_pre, g_fine, own_grad, behind, *pieces = call(
         functools.partial(fine_backward_kernel, block=block), "fine_backward",
         (edge_count, fr, dagg, d_fine, eg, f_std, f_normed, edge_w2, f_slope, edge_w1, fs, base),
         [SM] + [VM] * 8 + [Rows(3), VM, VM],
-        [shape((fine, width), BF16)] * 3 + [shape((own, width), F32)] + [shape((tile, width), BF16)] * slots,
-        scratch=[pltpu.VMEM((space_rows, width), F32)],
+        [shape((fine, width), BF16)] * 3 + [shape((own, width), F32), shape((8, 128), F32)]
+        + [shape((tile, width), BF16)] * slots,
+        scratch=[pltpu.VMEM((fine, width), BF16)] * 2,
         flops=2 * fine * width * (4 * width + space_rows + 2 * own),
     )
     returned = [passed_along(pieces[slot], axis, -offset) for slot, offset in enumerate(offsets)]
     if ordered:
+        node_taken = exchanged(node_given, axis, 2)
+        node_kept, node_given, _ = halving(node_kept, node_taken, (behind,))
         node_taken = exchanged(node_given, axis, 4)
     pair = [Rows(joined=2), None]
     more = [Rows(extra=coarse)]
@@ -688,8 +690,9 @@
         kept2, given2 = first_halving(kept2, taken2)
         taken2 = exchanged(given2, axis, steps2[0])
         for k in range(1, len(steps1)):
-            node_kept, given = halving(node_kept, node_taken)
-            node_taken = exchanged(given, axis, steps2[k])
+            if k > 1:
+                node_kept, given = halving(node_kept, node_taken)
+                node_taken = exchanged(given, axis, steps1[k])
             kept1, given1 = halving(kept1, taken1)
             taken1 = exchanged(given1, axis, steps1[k])
             kept2, given2 = halving(kept2, taken2)

time: 105 us -> 107 us (1.019)
  waiting for transfers between devices: 21 us -> 24.1 us
  starting transfers between devices: 41.3 us -> 39.4 us
  local copies, waits for them, and re-layouts: 4.19 us -> 5.49 us
    ppermute x12, waiting for transfers between devices: 20.6 us -> 23.6 us  [exchanged(): lax.ppermute(block, axis, [(i, i ^ distance) for i in range(lax.axis_size...]
    add x1 -> x0, other arithmetic: 1.32 us -> none  [first_halving(): return (kept[:half].astype(F32) + taken[:half].astype(F32), give)]
    convert_element_type x2 -> x3, other arithmetic: 0.29 us -> 1.59 us  [first_halving(): give = (kept[half:].astype(F32) + taken[half:].astype(F32)).astype(BF16)]
    all_to_all x3, starting transfers between devices: 17.2 us -> 16.1 us  [exchanged_with_all(): return lax.all_to_all(blocks, axis, 0, 0)]
  transfers between devices with their start and end apart: 23 -> 23, of which waited for: 7 -> 8; matrix products, arithmetic and copies ran while one was open for 2% -> 0% of each run, Pallas kernels for 26% -> 26%
where the time goes in v13:
time: 107 us
  starting transfers between devices  39.4 us (37%)
  Pallas kernels  34.7 us (32%)
  waiting for transfers between devices  24.1 us (23%)
  local copies, waits for them, and re-layouts  5.49 us (5%)
  between operations  1.66 us (2%)
  other arithmetic  1.59 us (1%)
    pallas_call x6, Pallas kernels, call(): pl.pallas_call(functools.partial(staged_kernel, kernel, in_specs, out_spe...  32.5 us
    ppermute x12, waiting for transfers between devices, exchanged(): lax.ppermute(block, axis, [(i, i ^ distance) for i in range(lax.axis_size...  23.6 us
    all_to_all x3, starting transfers between devices, exchanged_with_all(): return lax.all_to_all(blocks, axis, 0, 0)  16.1 us
    ppermute x12, starting transfers between devices, exchanged(): lax.ppermute(block, axis, [(i, i ^ distance) for i in range(lax.axis_size...  12.1 us
    ppermute x8, starting transfers between devices, passed_along(): return lax.ppermute(block, axis, route)  11.2 us
    unnamed x44, local copies, waits for them, and re-layouts  4.12 us
    pallas_call x10, Pallas kernels, small_call(): pl.pallas_call(kernel, out_shape=tuple(outs), input_output_aliases={first...  2.21 us
  transfers between devices with their start and end apart: 23, of which 8 were waited for; matrix products, arithmetic and copies ran while one was open for 0% of the time, Pallas kernels for 26%

profile of v13, /device:TPU:0, one launch (start us, length us, event | category | flops | bytes accessed | tf_op | source)
XLA Modules:
  0.0 106.9 jit_solution(4921876784905732870)
XLA Ops:
  0.6 0.7 slice.39
  1.3 0.7 broadcast_in_dim.2
  2.0 7.4 %all-to-all-start = ((bf16[16,8,512]{2,1,0:T(8,128)(2,1)}), bf16[16,8,512]{2,1,0:T(8,128)(2,1)S(1)}, u32[]{:S(2)}, u32[]{:S(2)}) async-start(bf16[16,8,512]{2,1,0:T(8,128)(2,1)} %broadcast_in_dim.2), calls=%async_computation | async-start | bytes 262144 | tf_op jit(solution)/shard_map/all_to_all | solution.py:522
  9.4 2.6 %tiles.1 = (bf16[128,512]{1,0:T(8,128)(2,1)}, bf16[128,512]{1,0:T(8,128)(2,1)}, bf16[128,512]{1,0:T(8,128)(2,1)}, bf16[128,512]{1,0:T(8,128)(2,1)}) custom-call(bf16[256,512]{1,0:T(8,128)(2,1)} %refs_1_.5, s32[4,128]{1,0:T(4,128)} %bitcast.8), custom_call_target="tpu_custom_call" | custom-call | bytes 788480 | tf_op jit(solution)/shard_map/tiles/pallas_call | solution.py:483
  12.0 0.5 collective-permute-start
  12.4 1.7 %collective-permute-start.1 = (bf16[128,512]{1,0:T(8,128)(2,1)}, bf16[128,512]{1,0:T(8,128)(2,1)S(1)}, u32[]{:S(2)}, u32[]{:S(2)}) collective-permute-start(bf16[128,512]{1,0:T(8,128)(2,1)} %get-tuple-element.74), channel_id=1, source_target_pairs={{14,0},{15,1},{0,2},{1,3},{2,4},{3,5},{4,6},{5,7},{6,8},{7,9},{8,1... | collective-permute-start | bytes 393224 | tf_op jit(solution)/shard_map/ppermute | solution.py:514
  14.1 4.0 %collective-permute-start.2 = (bf16[128,512]{1,0:T(8,128)(2,1)}, bf16[128,512]{1,0:T(8,128)(2,1)S(1)}, u32[]{:S(2)}, u32[]{:S(2)}) collective-permute-start(bf16[128,512]{1,0:T(8,128)(2,1)} %get-tuple-element.75), channel_id=1, source_target_pairs={{1,0},{2,1},{3,2},{4,3},{5,4},{6,5},{7,6},{8,7},{9,8},{10,9},{11,1... | collective-permute-start | bytes 393224 | tf_op jit(solution)/shard_map/ppermute | solution.py:514
  18.1 0.3 collective-permute-start.3
  18.4 0.7 copy-done.15
  19.0 4.0 %coarse_forward.1 = (bf16[128,512]{1,0:T(8,128)(2,1)}, bf16[16,8,512]{2,1,0:T(8,128)(2,1)}, bf16[128,512]{1,0:T(8,128)(2,1)}, bf16[128,512]{1,0:T(8,128)(2,1)}, ...) custom-call(bf16[16,8,512]{2,1,0:T(8,128)(2,1)} %copy-done.15, ...), custom_call_target="tpu_custom_call" | custom-call | flops 268435456 | bytes 3345408 | tf_op jit(solution)/shard_map/coarse_forward/pallas_call | solution.py:483
  23.0 4.0 %all-to-all-start.1 = ((bf16[16,8,512]{2,1,0:T(8,128)(2,1)}), bf16[16,8,512]{2,1,0:T(8,128)(2,1)S(1)}, u32[]{:S(2)}, u32[]{:S(2)}) async-start(bf16[16,8,512]{2,1,0:T(8,128)(2,1)} %get-tuple-element.78), calls=%async_computation.1 | async-start | bytes 262144 | tf_op jit(solution)/shard_map/all_to_all | solution.py:522
  27.7 0.0 copy-start.18
  27.8 0.0 copy-start.21
  27.8 0.6 copy-done.18
  28.4 0.0 copy-done.19
  28.4 0.0 copy-done.20
  28.5 0.0 copy-done.21
  28.5 6.7 %fine_forward.1 = (bf16[512,512]{1,0:T(8,128)(2,1)}, f32[256,512]{1,0:T(8,128)}, bf16[512,512]{1,0:T(8,128)(2,1)}, bf16[512,512]{1,0:T(8,128)(2,1)}, bf16[512,51...) custom-call(s32[1]{0:T(128)S(6)} %copy.42.refs_0_, ...), custom_call_target="tpu_custom_call" | custom-call | flops 1879048192 | bytes 7346180 | tf_op jit(solution)/shard_map/fine_forward/pallas_call | solution.py:483
  35.3 0.0 copy-start.17
  35.3 0.6 copy-done.17
  35.9 5.8 %node_both.1 = (bf16[256,512]{1,0:T(8,128)(2,1)}, f32[256,512]{1,0:T(8,128)}, bf16[256,512]{1,0:T(8,128)(2,1)}, bf16[16,8,512]{2,1,0:T(8,128)(2,1)}, bf16[8,96,5...) custom-call(s32[1]{0:T(128)} %bitcast.refs_0_, bf16[256,512]{1,0:T(8,128)(2,1)} %refs_1_.5, ...), custom_call_target="tpu_custom_call" | custom-call | flops 1207959552 | bytes 5507076 | tf_op jit(solution)/shard_map/node_both/pallas_call | solution.py:483
  41.7 0.5 collective-permute-start.4
  42.2 2.1 %collective-permute-done.4 = bf16[8,96,512]{2,1,0:T(8,128)(2,1)S(1)} collective-permute-done((bf16[8,96,512]{2,1,0:T(8,128)(2,1)}, bf16[8,96,512]{2,1,0:T(8,128)(2,1)S(1)}, u32[]{:S(2)}, u32[]{:S(2)}) %collective-permute-start.4) | collective-permute-done | bytes 786464 | tf_op jit(solution)/shard_map/ppermute | solution.py:518
  44.4 1.3 %add_convert_fusion = (bf16[4,96,512]{2,1,0:T(8,128)(2,1)S(1)}, f32[4,96,512]{2,1,0:T(8,128)S(1)}) fusion(bf16[8,96,512]{2,1,0:T(8,128)(2,1)S(1)} %collective-permute-done.4, bf16[8,96,512]{2,1,0:T(8,128)(2,1)} %get-tuple-element.101), kind=kLoop, calls=%fused_computation | loop fusion | flops 1376256 | bytes 2752512 | tf_op jit(solution)/shard_map/convert_element_type | solution.py:527
  45.7 1.9 %collective-permute-start.5 = (bf16[4,96,512]{2,1,0:T(8,128)(2,1)S(1)}, bf16[4,96,512]{2,1,0:T(8,128)(2,1)S(1)}, u32[]{:S(2)}, u32[]{:S(2)}) collective-permute-start(bf16[4,96,512]{2,1,0:T(8,128)(2,1)S(1)} %get-tuple-element.136), channel_id=1, source_target_pairs={{0,2},{1,3},{2,0},{3,1},{4,6},{5,7},{6,4},{7,5},{8,10},{9,11},{10,... | collective-permute-start | bytes 1179656 | tf_op jit(solution)/shard_map/ppermute | solution.py:518
  47.6 4.7 %all-to-all-start.2 = ((bf16[16,8,512]{2,1,0:T(8,128)(2,1)}), bf16[16,8,512]{2,1,0:T(8,128)(2,1)S(1)}, u32[]{:S(2)}, u32[]{:S(2)}) async-start(bf16[16,8,512]{2,1,0:T(8,128)(2,1)} %get-tuple-element.82), calls=%async_computation.2 | async-start | bytes 262144 | tf_op jit(solution)/shard_map/all_to_all | solution.py:522
  52.3 6.6 %fine_backward.1 = (bf16[512,512]{1,0:T(8,128)(2,1)}, bf16[512,512]{1,0:T(8,128)(2,1)}, bf16[512,512]{1,0:T(8,128)(2,1)}, f32[256,512]{1,0:T(8,128)}, f32[8,128]...) custom-call(s32[1]{0:T(128)S(6)} %copy.42.refs_0_, ...), custom_call_target="tpu_custom_call" | custom-call | flops 1744830464 | bytes 7350276 | tf_op jit(solution)/shard_map/fine_backward/pallas_call | solution.py:483
  58.9 0.0 copy-start.12
  58.9 0.7 copy-done.12
  59.6 0.1 halving.6
  59.7 2.0 %collective-permute-start.6 = (bf16[2,96,512]{2,1,0:T(8,128)(2,1)S(1)}, bf16[2,96,512]{2,1,0:T(8,128)(2,1)S(1)}, u32[]{:S(2)}, u32[]{:S(2)}) collective-permute-start(bf16[2,96,512]{2,1,0:T(8,128)(2,1)S(1)} %get-tuple-element.104), channel_id=1, source_target_pairs={{0,4},{1,5},{2,6},{3,7},{4,0},{5,1},{6,2},{7,3},{8,12},{9,13},{10,... | collective-permute-start | bytes 589832 | tf_op jit(solution)/shard_map/ppermute | solution.py:518
  61.6 2.7 %collective-permute-start.7 = (bf16[128,512]{1,0:T(8,128)(2,1)}, bf16[128,512]{1,0:T(8,128)(2,1)S(1)}, u32[]{:S(2)}, u32[]{:S(2)}) collective-permute-start(bf16[128,512]{1,0:T(8,128)(2,1)} %get-tuple-element.105), channel_id=1, source_target_pairs={{1,0},{2,1},{3,2},{4,3},{5,4},{6,5},{7,6},{8,7},{9,8},{10,9},{11,1... | collective-permute-start | bytes 393224 | tf_op jit(solution)/shard_map/ppermute | solution.py:514
  64.4 0.6 collective-permute-start.8
  64.9 0.2 collective-permute-start.9
  65.1 1.3 %collective-permute-start.10 = (bf16[128,512]{1,0:T(8,128)(2,1)}, bf16[128,512]{1,0:T(8,128)(2,1)S(1)}, u32[]{:S(2)}, u32[]{:S(2)}) collective-permute-start(bf16[128,512]{1,0:T(8,128)(2,1)} %get-tuple-element.108), channel_id=1, source_target_pairs={{14,0},{15,1},{0,2},{1,3},{2,4},{3,5},{4,6},{5,7},{6,8},{7,9},{8,1... | collective-permute-start | bytes 393224 | tf_op jit(solution)/shard_map/ppermute | solution.py:514
  66.4 0.7 copy-done.16
  67.1 6.8 %coarse_backward.1 = (bf16[128,512]{1,0:T(8,128)(2,1)}, bf16[8,80,512]{2,1,0:T(8,128)(2,1)}, bf16[8,80,512]{2,1,0:T(8,128)(2,1)}, bf16[8,64,512]{2,1,0:T(8,128)(2,1)}, bf16[8,64,512]{2,1,0:T(8,128)(2,1)}) custom-call(s32[1]{0:T(128)} %bitcast.refs_0_, s32[1,128]{1,0:T(1,128)} %bitcast.17, bf16[16,8,512]{2,1,0:T(8,128)(2,1)} %copy-done.16, ...), custom_call_target="tpu_custom_call" | custom-call | flops 1879048192 | bytes 8850436 | tf_op jit(solution)/shard_map/coarse_backward/pallas_call | solution.py:483
  74.0 0.4 collective-permute-done.10.refs_5_
  74.4 0.2 copy-done.3
  74.6 0.0 copy-done.5
  74.6 0.0 copy-done.7
  74.6 0.4 copy-done.9
  75.0 0.1 copy-done
  75.1 0.5 collective-permute-start.11
  75.6 0.0 collective-permute-start.15
  75.6 1.9 %collective-permute-done.11 = bf16[8,80,512]{2,1,0:T(8,128)(2,1)S(1)} collective-permute-done((bf16[8,80,512]{2,1,0:T(8,128)(2,1)}, bf16[8,80,512]{2,1,0:T(8,128)(2,1)S(1)}, u32[]{:S(2)}, u32[]{:S(2)}) %collective-permute-start.11) | collective-permute-done | bytes 655392 | tf_op jit(solution)/shard_map/ppermute | solution.py:518
  77.5 0.2 add_convert_fusion.1
  77.7 1.8 %collective-permute-start.12 = (bf16[4,80,512]{2,1,0:T(8,128)(2,1)S(1)}, bf16[4,80,512]{2,1,0:T(8,128)(2,1)S(1)}, u32[]{:S(2)}, u32[]{:S(2)}) collective-permute-start(bf16[4,80,512]{2,1,0:T(8,128)(2,1)S(1)} %get-tuple-element.138), channel_id=1, source_target_pairs={{0,2},{1,3},{2,0},{3,1},{4,6},{5,7},{6,4},{7,5},{8,10},{9,11},{10,... | collective-permute-start | bytes 983048 | tf_op jit(solution)/shard_map/ppermute | solution.py:518
  79.5 0.1 add_convert_fusion.2
  79.7 0.1 collective-permute-start.16
  79.7 8.0 %collective-permute-done.12.taken_ref = bf16[4,80,512]{2,1,0:T(8,128)(2,1)S(1)} collective-permute-done((bf16[4,80,512]{2,1,0:T(8,128)(2,1)S(1)}, bf16[4,80,512]{2,1,0:T(8,128)(2,1)S(1)}, u32[]{:S(2)}, u32[]{:S(2)}) %collective-permute-start.12) | collective-permute-done | bytes 327712 | tf_op jit(solution)/shard_map/ppermute | solution.py:518
  87.8 0.1 halving.7
  87.9 0.1 collective-permute-start.13
  88.0 0.1 collective-permute-done.16.taken_ref
  88.1 3.3 %collective-permute-start.17 = (bf16[2,64,512]{2,1,0:T(8,128)(2,1)S(1)}, bf16[2,64,512]{2,1,0:T(8,128)(2,1)S(1)}, u32[]{:S(2)}, u32[]{:S(2)}) collective-permute-start(bf16[2,64,512]{2,1,0:T(8,128)(2,1)S(1)} %get-tuple-element.117), channel_id=1, source_target_pairs={{0,8},{1,9},{2,10},{3,11},{4,12},{5,13},{6,14},{7,15},{8,0},{9,1},... | collective-permute-start | bytes 393224 | tf_op jit(solution)/shard_map/ppermute | solution.py:518
  91.4 0.1 collective-permute-start.19
  91.5 5.3 %collective-permute-done.13.taken_ref = bf16[2,80,512]{2,1,0:T(8,128)(2,1)S(1)} collective-permute-done((bf16[2,80,512]{2,1,0:T(8,128)(2,1)S(1)}, bf16[2,80,512]{2,1,0:T(8,128)(2,1)S(1)}, u32[]{:S(2)}, u32[]{:S(2)}) %collective-permute-start.13) | collective-permute-done | bytes 163872 | tf_op jit(solution)/shard_map/ppermute | solution.py:518
  96.8 0.1 collective-permute-start.14
  96.9 4.8 %collective-permute-done.17.taken_ref = bf16[2,64,512]{2,1,0:T(8,128)(2,1)S(1)} collective-permute-done((bf16[2,64,512]{2,1,0:T(8,128)(2,1)S(1)}, bf16[2,64,512]{2,1,0:T(8,128)(2,1)S(1)}, u32[]{:S(2)}, u32[]{:S(2)}) %collective-permute-start.17) | collective-permute-done | bytes 131104 | tf_op jit(solution)/shard_map/ppermute | solution.py:518
  101.7 1.7 %collective-permute-start.18 = (bf16[1,64,512]{2,1,0:T(8,128)(2,1)S(1)}, bf16[1,64,512]{2,1,0:T(8,128)(2,1)S(1)}, u32[]{:S(2)}, u32[]{:S(2)}) collective-permute-start(bf16[1,64,512]{2,1,0:T(8,128)(2,1)S(1)} %get-tuple-element.119), channel_id=1, source_target_pairs={{0,2},{1,3},{2,0},{3,1},{4,6},{5,7},{6,4},{7,5},{8,10},{9,11},{10,... | collective-permute-start | bytes 196616 | tf_op jit(solution)/shard_map/ppermute | solution.py:518
  103.4 0.4 node_gradient.1.refs_4_
  103.9 0.7 last_sum.3
  104.6 1.5 %collective-permute-done.18.refs_3_ = bf16[1,64,512]{2,1,0:T(8,128)(2,1)S(1)} collective-permute-done((bf16[1,64,512]{2,1,0:T(8,128)(2,1)S(1)}, bf16[1,64,512]{2,1,0:T(8,128)(2,1)S(1)}, u32[]{:S(2)}, u32[]{:S(2)}) %collective-permute-start.18) | collective-permute-done | bytes 65568 | tf_op jit(solution)/shard_map/ppermute | solution.py:518
  106.0 0.8 last_sum.2
  (47 shorter events, 0.2 us)
Async XLA Ops:
  2.0 16.4 %all-to-all-start = ((bf16[16,8,512]{2,1,0:T(8,128)(2,1)}), bf16[16,8,512]{2,1,0:T(8,128)(2,1)S(1)}, u32[]{:S(2)}, u32[]{:S(2)}) async-start(bf16[16,8,512]{2,1,0:T(8,128)(2,1)} %broadcast_in_dim.2), calls=%async_computation | async-start | bytes 262144 | tf_op jit(solution)/shard_map/all_to_all | solution.py:522
  12.0 15.8 %collective-permute-start = (bf16[128,512]{1,0:T(8,128)(2,1)}, bf16[128,512]{1,0:T(8,128)(2,1)S(1)}, u32[]{:S(2)}, u32[]{:S(2)}) collective-permute-start(bf16[128,512]{1,0:T(8,128)(2,1)} %get-tuple-element.73), channel_id=1, source_target_pairs={{15,0},{0,1},{1,2},{2,3},{3,4},{4,5},{5,6},{6,7},{7,8},{8,9},{9,10... | collective-permute-start | bytes 393224 | tf_op jit(solution)/shard_map/ppermute | solution.py:514
  12.4 15.4 %collective-permute-start.1 = (bf16[128,512]{1,0:T(8,128)(2,1)}, bf16[128,512]{1,0:T(8,128)(2,1)S(1)}, u32[]{:S(2)}, u32[]{:S(2)}) collective-permute-start(bf16[128,512]{1,0:T(8,128)(2,1)} %get-tuple-element.74), channel_id=1, source_target_pairs={{14,0},{15,1},{0,2},{1,3},{2,4},{3,5},{4,6},{5,7},{6,8},{7,9},{8,1... | collective-permute-start | bytes 393224 | tf_op jit(solution)/shard_map/ppermute | solution.py:514
  14.1 13.7 %collective-permute-start.2 = (bf16[128,512]{1,0:T(8,128)(2,1)}, bf16[128,512]{1,0:T(8,128)(2,1)S(1)}, u32[]{:S(2)}, u32[]{:S(2)}) collective-permute-start(bf16[128,512]{1,0:T(8,128)(2,1)} %get-tuple-element.75), channel_id=1, source_target_pairs={{1,0},{2,1},{3,2},{4,3},{5,4},{6,5},{7,6},{8,7},{9,8},{10,9},{11,1... | collective-permute-start | bytes 393224 | tf_op jit(solution)/shard_map/ppermute | solution.py:514
  18.1 9.7 %collective-permute-start.3 = (bf16[128,512]{1,0:T(8,128)(2,1)}, bf16[128,512]{1,0:T(8,128)(2,1)S(1)}, u32[]{:S(2)}, u32[]{:S(2)}) collective-permute-start(bf16[128,512]{1,0:T(8,128)(2,1)} %get-tuple-element.76), channel_id=1, source_target_pairs={{2,0},{3,1},{4,2},{5,3},{6,4},{7,5},{8,6},{9,7},{10,8},{11,9},{12,... | collective-permute-start | bytes 393224 | tf_op jit(solution)/shard_map/ppermute | solution.py:514
  18.4 0.7 copy-start.15
  23.0 12.2 %all-to-all-start.1 = ((bf16[16,8,512]{2,1,0:T(8,128)(2,1)}), bf16[16,8,512]{2,1,0:T(8,128)(2,1)S(1)}, u32[]{:S(2)}, u32[]{:S(2)}) async-start(bf16[16,8,512]{2,1,0:T(8,128)(2,1)} %get-tuple-element.78), calls=%async_computation.1 | async-start | bytes 262144 | tf_op jit(solution)/shard_map/all_to_all | solution.py:522
  27.7 0.7 copy-start.18
  27.8 0.7 copy-start.19
  27.8 0.7 copy-start.20
  27.8 0.7 copy-start.21
  35.3 0.7 copy-start.17
  41.7 2.6 %collective-permute-start.4 = (bf16[8,96,512]{2,1,0:T(8,128)(2,1)}, bf16[8,96,512]{2,1,0:T(8,128)(2,1)S(1)}, u32[]{:S(2)}, u32[]{:S(2)}) collective-permute-start(bf16[8,96,512]{2,1,0:T(8,128)(2,1)} %get-tuple-element.102), channel_id=1, source_target_pairs={{0,1},{1,0},{2,3},{3,2},{4,5},{5,4},{6,7},{7,6},{8,9},{9,8},{10,11... | collective-permute-start | bytes 2359304 | tf_op jit(solution)/shard_map/ppermute | solution.py:518
  45.7 13.2 %collective-permute-start.5 = (bf16[4,96,512]{2,1,0:T(8,128)(2,1)S(1)}, bf16[4,96,512]{2,1,0:T(8,128)(2,1)S(1)}, u32[]{:S(2)}, u32[]{:S(2)}) collective-permute-start(bf16[4,96,512]{2,1,0:T(8,128)(2,1)S(1)} %get-tuple-element.136), channel_id=1, source_target_pairs={{0,2},{1,3},{2,0},{3,1},{4,6},{5,7},{6,4},{7,5},{8,10},{9,11},{10,... | collective-permute-start | bytes 1179656 | tf_op jit(solution)/shard_map/ppermute | solution.py:518
  47.6 18.8 %all-to-all-start.2 = ((bf16[16,8,512]{2,1,0:T(8,128)(2,1)}), bf16[16,8,512]{2,1,0:T(8,128)(2,1)S(1)}, u32[]{:S(2)}, u32[]{:S(2)}) async-start(bf16[16,8,512]{2,1,0:T(8,128)(2,1)} %get-tuple-element.82), calls=%async_computation.2 | async-start | bytes 262144 | tf_op jit(solution)/shard_map/all_to_all | solution.py:522
  58.9 0.7 copy-start.12
  59.7 14.7 %collective-permute-start.6 = (bf16[2,96,512]{2,1,0:T(8,128)(2,1)S(1)}, bf16[2,96,512]{2,1,0:T(8,128)(2,1)S(1)}, u32[]{:S(2)}, u32[]{:S(2)}) collective-permute-start(bf16[2,96,512]{2,1,0:T(8,128)(2,1)S(1)} %get-tuple-element.104), channel_id=1, source_target_pairs={{0,4},{1,5},{2,6},{3,7},{4,0},{5,1},{6,2},{7,3},{8,12},{9,13},{10,... | collective-permute-start | bytes 589832 | tf_op jit(solution)/shard_map/ppermute | solution.py:518
  61.6 12.3 %collective-permute-start.7 = (bf16[128,512]{1,0:T(8,128)(2,1)}, bf16[128,512]{1,0:T(8,128)(2,1)S(1)}, u32[]{:S(2)}, u32[]{:S(2)}) collective-permute-start(bf16[128,512]{1,0:T(8,128)(2,1)} %get-tuple-element.105), channel_id=1, source_target_pairs={{1,0},{2,1},{3,2},{4,3},{5,4},{6,5},{7,6},{8,7},{9,8},{10,9},{11,1... | collective-permute-start | bytes 393224 | tf_op jit(solution)/shard_map/ppermute | solution.py:514
  64.4 9.6 %collective-permute-start.8 = (bf16[128,512]{1,0:T(8,128)(2,1)}, bf16[128,512]{1,0:T(8,128)(2,1)S(1)}, u32[]{:S(2)}, u32[]{:S(2)}) collective-permute-start(bf16[128,512]{1,0:T(8,128)(2,1)} %get-tuple-element.106), channel_id=1, source_target_pairs={{2,0},{3,1},{4,2},{5,3},{6,4},{7,5},{8,6},{9,7},{10,8},{11,9},{12,... | collective-permute-start | bytes 393224 | tf_op jit(solution)/shard_map/ppermute | solution.py:514
  64.9 9.0 %collective-permute-start.9 = (bf16[128,512]{1,0:T(8,128)(2,1)}, bf16[128,512]{1,0:T(8,128)(2,1)S(1)}, u32[]{:S(2)}, u32[]{:S(2)}) collective-permute-start(bf16[128,512]{1,0:T(8,128)(2,1)} %get-tuple-element.107), channel_id=1, source_target_pairs={{15,0},{0,1},{1,2},{2,3},{3,4},{4,5},{5,6},{6,7},{7,8},{8,9},{9,10... | collective-permute-start | bytes 393224 | tf_op jit(solution)/shard_map/ppermute | solution.py:514
  65.1 9.2 %collective-permute-start.10 = (bf16[128,512]{1,0:T(8,128)(2,1)}, bf16[128,512]{1,0:T(8,128)(2,1)S(1)}, u32[]{:S(2)}, u32[]{:S(2)}) collective-permute-start(bf16[128,512]{1,0:T(8,128)(2,1)} %get-tuple-element.108), channel_id=1, source_target_pairs={{14,0},{15,1},{0,2},{1,3},{2,4},{3,5},{4,6},{5,7},{6,8},{7,9},{8,1... | collective-permute-start | bytes 393224 | tf_op jit(solution)/shard_map/ppermute | solution.py:514
  66.4 0.7 copy-start.16
  73.9 3.6 %copy-start.13 = (bf16[8,80,512]{2,1,0:T(8,128)(2,1)S(1)}, bf16[8,80,512]{2,1,0:T(8,128)(2,1)}, u32[]{:S(2)}) copy-start(bf16[8,80,512]{2,1,0:T(8,128)(2,1)} %get-tuple-element.99) | copy-start | bytes 1966084
  73.9 0.7 copy-start.3
  73.9 0.7 copy-start.5
  73.9 0.7 copy-start.7
  74.4 0.7 copy-start.9
  74.4 0.7 copy-start
  75.1 4.5 %copy-start.14 = (bf16[8,64,512]{2,1,0:T(8,128)(2,1)S(1)}, bf16[8,64,512]{2,1,0:T(8,128)(2,1)}, u32[]{:S(2)}) copy-start(bf16[8,64,512]{2,1,0:T(8,128)(2,1)} %get-tuple-element.114) | copy-start | bytes 1572868
  75.1 2.4 %collective-permute-start.11 = (bf16[8,80,512]{2,1,0:T(8,128)(2,1)}, bf16[8,80,512]{2,1,0:T(8,128)(2,1)S(1)}, u32[]{:S(2)}, u32[]{:S(2)}) collective-permute-start(bf16[8,80,512]{2,1,0:T(8,128)(2,1)} %get-tuple-element.109), channel_id=1, source_target_pairs={{0,1},{1,0},{2,3},{3,2},{4,5},{5,4},{6,7},{7,6},{8,9},{9,8},{10,11... | collective-permute-start | bytes 1966088 | tf_op jit(solution)/shard_map/ppermute | solution.py:518
  75.6 4.0 %collective-permute-start.15 = (bf16[8,64,512]{2,1,0:T(8,128)(2,1)}, bf16[8,64,512]{2,1,0:T(8,128)(2,1)S(1)}, u32[]{:S(2)}, u32[]{:S(2)}) collective-permute-start(bf16[8,64,512]{2,1,0:T(8,128)(2,1)} %get-tuple-element.115), channel_id=1, source_target_pairs={{0,1},{1,0},{2,3},{3,2},{4,5},{5,4},{6,7},{7,6},{8,9},{9,8},{10,11... | collective-permute-start | bytes 1572872 | tf_op jit(solution)/shard_map/ppermute | solution.py:518
  77.7 10.1 %collective-permute-start.12 = (bf16[4,80,512]{2,1,0:T(8,128)(2,1)S(1)}, bf16[4,80,512]{2,1,0:T(8,128)(2,1)S(1)}, u32[]{:S(2)}, u32[]{:S(2)}) collective-permute-start(bf16[4,80,512]{2,1,0:T(8,128)(2,1)S(1)} %get-tuple-element.138), channel_id=1, source_target_pairs={{0,2},{1,3},{2,0},{3,1},{4,6},{5,7},{6,4},{7,5},{8,10},{9,11},{10,... | collective-permute-start | bytes 983048 | tf_op jit(solution)/shard_map/ppermute | solution.py:518
  79.5 11.9 %copy-start.1 = (bf16[2,96,512]{2,1,0:T(8,128)(2,1)S(1)}, bf16[2,96,512]{2,1,0:T(8,128)(2,1)}, u32[]{:S(2)}) copy-start(bf16[2,96,512]{2,1,0:T(8,128)(2,1)} %get-tuple-element.131.taken_ref) | copy-start | bytes 589828
  79.7 8.4 %collective-permute-start.16 = (bf16[4,64,512]{2,1,0:T(8,128)(2,1)S(1)}, bf16[4,64,512]{2,1,0:T(8,128)(2,1)S(1)}, u32[]{:S(2)}, u32[]{:S(2)}) collective-permute-start(bf16[4,64,512]{2,1,0:T(8,128)(2,1)S(1)} %get-tuple-element.140), channel_id=1, source_target_pairs={{0,4},{1,5},{2,6},{3,7},{4,0},{5,1},{6,2},{7,3},{8,12},{9,13},{10,... | collective-permute-start | bytes 786440 | tf_op jit(solution)/shard_map/ppermute | solution.py:518
  87.8 15.6 %copy-start.2 = (f32[256,512]{1,0:T(8,128)S(1)}, f32[256,512]{1,0:T(8,128)}, u32[]{:S(2)}) copy-start(f32[256,512]{1,0:T(8,128)} %get-tuple-element.120.own_ref) | copy-start | bytes 1572868
  87.8 15.7 %copy-start.4 = (bf16[128,512]{1,0:T(8,128)(2,1)S(1)}, bf16[128,512]{1,0:T(8,128)(2,1)}, u32[]{:S(2)}) copy-start(bf16[128,512]{1,0:T(8,128)(2,1)} %get-tuple-element.121.refs_0_) | copy-start | bytes 393220
  87.8 15.7 %copy-start.6 = (bf16[128,512]{1,0:T(8,128)(2,1)S(1)}, bf16[128,512]{1,0:T(8,128)(2,1)}, u32[]{:S(2)}) copy-start(bf16[128,512]{1,0:T(8,128)(2,1)} %get-tuple-element.122.refs_1_) | copy-start | bytes 393220
  87.8 15.7 %copy-start.8 = (bf16[128,512]{1,0:T(8,128)(2,1)S(1)}, bf16[128,512]{1,0:T(8,128)(2,1)}, u32[]{:S(2)}) copy-start(bf16[128,512]{1,0:T(8,128)(2,1)} %get-tuple-element.123.refs_2_) | copy-start | bytes 393220
  87.8 15.7 %copy-start.10 = (bf16[128,512]{1,0:T(8,128)(2,1)S(1)}, bf16[128,512]{1,0:T(8,128)(2,1)}, u32[]{:S(2)}) copy-start(bf16[128,512]{1,0:T(8,128)(2,1)} %get-tuple-element.124.refs_3_) | copy-start | bytes 393220
  87.8 15.7 %copy-start.11 = (s32[1,4,128]{2,1,0:T(4,128)S(1)}, s32[1,4,128]{2,1,0:T(4,128)}, u32[]{:S(2)}) copy-start(s32[1,4,128]{2,1,0:T(4,128)} %param.25) | copy-start | bytes 6148
  87.9 8.9 %collective-permute-start.13 = (bf16[2,80,512]{2,1,0:T(8,128)(2,1)S(1)}, bf16[2,80,512]{2,1,0:T(8,128)(2,1)S(1)}, u32[]{:S(2)}, u32[]{:S(2)}) collective-permute-start(bf16[2,80,512]{2,1,0:T(8,128)(2,1)S(1)} %get-tuple-element.111), channel_id=1, source_target_pairs={{0,4},{1,5},{2,6},{3,7},{4,0},{5,1},{6,2},{7,3},{8,12},{9,13},{10,... | collective-permute-start | bytes 491528 | tf_op jit(solution)/shard_map/ppermute | solution.py:518
  88.1 13.6 %collective-permute-start.17 = (bf16[2,64,512]{2,1,0:T(8,128)(2,1)S(1)}, bf16[2,64,512]{2,1,0:T(8,128)(2,1)S(1)}, u32[]{:S(2)}, u32[]{:S(2)}) collective-permute-start(bf16[2,64,512]{2,1,0:T(8,128)(2,1)S(1)} %get-tuple-element.117), channel_id=1, source_target_pairs={{0,8},{1,9},{2,10},{3,11},{4,12},{5,13},{6,14},{7,15},{8,0},{9,1},... | collective-permute-start | bytes 393224 | tf_op jit(solution)/shard_map/ppermute | solution.py:518
  91.4 12.4 %collective-permute-start.19 = (bf16[1,96,512]{2,1,0:T(8,128)(2,1)S(1)}, bf16[1,96,512]{2,1,0:T(8,128)(2,1)S(1)}, u32[]{:S(2)}, u32[]{:S(2)}) collective-permute-start(bf16[1,96,512]{2,1,0:T(8,128)(2,1)S(1)} %get-tuple-element.133), channel_id=1, source_target_pairs={{0,8},{1,9},{2,10},{3,11},{4,12},{5,13},{6,14},{7,15},{8,0},{9,1},... | collective-permute-start | bytes 294920 | tf_op jit(solution)/shard_map/ppermute | solution.py:518
  96.8 9.2 %collective-permute-start.14 = (bf16[1,80,512]{2,1,0:T(8,128)(2,1)S(1)}, bf16[1,80,512]{2,1,0:T(8,128)(2,1)S(1)}, u32[]{:S(2)}, u32[]{:S(2)}) collective-permute-start(bf16[1,80,512]{2,1,0:T(8,128)(2,1)S(1)} %get-tuple-element.113), channel_id=1, source_target_pairs={{0,8},{1,9},{2,10},{3,11},{4,12},{5,13},{6,14},{7,15},{8,0},{9,1},... | collective-permute-start | bytes 245768 | tf_op jit(solution)/shard_map/ppermute | solution.py:518
  101.7 4.3 %collective-permute-start.18 = (bf16[1,64,512]{2,1,0:T(8,128)(2,1)S(1)}, bf16[1,64,512]{2,1,0:T(8,128)(2,1)S(1)}, u32[]{:S(2)}, u32[]{:S(2)}) collective-permute-start(bf16[1,64,512]{2,1,0:T(8,128)(2,1)S(1)} %get-tuple-element.119), channel_id=1, source_target_pairs={{0,2},{1,3},{2,0},{3,1},{4,6},{5,7},{6,4},{7,5},{8,10},{9,11},{10,... | collective-permute-start | bytes 196616 | tf_op jit(solution)/shard_map/ppermute | solution.py:518

commit v14 on v11

--- a/solution.py
+++ b/solution.py
@@ -165,7 +165,7 @@
 
 
 def first_rows(rows):
-    return rows * 5 // 6 // 16 * 16
+    return rows
 
 
 def by_distance(me, peers, steps, sums, kept_ref, given_ref):
@@ -181,6 +181,8 @@
         for total, first, last in sums:
             whole = total.shape[0] // peers
             rows = last - first
+            if rows == 0:
+                continue
             part = total[pl.ds(pl.multiple_of(to * whole + first, 8), rows), :]
             if rows % 16:
                 part = jnp.concatenate([part, jnp.zeros((-rows % 16, part.shape[1]), F32)], 0)
@@ -348,7 +350,8 @@
         return
     rest = totals[1]
     first_ref[0:done, :] = totals[0]
-    first_ref[done:cut, :] = rest[: cut - done]
+    if done < cut:
+        first_ref[done:cut, :] = rest[: cut - done]
     start = cut - done + second_ref.shape[0]
     second_ref[...] = rest[cut - done : start]
     g_ref[...] = nodes_ref[...].astype(BF16)
@@ -494,7 +497,7 @@
     )(*ins)
 
 
-def small_call(kernel, name, ins, outs, passing=()):
+def small_call(kernel, name, ins, outs, passing=(), limit=SMALL_LIMIT):
     first = len(ins)
     last = len(outs)
     outs = list(outs) + [shape(a.shape, a.dtype) for a in passing]
@@ -506,7 +509,7 @@
         out_specs=tuple([VM] * last + [ANY] * len(passing)),
         name=name,
         cost_estimate=cost(ins, outs, 0),
-        compiler_params=pltpu.CompilerParams(vmem_limit_bytes=SMALL_LIMIT),
+        compiler_params=pltpu.CompilerParams(vmem_limit_bytes=limit),
     )(*ins, *passing)
 
 
@@ -679,7 +682,7 @@
     if ordered:
         kept1, given1, kept2, given2 = edge_parts
         given1, node_taken, *returned = small_call(
-            order_kernel, "order", (), [], (given1, node_taken, *returned)
+            order_kernel, "order", (), [], (given1, node_taken, *returned), VMEM_LIMIT
         )
         taken1 = exchanged(given1, axis, 1)
         taken2 = exchanged(given2, axis, 1)

time: 103 us -> 103 us (level)
    unnamed x24 -> x44, local copies, waits for them, and re-layouts: 3.79 us -> 3.53 us
where the time goes in v14:
time: 103 us
  starting transfers between devices  43.6 us (42%)
  Pallas kernels  34.4 us (33%)
  waiting for transfers between devices  16.3 us (16%)
  local copies, waits for them, and re-layouts  4.89 us (5%)
  between operations  1.69 us (2%)
  other arithmetic  1.62 us (2%)
    pallas_call x6, Pallas kernels, call(): pl.pallas_call(functools.partial(staged_kernel, kernel, in_specs, out_spe...  32.3 us
    all_to_all x3, starting transfers between devices, exchanged_with_all(): return lax.all_to_all(blocks, axis, 0, 0)  17.1 us
    ppermute x12, waiting for transfers between devices, exchanged(): lax.ppermute(block, axis, [(i, i ^ distance) for i in range(lax.axis_size...  15.9 us
    ppermute x12, starting transfers between devices, exchanged(): lax.ppermute(block, axis, [(i, i ^ distance) for i in range(lax.axis_size...  15.2 us
    ppermute x8, starting transfers between devices, passed_along(): return lax.ppermute(block, axis, route)  11.3 us
    unnamed x44, local copies, waits for them, and re-layouts  3.53 us
    pallas_call x10, Pallas kernels, small_call(): pl.pallas_call(kernel, out_shape=tuple(outs), input_output_aliases={first...  2.19 us
  transfers between devices with their start and end apart: 23, of which 6 were waited for; matrix products, arithmetic and copies ran while one was open for 2% of the time, Pallas kernels for 27%

profile of v14, /device:TPU:0, one launch (start us, length us, event | category | flops | bytes accessed | tf_op | source)
XLA Modules:
  0.0 102.6 jit_solution(9258706389854641619)
XLA Ops:
  0.6 0.7 slice.39
  1.3 0.7 broadcast_in_dim.2
  2.0 7.4 %all-to-all-start = ((bf16[16,8,512]{2,1,0:T(8,128)(2,1)}), bf16[16,8,512]{2,1,0:T(8,128)(2,1)S(1)}, u32[]{:S(2)}, u32[]{:S(2)}) async-start(bf16[16,8,512]{2,1,0:T(8,128)(2,1)} %broadcast_in_dim.2), calls=%async_computation | async-start | bytes 262144 | tf_op jit(solution)/shard_map/all_to_all | solution.py:527
  9.4 2.6 %tiles.1 = (bf16[128,512]{1,0:T(8,128)(2,1)}, bf16[128,512]{1,0:T(8,128)(2,1)}, bf16[128,512]{1,0:T(8,128)(2,1)}, bf16[128,512]{1,0:T(8,128)(2,1)}) custom-call(bf16[256,512]{1,0:T(8,128)(2,1)} %refs_1_.5, s32[4,128]{1,0:T(4,128)} %bitcast.8), custom_call_target="tpu_custom_call" | custom-call | bytes 788480 | tf_op jit(solution)/shard_map/tiles/pallas_call | solution.py:488
  12.0 0.5 collective-permute-start
  12.4 1.7 %collective-permute-start.1 = (bf16[128,512]{1,0:T(8,128)(2,1)}, bf16[128,512]{1,0:T(8,128)(2,1)S(1)}, u32[]{:S(2)}, u32[]{:S(2)}) collective-permute-start(bf16[128,512]{1,0:T(8,128)(2,1)} %get-tuple-element.75), channel_id=1, source_target_pairs={{14,0},{15,1},{0,2},{1,3},{2,4},{3,5},{4,6},{5,7},{6,8},{7,9},{8,1... | collective-permute-start | bytes 393224 | tf_op jit(solution)/shard_map/ppermute | solution.py:519
  14.1 4.0 %collective-permute-start.2 = (bf16[128,512]{1,0:T(8,128)(2,1)}, bf16[128,512]{1,0:T(8,128)(2,1)S(1)}, u32[]{:S(2)}, u32[]{:S(2)}) collective-permute-start(bf16[128,512]{1,0:T(8,128)(2,1)} %get-tuple-element.76), channel_id=1, source_target_pairs={{1,0},{2,1},{3,2},{4,3},{5,4},{6,5},{7,6},{8,7},{9,8},{10,9},{11,1... | collective-permute-start | bytes 393224 | tf_op jit(solution)/shard_map/ppermute | solution.py:519
  18.1 0.3 collective-permute-start.3
  18.4 0.7 copy-done.13
  19.0 4.0 %coarse_forward.1 = (bf16[128,512]{1,0:T(8,128)(2,1)}, bf16[16,8,512]{2,1,0:T(8,128)(2,1)}, bf16[128,512]{1,0:T(8,128)(2,1)}, bf16[128,512]{1,0:T(8,128)(2,1)}, ...) custom-call(bf16[16,8,512]{2,1,0:T(8,128)(2,1)} %copy-done.13, ...), custom_call_target="tpu_custom_call" | custom-call | flops 268435456 | bytes 3345408 | tf_op jit(solution)/shard_map/coarse_forward/pallas_call | solution.py:488
  23.0 4.0 %all-to-all-start.1 = ((bf16[16,8,512]{2,1,0:T(8,128)(2,1)}), bf16[16,8,512]{2,1,0:T(8,128)(2,1)S(1)}, u32[]{:S(2)}, u32[]{:S(2)}) async-start(bf16[16,8,512]{2,1,0:T(8,128)(2,1)} %get-tuple-element.79), calls=%async_computation.1 | async-start | bytes 262144 | tf_op jit(solution)/shard_map/all_to_all | solution.py:527
  27.7 0.0 copy-start.18
  27.8 0.0 copy-start.19
  27.8 0.0 copy-start.20
  27.8 0.0 copy-start.21
  27.8 0.6 copy-done.18
  28.4 0.0 copy-done.19
  28.4 0.0 copy-done.20
  28.5 0.0 copy-done.21
  28.5 6.7 %fine_forward.1 = (bf16[512,512]{1,0:T(8,128)(2,1)}, f32[256,512]{1,0:T(8,128)}, bf16[512,512]{1,0:T(8,128)(2,1)}, bf16[512,512]{1,0:T(8,128)(2,1)}, bf16[512,51...) custom-call(s32[1]{0:T(128)S(6)} %copy.44.refs_0_, ...), custom_call_target="tpu_custom_call" | custom-call | flops 1879048192 | bytes 7346180 | tf_op jit(solution)/shard_map/fine_forward/pallas_call | solution.py:488
  35.3 0.6 copy-done.16
  35.9 5.8 %node_both.1 = (bf16[256,512]{1,0:T(8,128)(2,1)}, f32[256,512]{1,0:T(8,128)}, bf16[256,512]{1,0:T(8,128)(2,1)}, bf16[16,8,512]{2,1,0:T(8,128)(2,1)}, bf16[8,96,5...) custom-call(s32[1]{0:T(128)} %bitcast.refs_0_, bf16[256,512]{1,0:T(8,128)(2,1)} %refs_1_.5, ...), custom_call_target="tpu_custom_call" | custom-call | flops 1207959552 | bytes 5507076 | tf_op jit(solution)/shard_map/node_both/pallas_call | solution.py:488
  41.7 0.5 collective-permute-start.6
  42.2 5.8 %all-to-all-start.2 = ((bf16[16,8,512]{2,1,0:T(8,128)(2,1)}), bf16[16,8,512]{2,1,0:T(8,128)(2,1)S(1)}, u32[]{:S(2)}, u32[]{:S(2)}) async-start(bf16[16,8,512]{2,1,0:T(8,128)(2,1)} %get-tuple-element.83), calls=%async_computation.2 | async-start | bytes 262144 | tf_op jit(solution)/shard_map/all_to_all | solution.py:527
  48.0 1.3 %add_convert_fusion.1 = (bf16[4,96,512]{2,1,0:T(8,128)(2,1)S(1)}, f32[4,96,512]{2,1,0:T(8,128)S(1)}) fusion(bf16[8,96,512]{2,1,0:T(8,128)(2,1)S(1)} %collective-permute-done.6, bf16[8,96,512]{2,1,0:T(8,128)(2,1)} %get-tuple-element.102), kind=kLoop, calls=%fused_computation.2 | loop fusion | flops 1376256 | bytes 2752512 | tf_op jit(solution)/shard_map/convert_element_type | solution.py:532
  49.3 2.0 %collective-permute-start.7 = (bf16[4,96,512]{2,1,0:T(8,128)(2,1)S(1)}, bf16[4,96,512]{2,1,0:T(8,128)(2,1)S(1)}, u32[]{:S(2)}, u32[]{:S(2)}) collective-permute-start(bf16[4,96,512]{2,1,0:T(8,128)(2,1)S(1)} %get-tuple-element.140), channel_id=1, source_target_pairs={{0,4},{1,5},{2,6},{3,7},{4,0},{5,1},{6,2},{7,3},{8,12},{9,13},{10,... | collective-permute-start | bytes 1179656 | tf_op jit(solution)/shard_map/ppermute | solution.py:523
  51.3 6.4 %fine_backward.1 = (bf16[512,512]{1,0:T(8,128)(2,1)}, bf16[512,512]{1,0:T(8,128)(2,1)}, bf16[512,512]{1,0:T(8,128)(2,1)}, f32[256,512]{1,0:T(8,128)}, bf16[128,5...) custom-call(s32[1]{0:T(128)S(6)} %copy.44.refs_0_, ...), custom_call_target="tpu_custom_call" | custom-call | flops 1744830464 | bytes 7346180 | tf_op jit(solution)/shard_map/fine_backward/pallas_call | solution.py:488
  57.7 2.8 %collective-permute-start.8 = (bf16[128,512]{1,0:T(8,128)(2,1)}, bf16[128,512]{1,0:T(8,128)(2,1)S(1)}, u32[]{:S(2)}, u32[]{:S(2)}) collective-permute-start(bf16[128,512]{1,0:T(8,128)(2,1)} %get-tuple-element.105), channel_id=1, source_target_pairs={{1,0},{2,1},{3,2},{4,3},{5,4},{6,5},{7,6},{8,7},{9,8},{10,9},{11,1... | collective-permute-start | bytes 393224 | tf_op jit(solution)/shard_map/ppermute | solution.py:519
  60.5 0.6 collective-permute-start.9
  61.1 0.2 collective-permute-start.10
  61.3 1.3 %collective-permute-start.11 = (bf16[128,512]{1,0:T(8,128)(2,1)}, bf16[128,512]{1,0:T(8,128)(2,1)S(1)}, u32[]{:S(2)}, u32[]{:S(2)}) collective-permute-start(bf16[128,512]{1,0:T(8,128)(2,1)} %get-tuple-element.108), channel_id=1, source_target_pairs={{14,0},{15,1},{0,2},{1,3},{2,4},{3,5},{4,6},{5,7},{6,8},{7,9},{8,1... | collective-permute-start | bytes 393224 | tf_op jit(solution)/shard_map/ppermute | solution.py:519
  62.6 0.7 copy-done.15
  63.2 6.8 %coarse_backward.1 = (bf16[128,512]{1,0:T(8,128)(2,1)}, bf16[8,96,512]{2,1,0:T(8,128)(2,1)}, bf16[8,96,512]{2,1,0:T(8,128)(2,1)}, bf16[8,48,512]{2,1,0:T(8,128)(2,1)}, bf16[8,48,512]{2,1,0:T(8,128)(2,1)}) custom-call(s32[1]{0:T(128)} %bitcast.refs_0_, s32[1,128]{1,0:T(1,128)} %bitcast.17, bf16[16,8,512]{2,1,0:T(8,128)(2,1)} %copy-done.15, ...), custom_call_target="tpu_custom_call" | custom-call | flops 1879048192 | bytes 8850436 | tf_op jit(solution)/shard_map/coarse_backward/pallas_call | solution.py:488
  70.1 0.0 copy-start.5
  70.1 0.4 collective-permute-done.11.refs_5_
  70.5 0.2 copy-done.3
  70.7 0.0 copy-done.5
  70.7 0.0 copy-done.7
  70.8 0.4 copy-done.9
  71.2 0.1 copy-done
  71.3 0.5 collective-permute-start.12
  71.8 0.1 collective-permute-start.4
  71.9 2.4 %collective-permute-done.12 = bf16[8,96,512]{2,1,0:T(8,128)(2,1)S(1)} collective-permute-done((bf16[8,96,512]{2,1,0:T(8,128)(2,1)}, bf16[8,96,512]{2,1,0:T(8,128)(2,1)S(1)}, u32[]{:S(2)}, u32[]{:S(2)}) %collective-permute-start.12) | collective-permute-done | bytes 786464 | tf_op jit(solution)/shard_map/ppermute | solution.py:523
  74.4 0.2 add_convert_fusion
  74.6 0.8 collective-permute-start.13
  75.4 0.1 add_convert_fusion.2
  75.5 0.5 collective-permute-start.5
  76.0 0.1 halving.6
  76.0 3.9 %collective-permute-start.18 = (bf16[2,96,512]{2,1,0:T(8,128)(2,1)S(1)}, bf16[2,96,512]{2,1,0:T(8,128)(2,1)S(1)}, u32[]{:S(2)}, u32[]{:S(2)}) collective-permute-start(bf16[2,96,512]{2,1,0:T(8,128)(2,1)S(1)} %get-tuple-element.133), channel_id=1, source_target_pairs={{0,8},{1,9},{2,10},{3,11},{4,12},{5,13},{6,14},{7,15},{8,0},{9,1},... | collective-permute-start | bytes 589832 | tf_op jit(solution)/shard_map/ppermute | solution.py:523
  79.9 6.3 %collective-permute-done.5.taken_ref = bf16[4,48,512]{2,1,0:T(8,128)(2,1)S(1)} collective-permute-done((bf16[4,48,512]{2,1,0:T(8,128)(2,1)S(1)}, bf16[4,48,512]{2,1,0:T(8,128)(2,1)S(1)}, u32[]{:S(2)}, u32[]{:S(2)}) %collective-permute-start.5) | collective-permute-done | bytes 196640 | tf_op jit(solution)/shard_map/ppermute | solution.py:523
  86.3 0.0 copy-start.8
  86.4 0.0 copy-start.11
  86.4 0.1 halving.8
  86.5 0.1 collective-permute-start.14
  86.5 2.9 %collective-permute-start.16 = (bf16[2,48,512]{2,1,0:T(8,128)(2,1)S(1)}, bf16[2,48,512]{2,1,0:T(8,128)(2,1)S(1)}, u32[]{:S(2)}, u32[]{:S(2)}) collective-permute-start(bf16[2,48,512]{2,1,0:T(8,128)(2,1)S(1)} %get-tuple-element.119), channel_id=1, source_target_pairs={{0,8},{1,9},{2,10},{3,11},{4,12},{5,13},{6,14},{7,15},{8,0},{9,1},... | collective-permute-start | bytes 294920 | tf_op jit(solution)/shard_map/ppermute | solution.py:523
  89.4 1.8 %collective-permute-start.19 = (bf16[1,96,512]{2,1,0:T(8,128)(2,1)S(1)}, bf16[1,96,512]{2,1,0:T(8,128)(2,1)S(1)}, u32[]{:S(2)}, u32[]{:S(2)}) collective-permute-start(bf16[1,96,512]{2,1,0:T(8,128)(2,1)S(1)} %get-tuple-element.135), channel_id=1, source_target_pairs={{0,2},{1,3},{2,0},{3,1},{4,6},{5,7},{6,4},{7,5},{8,10},{9,11},{10,... | collective-permute-start | bytes 294920 | tf_op jit(solution)/shard_map/ppermute | solution.py:523
  91.2 3.8 %collective-permute-done.14.taken_ref = bf16[2,96,512]{2,1,0:T(8,128)(2,1)S(1)} collective-permute-done((bf16[2,96,512]{2,1,0:T(8,128)(2,1)S(1)}, bf16[2,96,512]{2,1,0:T(8,128)(2,1)S(1)}, u32[]{:S(2)}, u32[]{:S(2)}) %collective-permute-start.14) | collective-permute-done | bytes 196640 | tf_op jit(solution)/shard_map/ppermute | solution.py:523
  95.1 0.9 collective-permute-start.15
  96.0 1.3 %collective-permute-start.17 = (bf16[1,48,512]{2,1,0:T(8,128)(2,1)S(1)}, bf16[1,48,512]{2,1,0:T(8,128)(2,1)S(1)}, u32[]{:S(2)}, u32[]{:S(2)}) collective-permute-start(bf16[1,48,512]{2,1,0:T(8,128)(2,1)S(1)} %get-tuple-element.121), channel_id=1, source_target_pairs={{0,2},{1,3},{2,0},{3,1},{4,6},{5,7},{6,4},{7,5},{8,10},{9,11},{10,... | collective-permute-start | bytes 147464 | tf_op jit(solution)/shard_map/ppermute | solution.py:523
  97.3 0.4 node_gradient.1.refs_4_
  97.8 0.7 last_sum.3
  98.5 1.6 %collective-permute-done.17.refs_3_ = bf16[1,48,512]{2,1,0:T(8,128)(2,1)S(1)} collective-permute-done((bf16[1,48,512]{2,1,0:T(8,128)(2,1)S(1)}, bf16[1,48,512]{2,1,0:T(8,128)(2,1)S(1)}, u32[]{:S(2)}, u32[]{:S(2)}) %collective-permute-start.17) | collective-permute-done | bytes 49184 | tf_op jit(solution)/shard_map/ppermute | solution.py:523
  100.1 1.6 %collective-permute-done.15.refs_1_ = bf16[1,96,512]{2,1,0:T(8,128)(2,1)S(1)} collective-permute-done((bf16[1,96,512]{2,1,0:T(8,128)(2,1)S(1)}, bf16[1,96,512]{2,1,0:T(8,128)(2,1)S(1)}, u32[]{:S(2)}, u32[]{:S(2)}) %collective-permute-start.15) | collective-permute-done | bytes 98336 | tf_op jit(solution)/shard_map/ppermute | solution.py:523
  101.8 0.8 last_sum.2
  (47 shorter events, 0.2 us)
Async XLA Ops:
  2.0 16.4 %all-to-all-start = ((bf16[16,8,512]{2,1,0:T(8,128)(2,1)}), bf16[16,8,512]{2,1,0:T(8,128)(2,1)S(1)}, u32[]{:S(2)}, u32[]{:S(2)}) async-start(bf16[16,8,512]{2,1,0:T(8,128)(2,1)} %broadcast_in_dim.2), calls=%async_computation | async-start | bytes 262144 | tf_op jit(solution)/shard_map/all_to_all | solution.py:527
  12.0 15.8 %collective-permute-start = (bf16[128,512]{1,0:T(8,128)(2,1)}, bf16[128,512]{1,0:T(8,128)(2,1)S(1)}, u32[]{:S(2)}, u32[]{:S(2)}) collective-permute-start(bf16[128,512]{1,0:T(8,128)(2,1)} %get-tuple-element.74), channel_id=1, source_target_pairs={{15,0},{0,1},{1,2},{2,3},{3,4},{4,5},{5,6},{6,7},{7,8},{8,9},{9,10... | collective-permute-start | bytes 393224 | tf_op jit(solution)/shard_map/ppermute | solution.py:519
  12.4 15.4 %collective-permute-start.1 = (bf16[128,512]{1,0:T(8,128)(2,1)}, bf16[128,512]{1,0:T(8,128)(2,1)S(1)}, u32[]{:S(2)}, u32[]{:S(2)}) collective-permute-start(bf16[128,512]{1,0:T(8,128)(2,1)} %get-tuple-element.75), channel_id=1, source_target_pairs={{14,0},{15,1},{0,2},{1,3},{2,4},{3,5},{4,6},{5,7},{6,8},{7,9},{8,1... | collective-permute-start | bytes 393224 | tf_op jit(solution)/shard_map/ppermute | solution.py:519
  14.1 13.7 %collective-permute-start.2 = (bf16[128,512]{1,0:T(8,128)(2,1)}, bf16[128,512]{1,0:T(8,128)(2,1)S(1)}, u32[]{:S(2)}, u32[]{:S(2)}) collective-permute-start(bf16[128,512]{1,0:T(8,128)(2,1)} %get-tuple-element.76), channel_id=1, source_target_pairs={{1,0},{2,1},{3,2},{4,3},{5,4},{6,5},{7,6},{8,7},{9,8},{10,9},{11,1... | collective-permute-start | bytes 393224 | tf_op jit(solution)/shard_map/ppermute | solution.py:519
  18.1 9.7 %collective-permute-start.3 = (bf16[128,512]{1,0:T(8,128)(2,1)}, bf16[128,512]{1,0:T(8,128)(2,1)S(1)}, u32[]{:S(2)}, u32[]{:S(2)}) collective-permute-start(bf16[128,512]{1,0:T(8,128)(2,1)} %get-tuple-element.77), channel_id=1, source_target_pairs={{2,0},{3,1},{4,2},{5,3},{6,4},{7,5},{8,6},{9,7},{10,8},{11,9},{12,... | collective-permute-start | bytes 393224 | tf_op jit(solution)/shard_map/ppermute | solution.py:519
  18.4 0.7 copy-start.13
  23.0 12.2 %all-to-all-start.1 = ((bf16[16,8,512]{2,1,0:T(8,128)(2,1)}), bf16[16,8,512]{2,1,0:T(8,128)(2,1)S(1)}, u32[]{:S(2)}, u32[]{:S(2)}) async-start(bf16[16,8,512]{2,1,0:T(8,128)(2,1)} %get-tuple-element.79), calls=%async_computation.1 | async-start | bytes 262144 | tf_op jit(solution)/shard_map/all_to_all | solution.py:527
  27.7 0.7 copy-start.18
  27.8 0.7 copy-start.19
  27.8 0.7 copy-start.20
  27.8 0.7 copy-start.21
  35.3 0.7 copy-start.16
  41.7 6.3 %collective-permute-start.6 = (bf16[8,96,512]{2,1,0:T(8,128)(2,1)}, bf16[8,96,512]{2,1,0:T(8,128)(2,1)S(1)}, u32[]{:S(2)}, u32[]{:S(2)}) collective-permute-start(bf16[8,96,512]{2,1,0:T(8,128)(2,1)} %get-tuple-element.103), channel_id=1, source_target_pairs={{0,1},{1,0},{2,3},{3,2},{4,5},{5,4},{6,7},{7,6},{8,9},{9,8},{10,11... | collective-permute-start | bytes 2359304 | tf_op jit(solution)/shard_map/ppermute | solution.py:523
  42.2 20.3 %all-to-all-start.2 = ((bf16[16,8,512]{2,1,0:T(8,128)(2,1)}), bf16[16,8,512]{2,1,0:T(8,128)(2,1)S(1)}, u32[]{:S(2)}, u32[]{:S(2)}) async-start(bf16[16,8,512]{2,1,0:T(8,128)(2,1)} %get-tuple-element.83), calls=%async_computation.2 | async-start | bytes 262144 | tf_op jit(solution)/shard_map/all_to_all | solution.py:527
  49.3 21.2 %collective-permute-start.7 = (bf16[4,96,512]{2,1,0:T(8,128)(2,1)S(1)}, bf16[4,96,512]{2,1,0:T(8,128)(2,1)S(1)}, u32[]{:S(2)}, u32[]{:S(2)}) collective-permute-start(bf16[4,96,512]{2,1,0:T(8,128)(2,1)S(1)} %get-tuple-element.140), channel_id=1, source_target_pairs={{0,4},{1,5},{2,6},{3,7},{4,0},{5,1},{6,2},{7,3},{8,12},{9,13},{10,... | collective-permute-start | bytes 1179656 | tf_op jit(solution)/shard_map/ppermute | solution.py:523
  57.7 12.3 %collective-permute-start.8 = (bf16[128,512]{1,0:T(8,128)(2,1)}, bf16[128,512]{1,0:T(8,128)(2,1)S(1)}, u32[]{:S(2)}, u32[]{:S(2)}) collective-permute-start(bf16[128,512]{1,0:T(8,128)(2,1)} %get-tuple-element.105), channel_id=1, source_target_pairs={{1,0},{2,1},{3,2},{4,3},{5,4},{6,5},{7,6},{8,7},{9,8},{10,9},{11,1... | collective-permute-start | bytes 393224 | tf_op jit(solution)/shard_map/ppermute | solution.py:519
  60.5 9.5 %collective-permute-start.9 = (bf16[128,512]{1,0:T(8,128)(2,1)}, bf16[128,512]{1,0:T(8,128)(2,1)S(1)}, u32[]{:S(2)}, u32[]{:S(2)}) collective-permute-start(bf16[128,512]{1,0:T(8,128)(2,1)} %get-tuple-element.106), channel_id=1, source_target_pairs={{2,0},{3,1},{4,2},{5,3},{6,4},{7,5},{8,6},{9,7},{10,8},{11,9},{12,... | collective-permute-start | bytes 393224 | tf_op jit(solution)/shard_map/ppermute | solution.py:519
  61.1 9.0 %collective-permute-start.10 = (bf16[128,512]{1,0:T(8,128)(2,1)}, bf16[128,512]{1,0:T(8,128)(2,1)S(1)}, u32[]{:S(2)}, u32[]{:S(2)}) collective-permute-start(bf16[128,512]{1,0:T(8,128)(2,1)} %get-tuple-element.107), channel_id=1, source_target_pairs={{15,0},{0,1},{1,2},{2,3},{3,4},{4,5},{5,6},{6,7},{7,8},{8,9},{9,10... | collective-permute-start | bytes 393224 | tf_op jit(solution)/shard_map/ppermute | solution.py:519
  61.3 9.2 %collective-permute-start.11 = (bf16[128,512]{1,0:T(8,128)(2,1)}, bf16[128,512]{1,0:T(8,128)(2,1)S(1)}, u32[]{:S(2)}, u32[]{:S(2)}) collective-permute-start(bf16[128,512]{1,0:T(8,128)(2,1)} %get-tuple-element.108), channel_id=1, source_target_pairs={{14,0},{15,1},{0,2},{1,3},{2,4},{3,5},{4,6},{5,7},{6,8},{7,9},{8,1... | collective-permute-start | bytes 393224 | tf_op jit(solution)/shard_map/ppermute | solution.py:519
  62.6 0.7 copy-start.15
  70.0 1.8 %copy-start.17 = (bf16[8,48,512]{2,1,0:T(8,128)(2,1)S(1)}, bf16[8,48,512]{2,1,0:T(8,128)(2,1)}, u32[]{:S(2)}) copy-start(bf16[8,48,512]{2,1,0:T(8,128)(2,1)} %get-tuple-element.101) | copy-start | bytes 1179652
  70.0 4.3 %copy-start.12 = (bf16[8,96,512]{2,1,0:T(8,128)(2,1)S(1)}, bf16[8,96,512]{2,1,0:T(8,128)(2,1)}, u32[]{:S(2)}) copy-start(bf16[8,96,512]{2,1,0:T(8,128)(2,1)} %get-tuple-element.110) | copy-start | bytes 2359300
  70.0 0.7 copy-start.3
  70.1 0.7 copy-start.5
  70.1 0.7 copy-start.7
  70.5 0.7 copy-start.9
  70.5 0.8 copy-start
  71.3 4.1 %copy-start.14 = (bf16[8,48,512]{2,1,0:T(8,128)(2,1)S(1)}, bf16[8,48,512]{2,1,0:T(8,128)(2,1)}, u32[]{:S(2)}) copy-start(bf16[8,48,512]{2,1,0:T(8,128)(2,1)} %get-tuple-element.100) | copy-start | bytes 1179652
  71.3 3.1 %collective-permute-start.12 = (bf16[8,96,512]{2,1,0:T(8,128)(2,1)}, bf16[8,96,512]{2,1,0:T(8,128)(2,1)S(1)}, u32[]{:S(2)}, u32[]{:S(2)}) collective-permute-start(bf16[8,96,512]{2,1,0:T(8,128)(2,1)} %get-tuple-element.111), channel_id=1, source_target_pairs={{0,1},{1,0},{2,3},{3,2},{4,5},{5,4},{6,7},{7,6},{8,9},{9,8},{10,11... | collective-permute-start | bytes 2359304 | tf_op jit(solution)/shard_map/ppermute | solution.py:523
  71.8 3.5 %collective-permute-start.4 = (bf16[8,48,512]{2,1,0:T(8,128)(2,1)S(1)}, bf16[8,48,512]{2,1,0:T(8,128)(2,1)S(1)}, u32[]{:S(2)}, u32[]{:S(2)}) collective-permute-start(bf16[8,48,512]{2,1,0:T(8,128)(2,1)S(1)} %copy-done.17), channel_id=1, source_target_pairs={{0,1},{1,0},{2,3},{3,2},{4,5},{5,4},{6,7},{7,6},{8,9},{9,8},{10,11... | collective-permute-start | bytes 1179656 | tf_op jit(solution)/shard_map/ppermute | solution.py:523
  74.4 1.6 %copy-start.1 = (bf16[4,96,512]{2,1,0:T(8,128)(2,1)S(1)}, bf16[4,96,512]{2,1,0:T(8,128)(2,1)}, u32[]{:S(2)}) copy-start(bf16[4,96,512]{2,1,0:T(8,128)(2,1)} %get-tuple-element.109.taken_ref) | copy-start | bytes 1179652
  74.6 11.8 %collective-permute-start.13 = (bf16[4,96,512]{2,1,0:T(8,128)(2,1)S(1)}, bf16[4,96,512]{2,1,0:T(8,128)(2,1)S(1)}, u32[]{:S(2)}, u32[]{:S(2)}) collective-permute-start(bf16[4,96,512]{2,1,0:T(8,128)(2,1)S(1)} %get-tuple-element.138), channel_id=1, source_target_pairs={{0,2},{1,3},{2,0},{3,1},{4,6},{5,7},{6,4},{7,5},{8,10},{9,11},{10,... | collective-permute-start | bytes 1179656 | tf_op jit(solution)/shard_map/ppermute | solution.py:523
  75.5 10.8 %collective-permute-start.5 = (bf16[4,48,512]{2,1,0:T(8,128)(2,1)S(1)}, bf16[4,48,512]{2,1,0:T(8,128)(2,1)S(1)}, u32[]{:S(2)}, u32[]{:S(2)}) collective-permute-start(bf16[4,48,512]{2,1,0:T(8,128)(2,1)S(1)} %get-tuple-element.142), channel_id=1, source_target_pairs={{0,4},{1,5},{2,6},{3,7},{4,0},{5,1},{6,2},{7,3},{8,12},{9,13},{10,... | collective-permute-start | bytes 589832 | tf_op jit(solution)/shard_map/ppermute | solution.py:523
  76.0 13.4 %collective-permute-start.18 = (bf16[2,96,512]{2,1,0:T(8,128)(2,1)S(1)}, bf16[2,96,512]{2,1,0:T(8,128)(2,1)S(1)}, u32[]{:S(2)}, u32[]{:S(2)}) collective-permute-start(bf16[2,96,512]{2,1,0:T(8,128)(2,1)S(1)} %get-tuple-element.133), channel_id=1, source_target_pairs={{0,8},{1,9},{2,10},{3,11},{4,12},{5,13},{6,14},{7,15},{8,0},{9,1},... | collective-permute-start | bytes 589832 | tf_op jit(solution)/shard_map/ppermute | solution.py:523
  86.3 11.0 %copy-start.2 = (f32[256,512]{1,0:T(8,128)S(1)}, f32[256,512]{1,0:T(8,128)}, u32[]{:S(2)}) copy-start(f32[256,512]{1,0:T(8,128)} %get-tuple-element.122.own_ref) | copy-start | bytes 1572868
  86.3 11.0 %copy-start.4 = (bf16[128,512]{1,0:T(8,128)(2,1)S(1)}, bf16[128,512]{1,0:T(8,128)(2,1)}, u32[]{:S(2)}) copy-start(bf16[128,512]{1,0:T(8,128)(2,1)} %get-tuple-element.123.refs_0_) | copy-start | bytes 393220
  86.3 11.0 %copy-start.6 = (bf16[128,512]{1,0:T(8,128)(2,1)S(1)}, bf16[128,512]{1,0:T(8,128)(2,1)}, u32[]{:S(2)}) copy-start(bf16[128,512]{1,0:T(8,128)(2,1)} %get-tuple-element.124.refs_1_) | copy-start | bytes 393220
  86.3 11.0 %copy-start.8 = (bf16[128,512]{1,0:T(8,128)(2,1)S(1)}, bf16[128,512]{1,0:T(8,128)(2,1)}, u32[]{:S(2)}) copy-start(bf16[128,512]{1,0:T(8,128)(2,1)} %get-tuple-element.125.refs_2_) | copy-start | bytes 393220
  86.4 11.0 %copy-start.10 = (bf16[128,512]{1,0:T(8,128)(2,1)S(1)}, bf16[128,512]{1,0:T(8,128)(2,1)}, u32[]{:S(2)}) copy-start(bf16[128,512]{1,0:T(8,128)(2,1)} %get-tuple-element.126.refs_3_) | copy-start | bytes 393220
  86.4 11.0 %copy-start.11 = (s32[1,4,128]{2,1,0:T(4,128)S(1)}, s32[1,4,128]{2,1,0:T(4,128)}, u32[]{:S(2)}) copy-start(s32[1,4,128]{2,1,0:T(4,128)} %param.25) | copy-start | bytes 6148
  86.5 8.6 %collective-permute-start.14 = (bf16[2,96,512]{2,1,0:T(8,128)(2,1)S(1)}, bf16[2,96,512]{2,1,0:T(8,128)(2,1)S(1)}, u32[]{:S(2)}, u32[]{:S(2)}) collective-permute-start(bf16[2,96,512]{2,1,0:T(8,128)(2,1)S(1)} %get-tuple-element.115), channel_id=1, source_target_pairs={{0,4},{1,5},{2,6},{3,7},{4,0},{5,1},{6,2},{7,3},{8,12},{9,13},{10,... | collective-permute-start | bytes 589832 | tf_op jit(solution)/shard_map/ppermute | solution.py:523
  86.5 9.4 %collective-permute-start.16 = (bf16[2,48,512]{2,1,0:T(8,128)(2,1)S(1)}, bf16[2,48,512]{2,1,0:T(8,128)(2,1)S(1)}, u32[]{:S(2)}, u32[]{:S(2)}) collective-permute-start(bf16[2,48,512]{2,1,0:T(8,128)(2,1)S(1)} %get-tuple-element.119), channel_id=1, source_target_pairs={{0,8},{1,9},{2,10},{3,11},{4,12},{5,13},{6,14},{7,15},{8,0},{9,1},... | collective-permute-start | bytes 294920 | tf_op jit(solution)/shard_map/ppermute | solution.py:523
  89.4 8.3 %collective-permute-start.19 = (bf16[1,96,512]{2,1,0:T(8,128)(2,1)S(1)}, bf16[1,96,512]{2,1,0:T(8,128)(2,1)S(1)}, u32[]{:S(2)}, u32[]{:S(2)}) collective-permute-start(bf16[1,96,512]{2,1,0:T(8,128)(2,1)S(1)} %get-tuple-element.135), channel_id=1, source_target_pairs={{0,2},{1,3},{2,0},{3,1},{4,6},{5,7},{6,4},{7,5},{8,10},{9,11},{10,... | collective-permute-start | bytes 294920 | tf_op jit(solution)/shard_map/ppermute | solution.py:523
  95.1 6.7 %collective-permute-start.15 = (bf16[1,96,512]{2,1,0:T(8,128)(2,1)S(1)}, bf16[1,96,512]{2,1,0:T(8,128)(2,1)S(1)}, u32[]{:S(2)}, u32[]{:S(2)}) collective-permute-start(bf16[1,96,512]{2,1,0:T(8,128)(2,1)S(1)} %get-tuple-element.117), channel_id=1, source_target_pairs={{0,8},{1,9},{2,10},{3,11},{4,12},{5,13},{6,14},{7,15},{8,0},{9,1},... | collective-permute-start | bytes 294920 | tf_op jit(solution)/shard_map/ppermute | solution.py:523
  96.0 4.2 %collective-permute-start.17 = (bf16[1,48,512]{2,1,0:T(8,128)(2,1)S(1)}, bf16[1,48,512]{2,1,0:T(8,128)(2,1)S(1)}, u32[]{:S(2)}, u32[]{:S(2)}) collective-permute-start(bf16[1,48,512]{2,1,0:T(8,128)(2,1)S(1)} %get-tuple-element.121), channel_id=1, source_target_pairs={{0,2},{1,3},{2,0},{3,1},{4,6},{5,7},{6,4},{7,5},{8,10},{9,11},{10,... | collective-permute-start | bytes 147464 | tf_op jit(solution)/shard_map/ppermute | solution.py:523

commit v15 on v11

--- a/solution.py
+++ b/solution.py
@@ -604,7 +604,7 @@
     )
     share = exchanged_with_all(coarse_part, axis)
 
-    block = 256 if fine % 256 == 0 else fine
+    block = 512 if fine % 512 == 0 else fine
     space_rows = own + slots * tile
     new_fine, fine_agg, *fine_saved = call(
         functools.partial(fine_forward_kernel, slots=slots, block=block), "fine_forward",

time: 103 us -> 103 us (level)
  no operation moved by 1% of the time
where the time goes in v15:
time: 103 us
  starting transfers between devices  43.1 us (42%)
  Pallas kernels  34.5 us (33%)
  waiting for transfers between devices  16.7 us (16%)
  local copies, waits for them, and re-layouts  5.15 us (5%)
  other arithmetic  1.6 us (2%)
  between operations  1.59 us (2%)
    pallas_call x6, Pallas kernels, call(): pl.pallas_call(functools.partial(staged_kernel, kernel, in_specs, out_spe...  32.3 us
    all_to_all x3, starting transfers between devices, exchanged_with_all(): return lax.all_to_all(blocks, axis, 0, 0)  17.2 us
    ppermute x12, waiting for transfers between devices, exchanged(): lax.ppermute(block, axis, [(i, i ^ distance) for i in range(lax.axis_size...  16.2 us
    ppermute x12, starting transfers between devices, exchanged(): lax.ppermute(block, axis, [(i, i ^ distance) for i in range(lax.axis_size...  14.7 us
    ppermute x8, starting transfers between devices, passed_along(): return lax.ppermute(block, axis, route)  11.3 us
    unnamed x24, local copies, waits for them, and re-layouts  3.79 us
    pallas_call x10, Pallas kernels, small_call(): pl.pallas_call(kernel, out_shape=tuple(outs), input_output_aliases={first...  2.19 us
  transfers between devices with their start and end apart: 23, of which 6 were waited for; matrix products, arithmetic and copies ran while one was open for 2% of the time, Pallas kernels for 27%

profile of v15, /device:TPU:0, one launch (start us, length us, event | category | flops | bytes accessed | tf_op | source)
XLA Modules:
  0.0 102.6 jit_solution(7208617762443419426)
XLA Ops:
  0.6 0.7 slice.39
  1.3 0.7 broadcast_in_dim.2
  2.0 7.4 %all-to-all-start = ((bf16[16,8,512]{2,1,0:T(8,128)(2,1)}), bf16[16,8,512]{2,1,0:T(8,128)(2,1)S(1)}, u32[]{:S(2)}, u32[]{:S(2)}) async-start(bf16[16,8,512]{2,1,0:T(8,128)(2,1)} %broadcast_in_dim.2), calls=%async_computation | async-start | bytes 262144 | tf_op jit(solution)/shard_map/all_to_all | solution.py:524
  9.4 2.6 %tiles.1 = (bf16[128,512]{1,0:T(8,128)(2,1)}, bf16[128,512]{1,0:T(8,128)(2,1)}, bf16[128,512]{1,0:T(8,128)(2,1)}, bf16[128,512]{1,0:T(8,128)(2,1)}) custom-call(bf16[256,512]{1,0:T(8,128)(2,1)} %refs_1_.5, s32[4,128]{1,0:T(4,128)} %bitcast.8), custom_call_target="tpu_custom_call" | custom-call | bytes 788480 | tf_op jit(solution)/shard_map/tiles/pallas_call | solution.py:485
  12.0 0.5 collective-permute-start
  12.4 1.7 %collective-permute-start.1 = (bf16[128,512]{1,0:T(8,128)(2,1)}, bf16[128,512]{1,0:T(8,128)(2,1)S(1)}, u32[]{:S(2)}, u32[]{:S(2)}) collective-permute-start(bf16[128,512]{1,0:T(8,128)(2,1)} %get-tuple-element.75), channel_id=1, source_target_pairs={{14,0},{15,1},{0,2},{1,3},{2,4},{3,5},{4,6},{5,7},{6,8},{7,9},{8,1... | collective-permute-start | bytes 393224 | tf_op jit(solution)/shard_map/ppermute | solution.py:516
  14.1 4.0 %collective-permute-start.2 = (bf16[128,512]{1,0:T(8,128)(2,1)}, bf16[128,512]{1,0:T(8,128)(2,1)S(1)}, u32[]{:S(2)}, u32[]{:S(2)}) collective-permute-start(bf16[128,512]{1,0:T(8,128)(2,1)} %get-tuple-element.76), channel_id=1, source_target_pairs={{1,0},{2,1},{3,2},{4,3},{5,4},{6,5},{7,6},{8,7},{9,8},{10,9},{11,1... | collective-permute-start | bytes 393224 | tf_op jit(solution)/shard_map/ppermute | solution.py:516
  18.1 0.3 collective-permute-start.3
  18.4 0.7 copy-done.5
  19.0 4.0 %coarse_forward.1 = (bf16[128,512]{1,0:T(8,128)(2,1)}, bf16[16,8,512]{2,1,0:T(8,128)(2,1)}, bf16[128,512]{1,0:T(8,128)(2,1)}, bf16[128,512]{1,0:T(8,128)(2,1)}, ...) custom-call(bf16[16,8,512]{2,1,0:T(8,128)(2,1)} %copy-done.5, ...), custom_call_target="tpu_custom_call" | custom-call | flops 268435456 | bytes 3345408 | tf_op jit(solution)/shard_map/coarse_forward/pallas_call | solution.py:485
  23.0 4.0 %all-to-all-start.1 = ((bf16[16,8,512]{2,1,0:T(8,128)(2,1)}), bf16[16,8,512]{2,1,0:T(8,128)(2,1)S(1)}, u32[]{:S(2)}, u32[]{:S(2)}) async-start(bf16[16,8,512]{2,1,0:T(8,128)(2,1)} %get-tuple-element.79), calls=%async_computation.1 | async-start | bytes 262144 | tf_op jit(solution)/shard_map/all_to_all | solution.py:524
  27.7 0.0 collective-permute-done.refs_2_
  27.7 0.0 copy-start.8
  27.8 0.0 copy-start.9
  27.8 0.0 collective-permute-done.2.refs_4_
  27.8 0.0 copy-start.10
  27.8 0.0 collective-permute-done.3.refs_5_
  27.8 0.0 copy-start.11
  27.8 0.6 copy-done.8
  28.4 0.0 copy-done.9
  28.4 0.0 copy-done.10
  28.5 0.0 copy-done.11
  28.5 6.9 %fine_forward.1 = (bf16[512,512]{1,0:T(8,128)(2,1)}, f32[256,512]{1,0:T(8,128)}, bf16[512,512]{1,0:T(8,128)(2,1)}, bf16[512,512]{1,0:T(8,128)(2,1)}, bf16[512,51...) custom-call(s32[1]{0:T(128)S(6)} %copy.44.refs_0_, ...), custom_call_target="tpu_custom_call" | custom-call | flops 1879048192 | bytes 7346180 | tf_op jit(solution)/shard_map/fine_forward/pallas_call | solution.py:485
  35.5 0.0 copy-start.7
  35.5 0.6 copy-done.7
  36.2 5.8 %node_both.1 = (bf16[256,512]{1,0:T(8,128)(2,1)}, f32[256,512]{1,0:T(8,128)}, bf16[256,512]{1,0:T(8,128)(2,1)}, bf16[16,8,512]{2,1,0:T(8,128)(2,1)}, bf16[8,96,5...) custom-call(s32[1]{0:T(128)} %bitcast.refs_0_, bf16[256,512]{1,0:T(8,128)(2,1)} %refs_1_.5, ...), custom_call_target="tpu_custom_call" | custom-call | flops 1207959552 | bytes 5507076 | tf_op jit(solution)/shard_map/node_both/pallas_call | solution.py:485
  42.0 0.5 collective-permute-start.6
  42.5 5.8 %all-to-all-start.2 = ((bf16[16,8,512]{2,1,0:T(8,128)(2,1)}), bf16[16,8,512]{2,1,0:T(8,128)(2,1)S(1)}, u32[]{:S(2)}, u32[]{:S(2)}) async-start(bf16[16,8,512]{2,1,0:T(8,128)(2,1)} %get-tuple-element.83), calls=%async_computation.2 | async-start | bytes 262144 | tf_op jit(solution)/shard_map/all_to_all | solution.py:524
  48.3 1.3 %add_convert_fusion = (bf16[4,96,512]{2,1,0:T(8,128)(2,1)S(1)}, f32[4,96,512]{2,1,0:T(8,128)S(1)}) fusion(bf16[8,96,512]{2,1,0:T(8,128)(2,1)S(1)} %collective-permute-done.6, bf16[8,96,512]{2,1,0:T(8,128)(2,1)} %get-tuple-element.102), kind=kLoop, calls=%fused_computation | loop fusion | flops 1376256 | bytes 2752512 | tf_op jit(solution)/shard_map/convert_element_type | solution.py:529
  49.6 2.0 %collective-permute-start.7 = (bf16[4,96,512]{2,1,0:T(8,128)(2,1)S(1)}, bf16[4,96,512]{2,1,0:T(8,128)(2,1)S(1)}, u32[]{:S(2)}, u32[]{:S(2)}) collective-permute-start(bf16[4,96,512]{2,1,0:T(8,128)(2,1)S(1)} %get-tuple-element.138), channel_id=1, source_target_pairs={{0,4},{1,5},{2,6},{3,7},{4,0},{5,1},{6,2},{7,3},{8,12},{9,13},{10,... | collective-permute-start | bytes 1179656 | tf_op jit(solution)/shard_map/ppermute | solution.py:520
  51.6 6.2 %fine_backward.1 = (bf16[512,512]{1,0:T(8,128)(2,1)}, bf16[512,512]{1,0:T(8,128)(2,1)}, bf16[512,512]{1,0:T(8,128)(2,1)}, f32[256,512]{1,0:T(8,128)}, bf16[128,5...) custom-call(s32[1]{0:T(128)S(6)} %copy.44.refs_0_, ...), custom_call_target="tpu_custom_call" | custom-call | flops 1744830464 | bytes 7346180 | tf_op jit(solution)/shard_map/fine_backward/pallas_call | solution.py:485
  57.8 2.8 %collective-permute-start.8 = (bf16[128,512]{1,0:T(8,128)(2,1)}, bf16[128,512]{1,0:T(8,128)(2,1)S(1)}, u32[]{:S(2)}, u32[]{:S(2)}) collective-permute-start(bf16[128,512]{1,0:T(8,128)(2,1)} %get-tuple-element.105), channel_id=1, source_target_pairs={{1,0},{2,1},{3,2},{4,3},{5,4},{6,5},{7,6},{8,7},{9,8},{10,9},{11,1... | collective-permute-start | bytes 393224 | tf_op jit(solution)/shard_map/ppermute | solution.py:516
  60.6 0.6 collective-permute-start.9
  61.2 0.2 collective-permute-start.10
  61.3 1.3 %collective-permute-start.11 = (bf16[128,512]{1,0:T(8,128)(2,1)}, bf16[128,512]{1,0:T(8,128)(2,1)S(1)}, u32[]{:S(2)}, u32[]{:S(2)}) collective-permute-start(bf16[128,512]{1,0:T(8,128)(2,1)} %get-tuple-element.108), channel_id=1, source_target_pairs={{14,0},{15,1},{0,2},{1,3},{2,4},{3,5},{4,6},{5,7},{6,8},{7,9},{8,1... | collective-permute-start | bytes 393224 | tf_op jit(solution)/shard_map/ppermute | solution.py:516
  62.6 0.7 copy-done.6
  63.3 6.8 %coarse_backward.1 = (bf16[128,512]{1,0:T(8,128)(2,1)}, bf16[8,80,512]{2,1,0:T(8,128)(2,1)}, bf16[8,80,512]{2,1,0:T(8,128)(2,1)}, bf16[8,64,512]{2,1,0:T(8,128)(2,1)}, bf16[8,64,512]{2,1,0:T(8,128)(2,1)}) custom-call(s32[1]{0:T(128)} %bitcast.refs_0_, s32[1,128]{1,0:T(1,128)} %bitcast.17, bf16[16,8,512]{2,1,0:T(8,128)(2,1)} %copy-done.6, ...), custom_call_target="tpu_custom_call" | custom-call | flops 1879048192 | bytes 8850436 | tf_op jit(solution)/shard_map/coarse_backward/pallas_call | solution.py:485
  70.1 0.0 collective-permute-done.8.refs_2_
  70.1 0.5 collective-permute-done.11.refs_5_
  70.6 1.1 %copy-done = bf16[8,80,512]{2,1,0:T(8,128)(2,1)S(1)} copy-done((bf16[8,80,512]{2,1,0:T(8,128)(2,1)S(1)}, bf16[8,80,512]{2,1,0:T(8,128)(2,1)}, u32[]{:S(2)}) %copy-start) | copy-done | bytes 655384
  71.7 0.5 collective-permute-start.12
  72.2 0.1 collective-permute-start.4
  72.3 1.9 %collective-permute-done.12 = bf16[8,80,512]{2,1,0:T(8,128)(2,1)S(1)} collective-permute-done((bf16[8,80,512]{2,1,0:T(8,128)(2,1)S(1)}, bf16[8,80,512]{2,1,0:T(8,128)(2,1)S(1)}, u32[]{:S(2)}, u32[]{:S(2)}) %collective-permute-start.12) | collective-permute-done | bytes 655392 | tf_op jit(solution)/shard_map/ppermute | solution.py:520
  74.1 0.2 add_convert_fusion.1
  74.3 1.0 collective-permute-start.13
  75.3 0.1 add_convert_fusion.2
  75.4 0.3 collective-permute-start.5
  75.7 0.1 halving.6
  75.8 3.9 %collective-permute-start.18 = (bf16[2,96,512]{2,1,0:T(8,128)(2,1)S(1)}, bf16[2,96,512]{2,1,0:T(8,128)(2,1)S(1)}, u32[]{:S(2)}, u32[]{:S(2)}) collective-permute-start(bf16[2,96,512]{2,1,0:T(8,128)(2,1)S(1)} %get-tuple-element.133), channel_id=1, source_target_pairs={{0,8},{1,9},{2,10},{3,11},{4,12},{5,13},{6,14},{7,15},{8,0},{9,1},... | collective-permute-start | bytes 589832 | tf_op jit(solution)/shard_map/ppermute | solution.py:520
  79.7 8.3 %collective-permute-done.5.taken_ref = bf16[4,64,512]{2,1,0:T(8,128)(2,1)S(1)} collective-permute-done((bf16[4,64,512]{2,1,0:T(8,128)(2,1)S(1)}, bf16[4,64,512]{2,1,0:T(8,128)(2,1)S(1)}, u32[]{:S(2)}, u32[]{:S(2)}) %collective-permute-start.5) | collective-permute-done | bytes 262176 | tf_op jit(solution)/shard_map/ppermute | solution.py:520
  88.0 0.1 halving.7
  88.1 0.0 copy-start.2
  88.1 0.1 halving.8
  88.1 0.1 collective-permute-start.14
  88.2 4.1 %collective-permute-start.16 = (bf16[2,64,512]{2,1,0:T(8,128)(2,1)S(1)}, bf16[2,64,512]{2,1,0:T(8,128)(2,1)S(1)}, u32[]{:S(2)}, u32[]{:S(2)}) collective-permute-start(bf16[2,64,512]{2,1,0:T(8,128)(2,1)S(1)} %get-tuple-element.119), channel_id=1, source_target_pairs={{0,8},{1,9},{2,10},{3,11},{4,12},{5,13},{6,14},{7,15},{8,0},{9,1},... | collective-permute-start | bytes 393224 | tf_op jit(solution)/shard_map/ppermute | solution.py:520
  92.3 0.8 collective-permute-start.19
  93.2 3.2 %collective-permute-done.14.taken_ref = bf16[2,80,512]{2,1,0:T(8,128)(2,1)S(1)} collective-permute-done((bf16[2,80,512]{2,1,0:T(8,128)(2,1)S(1)}, bf16[2,80,512]{2,1,0:T(8,128)(2,1)S(1)}, u32[]{:S(2)}, u32[]{:S(2)}) %collective-permute-start.14) | collective-permute-done | bytes 163872 | tf_op jit(solution)/shard_map/ppermute | solution.py:520
  96.4 0.2 collective-permute-start.15
  96.6 1.3 %collective-permute-start.17 = (bf16[1,64,512]{2,1,0:T(8,128)(2,1)S(1)}, bf16[1,64,512]{2,1,0:T(8,128)(2,1)S(1)}, u32[]{:S(2)}, u32[]{:S(2)}) collective-permute-start(bf16[1,64,512]{2,1,0:T(8,128)(2,1)S(1)} %get-tuple-element.121), channel_id=1, source_target_pairs={{0,2},{1,3},{2,0},{3,1},{4,6},{5,7},{6,4},{7,5},{8,10},{9,11},{10,... | collective-permute-start | bytes 196616 | tf_op jit(solution)/shard_map/ppermute | solution.py:520
  97.9 0.4 node_gradient.1.refs_4_
  98.3 0.7 last_sum.3
  99.0 1.9 %collective-permute-done.17.refs_3_ = bf16[1,64,512]{2,1,0:T(8,128)(2,1)S(1)} collective-permute-done((bf16[1,64,512]{2,1,0:T(8,128)(2,1)S(1)}, bf16[1,64,512]{2,1,0:T(8,128)(2,1)S(1)}, u32[]{:S(2)}, u32[]{:S(2)}) %collective-permute-start.17) | collective-permute-done | bytes 65568 | tf_op jit(solution)/shard_map/ppermute | solution.py:520
  100.9 0.9 collective-permute-done.15.refs_1_
  101.8 0.8 last_sum.2
  (27 shorter events, 0.1 us)
Async XLA Ops:
  2.0 16.4 %all-to-all-start = ((bf16[16,8,512]{2,1,0:T(8,128)(2,1)}), bf16[16,8,512]{2,1,0:T(8,128)(2,1)S(1)}, u32[]{:S(2)}, u32[]{:S(2)}) async-start(bf16[16,8,512]{2,1,0:T(8,128)(2,1)} %broadcast_in_dim.2), calls=%async_computation | async-start | bytes 262144 | tf_op jit(solution)/shard_map/all_to_all | solution.py:524
  12.0 15.8 %collective-permute-start = (bf16[128,512]{1,0:T(8,128)(2,1)}, bf16[128,512]{1,0:T(8,128)(2,1)S(1)}, u32[]{:S(2)}, u32[]{:S(2)}) collective-permute-start(bf16[128,512]{1,0:T(8,128)(2,1)} %get-tuple-element.74), channel_id=1, source_target_pairs={{15,0},{0,1},{1,2},{2,3},{3,4},{4,5},{5,6},{6,7},{7,8},{8,9},{9,10... | collective-permute-start | bytes 393224 | tf_op jit(solution)/shard_map/ppermute | solution.py:516
  12.4 15.4 %collective-permute-start.1 = (bf16[128,512]{1,0:T(8,128)(2,1)}, bf16[128,512]{1,0:T(8,128)(2,1)S(1)}, u32[]{:S(2)}, u32[]{:S(2)}) collective-permute-start(bf16[128,512]{1,0:T(8,128)(2,1)} %get-tuple-element.75), channel_id=1, source_target_pairs={{14,0},{15,1},{0,2},{1,3},{2,4},{3,5},{4,6},{5,7},{6,8},{7,9},{8,1... | collective-permute-start | bytes 393224 | tf_op jit(solution)/shard_map/ppermute | solution.py:516
  14.1 13.7 %collective-permute-start.2 = (bf16[128,512]{1,0:T(8,128)(2,1)}, bf16[128,512]{1,0:T(8,128)(2,1)S(1)}, u32[]{:S(2)}, u32[]{:S(2)}) collective-permute-start(bf16[128,512]{1,0:T(8,128)(2,1)} %get-tuple-element.76), channel_id=1, source_target_pairs={{1,0},{2,1},{3,2},{4,3},{5,4},{6,5},{7,6},{8,7},{9,8},{10,9},{11,1... | collective-permute-start | bytes 393224 | tf_op jit(solution)/shard_map/ppermute | solution.py:516
  18.1 9.7 %collective-permute-start.3 = (bf16[128,512]{1,0:T(8,128)(2,1)}, bf16[128,512]{1,0:T(8,128)(2,1)S(1)}, u32[]{:S(2)}, u32[]{:S(2)}) collective-permute-start(bf16[128,512]{1,0:T(8,128)(2,1)} %get-tuple-element.77), channel_id=1, source_target_pairs={{2,0},{3,1},{4,2},{5,3},{6,4},{7,5},{8,6},{9,7},{10,8},{11,9},{12,... | collective-permute-start | bytes 393224 | tf_op jit(solution)/shard_map/ppermute | solution.py:516
  18.4 0.7 copy-start.5
  23.0 12.4 %all-to-all-start.1 = ((bf16[16,8,512]{2,1,0:T(8,128)(2,1)}), bf16[16,8,512]{2,1,0:T(8,128)(2,1)S(1)}, u32[]{:S(2)}, u32[]{:S(2)}) async-start(bf16[16,8,512]{2,1,0:T(8,128)(2,1)} %get-tuple-element.79), calls=%async_computation.1 | async-start | bytes 262144 | tf_op jit(solution)/shard_map/all_to_all | solution.py:524
  27.7 0.7 copy-start.8
  27.8 0.7 copy-start.9
  27.8 0.7 copy-start.10
  27.8 0.7 copy-start.11
  35.5 0.7 copy-start.7
  42.0 6.2 %collective-permute-start.6 = (bf16[8,96,512]{2,1,0:T(8,128)(2,1)}, bf16[8,96,512]{2,1,0:T(8,128)(2,1)S(1)}, u32[]{:S(2)}, u32[]{:S(2)}) collective-permute-start(bf16[8,96,512]{2,1,0:T(8,128)(2,1)} %get-tuple-element.103), channel_id=1, source_target_pairs={{0,1},{1,0},{2,3},{3,2},{4,5},{5,4},{6,7},{7,6},{8,9},{9,8},{10,11... | collective-permute-start | bytes 2359304 | tf_op jit(solution)/shard_map/ppermute | solution.py:520
  42.5 20.2 %all-to-all-start.2 = ((bf16[16,8,512]{2,1,0:T(8,128)(2,1)}), bf16[16,8,512]{2,1,0:T(8,128)(2,1)S(1)}, u32[]{:S(2)}, u32[]{:S(2)}) async-start(bf16[16,8,512]{2,1,0:T(8,128)(2,1)} %get-tuple-element.83), calls=%async_computation.2 | async-start | bytes 262144 | tf_op jit(solution)/shard_map/all_to_all | solution.py:524
  49.6 21.0 %collective-permute-start.7 = (bf16[4,96,512]{2,1,0:T(8,128)(2,1)S(1)}, bf16[4,96,512]{2,1,0:T(8,128)(2,1)S(1)}, u32[]{:S(2)}, u32[]{:S(2)}) collective-permute-start(bf16[4,96,512]{2,1,0:T(8,128)(2,1)S(1)} %get-tuple-element.138), channel_id=1, source_target_pairs={{0,4},{1,5},{2,6},{3,7},{4,0},{5,1},{6,2},{7,3},{8,12},{9,13},{10,... | collective-permute-start | bytes 1179656 | tf_op jit(solution)/shard_map/ppermute | solution.py:520
  57.8 12.3 %collective-permute-start.8 = (bf16[128,512]{1,0:T(8,128)(2,1)}, bf16[128,512]{1,0:T(8,128)(2,1)S(1)}, u32[]{:S(2)}, u32[]{:S(2)}) collective-permute-start(bf16[128,512]{1,0:T(8,128)(2,1)} %get-tuple-element.105), channel_id=1, source_target_pairs={{1,0},{2,1},{3,2},{4,3},{5,4},{6,5},{7,6},{8,7},{9,8},{10,9},{11,1... | collective-permute-start | bytes 393224 | tf_op jit(solution)/shard_map/ppermute | solution.py:516
  60.6 9.5 %collective-permute-start.9 = (bf16[128,512]{1,0:T(8,128)(2,1)}, bf16[128,512]{1,0:T(8,128)(2,1)S(1)}, u32[]{:S(2)}, u32[]{:S(2)}) collective-permute-start(bf16[128,512]{1,0:T(8,128)(2,1)} %get-tuple-element.106), channel_id=1, source_target_pairs={{2,0},{3,1},{4,2},{5,3},{6,4},{7,5},{8,6},{9,7},{10,8},{11,9},{12,... | collective-permute-start | bytes 393224 | tf_op jit(solution)/shard_map/ppermute | solution.py:516
  61.2 8.9 %collective-permute-start.10 = (bf16[128,512]{1,0:T(8,128)(2,1)}, bf16[128,512]{1,0:T(8,128)(2,1)S(1)}, u32[]{:S(2)}, u32[]{:S(2)}) collective-permute-start(bf16[128,512]{1,0:T(8,128)(2,1)} %get-tuple-element.107), channel_id=1, source_target_pairs={{15,0},{0,1},{1,2},{2,3},{3,4},{4,5},{5,6},{6,7},{7,8},{8,9},{9,10... | collective-permute-start | bytes 393224 | tf_op jit(solution)/shard_map/ppermute | solution.py:516
  61.3 9.2 %collective-permute-start.11 = (bf16[128,512]{1,0:T(8,128)(2,1)}, bf16[128,512]{1,0:T(8,128)(2,1)S(1)}, u32[]{:S(2)}, u32[]{:S(2)}) collective-permute-start(bf16[128,512]{1,0:T(8,128)(2,1)} %get-tuple-element.108), channel_id=1, source_target_pairs={{14,0},{15,1},{0,2},{1,3},{2,4},{3,5},{4,6},{5,7},{6,8},{7,9},{8,1... | collective-permute-start | bytes 393224 | tf_op jit(solution)/shard_map/ppermute | solution.py:516
  62.6 0.7 copy-start.6
  70.6 1.1 %copy-start = (bf16[8,80,512]{2,1,0:T(8,128)(2,1)S(1)}, bf16[8,80,512]{2,1,0:T(8,128)(2,1)}, u32[]{:S(2)}) copy-start(bf16[8,80,512]{2,1,0:T(8,128)(2,1)} %get-tuple-element.104.refs_0_) | copy-start | bytes 1966084
  71.6 2.5 %copy-start.3 = (bf16[8,80,512]{2,1,0:T(8,128)(2,1)S(1)}, bf16[8,80,512]{2,1,0:T(8,128)(2,1)}, u32[]{:S(2)}) copy-start(bf16[8,80,512]{2,1,0:T(8,128)(2,1)} %get-tuple-element.110) | copy-start | bytes 1966084
  71.6 3.6 %copy-start.4 = (bf16[8,64,512]{2,1,0:T(8,128)(2,1)S(1)}, bf16[8,64,512]{2,1,0:T(8,128)(2,1)}, u32[]{:S(2)}) copy-start(bf16[8,64,512]{2,1,0:T(8,128)(2,1)} %get-tuple-element.100) | copy-start | bytes 1572868
  71.7 2.5 %collective-permute-start.12 = (bf16[8,80,512]{2,1,0:T(8,128)(2,1)S(1)}, bf16[8,80,512]{2,1,0:T(8,128)(2,1)S(1)}, u32[]{:S(2)}, u32[]{:S(2)}) collective-permute-start(bf16[8,80,512]{2,1,0:T(8,128)(2,1)S(1)} %get-tuple-element.111), channel_id=1, source_target_pairs={{0,1},{1,0},{2,3},{3,2},{4,5},{5,4},{6,7},{7,6},{8,9},{9,8},{10,11... | collective-permute-start | bytes 1966088 | tf_op jit(solution)/shard_map/ppermute | solution.py:520
  72.2 3.1 %collective-permute-start.4 = (bf16[8,64,512]{2,1,0:T(8,128)(2,1)}, bf16[8,64,512]{2,1,0:T(8,128)(2,1)S(1)}, u32[]{:S(2)}, u32[]{:S(2)}) collective-permute-start(bf16[8,64,512]{2,1,0:T(8,128)(2,1)} %get-tuple-element.101), channel_id=1, source_target_pairs={{0,1},{1,0},{2,3},{3,2},{4,5},{5,4},{6,7},{7,6},{8,9},{9,8},{10,11... | collective-permute-start | bytes 1572872 | tf_op jit(solution)/shard_map/ppermute | solution.py:520
  74.3 13.8 %collective-permute-start.13 = (bf16[4,80,512]{2,1,0:T(8,128)(2,1)S(1)}, bf16[4,80,512]{2,1,0:T(8,128)(2,1)S(1)}, u32[]{:S(2)}, u32[]{:S(2)}) collective-permute-start(bf16[4,80,512]{2,1,0:T(8,128)(2,1)S(1)} %get-tuple-element.140), channel_id=1, source_target_pairs={{0,2},{1,3},{2,0},{3,1},{4,6},{5,7},{6,4},{7,5},{8,10},{9,11},{10,... | collective-permute-start | bytes 983048 | tf_op jit(solution)/shard_map/ppermute | solution.py:520
  75.4 12.6 %collective-permute-start.5 = (bf16[4,64,512]{2,1,0:T(8,128)(2,1)S(1)}, bf16[4,64,512]{2,1,0:T(8,128)(2,1)S(1)}, u32[]{:S(2)}, u32[]{:S(2)}) collective-permute-start(bf16[4,64,512]{2,1,0:T(8,128)(2,1)S(1)} %get-tuple-element.142), channel_id=1, source_target_pairs={{0,4},{1,5},{2,6},{3,7},{4,0},{5,1},{6,2},{7,3},{8,12},{9,13},{10,... | collective-permute-start | bytes 786440 | tf_op jit(solution)/shard_map/ppermute | solution.py:520
  75.8 16.5 %collective-permute-start.18 = (bf16[2,96,512]{2,1,0:T(8,128)(2,1)S(1)}, bf16[2,96,512]{2,1,0:T(8,128)(2,1)S(1)}, u32[]{:S(2)}, u32[]{:S(2)}) collective-permute-start(bf16[2,96,512]{2,1,0:T(8,128)(2,1)S(1)} %get-tuple-element.133), channel_id=1, source_target_pairs={{0,8},{1,9},{2,10},{3,11},{4,12},{5,13},{6,14},{7,15},{8,0},{9,1},... | collective-permute-start | bytes 589832 | tf_op jit(solution)/shard_map/ppermute | solution.py:520
  88.0 9.9 %copy-start.1 = (f32[256,512]{1,0:T(8,128)S(1)}, f32[256,512]{1,0:T(8,128)}, u32[]{:S(2)}) copy-start(f32[256,512]{1,0:T(8,128)} %get-tuple-element.122.own_ref) | copy-start | bytes 1572868
  88.1 9.8 %copy-start.2 = (s32[1,4,128]{2,1,0:T(4,128)S(1)}, s32[1,4,128]{2,1,0:T(4,128)}, u32[]{:S(2)}) copy-start(s32[1,4,128]{2,1,0:T(4,128)} %param.25) | copy-start | bytes 6148
  88.1 8.2 %collective-permute-start.14 = (bf16[2,80,512]{2,1,0:T(8,128)(2,1)S(1)}, bf16[2,80,512]{2,1,0:T(8,128)(2,1)S(1)}, u32[]{:S(2)}, u32[]{:S(2)}) collective-permute-start(bf16[2,80,512]{2,1,0:T(8,128)(2,1)S(1)} %get-tuple-element.115), channel_id=1, source_target_pairs={{0,4},{1,5},{2,6},{3,7},{4,0},{5,1},{6,2},{7,3},{8,12},{9,13},{10,... | collective-permute-start | bytes 491528 | tf_op jit(solution)/shard_map/ppermute | solution.py:520
  88.2 8.3 %collective-permute-start.16 = (bf16[2,64,512]{2,1,0:T(8,128)(2,1)S(1)}, bf16[2,64,512]{2,1,0:T(8,128)(2,1)S(1)}, u32[]{:S(2)}, u32[]{:S(2)}) collective-permute-start(bf16[2,64,512]{2,1,0:T(8,128)(2,1)S(1)} %get-tuple-element.119), channel_id=1, source_target_pairs={{0,8},{1,9},{2,10},{3,11},{4,12},{5,13},{6,14},{7,15},{8,0},{9,1},... | collective-permute-start | bytes 393224 | tf_op jit(solution)/shard_map/ppermute | solution.py:520
  92.3 6.0 %collective-permute-start.19 = (bf16[1,96,512]{2,1,0:T(8,128)(2,1)S(1)}, bf16[1,96,512]{2,1,0:T(8,128)(2,1)S(1)}, u32[]{:S(2)}, u32[]{:S(2)}) collective-permute-start(bf16[1,96,512]{2,1,0:T(8,128)(2,1)S(1)} %get-tuple-element.135), channel_id=1, source_target_pairs={{0,2},{1,3},{2,0},{3,1},{4,6},{5,7},{6,4},{7,5},{8,10},{9,11},{10,... | collective-permute-start | bytes 294920 | tf_op jit(solution)/shard_map/ppermute | solution.py:520
  96.4 5.4 %collective-permute-start.15 = (bf16[1,80,512]{2,1,0:T(8,128)(2,1)S(1)}, bf16[1,80,512]{2,1,0:T(8,128)(2,1)S(1)}, u32[]{:S(2)}, u32[]{:S(2)}) collective-permute-start(bf16[1,80,512]{2,1,0:T(8,128)(2,1)S(1)} %get-tuple-element.117), channel_id=1, source_target_pairs={{0,8},{1,9},{2,10},{3,11},{4,12},{5,13},{6,14},{7,15},{8,0},{9,1},... | collective-permute-start | bytes 245768 | tf_op jit(solution)/shard_map/ppermute | solution.py:520
  96.6 4.3 %collective-permute-start.17 = (bf16[1,64,512]{2,1,0:T(8,128)(2,1)S(1)}, bf16[1,64,512]{2,1,0:T(8,128)(2,1)S(1)}, u32[]{:S(2)}, u32[]{:S(2)}) collective-permute-start(bf16[1,64,512]{2,1,0:T(8,128)(2,1)S(1)} %get-tuple-element.121), channel_id=1, source_target_pairs={{0,2},{1,3},{2,0},{3,1},{4,6},{5,7},{6,4},{7,5},{8,10},{9,11},{10,... | collective-permute-start | bytes 196616 | tf_op jit(solution)/shard_map/ppermute | solution.py:520
